TPU v7x, 32 devices: a whole 2x2x4 slice. The times are simulated.
32 devices in a mesh: groups: 2 (over y), gx: 4 (over x, core), gy: 4 (over z).
Axes of the slice: x: 2, y: 2, z: 4, core: 2. Of those that a mesh axis runs over, the one named last changes fastest.
Arguments:
- tokens: bfloat16 [1024, 8192], P(('groups', 'gy'), 'gx'), parts along dimension 0, may hold values from -120 to 120
- gate_matrix: bfloat16 [8192, 26624], P('gx', 'gy'), may hold values from -0.0625 to 0.0625
- up_matrix: bfloat16 [8192, 26624], P('gx', 'gy'), may hold values from -0.0625 to 0.0625
- down_matrix: bfloat16 [26624, 8192], P('gy', 'gx'), may hold values from -0.0390625 to 0.0390625
Outputs:
- mixed: bfloat16 [1024, 8192], P(('groups', 'gy'), 'gx'), parts along dimension 0
There are 2 independent parts, one for each index of `groups`. A program takes and returns all parts, laid end to end along the dimension named above; an argument that names none is the same for every part. Nothing has to cross between parts.
All inputs are finite; a program needn't handle non-finite values.
Results may differ from a plain program's by a relative error of at most 0.019.
Values may be sent and summed in bfloat16 or wider, within the bound.
No kernel may reach another device: no remote copies, remote signals or barrier semaphores. Data moves between devices by JAX's collectives and lax.ppermute only.
A program may use at most 256 MiB of HBM per device.

v0:
```python
import jax
import jax.numpy as jnp
from jax import lax
from jax.sharding import PartitionSpec as P

D = 8192


def on_device(tokens, gate_matrix, up_matrix, down_matrix):
    values = tokens.astype(jnp.float32)
    squares = jnp.sum(values * values, axis=1, keepdims=True)
    totals = lax.psum(squares, "gx")
    normed = (values * lax.rsqrt(totals / D + 1e-05)).astype(jnp.bfloat16)
    gathered = lax.all_gather(normed, "gy", axis=0, tiled=True)
    gate_part = jnp.dot(gathered, gate_matrix, preferred_element_type=jnp.float32)
    up_part = jnp.dot(gathered, up_matrix, preferred_element_type=jnp.float32)
    gate_share, up_share = (
        lax.psum_scatter(
            gate_part.astype(jnp.bfloat16), "gx", scatter_dimension=1, tiled=True
        ).astype(jnp.float32),
        lax.psum_scatter(
            up_part.astype(jnp.bfloat16), "gx", scatter_dimension=1, tiled=True
        ).astype(jnp.float32),
    )
    hidden = (jax.nn.silu(gate_share) * up_share).astype(jnp.bfloat16)
    partial_out = jnp.dot(
        lax.all_gather(hidden, "gx", axis=1, tiled=True),
        down_matrix,
        preferred_element_type=jnp.float32,
    )
    return lax.psum_scatter(partial_out.astype(jnp.bfloat16), "gy", scatter_dimension=0, tiled=True)


def solution(mesh):
    placed = (P(("groups", "gy"), "gx"), P("gx", "gy"), P("gx", "gy"), P("gy", "gx"))
    return jax.shard_map(
        on_device, mesh=mesh, in_specs=placed, out_specs=P(("groups", "gy"), "gx"), check_vma=False
    )
```

profile of v0, /device:TPU:0, one launch (start us, length us, event | category | flops | bytes accessed | tf_op | source)
XLA Modules:
  0.0 348.8 jit_solution(4763802702190729778)
XLA Ops:
  6.5 1.2 fusion.5
  7.8 8.3 %psum.7 = f32[128,1]{0,1:T(1,128)S(1)} all-reduce(f32[128,1]{0,1:T(1,128)S(1)} %bitcast.17), channel_id=1, replica_groups=mesh['groups'=2,'gx'=4,'gy'=4] {'gx'}, use_global_device_ids=true, to_apply=%region_1.0 | all-reduce | flops 128 | bytes 1024 | tf_op jit(solution)/shard_map/psum | solution.py:12
  16.1 2.0 fusion.6
  18.1 0.0 reduce-scatter.12.cloned.1.call-start
  18.2 46.4 %all-gather.3.cloned.1.call-done = bf16[512,2048]{1,0:T(8,128)(2,1)} async-done(((bf16[128,2048]{1,0:T(8,128)(2,1)}), bf16[512,2048]{1,0:T(8,128)(2,1)}) %all-gather.3.cloned.1.call-update) | async-done | bytes 2097168 | tf_op jit(solution)/shard_map/all_gather | solution.py:14
  64.5 21.6 %convolution_convert_fusion = bf16[512,6656]{1,0:T(8,128)(2,1)} fusion(bf16[512,2048]{1,0:T(8,128)(2,1)} %all-gather.3.cloned.1.call-done, bf16[2048,6656]{1,0:T(8,128)(2,1)} %param.6), kind=kOutput, calls=%fused_computation | convolution fusion | flops 13962051584 | bytes 36175872 | tf_op jit(solution)/shard_map/dot_general | solution.py:16
  86.2 9.9 %copy.7 = bf16[512,6656]{0,1:T(8,128)(2,1)} copy(bf16[512,6656]{1,0:T(8,128)(2,1)} %convolution_convert_fusion) | data formatting | bytes 13631488
  96.1 0.0 reduce-scatter.12.cloned.1.call-update
  96.1 0.0 reduce-scatter.10.cloned.1.call-start
  96.2 1.5 copy-done
  97.7 22.6 %convolution_convert_fusion.1 = bf16[512,6656]{1,0:T(8,128)(2,1)} fusion(bf16[512,2048]{1,0:T(8,128)(2,1)S(1)} %copy-done, bf16[2048,6656]{1,0:T(8,128)(2,1)} %param.5), kind=kOutput, calls=%fused_computation.1 | convolution fusion | flops 13962051584 | bytes 36175872 | tf_op jit(solution)/shard_map/dot_general | solution.py:15
  120.3 10.0 %copy.5 = bf16[512,6656]{0,1:T(8,128)(2,1)} copy(bf16[512,6656]{1,0:T(8,128)(2,1)} %convolution_convert_fusion.1) | data formatting | bytes 13631488
  130.3 0.0 reduce-scatter.10.cloned.1.call-update
  130.3 0.2 all-gather.5.cloned.1.call-start
  130.5 26.3 %reduce-scatter.12.cloned.1.call-done = bf16[1664,512]{1,0:T(8,128)(2,1)} async-done(((bf16[6656,512]{1,0:T(8,128)(2,1)}), bf16[1664,512]{1,0:T(8,128)(2,1)}) %reduce-scatter.12.cloned.1.call-update) | async-done | bytes 1703952
  156.8 2.7 copy.8
  159.6 61.9 %reduce-scatter.10.cloned.1.call-done = bf16[1664,512]{1,0:T(8,128)(2,1)} async-done(((bf16[6656,512]{1,0:T(8,128)(2,1)}), bf16[1664,512]{1,0:T(8,128)(2,1)}) %reduce-scatter.10.cloned.1.call-update) | async-done | bytes 1703952
  221.4 2.7 copy.6
  224.2 2.3 fusion.4
  226.5 0.0 all-gather.5.cloned.1.call-update
  226.5 0.0 reduce-scatter.8.cloned.1.call-start
  226.5 49.5 %all-gather.5.cloned.1.call-done = bf16[512,6656]{1,0:T(8,128)(2,1)} async-done(((bf16[512,1664]{1,0:T(8,128)(2,1)}), bf16[512,6656]{1,0:T(8,128)(2,1)}) %all-gather.5.cloned.1.call-update) | async-done | bytes 6815760 | tf_op jit(solution)/shard_map/all_gather | solution.py:27
  276.0 22.2 %convolution_convert_fusion.2 = bf16[512,2048]{1,0:T(8,128)(2,1)} fusion(bf16[512,6656]{1,0:T(8,128)(2,1)} %all-gather.5.cloned.1.call-done, bf16[6656,2048]{1,0:T(8,128)(2,1)} %param.7), kind=kOutput, calls=%fused_computation.9 | convolution fusion | flops 13959692288 | bytes 36175872 | tf_op jit(solution)/shard_map/dot_general | solution.py:26
  298.2 44.0 %reduce-scatter.8.cloned.1.call-done = bf16[128,2048]{1,0:T(8,128)(2,1)} async-done(((bf16[512,2048]{1,0:T(8,128)(2,1)}), bf16[128,2048]{1,0:T(8,128)(2,1)}) %reduce-scatter.8.cloned.1.call-update) | async-done | bytes 524304 | tf_op jit(solution)/shard_map/reduce_scatter | solution.py:31
  (5 shorter events, 0.0 us)
Async XLA Ops:
  6.5 58.0 %all-gather.3.cloned.1.call-start = ((), (), s32[]{:S(2)}) async-start(), calls=%async_computation.3 | async-start | bytes 2621440 | tf_op jit(solution)/shard_map/all_gather | solution.py:14
  18.1 138.7 %reduce-scatter.12.cloned.1.call-start = ((), (), s32[]{:S(2)}) async-start(), calls=%async_computation.7 | async-start | bytes 8519680
  96.1 1.6 copy-start
  96.1 125.3 %reduce-scatter.10.cloned.1.call-start = ((), (), s32[]{:S(2)}) async-start(), calls=%async_computation.6 | async-start | bytes 8519680
  130.3 145.7 %all-gather.5.cloned.1.call-start = ((), (), s32[]{:S(2)}) async-start(), calls=%async_computation.4 | async-start | bytes 8519680 | tf_op jit(solution)/shard_map/all_gather | solution.py:27
  226.5 115.8 %reduce-scatter.8.cloned.1.call-start = ((), (), s32[]{:S(2)}) async-start(), calls=%async_computation.5 | async-start | bytes 2621440 | tf_op jit(solution)/shard_map/reduce_scatter | solution.py:31
Sparse Core Ops, SparseCore 0:
  18.2 46.2 all-gather.2
  96.3 60.5 reduce-scatter.11
  159.5 61.8 reduce-scatter.9
  226.6 49.3 all-gather.4
  298.4 43.8 reduce-scatter.7
where the time goes:
time: 350 us; the launch traced here: 349 us
  waiting for transfers between devices  228 us (65%)
  matrix products  66.5 us (19%)
  local copies, waits for them, and re-layouts  26.9 us (8%)
  between operations  13.2 us (4%)
  blocking collectives  8.34 us (2%)
  other arithmetic  5.48 us (2%)
    unnamed x7, waiting for transfers between devices  88.3 us
    all_gather x1, waiting for transfers between devices, on_device(): lax.all_gather(hidden, 'gx', axis=1, tiled=True)  49.5 us
    all_gather x1, waiting for transfers between devices, on_device(): gathered = lax.all_gather(normed, 'gy', axis=0, tiled=True)  46.4 us
    reduce_scatter x1, waiting for transfers between devices, on_device(): lax.psum_scatter(partial_out.astype(jnp.bfloat16), 'gy', scatter_dimensio...  44 us
    unnamed x6, local copies, waits for them, and re-layouts  26.9 us
    dot_general x1, matrix products, on_device(): jnp.dot(gathered, gate_matrix, preferred_element_type=jnp.float32)  22.6 us
    dot_general x1, matrix products, on_device(): jnp.dot(lax.all_gather(hidden, 'gx', axis=1, tiled=True), down_matrix, pr...  22.2 us
    dot_general x1, matrix products, on_device(): up_part = jnp.dot(gathered, up_matrix, preferred_element_type=jnp.float32)  21.6 us
  transfers between devices with their start and end apart: 5, of which 5 were waited for; matrix products, arithmetic and copies ran while one was open for 10% of the time, Pallas kernels for 0%

commit v1 on v0

v1 whole, which is shorter than its diff:
```python
import functools

import jax
import jax.numpy as jnp
from jax import lax
from jax.experimental import pallas as pl
from jax.experimental.pallas import tpu as pltpu
from jax.sharding import PartitionSpec as P

D = 8192
EPS = 1e-05
LANES = 128
GU_TILE = 256
OUT_TILE = 512
VMEM_LIMIT = 64 * 1024 * 1024 - 64 * 1024
ANY = pl.BlockSpec(memory_space=pl.ANY)
SMEM = pl.BlockSpec(memory_space=pltpu.SMEM)
VMEM = pl.BlockSpec(memory_space=pltpu.VMEM)


def swap(value, axis, size, mask):
    return lax.ppermute(value, axis, [(i, i ^ mask) for i in range(size)])


def silu_product(gate, up, scale):
    gate = gate * scale
    return gate / (1.0 + jnp.exp(-gate)) * (up * scale)


def gu_kernel(n_tok, n_recv, width, with_hidden, start_ref, *refs):
    toks = refs[:n_tok]
    gate_ref, up_ref = refs[n_tok : n_tok + 2]
    recvs = refs[n_tok + 2 : n_tok + 2 + n_recv]
    at = n_tok + 2 + n_recv
    scale_ref = refs[at] if with_hidden else None
    at += 1 if with_hidden else 0
    out_ref, xbuf, wbuf, rbuf, obuf, xsem, wsem, rsem, osem = refs[at + 1 :]
    full, rest = divmod(width, GU_TILE)
    base = pl.multiple_of(start_ref[0], LANES)

    def weights(j, n):
        columns = pl.ds(pl.multiple_of(base + j * GU_TILE, LANES), n)
        return (
            pltpu.make_async_copy(gate_ref.at[:, columns], wbuf.at[j, :, pl.ds(0, n)], wsem.at[0, j]),
            pltpu.make_async_copy(up_ref.at[:, columns], wbuf.at[j, :, pl.ds(n, n)], wsem.at[1, j]),
        )

    def receive(r, j, n):
        columns = pl.ds(pl.multiple_of(j * GU_TILE, LANES), n)
        return pltpu.make_async_copy(recvs[r].at[:, :, columns], rbuf.at[r, j, :, :, pl.ds(0, n)], rsem.at[r, j])

    def write(j, n):
        columns = pl.ds(pl.multiple_of(j * GU_TILE, LANES), n)
        if with_hidden:
            return pltpu.make_async_copy(obuf.at[j, 0, :, pl.ds(0, n)], out_ref.at[:, columns], osem.at[j])
        return pltpu.make_async_copy(obuf.at[j, :, :, pl.ds(0, n)], out_ref.at[:, :, columns], osem.at[j])

    copies, row = [], 0
    for i, tok in enumerate(toks):
        copies.append(pltpu.make_async_copy(tok, xbuf.at[pl.ds(row, tok.shape[0])], xsem.at[i]))
        row += tok.shape[0]
    for copy in copies:
        copy.start()

    def begin(j, n):
        for copy in weights(j, n):
            copy.start()
        for r in range(n_recv):
            receive(r, j, n).start()

    def over_tiles(step):
        if full:
            @pl.loop(0, full)
            def _(j):
                step(j, GU_TILE)
        if rest:
            step(full, rest)

    def multiply(j, n):
        for copy in weights(j, n):
            copy.wait()
        both = jnp.dot(xbuf[...], wbuf[j, :, pl.ds(0, 2 * n)], preferred_element_type=jnp.float32)
        gate, up = both[:, :n], both[:, n:]
        for r in range(n_recv):
            receive(r, j, n).wait()
            gate = gate + rbuf[r, j, 0, :, pl.ds(0, n)].astype(jnp.float32)
            up = up + rbuf[r, j, 1, :, pl.ds(0, n)].astype(jnp.float32)
        if with_hidden:
            obuf[j, 0, :, pl.ds(0, n)] = silu_product(gate, up, scale_ref[...]).astype(jnp.bfloat16)
        else:
            obuf[j, 0, :, pl.ds(0, n)] = gate.astype(jnp.bfloat16)
            obuf[j, 1, :, pl.ds(0, n)] = up.astype(jnp.bfloat16)
        write(j, n).start()

    over_tiles(begin)
    for copy in copies:
        copy.wait()
    over_tiles(multiply)
    over_tiles(lambda j, n: write(j, n).wait())


def gate_up(toks, gate_matrix, up_matrix, start, width, recvs, scale, dep):
    rows, depth = sum(t.shape[0] for t in toks), gate_matrix.shape[0]
    with_hidden = scale is not None
    if width % LANES:
        tok = jnp.concatenate(toks, axis=0)
        gate, up = (
            jnp.dot(tok, lax.dynamic_slice_in_dim(m, start, width, 1), preferred_element_type=jnp.float32)
            for m in (gate_matrix, up_matrix)
        )
        for r in recvs:
            gate, up = gate + r[0].astype(jnp.float32), up + r[1].astype(jnp.float32)
        if with_hidden:
            return silu_product(gate, up, scale).astype(jnp.bfloat16)
        return jnp.stack([gate, up]).astype(jnp.bfloat16)
    tiles = pl.cdiv(width, GU_TILE)
    kernel = functools.partial(gu_kernel, len(toks), len(recvs), width, with_hidden)
    shape = (rows, width) if with_hidden else (2, rows, width)
    n_recv = max(len(recvs), 1)
    return pl.pallas_call(
        kernel,
        out_shape=jax.ShapeDtypeStruct(shape, jnp.bfloat16),
        in_specs=[SMEM] + [ANY] * (len(toks) + 2 + len(recvs)) + [VMEM] * with_hidden + [ANY],
        out_specs=ANY,
        scratch_shapes=[
            pltpu.VMEM((rows, depth), jnp.bfloat16),
            pltpu.VMEM((tiles, depth, 2 * GU_TILE), jnp.bfloat16),
            pltpu.VMEM((n_recv, tiles if recvs else 1, 2, rows if recvs else 16, GU_TILE), jnp.bfloat16),
            pltpu.VMEM((tiles, 1 if with_hidden else 2, rows, GU_TILE), jnp.bfloat16),
            pltpu.SemaphoreType.DMA((len(toks),)),
            pltpu.SemaphoreType.DMA((2, tiles)),
            pltpu.SemaphoreType.DMA((n_recv, tiles)),
            pltpu.SemaphoreType.DMA((tiles,)),
        ],
        compiler_params=pltpu.CompilerParams(vmem_limit_bytes=VMEM_LIMIT),
        cost_estimate=pl.CostEstimate(
            flops=4 * rows * depth * width,
            bytes_accessed=4 * depth * width + 2 * rows * depth + 4 * rows * width * (1 + len(recvs)),
            transcendentals=0,
        ),
        name="gate_up",
    )(
        start.astype(jnp.int32).reshape(1), *toks, gate_matrix, up_matrix, *recvs,
        *([scale] if with_hidden else []), dep,
    )


def down_kernel(n_pieces, with_total, starts_ref, *refs):
    pieces, down_ref = refs[:n_pieces], refs[n_pieces]
    at = n_pieces + 1
    total_ref = refs[at] if with_total else None
    at += 1 if with_total else 0
    out_ref = refs[at + 1]
    at += 2
    hbufs, dbufs = refs[at : at + n_pieces], refs[at + n_pieces : at + 2 * n_pieces]
    tbuf, obuf, hsem, dsem, tsem, osem = refs[at + 2 * n_pieces :]
    tiles, tile = obuf.shape[0], obuf.shape[2]

    def columns(j):
        return pl.ds(pl.multiple_of(j * tile, LANES), tile)

    def weights(p, j):
        rows = pl.ds(pl.multiple_of(starts_ref[p], LANES), dbufs[p].shape[1])
        return pltpu.make_async_copy(down_ref.at[rows, columns(j)], dbufs[p].at[j], dsem.at[p, j])

    def total(j):
        return pltpu.make_async_copy(total_ref.at[:, columns(j)], tbuf.at[j], tsem.at[j])

    def write(j):
        return pltpu.make_async_copy(obuf.at[j], out_ref.at[:, columns(j)], osem.at[j])

    copies = [pltpu.make_async_copy(pieces[p], hbufs[p], hsem.at[p]) for p in range(n_pieces)]
    for copy in copies:
        copy.start()

    @pl.loop(0, tiles)
    def _(j):
        for p in range(n_pieces):
            weights(p, j).start()
        if with_total:
            total(j).start()

    for copy in copies:
        copy.wait()

    @pl.loop(0, tiles)
    def _(j):
        result = None
        for p in range(n_pieces):
            weights(p, j).wait()
            term = jnp.dot(hbufs[p][...], dbufs[p][j], preferred_element_type=jnp.float32)
            result = term if result is None else result + term
        if with_total:
            total(j).wait()
            result = result + tbuf[j]
        obuf[j] = result.astype(obuf.dtype)
        write(j).start()

    @pl.loop(0, tiles)
    def _(j):
        write(j).wait()


def down_product(pieces, starts, down_matrix, total, out_dtype, dep):
    rows, columns = pieces[0].shape[0], down_matrix.shape[1]
    if any(p.shape[1] % LANES for p in pieces) or columns % LANES:
        result = sum(
            jnp.dot(p, lax.dynamic_slice_in_dim(down_matrix, s, p.shape[1], 0), preferred_element_type=jnp.float32)
            for p, s in zip(pieces, starts)
        )
        return (result if total is None else result + total).astype(out_dtype)
    tile = OUT_TILE if columns % OUT_TILE == 0 else LANES
    tiles = columns // tile
    with_total = total is not None
    depth = sum(p.shape[1] for p in pieces)
    return pl.pallas_call(
        functools.partial(down_kernel, len(pieces), with_total),
        out_shape=jax.ShapeDtypeStruct((rows, columns), out_dtype),
        in_specs=[SMEM] + [ANY] * (len(pieces) + 2 + with_total),
        out_specs=ANY,
        scratch_shapes=[pltpu.VMEM(p.shape, jnp.bfloat16) for p in pieces]
        + [pltpu.VMEM((tiles, p.shape[1], tile), jnp.bfloat16) for p in pieces]
        + [
            pltpu.VMEM((tiles, rows, tile) if with_total else (1, 8, LANES), jnp.float32),
            pltpu.VMEM((tiles, rows, tile), out_dtype),
            pltpu.SemaphoreType.DMA((len(pieces),)),
            pltpu.SemaphoreType.DMA((len(pieces), tiles)),
            pltpu.SemaphoreType.DMA((tiles,)),
            pltpu.SemaphoreType.DMA((tiles,)),
        ],
        compiler_params=pltpu.CompilerParams(vmem_limit_bytes=VMEM_LIMIT),
        cost_estimate=pl.CostEstimate(
            flops=2 * rows * depth * columns,
            bytes_accessed=2 * depth * columns + 2 * rows * (depth + 2 * columns),
            transcendentals=0,
        ),
        name="down",
    )(jnp.stack(starts).astype(jnp.int32), *pieces, down_matrix, *([total] if with_total else []), dep)


def on_device(n_gx, n_gy, tokens, gate_matrix, up_matrix, down_matrix):
    features = tokens.shape[1] * n_gx
    width = gate_matrix.shape[1] // n_gx
    me = lax.axis_index("gx")
    far = [2 * k for k in range(1, n_gx // 2)]

    def core(value):
        return swap(value, "gx", n_gx, 1)

    def summed_squares(toks):
        values = jnp.concatenate(toks, axis=0).astype(jnp.float32)
        total = jnp.sum(values * values, axis=1)
        mask = 1
        while mask < n_gx:
            total = total + swap(total, "gx", n_gx, mask)
            mask *= 2
        return lax.rsqrt(total / features + EPS)[:, None]

    blocks = {0: tokens}
    mask = n_gy // 2
    while mask:
        for j in list(blocks):
            blocks[j ^ mask] = swap(blocks[j], "gy", n_gy, mask)
        mask //= 2

    half = (width // LANES + 1) // 2 * LANES if width % LANES == 0 else width // 2
    groups = [[0], list(range(2, n_gy)), [1]]
    scales = [summed_squares([blocks[j] for j in group]) for group in groups]
    jobs = [(0, 0, width), (1, 0, half), (1, half, width - half), (2, 0, width)]
    state = [dict() for _ in jobs]
    chain = [tokens]

    def product(job, piece, recvs, scale=None):
        group, low, n = jobs[job]
        toks = [blocks[j] for j in groups[group]]
        result = gate_up(toks, gate_matrix, up_matrix, piece * width + low, n, recvs, scale, chain[0])
        chain[0] = result
        return result

    def front(job):
        st = state[job]
        lent = [core(product(job, (me ^ k) ^ 1, [])) for k in far]
        st["lent"] = core(product(job, me ^ 1, []))
        st["far"] = [
            swap(product(job, me ^ k, [r]), "gx", n_gx, k) for k, r in zip(far, lent)
        ]

    def own(job):
        st = state[job]
        st["own"] = product(job, me, [st["lent"]])

    def finish(job, fused):
        st = state[job]
        scale = scales[jobs[job][0]]
        if fused:
            hidden = product(job, me, [st["lent"], *st["far"]], scale)
        else:
            both = [r.astype(jnp.float32) for r in [st["own"], *st["far"]]]
            gate, up = sum(b[0] for b in both), sum(b[1] for b in both)
            hidden = silu_product(gate, up, scale).astype(jnp.bfloat16)
        st["near"] = [(hidden, me), (core(hidden), me ^ 1)]
        over = [(swap(hidden, "gx", n_gx, k), me ^ k) for k in far]
        st["over"] = over + [(core(h), q ^ 1) for h, q in over]

    def down(job, pieces, total, dtype):
        low = jobs[job][1]
        result = down_product(
            [h for h, _ in pieces], [q * width + low for _, q in pieces], down_matrix, total, dtype, chain[0]
        )
        chain[0] = result
        return result

    def down_all(job, total, dtype):
        return down(job, state[job]["near"] + state[job]["over"], total, dtype)

    front(0)
    own(0)
    front(1)
    finish(0, False)
    front(2)
    finish(1, True)
    result = down_all(0, None, jnp.float32)
    front(3)
    finish(2, True)
    part = down_all(1, None, jnp.float32)
    own(3)
    part = down_all(2, part, jnp.bfloat16)
    finish(3, False)

    rows = tokens.shape[0]
    parts = {j: part[i * rows : (i + 1) * rows] for i, j in enumerate(groups[1])}
    parts[0] = result
    mask = 1
    while mask < n_gy:
        for j in [j for j in parts if j & mask]:
            arrived = swap(parts.pop(j), "gy", n_gy, mask).astype(jnp.float32)
            total = parts[j ^ mask].astype(jnp.float32) + arrived
            parts[j ^ mask] = total if j == mask else total.astype(jnp.bfloat16)
        mask *= 2

    last = down(3, state[3]["near"], None, jnp.float32)
    last = down(3, state[3]["over"], last, jnp.bfloat16)
    last = swap(last, "gy", n_gy, 1).astype(jnp.float32)
    return (parts[0] + last).astype(jnp.bfloat16)


def solution(mesh):
    n_gx, n_gy = mesh.shape["gx"], mesh.shape["gy"]
    placed = (P(("groups", "gy"), "gx"), P("gx", "gy"), P("gx", "gy"), P("gy", "gx"))
    return jax.shard_map(
        functools.partial(on_device, n_gx, n_gy),
        mesh=mesh,
        in_specs=placed,
        out_specs=P(("groups", "gy"), "gx"),
        check_vma=False,
    )
```

time: 350 us -> 291 us (0.83)
  Pallas kernels: 0 us -> 144 us
  waiting for transfers between devices: 228 us -> 91.1 us
  matrix products: 66.5 us -> 0 us
  starting transfers between devices: 0.35 us -> 27.5 us
  local copies, waits for them, and re-layouts: 26.9 us -> 2.69 us
  other arithmetic: 5.48 us -> 24.8 us
  between operations: 13.2 us -> 0.37 us
  blocking collectives: 8.34 us -> 0 us
    pallas_call x0 -> x21, Pallas kernels: none -> 144 us  [the longest x16 99.2 us: gate_up(): pl.pallas_call(kernel, out_shape=jax.ShapeDtypeStruct(shape, jnp.bfloat16...]
    all_gather x2 -> x0, waiting for transfers between devices: 95.8 us -> none  [the longest x1 49.5 us: on_device(): lax.all_gather(hidden, 'gx', axis=1, tiled=True)]
    ppermute x0 -> x36, waiting for transfers between devices: none -> 91.1 us  [swap(): return lax.ppermute(value, axis, [(i, i ^ mask) for i in range(size)])]
    unnamed x7 -> x0, waiting for transfers between devices: 88.3 us -> none
    dot_general x3 -> x0, matrix products: 66.5 us -> none  [the longest x1 22.6 us: on_device(): jnp.dot(gathered, gate_matrix, preferred_element_type=jnp.float32)]
    reduce_scatter x1 -> x0, waiting for transfers between devices: 44 us -> none  [on_device(): lax.psum_scatter(partial_out.astype(jnp.bfloat16), 'gy', scatter_dimensio...]
    ppermute x0 -> x36, starting transfers between devices: none -> 27.5 us  [swap(): return lax.ppermute(value, axis, [(i, i ^ mask) for i in range(size)])]
    unnamed x6 -> x2, local copies, waits for them, and re-layouts: 26.9 us -> 0.01 us
  transfers between devices with their start and end apart: 5 -> 36, of which waited for: 5 -> 11; matrix products, arithmetic and copies ran while one was open for 10% -> 9% of each run, Pallas kernels for 0% -> 45%
where the time goes in v1:
time: 291 us; the launch traced here: 290 us
  Pallas kernels  144 us (49%)
  waiting for transfers between devices  91.1 us (31%)
  starting transfers between devices  27.5 us (9%)
  other arithmetic  24.8 us (9%)
    pallas_call x16, Pallas kernels, gate_up(): pl.pallas_call(kernel, out_shape=jax.ShapeDtypeStruct(shape, jnp.bfloat16...  99.2 us
    ppermute x36, waiting for transfers between devices, swap(): return lax.ppermute(value, axis, [(i, i ^ mask) for i in range(size)])  91.1 us
    pallas_call x5, Pallas kernels, down_product(): pl.pallas_call(functools.partial(down_kernel, len(pieces), with_total), o...  44.9 us
    ppermute x36, starting transfers between devices, swap(): return lax.ppermute(value, axis, [(i, i ^ mask) for i in range(size)])  27.5 us
    convert_element_type x4, other arithmetic, finish(): both = [r.astype(jnp.float32) for r in [st['own'], *st['far']]]  7.48 us
  transfers between devices with their start and end apart: 36, of which 11 were waited for; matrix products, arithmetic and copies ran while one was open for 9% of the time, Pallas kernels for 45%

profile of v1, /device:TPU:0, one launch (start us, length us, event | category | flops | bytes accessed | tf_op | source)
XLA Modules:
  0.0 290.4 jit_solution(14870120923247861276)
XLA Ops:
  4.0 6.7 %gate_up.16.refs_3_ = bf16[2,128,1664]{2,1,0:T(8,128)(2,1)} custom-call(s32[1]{0:T(128)} %bitcast.3.start_ref, bf16[128,2048]{1,0:T(8,128)(2,1)} %refs_0_.7, bf16[2048,6656]{1,0:T(8,128)(2,1)} %refs_1_.15, bf16[2048,6656]{1,0:T(8,128)(2,1)} %refs_2_.33, bf16[128,2048]{1,0:T(8,128)(2,1)} %refs_0_.7), custom_call_target="tpu_custom_call" | custom-call | flops 1744830464 | bytes 15007744 | tf_op jit(solution)/shard_map/gate_up/pallas_call | solution.py:120
  10.9 6.7 %gate_up.17.refs_4_ = bf16[2,128,1664]{2,1,0:T(8,128)(2,1)} custom-call(s32[1]{0:T(128)} %bitcast.1.start_ref, bf16[128,2048]{1,0:T(8,128)(2,1)} %refs_0_.7, bf16[2048,6656]{1,0:T(8,128)(2,1)} %refs_1_.15, bf16[2048,6656]{1,0:T(8,128)(2,1)} %refs_2_.33, bf16[2,128,1664]{2,1,0:T(8,128)(2,1)} %gate_up.16.refs_3_), custom_call_target="tpu_custom_call" | custom-call | flops 1744830464 | bytes 15007744 | tf_op jit(solution)/shard_map/gate_up/pallas_call | solution.py:120
  18.1 9.4 %collective-permute-done.8.refs_0_ = bf16[128,2048]{1,0:T(8,128)(2,1)} collective-permute-done((bf16[128,2048]{1,0:T(8,128)(2,1)}, bf16[128,2048]{1,0:T(8,128)(2,1)}, u32[]{:S(2)}, u32[]{:S(2)}) %collective-permute-start.8) | collective-permute-done | bytes 524320 | tf_op jit(solution)/shard_map/ppermute | solution.py:22
  28.2 7.0 %gate_up.18.refs_4_ = bf16[2,128,1664]{2,1,0:T(8,128)(2,1)} custom-call(s32[1]{0:T(128)} %bitcast.2.start_ref, bf16[128,2048]{1,0:T(8,128)(2,1)} %refs_0_.7, bf16[2048,6656]{1,0:T(8,128)(2,1)} %refs_1_.15, bf16[2048,6656]{1,0:T(8,128)(2,1)} %refs_2_.33, bf16[2,128,1664]{2,1,0:T(8,128)(2,1)} %collective-permute-done.1.refs_3_, ...), custom_call_target="tpu_custom_call" | custom-call | flops 1744830464 | bytes 15859712 | tf_op jit(solution)/shard_map/gate_up/pallas_call | solution.py:120
  35.3 7.0 %gate_up.19.refs_4_ = bf16[2,128,1664]{2,1,0:T(8,128)(2,1)} custom-call(s32[1]{0:T(128)} %bitcast.start_ref, bf16[128,2048]{1,0:T(8,128)(2,1)} %refs_0_.7, bf16[2048,6656]{1,0:T(8,128)(2,1)} %refs_1_.15, bf16[2048,6656]{1,0:T(8,128)(2,1)} %refs_2_.33, bf16[2,128,1664]{2,1,0:T(8,128)(2,1)} %collective-permute-done.refs_3_, bf16[2,128,1664]{2,1,0:T(8,128)(2,1)} %gate_up.18.refs_4_), custom_call_target="tpu_custom_call" | custom-call | flops 1744830464 | bytes 15859712 | tf_op jit(solution)/shard_map/gate_up/pallas_call | solution.py:120
  42.3 5.3 %gate_up.20.refs_4_ = bf16[2,256,896]{2,1,0:T(8,128)(2,1)} custom-call(s32[1]{0:T(128)} %bitcast.3.start_ref, bf16[128,2048]{1,0:T(8,128)(2,1)} %collective-permute-done.8.refs_0_, bf16[128,2048]{1,0:T(8,128)(2,1)} %collective-permute-done.9.refs_1_, bf16[2048,6656]{1,0:T(8,128)(2,1)} %refs_1_.15, bf16[2048,6656]{1,0:T(8,128)(2,1)} %refs_2_.33, ...), custom_call_target="tpu_custom_call" | custom-call | flops 1879048192 | bytes 9306112 | tf_op jit(solution)/shard_map/gate_up/pallas_call | solution.py:120
  52.2 17.2 %collective-permute-done.4 = f32[128]{0:T(128)S(1)} collective-permute-done((f32[128]{0:T(128)S(1)}, f32[128]{0:T(128)S(1)}, u32[]{:S(2)}, u32[]{:S(2)}) %collective-permute-start.4) | collective-permute-done | bytes 544 | tf_op jit(solution)/shard_map/ppermute | solution.py:22
  72.4 5.3 %gate_up.21.refs_5_ = bf16[2,256,896]{2,1,0:T(8,128)(2,1)} custom-call(s32[1]{0:T(128)} %bitcast.1.start_ref, bf16[128,2048]{1,0:T(8,128)(2,1)} %collective-permute-done.8.refs_0_, bf16[128,2048]{1,0:T(8,128)(2,1)} %collective-permute-done.9.refs_1_, bf16[2048,6656]{1,0:T(8,128)(2,1)} %refs_1_.15, bf16[2048,6656]{1,0:T(8,128)(2,1)} %refs_2_.33, ...), custom_call_target="tpu_custom_call" | custom-call | flops 1879048192 | bytes 9306112 | tf_op jit(solution)/shard_map/gate_up/pallas_call | solution.py:120
  80.2 5.4 %gate_up.22.refs_4_ = bf16[2,256,896]{2,1,0:T(8,128)(2,1)} custom-call(s32[1]{0:T(128)} %bitcast.2.start_ref, bf16[128,2048]{1,0:T(8,128)(2,1)} %collective-permute-done.8.refs_0_, bf16[128,2048]{1,0:T(8,128)(2,1)} %collective-permute-done.9.refs_1_, bf16[2048,6656]{1,0:T(8,128)(2,1)} %refs_1_.15, bf16[2048,6656]{1,0:T(8,128)(2,1)} %refs_2_.33, ...), custom_call_target="tpu_custom_call" | custom-call | flops 1879048192 | bytes 10223616 | tf_op jit(solution)/shard_map/gate_up/pallas_call | solution.py:120
  100.7 17.2 %collective-permute-done.14 = f32[256]{0:T(256)S(1)} collective-permute-done((f32[256]{0:T(256)S(1)}, f32[256]{0:T(256)S(1)}, u32[]{:S(2)}, u32[]{:S(2)}) %collective-permute-start.14) | collective-permute-done | bytes 1056 | tf_op jit(solution)/shard_map/ppermute | solution.py:22
  130.5 7.1 %gate_up.26.refs_5_.refs_0_ = bf16[256,896]{1,0:T(8,128)(2,1)} custom-call(s32[1]{0:T(128)} %bitcast.start_ref, bf16[128,2048]{1,0:T(8,128)(2,1)} %collective-permute-done.8.refs_0_, bf16[128,2048]{1,0:T(8,128)(2,1)} %collective-permute-done.9.refs_1_, bf16[2048,6656]{1,0:T(8,128)(2,1)} %refs_1_.15, bf16[2048,6656]{1,0:T(8,128)(2,1)} %refs_2_.33, ...), custom_call_target="tpu_custom_call" | custom-call | flops 1879048192 | bytes 11141120 | tf_op jit(solution)/shard_map/gate_up/pallas_call | solution.py:120
  137.6 11.9 %down.5.refs_3_ = f32[128,2048]{1,0:T(8,128)} custom-call(s32[4]{0:T(128)} %pad_add_fusion.starts_ref, bf16[128,1664]{1,0:T(8,128)(2,1)} %fusion.9.refs_0_, bf16[128,1664]{1,0:T(8,128)(2,1)} %collective-permute-done.5.refs_1_, bf16[128,1664]{1,0:T(8,128)(2,1)} %collective-permute-done.6.refs_2_, bf16[128,1664]{1,0:T(8,128)(2,1)} %collective-permute-done.7.refs_3_, ...), custom_call_target="tpu_custom_call" | custom-call | flops 3489660928 | bytes 30015488 | tf_op jit(solution)/shard_map/down/pallas_call | solution.py:216
  149.5 6.7 %gate_up.27.refs_3_ = bf16[2,128,1664]{2,1,0:T(8,128)(2,1)} custom-call(s32[1]{0:T(128)} %bitcast.3.start_ref, bf16[128,2048]{1,0:T(8,128)(2,1)} %collective-permute-done.18.refs_0_, bf16[2048,6656]{1,0:T(8,128)(2,1)} %refs_1_.15, bf16[2048,6656]{1,0:T(8,128)(2,1)} %refs_2_.33, f32[128,2048]{1,0:T(8,128)} %down.5.refs_3_), custom_call_target="tpu_custom_call" | custom-call | flops 1744830464 | bytes 15007744 | tf_op jit(solution)/shard_map/gate_up/pallas_call | solution.py:120
  163.4 6.7 %gate_up.28.refs_4_ = bf16[2,128,1664]{2,1,0:T(8,128)(2,1)} custom-call(s32[1]{0:T(128)} %bitcast.1.start_ref, bf16[128,2048]{1,0:T(8,128)(2,1)} %collective-permute-done.18.refs_0_, bf16[2048,6656]{1,0:T(8,128)(2,1)} %refs_1_.15, bf16[2048,6656]{1,0:T(8,128)(2,1)} %refs_2_.33, bf16[2,128,1664]{2,1,0:T(8,128)(2,1)} %gate_up.27.refs_3_), custom_call_target="tpu_custom_call" | custom-call | flops 1744830464 | bytes 15007744 | tf_op jit(solution)/shard_map/gate_up/pallas_call | solution.py:120
  170.1 16.4 %collective-permute-done.31 = f32[128]{0:T(128)} collective-permute-done((f32[128]{0:T(128)}, f32[128]{0:T(128)}, u32[]{:S(2)}, u32[]{:S(2)}) %collective-permute-start.31) | collective-permute-done | bytes 544 | tf_op jit(solution)/shard_map/ppermute | solution.py:22
  187.1 7.0 %gate_up.29.refs_7_ = bf16[2,128,1664]{2,1,0:T(8,128)(2,1)} custom-call(s32[1]{0:T(128)} %bitcast.2.start_ref, bf16[128,2048]{1,0:T(8,128)(2,1)} %collective-permute-done.18.refs_0_, bf16[2048,6656]{1,0:T(8,128)(2,1)} %refs_1_.15, bf16[2048,6656]{1,0:T(8,128)(2,1)} %refs_2_.33, bf16[2,128,1664]{2,1,0:T(8,128)(2,1)} %collective-permute-done.19.refs_3_, ...), custom_call_target="tpu_custom_call" | custom-call | flops 1744830464 | bytes 15859712 | tf_op jit(solution)/shard_map/gate_up/pallas_call | solution.py:120
  196.9 6.5 %gate_up.30.refs_5_.refs_0_ = bf16[256,768]{1,0:T(8,128)(2,1)} custom-call(s32[1]{0:T(128)} %bitcast.10.start_ref, bf16[128,2048]{1,0:T(8,128)(2,1)} %collective-permute-done.8.refs_0_, bf16[128,2048]{1,0:T(8,128)(2,1)} %collective-permute-done.9.refs_1_, bf16[2048,6656]{1,0:T(8,128)(2,1)} %refs_1_.15, bf16[2048,6656]{1,0:T(8,128)(2,1)} %refs_2_.33, ...), custom_call_target="tpu_custom_call" | custom-call | flops 1610612736 | bytes 9699328 | tf_op jit(solution)/shard_map/gate_up/pallas_call | solution.py:120
  203.9 9.4 %down.6.refs_4_.refs_5_ = f32[256,2048]{1,0:T(8,128)} custom-call(s32[4]{0:T(128)} %pad_add_fusion.starts_ref, bf16[256,896]{1,0:T(8,128)(2,1)} %gate_up.26.refs_5_.refs_0_, bf16[256,896]{1,0:T(8,128)(2,1)} %collective-permute-done.23.refs_1_, bf16[256,896]{1,0:T(8,128)(2,1)} %collective-permute-done.24.refs_2_, ...), custom_call_target="tpu_custom_call" | custom-call | flops 3758096384 | bytes 18612224 | tf_op jit(solution)/shard_map/down/pallas_call | solution.py:216
  213.3 7.0 %gate_up.31.refs_6_ = bf16[2,128,1664]{2,1,0:T(8,128)(2,1)} custom-call(s32[1]{0:T(128)} %bitcast.start_ref, bf16[128,2048]{1,0:T(8,128)(2,1)} %collective-permute-done.18.refs_0_, bf16[2048,6656]{1,0:T(8,128)(2,1)} %refs_1_.15, bf16[2048,6656]{1,0:T(8,128)(2,1)} %refs_2_.33, bf16[2,128,1664]{2,1,0:T(8,128)(2,1)} %collective-permute-done.26.refs_3_, ...), custom_call_target="tpu_custom_call" | custom-call | flops 1744830464 | bytes 15859712 | tf_op jit(solution)/shard_map/gate_up/pallas_call | solution.py:120
  228.7 8.2 %down.7.refs_3_ = bf16[256,2048]{1,0:T(8,128)(2,1)} custom-call(s32[4]{0:T(128)} %pad_add_fusion.1.starts_ref, bf16[256,768]{1,0:T(8,128)(2,1)} %gate_up.30.refs_5_.refs_0_, bf16[256,768]{1,0:T(8,128)(2,1)} %collective-permute-done.20.refs_1_, bf16[256,768]{1,0:T(8,128)(2,1)} %collective-permute-done.21.refs_2_, ...), custom_call_target="tpu_custom_call" | custom-call | flops 3221225472 | bytes 16252928 | tf_op jit(solution)/shard_map/down/pallas_call | solution.py:216
  240.7 7.7 %down.8.refs_3_.refs_4_ = f32[128,2048]{1,0:T(8,128)} custom-call(s32[2]{0:T(128)} %pad_add_fusion.3.starts_ref, bf16[128,1664]{1,0:T(8,128)(2,1)} %fusion.3.refs_0_, bf16[128,1664]{1,0:T(8,128)(2,1)} %collective-permute-done.34.refs_1_, bf16[6656,2048]{1,0:T(8,128)(2,1)} %refs_2_.35, bf16[256,2048]{1,0:T(8,128)(2,1)} %down.7.refs_3_), custom_call_target="tpu_custom_call" | custom-call | flops 1744830464 | bytes 15532032 | tf_op jit(solution)/shard_map/down/pallas_call | solution.py:216
  257.1 7.8 %down.9 = bf16[128,2048]{1,0:T(8,128)(2,1)} custom-call(s32[2]{0:T(128)} %pad_add_fusion.2.starts_ref, bf16[128,1664]{1,0:T(8,128)(2,1)} %collective-permute-done.32.refs_0_, bf16[128,1664]{1,0:T(8,128)(2,1)} %collective-permute-done.33.refs_1_, bf16[6656,2048]{1,0:T(8,128)(2,1)} %refs_2_.35, f32[128,2048]{1,0:T(8,128)} %down.8.refs_3_.refs_4_, ...), custom_call_target="tpu_custom_call" | custom-call | flops 1744830464 | bytes 15532032 | tf_op jit(solution)/shard_map/down/pallas_call | solution.py:216
  266.7 13.3 %collective-permute-done.28 = bf16[128,2048]{1,0:T(8,128)(2,1)} collective-permute-done((bf16[128,2048]{1,0:T(8,128)(2,1)}, bf16[128,2048]{1,0:T(8,128)(2,1)}, u32[]{:S(2)}, u32[]{:S(2)}) %collective-permute-start.28) | collective-permute-done | bytes 524320 | tf_op jit(solution)/shard_map/ppermute | solution.py:22
  280.0 8.1 %collective-permute-done.35 = bf16[128,2048]{1,0:T(8,128)(2,1)S(1)} collective-permute-done((bf16[128,2048]{1,0:T(8,128)(2,1)}, bf16[128,2048]{1,0:T(8,128)(2,1)S(1)}, u32[]{:S(2)}, u32[]{:S(2)}) %collective-permute-start.35) | collective-permute-done | bytes 524320 | tf_op jit(solution)/shard_map/ppermute | solution.py:22
  (94 shorter events, 79.2 us)
Async XLA Ops:
  0.0 27.5 %collective-permute-start.8 = (bf16[128,2048]{1,0:T(8,128)(2,1)}, bf16[128,2048]{1,0:T(8,128)(2,1)}, u32[]{:S(2)}, u32[]{:S(2)}) collective-permute-start(bf16[128,2048]{1,0:T(8,128)(2,1)} %refs_0_.7), channel_id=1, source_target_pairs={{0,2},{1,3},{2,0},{3,1},{4,6},{5,7},{6,4},{7,5},{8,10},{9,11},{10,... | collective-permute-start | bytes 1572872 | tf_op jit(solution)/shard_map/ppermute | solution.py:22
  17.6 17.7 %collective-permute-start = (bf16[2,128,1664]{2,1,0:T(8,128)(2,1)}, bf16[2,128,1664]{2,1,0:T(8,128)(2,1)}, u32[]{:S(2)}, u32[]{:S(2)}) collective-permute-start(bf16[2,128,1664]{2,1,0:T(8,128)(2,1)} %gate_up.17.refs_4_), channel_id=1, source_target_pairs={{0,4},{4,0},{8,12},{12,8},{1,5},{5,1},{9,13},{13,9},{2,6},{6,2},{1... | collective-permute-start | bytes 2555912 | tf_op jit(solution)/shard_map/ppermute | solution.py:22
  47.6 32.6 %collective-permute-start.11 = (bf16[2,256,896]{2,1,0:T(8,128)(2,1)}, bf16[2,256,896]{2,1,0:T(8,128)(2,1)}, u32[]{:S(2)}, u32[]{:S(2)}) collective-permute-start(bf16[2,256,896]{2,1,0:T(8,128)(2,1)} %gate_up.20.refs_4_), channel_id=1, source_target_pairs={{0,4},{4,0},{8,12},{12,8},{1,5},{5,1},{9,13},{13,9},{2,6},{6,2},{1... | collective-permute-start | bytes 2752520 | tf_op jit(solution)/shard_map/ppermute | solution.py:22
  47.7 30.0 %collective-permute-start.2 = (bf16[2,128,1664]{2,1,0:T(8,128)(2,1)}, bf16[2,128,1664]{2,1,0:T(8,128)(2,1)}, u32[]{:S(2)}, u32[]{:S(2)}) collective-permute-start(bf16[2,128,1664]{2,1,0:T(8,128)(2,1)} %gate_up.18.refs_4_), channel_id=1, source_target_pairs={{0,8},{4,12},{8,0},{12,4},{1,9},{5,13},{9,1},{13,5},{2,10},{6,14},... | collective-permute-start | bytes 2555912 | tf_op jit(solution)/shard_map/ppermute | solution.py:22
  51.6 17.8 %collective-permute-start.4 = (f32[128]{0:T(128)S(1)}, f32[128]{0:T(128)S(1)}, u32[]{:S(2)}, u32[]{:S(2)}) collective-permute-start(f32[128]{0:T(128)S(1)} %add.87), channel_id=1, source_target_pairs={{0,8},{4,12},{8,0},{12,4},{1,9},{5,13},{9,1},{13,5},{2,10},{6,14},... | collective-permute-start | bytes 1544 | tf_op jit(solution)/shard_map/ppermute | solution.py:22
  77.6 52.9 %collective-permute-start.10 = (bf16[2,256,896]{2,1,0:T(8,128)(2,1)}, bf16[2,256,896]{2,1,0:T(8,128)(2,1)}, u32[]{:S(2)}, u32[]{:S(2)}) collective-permute-start(bf16[2,256,896]{2,1,0:T(8,128)(2,1)} %gate_up.21.refs_5_), channel_id=1, source_target_pairs={{0,4},{4,0},{8,12},{12,8},{1,5},{5,1},{9,13},{13,9},{2,6},{6,2},{1... | collective-permute-start | bytes 2752520 | tf_op jit(solution)/shard_map/ppermute | solution.py:22
  85.6 44.9 %collective-permute-start.12 = (bf16[2,256,896]{2,1,0:T(8,128)(2,1)}, bf16[2,256,896]{2,1,0:T(8,128)(2,1)}, u32[]{:S(2)}, u32[]{:S(2)}) collective-permute-start(bf16[2,256,896]{2,1,0:T(8,128)(2,1)} %gate_up.22.refs_4_), channel_id=1, source_target_pairs={{0,8},{4,12},{8,0},{12,4},{1,9},{5,13},{9,1},{13,5},{2,10},{6,14},... | collective-permute-start | bytes 2752520 | tf_op jit(solution)/shard_map/ppermute | solution.py:22
  92.0 32.1 %collective-permute-start.15 = (bf16[2,256,768]{2,1,0:T(8,128)(2,1)}, bf16[2,256,768]{2,1,0:T(8,128)(2,1)}, u32[]{:S(2)}, u32[]{:S(2)}) collective-permute-start(bf16[2,256,768]{2,1,0:T(8,128)(2,1)} %gate_up.23.refs_4_), channel_id=1, source_target_pairs={{0,4},{4,0},{8,12},{12,8},{1,5},{5,1},{9,13},{13,9},{2,6},{6,2},{1... | collective-permute-start | bytes 2359304 | tf_op jit(solution)/shard_map/ppermute | solution.py:22
  95.4 23.4 %collective-permute-start.6 = (bf16[128,1664]{1,0:T(8,128)(2,1)}, bf16[128,1664]{1,0:T(8,128)(2,1)}, u32[]{:S(2)}, u32[]{:S(2)}) collective-permute-start(bf16[128,1664]{1,0:T(8,128)(2,1)} %fusion.9.refs_0_), channel_id=1, source_target_pairs={{0,8},{4,12},{8,0},{12,4},{1,9},{5,13},{9,1},{13,5},{2,10},{6,14},... | collective-permute-start | bytes 1277960 | tf_op jit(solution)/shard_map/ppermute | solution.py:22
  98.6 19.3 %collective-permute-start.14 = (f32[256]{0:T(256)S(1)}, f32[256]{0:T(256)S(1)}, u32[]{:S(2)}, u32[]{:S(2)}) collective-permute-start(f32[256]{0:T(256)S(1)} %add.93), channel_id=1, source_target_pairs={{0,8},{4,12},{8,0},{12,4},{1,9},{5,13},{9,1},{13,5},{2,10},{6,14},... | collective-permute-start | bytes 3080 | tf_op jit(solution)/shard_map/ppermute | solution.py:22
  118.7 18.9 %collective-permute-start.5 = (bf16[128,1664]{1,0:T(8,128)(2,1)}, bf16[128,1664]{1,0:T(8,128)(2,1)}, u32[]{:S(2)}, u32[]{:S(2)}) collective-permute-start(bf16[128,1664]{1,0:T(8,128)(2,1)} %fusion.9.refs_0_), channel_id=1, source_target_pairs={{0,4},{4,0},{8,12},{12,8},{1,5},{5,1},{9,13},{13,9},{2,6},{6,2},{1... | collective-permute-start | bytes 1277960 | tf_op jit(solution)/shard_map/ppermute | solution.py:22
  118.7 18.9 %collective-permute-start.7 = (bf16[128,1664]{1,0:T(8,128)(2,1)}, bf16[128,1664]{1,0:T(8,128)(2,1)}, u32[]{:S(2)}, u32[]{:S(2)}) collective-permute-start(bf16[128,1664]{1,0:T(8,128)(2,1)} %collective-permute-done.6.refs_2_), channel_id=1, source_target_pairs={{0,4},{4,0},{8,12},{12,8},{1,5},{5,1},{9,13},{13,9},{2,6},{6,2},{1... | collective-permute-start | bytes 1277960 | tf_op jit(solution)/shard_map/ppermute | solution.py:22
  124.1 25.3 %collective-permute-start.18 = (bf16[128,2048]{1,0:T(8,128)(2,1)}, bf16[128,2048]{1,0:T(8,128)(2,1)}, u32[]{:S(2)}, u32[]{:S(2)}) collective-permute-start(bf16[128,2048]{1,0:T(8,128)(2,1)} %refs_0_.7), channel_id=1, source_target_pairs={{0,1},{1,0},{2,3},{3,2},{4,5},{5,4},{6,7},{7,6},{8,9},{9,8},{10,11... | collective-permute-start | bytes 1572872 | tf_op jit(solution)/shard_map/ppermute | solution.py:22
  156.2 30.8 %collective-permute-start.19 = (bf16[2,128,1664]{2,1,0:T(8,128)(2,1)}, bf16[2,128,1664]{2,1,0:T(8,128)(2,1)}, u32[]{:S(2)}, u32[]{:S(2)}) collective-permute-start(bf16[2,128,1664]{2,1,0:T(8,128)(2,1)} %gate_up.27.refs_3_), channel_id=1, source_target_pairs={{0,4},{4,0},{8,12},{12,8},{1,5},{5,1},{9,13},{13,9},{2,6},{6,2},{1... | collective-permute-start | bytes 2555912 | tf_op jit(solution)/shard_map/ppermute | solution.py:22
  156.3 37.7 %collective-permute-start.16 = (bf16[2,256,768]{2,1,0:T(8,128)(2,1)}, bf16[2,256,768]{2,1,0:T(8,128)(2,1)}, u32[]{:S(2)}, u32[]{:S(2)}) collective-permute-start(bf16[2,256,768]{2,1,0:T(8,128)(2,1)} %gate_up.24.refs_5_), channel_id=1, source_target_pairs={{0,4},{4,0},{8,12},{12,8},{1,5},{5,1},{9,13},{13,9},{2,6},{6,2},{1... | collective-permute-start | bytes 2359304 | tf_op jit(solution)/shard_map/ppermute | solution.py:22
  156.8 29.7 %collective-permute-start.24 = (bf16[256,896]{1,0:T(8,128)(2,1)}, bf16[256,896]{1,0:T(8,128)(2,1)}, u32[]{:S(2)}, u32[]{:S(2)}) collective-permute-start(bf16[256,896]{1,0:T(8,128)(2,1)} %gate_up.26.refs_5_.refs_0_), channel_id=1, source_target_pairs={{0,8},{4,12},{8,0},{12,4},{1,9},{5,13},{9,1},{13,5},{2,10},{6,14},... | collective-permute-start | bytes 1376264 | tf_op jit(solution)/shard_map/ppermute | solution.py:22
  158.4 38.5 %collective-permute-start.17 = (bf16[2,256,768]{2,1,0:T(8,128)(2,1)}, bf16[2,256,768]{2,1,0:T(8,128)(2,1)}, u32[]{:S(2)}, u32[]{:S(2)}) collective-permute-start(bf16[2,256,768]{2,1,0:T(8,128)(2,1)} %gate_up.25.refs_7_), channel_id=1, source_target_pairs={{0,8},{4,12},{8,0},{12,4},{1,9},{5,13},{9,1},{13,5},{2,10},{6,14},... | collective-permute-start | bytes 2359304 | tf_op jit(solution)/shard_map/ppermute | solution.py:22
  161.8 24.7 %collective-permute-start.31 = (f32[128]{0:T(128)}, f32[128]{0:T(128)}, u32[]{:S(2)}, u32[]{:S(2)}) collective-permute-start(f32[128]{0:T(128)} %add.105), channel_id=1, source_target_pairs={{0,8},{4,12},{8,0},{12,4},{1,9},{5,13},{9,1},{13,5},{2,10},{6,14},... | collective-permute-start | bytes 1544 | tf_op jit(solution)/shard_map/ppermute | solution.py:22
  186.5 26.8 %collective-permute-start.26 = (bf16[2,128,1664]{2,1,0:T(8,128)(2,1)}, bf16[2,128,1664]{2,1,0:T(8,128)(2,1)}, u32[]{:S(2)}, u32[]{:S(2)}) collective-permute-start(bf16[2,128,1664]{2,1,0:T(8,128)(2,1)} %gate_up.28.refs_4_), channel_id=1, source_target_pairs={{0,4},{4,0},{8,12},{12,8},{1,5},{5,1},{9,13},{13,9},{2,6},{6,2},{1... | collective-permute-start | bytes 2555912 | tf_op jit(solution)/shard_map/ppermute | solution.py:22
  194.1 30.1 %collective-permute-start.29 = (bf16[2,128,1664]{2,1,0:T(8,128)(2,1)}, bf16[2,128,1664]{2,1,0:T(8,128)(2,1)}, u32[]{:S(2)}, u32[]{:S(2)}) collective-permute-start(bf16[2,128,1664]{2,1,0:T(8,128)(2,1)} %gate_up.29.refs_7_), channel_id=1, source_target_pairs={{0,8},{4,12},{8,0},{12,4},{1,9},{5,13},{9,1},{13,5},{2,10},{6,14},... | collective-permute-start | bytes 2555912 | tf_op jit(solution)/shard_map/ppermute | solution.py:22
  203.4 20.8 %collective-permute-start.21 = (bf16[256,768]{1,0:T(8,128)(2,1)}, bf16[256,768]{1,0:T(8,128)(2,1)}, u32[]{:S(2)}, u32[]{:S(2)}) collective-permute-start(bf16[256,768]{1,0:T(8,128)(2,1)} %gate_up.30.refs_5_.refs_0_), channel_id=1, source_target_pairs={{0,8},{4,12},{8,0},{12,4},{1,9},{5,13},{9,1},{13,5},{2,10},{6,14},... | collective-permute-start | bytes 1179656 | tf_op jit(solution)/shard_map/ppermute | solution.py:22
  203.9 24.8 %collective-permute-start.20 = (bf16[256,768]{1,0:T(8,128)(2,1)}, bf16[256,768]{1,0:T(8,128)(2,1)}, u32[]{:S(2)}, u32[]{:S(2)}) collective-permute-start(bf16[256,768]{1,0:T(8,128)(2,1)} %gate_up.30.refs_5_.refs_0_), channel_id=1, source_target_pairs={{0,4},{4,0},{8,12},{12,8},{1,5},{5,1},{9,13},{13,9},{2,6},{6,2},{1... | collective-permute-start | bytes 1179656 | tf_op jit(solution)/shard_map/ppermute | solution.py:22
  254.8 25.2 %collective-permute-start.28 = (bf16[128,2048]{1,0:T(8,128)(2,1)}, bf16[128,2048]{1,0:T(8,128)(2,1)}, u32[]{:S(2)}, u32[]{:S(2)}) collective-permute-start(bf16[128,2048]{1,0:T(8,128)(2,1)} %add_convert_fusion.1), channel_id=1, source_target_pairs={{0,2},{1,3},{2,0},{3,1},{4,6},{5,7},{6,4},{7,5},{8,10},{9,11},{10,... | collective-permute-start | bytes 1572872 | tf_op jit(solution)/shard_map/ppermute | solution.py:22
  264.9 23.2 %collective-permute-start.35 = (bf16[128,2048]{1,0:T(8,128)(2,1)}, bf16[128,2048]{1,0:T(8,128)(2,1)S(1)}, u32[]{:S(2)}, u32[]{:S(2)}) collective-permute-start(bf16[128,2048]{1,0:T(8,128)(2,1)} %down.9), channel_id=1, source_target_pairs={{0,1},{1,0},{2,3},{3,2},{4,5},{5,4},{6,7},{7,6},{8,9},{9,8},{10,11... | collective-permute-start | bytes 1572872 | tf_op jit(solution)/shard_map/ppermute | solution.py:22
  (13 other events, 137.8 us)

commit v2 on v0

v2 whole, which is shorter than its diff:
```python
import functools

import jax
import jax.numpy as jnp
from jax import lax
from jax.experimental import pallas as pl
from jax.experimental.pallas import tpu as pltpu
from jax.sharding import PartitionSpec as P

EPS = 1e-05
LANES = 128
GU_TILE = 256
OUT_TILE = 256
AHEAD = 3
SLOTS = AHEAD + 1
VMEM_LIMIT = 64 * 1024 * 1024 - 64 * 1024
ANY = pl.BlockSpec(memory_space=pl.ANY)
SMEM = pl.BlockSpec(memory_space=pltpu.SMEM)
VMEM = pl.BlockSpec(memory_space=pltpu.VMEM)


def swap(value, axis, size, mask):
    return lax.ppermute(value, axis, [(i, i ^ mask) for i in range(size)])


def silu_product(gate, up, scale):
    gate = gate * scale
    return gate / (1.0 + jnp.exp(-gate)) * (up * scale)


class GateUp:
    def __init__(self, toks, block, starts, width, recvs=(), scale=None):
        self.toks, self.block, self.width, self.recvs, self.scale = toks, block, width, list(recvs), scale
        self.columns, self.starts = starts, [*starts, *[row for _, row in toks]]
        self.rows = block * len(toks)
        shape = (self.rows, width * len(starts))
        self.outs = [jax.ShapeDtypeStruct(shape if scale is not None else (2, *shape), jnp.bfloat16)]

    def plain(self, gate_matrix, up_matrix, down_matrix):
        tok = jnp.concatenate([lax.dynamic_slice_in_dim(t, row, self.block, 0) for t, row in self.toks], axis=0)
        gate, up = (
            jnp.dot(
                tok,
                jnp.concatenate([lax.dynamic_slice_in_dim(m, s, self.width, 1) for s in self.columns], axis=1),
                preferred_element_type=jnp.float32,
            )
            for m in (gate_matrix, up_matrix)
        )
        for r, low in self.recvs:
            r = r[:, :, low : low + self.width].astype(jnp.float32)
            gate, up = gate + r[0], up + r[1]
        if self.scale is not None:
            return [silu_product(gate, up, self.scale).astype(jnp.bfloat16)]
        return [jnp.stack([gate, up]).astype(jnp.bfloat16)]

    def fits(self, down_matrix):
        return self.width % LANES == 0 and self.block % 16 == 0

    def arrays(self):
        return [*[t for t, _ in self.toks], *[r for r, _ in self.recvs]]

    def scratch(self, depth):
        pieces, tiles = len(self.columns), pl.cdiv(self.width, GU_TILE)
        return [
            pltpu.VMEM((self.rows, depth), jnp.bfloat16),
            pltpu.VMEM((max(len(self.recvs), 1), tiles, 2, self.rows if self.recvs else 16, GU_TILE), jnp.bfloat16),
            pltpu.VMEM((pieces * tiles, 2 if self.scale is None else 1, self.rows, GU_TILE), jnp.bfloat16),
            pltpu.SemaphoreType.DMA((len(self.toks),)),
            pltpu.SemaphoreType.DMA((max(len(self.recvs), 1), tiles)),
            pltpu.SemaphoreType.DMA((pieces * tiles,)),
        ]

    def bind(self, ctx, arrays, scale_ref, starts, outs, scratch):
        gate_ref, up_ref, wbuf, wsem, base = ctx["gate"], ctx["up"], ctx["wbuf"], ctx["wsem"], ctx["tiles"]
        xbuf, rbuf, obuf, xsem, rsem, osem = scratch
        toks, recvs = arrays[: len(self.toks)], arrays[len(self.toks) :]
        lows, width, pieces, hidden = [low for _, low in self.recvs], self.width, len(self.columns), self.scale is not None
        out_ref = outs[0]
        full, rest = divmod(width, GU_TILE)
        tiles = full + (rest > 0)
        ctx["tiles"] += pieces * tiles

        def weights(p, j, n):
            slot = (base + p * tiles + j) % SLOTS
            columns = pl.ds(pl.multiple_of(starts(p) + j * GU_TILE, LANES), n)
            return (
                pltpu.make_async_copy(gate_ref.at[:, columns], wbuf.at[slot, :, pl.ds(0, n)], wsem.at[0, slot]),
                pltpu.make_async_copy(up_ref.at[:, columns], wbuf.at[slot, :, pl.ds(n, n)], wsem.at[1, slot]),
            )

        def receive(r, j, n):
            columns = pl.ds(pl.multiple_of(lows[r] + j * GU_TILE, LANES), n)
            return pltpu.make_async_copy(recvs[r].at[:, :, columns], rbuf.at[r, j, :, :, pl.ds(0, n)], rsem.at[r, j])

        def write(p, j, n):
            t = p * tiles + j
            columns = pl.ds(pl.multiple_of(p * width + j * GU_TILE, LANES), n)
            if hidden:
                return pltpu.make_async_copy(obuf.at[t, 0, :, pl.ds(0, n)], out_ref.at[:, columns], osem.at[t])
            return pltpu.make_async_copy(obuf.at[t, :, :, pl.ds(0, n)], out_ref.at[:, :, columns], osem.at[t])

        def begin(p, j, n):
            for copy in weights(p, j, n):
                copy.start()
            for r in range(len(recvs)):
                receive(r, j, n).start()

        def begin_tile(t):
            if isinstance(t, int):
                if t < pieces * tiles:
                    begin(t // tiles, t % tiles, GU_TILE if t % tiles < full else rest)
                return
            p, j = t // tiles, t % tiles

            if full:
                @pl.when((p < pieces) & (j < full))
                def _():
                    begin(p, j, GU_TILE)

            if rest:
                @pl.when((p < pieces) & (j == full))
                def _():
                    begin(p, full, rest)

        block, copies = self.block, []
        for i, tok in enumerate(toks):
            rows = pl.ds(pl.multiple_of(starts(pieces + i), 16), block)
            copies.append(pltpu.make_async_copy(tok.at[rows], xbuf.at[pl.ds(i * block, block)], xsem.at[i]))

        def prefetch():
            for copy in copies:
                copy.start()
            for t in range(AHEAD):
                begin_tile(t)

        def multiply(p, j, n):
            slot = (base + p * tiles + j) % SLOTS
            for copy in weights(p, j, n):
                copy.wait()
            both = jnp.dot(xbuf[...], wbuf[slot, :, pl.ds(0, 2 * n)], preferred_element_type=jnp.float32)
            begin_tile(p * tiles + j + AHEAD)
            gate, up = both[:, :n], both[:, n:]
            for r in range(len(recvs)):
                receive(r, j, n).wait()
                gate = gate + rbuf[r, j, 0, :, pl.ds(0, n)].astype(jnp.float32)
                up = up + rbuf[r, j, 1, :, pl.ds(0, n)].astype(jnp.float32)
            t = p * tiles + j
            if hidden:
                obuf[t, 0, :, pl.ds(0, n)] = silu_product(gate, up, scale_ref[...]).astype(jnp.bfloat16)
            else:
                obuf[t, 0, :, pl.ds(0, n)] = gate.astype(jnp.bfloat16)
                obuf[t, 1, :, pl.ds(0, n)] = up.astype(jnp.bfloat16)
            write(p, j, n).start()

        def compute(then):
            for copy in copies:
                copy.wait()
            for p in range(pieces):
                last = p == pieces - 1
                looped = full - 1 if last and not rest else full
                if looped:
                    @pl.loop(0, looped)
                    def _(j):
                        multiply(p, j, GU_TILE)
                if last:
                    then()
                if last and not rest:
                    multiply(p, full - 1, GU_TILE)
                elif rest:
                    multiply(p, full, rest)

        def drain():
            for p in range(pieces):
                if full:
                    @pl.loop(0, full)
                    def _(j):
                        write(p, j, GU_TILE).wait()
                if rest:
                    write(p, full, rest).wait()

        return prefetch, compute, drain


class Down:
    def __init__(self, pieces, starts, total, block, columns, dtype):
        self.pieces, self.starts, self.total, self.block, self.dtype = pieces, starts, total, block, dtype
        self.rows, self.columns, self.scale = pieces[0].shape[0], columns, None
        self.outs = [jax.ShapeDtypeStruct((block, columns), dtype) for _ in range(self.rows // block)]

    def plain(self, gate_matrix, up_matrix, down_matrix):
        result = sum(
            jnp.dot(p, lax.dynamic_slice_in_dim(down_matrix, s, p.shape[1], 0), preferred_element_type=jnp.float32)
            for p, s in zip(self.pieces, self.starts)
        )
        if self.total is not None:
            result = result + jnp.concatenate(self.total, axis=0)
        return jnp.split(result.astype(self.dtype), len(self.outs))

    def fits(self, down_matrix):
        return all(p.shape[1] % LANES == 0 for p in self.pieces) and self.columns % OUT_TILE == 0

    def arrays(self):
        return [*self.pieces, *(self.total or [])]

    def scratch(self, depth):
        tiles, n = self.columns // OUT_TILE, len(self.pieces)
        return [
            *[pltpu.VMEM(p.shape, jnp.bfloat16) for p in self.pieces],
            *[pltpu.VMEM((SLOTS, p.shape[1], OUT_TILE), jnp.bfloat16) for p in self.pieces],
            pltpu.VMEM((SLOTS, self.rows, OUT_TILE) if self.total else (1, 8, LANES), jnp.float32),
            pltpu.VMEM((tiles, self.rows, OUT_TILE), self.dtype),
            pltpu.SemaphoreType.DMA((n,)),
            pltpu.SemaphoreType.DMA((n, SLOTS)),
            pltpu.SemaphoreType.DMA((len(self.outs), SLOTS)),
            pltpu.SemaphoreType.DMA((len(self.outs), tiles)),
        ]

    def bind(self, ctx, arrays, scale_ref, starts, outs, scratch):
        n, tiles, block = len(self.pieces), self.columns // OUT_TILE, self.block
        pieces, totals = arrays[:n], arrays[n:]
        hbufs, dbufs = scratch[:n], scratch[n : 2 * n]
        tbuf, obuf, hsem, dsem, tsem, osem = scratch[2 * n :]
        down_ref = ctx["down"]

        def columns(j):
            return pl.ds(pl.multiple_of(j * OUT_TILE, LANES), OUT_TILE)

        def weights(p, j):
            rows = pl.ds(pl.multiple_of(starts(p), LANES), dbufs[p].shape[1])
            return pltpu.make_async_copy(down_ref.at[rows, columns(j)], dbufs[p].at[j % SLOTS], dsem.at[p, j % SLOTS])

        def total(i, j):
            slot = j % SLOTS
            return pltpu.make_async_copy(
                totals[i].at[:, columns(j)], tbuf.at[slot, pl.ds(i * block, block)], tsem.at[i, slot]
            )

        def write(i, j):
            return pltpu.make_async_copy(
                obuf.at[j, pl.ds(i * block, block)], outs[i].at[:, columns(j)], osem.at[i, j]
            )

        def begin(j):
            for p in range(n):
                weights(p, j).start()
            for i in range(len(totals)):
                total(i, j).start()

        copies = [pltpu.make_async_copy(pieces[p], hbufs[p], hsem.at[p]) for p in range(n)]

        def prefetch():
            for copy in copies:
                copy.start()
            for j in range(min(AHEAD, tiles)):
                begin(j)

        def multiply(j):
            result = None
            for p in range(n):
                weights(p, j).wait()
                term = jnp.dot(hbufs[p][...], dbufs[p][j % SLOTS], preferred_element_type=jnp.float32)
                result = term if result is None else result + term
            if isinstance(j, int):
                if j + AHEAD < tiles:
                    begin(j + AHEAD)
            else:
                @pl.when(j + AHEAD < tiles)
                def _():
                    begin(j + AHEAD)
            for i in range(len(totals)):
                total(i, j).wait()
            if totals:
                result = result + tbuf[j % SLOTS]
            obuf[j] = result.astype(obuf.dtype)
            for i in range(len(outs)):
                write(i, j).start()

        def compute(then):
            for copy in copies:
                copy.wait()

            @pl.loop(0, tiles - 1)
            def _(j):
                multiply(j)

            then()
            multiply(tiles - 1)

        def drain():
            @pl.loop(0, tiles)
            def _(j):
                for i in range(len(outs)):
                    write(i, j).wait()

        return prefetch, compute, drain


def run(phases, gate_matrix, up_matrix, down_matrix, dep):
    if not all(p.fits(down_matrix) for p in phases):
        return [p.plain(gate_matrix, up_matrix, down_matrix) for p in phases]
    depth = gate_matrix.shape[0]
    operands = [gate_matrix, up_matrix, down_matrix]

    def index(array):
        for i, known in enumerate(operands):
            if known is array:
                return i
        operands.append(array)
        return len(operands) - 1

    where = [[index(a) for a in p.arrays()] for p in phases]
    index(dep)
    scales = [p.scale for p in phases if p.scale is not None]
    starts = [s for p in phases for s in p.starts]
    outs = [o for p in phases for o in p.outs]
    scratch = [p.scratch(depth) for p in phases]
    any_gate_up = any(isinstance(p, GateUp) for p in phases)

    def kernel(starts_ref, *refs):
        refs = list(refs)
        arrays = [refs.pop(0) for _ in operands]
        scale_refs = [refs.pop(0) for _ in scales]
        out_refs = [refs.pop(0) for _ in outs]
        ctx = {"gate": arrays[0], "up": arrays[1], "down": arrays[2], "tiles": 0}
        ctx["wbuf"], ctx["wsem"] = refs.pop(0), refs.pop(0)
        bound, first = [], 0
        for p, places, buffers in zip(phases, where, scratch):
            scale_ref = scale_refs.pop(0) if p.scale is not None else None
            mine = [out_refs.pop(0) for _ in p.outs]
            held = [refs.pop(0) for _ in buffers]
            start = functools.partial(lambda low, i: starts_ref[low + i], first)
            first += len(p.starts)
            bound.append(p.bind(ctx, [arrays[i] for i in places], scale_ref, start, mine, held))
        bound[0][0]()
        for i, (_, compute, _) in enumerate(bound):
            compute(bound[i + 1][0] if i + 1 < len(bound) else lambda: None)
        for _, _, drain in bound:
            drain()

    results = pl.pallas_call(
        kernel,
        out_shape=outs,
        in_specs=[SMEM] + [ANY] * len(operands) + [VMEM] * len(scales),
        out_specs=[ANY] * len(outs),
        scratch_shapes=[
            pltpu.VMEM((SLOTS, depth, 2 * GU_TILE) if any_gate_up else (1, 16, LANES), jnp.bfloat16),
            pltpu.SemaphoreType.DMA((2, SLOTS)),
            *[buffer for buffers in scratch for buffer in buffers],
        ],
        compiler_params=pltpu.CompilerParams(vmem_limit_bytes=VMEM_LIMIT),
        cost_estimate=pl.CostEstimate(flops=WORK, bytes_accessed=1024, transcendentals=0),
        name="step_" + "".join("g" if isinstance(p, GateUp) else "d" for p in phases),
    )(jnp.stack(starts).astype(jnp.int32), *operands, *scales)
    results, split = list(results), []
    for p in phases:
        split.append([results.pop(0) for _ in p.outs])
    return split


WORK = 10**3
STEPS = (
    "s0",
    "s1",
    "x0",
    "x1",
    "h0",
    "h1",
    "r0 s2",
    "r1 s3",
    "x2",
    "x3 s4 s5 d0 d1",
    "h2",
    "h3",
    "r2 x4 x5",
    "r3 d2 d3",
    "h4",
    "h5",
    "r4 d4",
    "r5 d5",
)


def cut(width, part, parts):
    unit = LANES if width % LANES == 0 else 1
    return width // unit * part // parts * unit


def on_device(n_gx, n_gy, tokens, gate_matrix, up_matrix, down_matrix):
    features = tokens.shape[1] * n_gx
    width = gate_matrix.shape[1] // n_gx
    block, columns = tokens.shape[0], down_matrix.shape[1]
    me = lax.axis_index("gx")
    far = [2 * k for k in range(1, n_gx // 2)]

    def core(value):
        return swap(value, "gx", n_gx, 1)

    values = tokens.astype(jnp.float32)
    squares = jnp.sum(values * values, axis=1)
    mask = 1
    while mask < n_gx:
        squares = squares + swap(squares, "gx", n_gx, mask)
        mask *= 2

    gathered = lax.all_gather(tokens, "gy", axis=0, tiled=True)
    here = lax.axis_index("gy")
    blocks = {j: (gathered, (here ^ j) * block) if j else (tokens, jnp.int32(0)) for j in range(n_gy)}
    factors = {0: lax.rsqrt(squares / features + EPS)}
    mask = n_gy // 2
    while mask:
        names = list(factors)
        arrived = swap(jnp.concatenate([factors[j] for j in names]), "gy", n_gy, mask)
        factors.update({j ^ mask: part for j, part in zip(names, jnp.split(arrived, len(names)))})
        mask //= 2

    groups = [[0], list(range(2, n_gy)), [1]]
    first, half = cut(width, 7, 13), cut(width, 7, 13)
    jobs = [(0, 0, first), (0, first, width), (1, 0, half), (1, half, width), (2, 0, half), (2, half, width)]
    jobs = [(group, low, high - low) for group, low, high in jobs]
    state = [dict() for _ in jobs]
    totals = {}
    chain = tokens

    def phase(kind, job):
        group, low, n = jobs[job]
        toks, st = [blocks[j] for j in groups[group]], state[job]
        start = lambda q: q * width + low
        if kind == "s":
            return [GateUp(toks, block, [start(me ^ k ^ 1)], n) for k in [*far, 0]]
        if kind == "x":
            return [GateUp(toks, block, [start(me ^ k)], n, [(st["lent"][i], 0)]) for i, k in enumerate(far)]
        if kind == "h":
            recvs = [(st["lent"][-1], 0)] + [(r, 0) for r in st["far"]]
            scale = jnp.concatenate([factors[j] for j in groups[group]])[:, None]
            return [GateUp(toks, block, [start(me)], n, recvs, scale)]
        last = all(g != group for g, _, _ in jobs[job + 1 :])
        dtype = jnp.bfloat16 if last and group else jnp.float32
        pieces = [(st["hidden"], me), (st["sibling"], me ^ 1)] + st["over"]
        return [Down([h for h, _ in pieces], [start(q) for _, q in pieces], totals.get(group), block, columns, dtype)]

    def deliver(kind, job, outs):
        group, st = jobs[job][0], state[job]
        if kind == "s":
            st["lent"] = [core(o[0]) for o in outs]
        elif kind == "x":
            st["far"] = [swap(o[0], "gx", n_gx, k) for o, k in zip(outs, far)]
        elif kind == "h":
            st["hidden"], st["sibling"] = outs[0][0], core(outs[0][0])
            st["crossed"] = [swap(outs[0][0], "gx", n_gx, k) for k in far]
        else:
            totals[group] = outs[0]

    def tied(values):
        nonlocal chain
        values, chain = lax.optimization_barrier((values, chain))
        return values

    def forward(job):
        crossed = tied(state[job]["crossed"])
        state[job]["over"] = [(h, me ^ k) for h, k in zip(crossed, far)]
        state[job]["over"] += [(core(h), me ^ k ^ 1) for h, k in zip(crossed, far)]

    for names in STEPS:
        items = []
        for name in names.split():
            if name[0] == "r":
                forward(int(name[1:]))
            else:
                items.append((name[0], int(name[1:])))
        waiting = [(kind, job, phase(kind, job)) for kind, job in items if kind != "d"]
        downs = [job for kind, job in items if kind == "d"]
        merged = []
        for job in downs:
            found = phase("d", job)[0]
            if merged and jobs[merged[-1][1]][0] == jobs[job][0]:
                before = merged[-1][2][0]
                both = Down(
                    before.pieces + found.pieces, before.starts + found.starts, before.total, block, columns, found.dtype
                )
                merged[-1] = ("d", job, [both])
            else:
                merged.append(("d", job, [found]))
        waiting += merged
        results = run([p for _, _, ps in waiting for p in ps], gate_matrix, up_matrix, down_matrix, chain)
        chain = results[0][0]
        for kind, job, ps in waiting:
            deliver(kind, job, [results.pop(0) for _ in ps])

    parts = dict(zip(groups[1], totals[1]))
    parts[0] = totals[0][0]
    mask = 1
    while mask < n_gy:
        for j in [j for j in parts if j & mask]:
            arrived = swap(parts.pop(j), "gy", n_gy, mask).astype(jnp.float32)
            total = parts[j ^ mask].astype(jnp.float32) + arrived
            parts[j ^ mask] = total if j == mask else total.astype(jnp.bfloat16)
        mask *= 2
    last = swap(totals[2][0], "gy", n_gy, 1).astype(jnp.float32)
    return (parts[0] + last).astype(jnp.bfloat16)


def solution(mesh):
    n_gx, n_gy = mesh.shape["gx"], mesh.shape["gy"]
    placed = (P(("groups", "gy"), "gx"), P("gx", "gy"), P("gx", "gy"), P("gy", "gx"))
    return jax.shard_map(
        functools.partial(on_device, n_gx, n_gy),
        mesh=mesh,
        in_specs=placed,
        out_specs=P(("groups", "gy"), "gx"),
        check_vma=False,
    )
```

time: 350 us -> 301 us (0.86)
  Pallas kernels: 0 us -> 198 us
  waiting for transfers between devices: 228 us -> 36.7 us
  matrix products: 66.5 us -> 0 us
  starting transfers between devices: 0.35 us -> 29.3 us
  local copies, waits for them, and re-layouts: 26.9 us -> 6.45 us
  other arithmetic: 5.48 us -> 15.5 us
  blocking collectives: 8.34 us -> 0 us
    pallas_call x0 -> x18, Pallas kernels: none -> 198 us  [run(): pl.pallas_call(kernel, out_shape=outs, in_specs=[SMEM] + [ANY] * len(oper...]
    all_gather x2 -> x1, waiting for transfers between devices: 95.8 us -> 0.02 us  [on_device(): gathered = lax.all_gather(tokens, 'gy', axis=0, tiled=True)]
    unnamed x7 -> x1, waiting for transfers between devices: 88.3 us -> 0.71 us
    dot_general x3 -> x0, matrix products: 66.5 us -> none  [the longest x1 22.6 us: on_device(): jnp.dot(gathered, gate_matrix, preferred_element_type=jnp.float32)]
    reduce_scatter x1 -> x0, waiting for transfers between devices: 44 us -> none  [on_device(): lax.psum_scatter(partial_out.astype(jnp.bfloat16), 'gy', scatter_dimensio...]
    ppermute x0 -> x43, waiting for transfers between devices: none -> 36 us  [swap(): return lax.ppermute(value, axis, [(i, i ^ mask) for i in range(size)])]
    ppermute x0 -> x43, starting transfers between devices: none -> 29.3 us  [swap(): return lax.ppermute(value, axis, [(i, i ^ mask) for i in range(size)])]
    unnamed x6 -> x2, local copies, waits for them, and re-layouts: 26.9 us -> 0.58 us
  transfers between devices with their start and end apart: 5 -> 44, of which waited for: 5 -> 9; matrix products, arithmetic and copies ran while one was open for 10% -> 6% of each run, Pallas kernels for 0% -> 62%
where the time goes in v2:
time: 301 us; the launch traced here: 300 us
  Pallas kernels  198 us (66%)
  waiting for transfers between devices  36.7 us (12%)
  starting transfers between devices  29.3 us (10%)
  other arithmetic  15.5 us (5%)
  between operations  13.7 us (5%)
  local copies, waits for them, and re-layouts  6.45 us (2%)
    pallas_call x18, Pallas kernels, run(): pl.pallas_call(kernel, out_shape=outs, in_specs=[SMEM] + [ANY] * len(oper...  198 us
    ppermute x43, waiting for transfers between devices, swap(): return lax.ppermute(value, axis, [(i, i ^ mask) for i in range(size)])  36 us
    ppermute x43, starting transfers between devices, swap(): return lax.ppermute(value, axis, [(i, i ^ mask) for i in range(size)])  29.3 us
    another operation x13, other arithmetic, run(): jnp.stack(starts).astype(jnp.int32)  7.94 us
  transfers between devices with their start and end apart: 44, of which 9 were waited for; matrix products, arithmetic and copies ran while one was open for 6% of the time, Pallas kernels for 62%

profile of v2, /device:TPU:0, one launch (start us, length us, event | category | flops | bytes accessed | tf_op | source)
XLA Modules:
  0.0 299.9 jit_solution(259907068339587288)
XLA Ops:
  7.9 9.4 %step_gg.5 = (bf16[2,128,896]{2,1,0:T(8,128)(2,1)}, bf16[2,128,896]{2,1,0:T(8,128)(2,1)}) custom-call(s32[4]{0:T(128)} %get-tuple-element.67.starts_ref, bf16[2048,6656]{1,0:T(8,128)(2,1)} %refs_0_.35, bf16[2048,6656]{1,0:T(8,128)(2,1)} %refs_1_.35, bf16[6656,2048]{1,0:T(8,128)(2,1)} %refs_2_.35, bf16[128,2048]{1,0:T(8,128)(2,1)} %refs_3_.11), custom_call_target="tpu_custom_call" | custom-call | flops 1000 | bytes 1024 | tf_op jit(solution)/shard_map/step_gg/pallas_call | solution.py:340
  17.9 9.6 %step_gg.6 = (bf16[2,128,768]{2,1,0:T(8,128)(2,1)}, bf16[2,128,768]{2,1,0:T(8,128)(2,1)}) custom-call(s32[4]{0:T(128)} %get-tuple-element.68.starts_ref, bf16[2048,6656]{1,0:T(8,128)(2,1)} %refs_0_.35, bf16[2048,6656]{1,0:T(8,128)(2,1)} %refs_1_.35, bf16[6656,2048]{1,0:T(8,128)(2,1)} %refs_2_.35, bf16[128,2048]{1,0:T(8,128)(2,1)} %refs_3_.11, ...), custom_call_target="tpu_custom_call" | custom-call | flops 1000 | bytes 1024 | tf_op jit(solution)/shard_map/step_gg/pallas_call | solution.py:340
  28.7 6.2 %step_g.9.refs_5_ = bf16[2,128,896]{2,1,0:T(8,128)(2,1)} custom-call(s32[2]{0:T(128)} %pad_add_fusion.1.starts_ref, bf16[2048,6656]{1,0:T(8,128)(2,1)} %refs_0_.35, bf16[2048,6656]{1,0:T(8,128)(2,1)} %refs_1_.35, bf16[6656,2048]{1,0:T(8,128)(2,1)} %refs_2_.35, bf16[128,2048]{1,0:T(8,128)(2,1)} %refs_3_.11, ...), custom_call_target="tpu_custom_call" | custom-call | flops 1000 | bytes 1024 | tf_op jit(solution)/shard_map/step_g/pallas_call | solution.py:340
  34.9 2.5 collective-permute-start.5
  41.0 5.7 %step_g.10.refs_6_ = bf16[2,128,768]{2,1,0:T(8,128)(2,1)} custom-call(s32[2]{0:T(128)} %pad_add_fusion.2.starts_ref, bf16[2048,6656]{1,0:T(8,128)(2,1)} %refs_0_.35, bf16[2048,6656]{1,0:T(8,128)(2,1)} %refs_1_.35, bf16[6656,2048]{1,0:T(8,128)(2,1)} %refs_2_.35, bf16[128,2048]{1,0:T(8,128)(2,1)} %refs_3_.11, ...), custom_call_target="tpu_custom_call" | custom-call | flops 1000 | bytes 1024 | tf_op jit(solution)/shard_map/step_g/pallas_call | solution.py:340
  50.8 6.8 %step_g.11.refs_6_.refs_5_ = bf16[128,896]{1,0:T(8,128)(2,1)} custom-call(s32[2]{0:T(128)} %pad_add_fusion.starts_ref, bf16[2048,6656]{1,0:T(8,128)(2,1)} %refs_0_.35, bf16[2048,6656]{1,0:T(8,128)(2,1)} %refs_1_.35, bf16[6656,2048]{1,0:T(8,128)(2,1)} %refs_2_.35, bf16[128,2048]{1,0:T(8,128)(2,1)} %refs_3_.11, ...), custom_call_target="tpu_custom_call" | custom-call | flops 1000 | bytes 1024 | tf_op jit(solution)/shard_map/step_g/pallas_call | solution.py:340
  60.7 6.4 %step_g.12.refs_4_.refs_9_ = bf16[128,768]{1,0:T(8,128)(2,1)} custom-call(s32[2]{0:T(128)} %pad_add_fusion.3.starts_ref, bf16[2048,6656]{1,0:T(8,128)(2,1)} %refs_0_.35, bf16[2048,6656]{1,0:T(8,128)(2,1)} %refs_1_.35, bf16[6656,2048]{1,0:T(8,128)(2,1)} %refs_2_.35, bf16[128,2048]{1,0:T(8,128)(2,1)} %refs_3_.11, ...), custom_call_target="tpu_custom_call" | custom-call | flops 1000 | bytes 1024 | tf_op jit(solution)/shard_map/step_g/pallas_call | solution.py:340
  67.1 12.0 %step_gg.7 = (bf16[2,256,896]{2,1,0:T(8,128)(2,1)}, bf16[2,256,896]{2,1,0:T(8,128)(2,1)}) custom-call(s32[6]{0:T(128)} %stack.77.starts_ref, bf16[2048,6656]{1,0:T(8,128)(2,1)} %refs_0_.35, bf16[2048,6656]{1,0:T(8,128)(2,1)} %refs_1_.35, bf16[6656,2048]{1,0:T(8,128)(2,1)} %refs_2_.35, bf16[512,2048]{1,0:T(8,128)(2,1)} %all-gather.2.cloned.1.call-done.refs_3_, ...), custom_call_target="tpu_custom_call" | custom-call | flops 1000 | bytes 1024 | tf_op jit(solution)/shard_map/step_gg/pallas_call | solution.py:340
  80.2 6.7 %collective-permute-done.8.refs_11_ = bf16[128,768]{1,0:T(8,128)(2,1)} collective-permute-done((bf16[128,768]{1,0:T(8,128)(2,1)}, bf16[128,768]{1,0:T(8,128)(2,1)}, u32[]{:S(2)}, u32[]{:S(2)}) %collective-permute-start.8) | collective-permute-done | bytes 196640 | tf_op jit(solution)/shard_map/ppermute | solution.py:23
  86.9 11.0 %step_gg.8 = (bf16[2,256,768]{2,1,0:T(8,128)(2,1)}, bf16[2,256,768]{2,1,0:T(8,128)(2,1)}) custom-call(s32[6]{0:T(128)} %stack.70.starts_ref, bf16[2048,6656]{1,0:T(8,128)(2,1)} %refs_0_.35, bf16[2048,6656]{1,0:T(8,128)(2,1)} %refs_1_.35, bf16[6656,2048]{1,0:T(8,128)(2,1)} %refs_2_.35, bf16[512,2048]{1,0:T(8,128)(2,1)} %all-gather.2.cloned.1.call-done.refs_3_, ...), custom_call_target="tpu_custom_call" | custom-call | flops 1000 | bytes 1024 | tf_op jit(solution)/shard_map/step_gg/pallas_call | solution.py:340
  99.6 7.3 %step_g.13.refs_13_ = bf16[2,256,896]{2,1,0:T(8,128)(2,1)} custom-call(s32[3]{0:T(128)} %add_add_fusion.starts_ref, bf16[2048,6656]{1,0:T(8,128)(2,1)} %refs_0_.35, bf16[2048,6656]{1,0:T(8,128)(2,1)} %refs_1_.35, bf16[6656,2048]{1,0:T(8,128)(2,1)} %refs_2_.35, bf16[512,2048]{1,0:T(8,128)(2,1)} %all-gather.2.cloned.1.call-done.refs_3_, ...), custom_call_target="tpu_custom_call" | custom-call | flops 1000 | bytes 1024 | tf_op jit(solution)/shard_map/step_g/pallas_call | solution.py:340
  109.2 37.2 %step_gggggd.1 = (bf16[2,256,768]{2,1,0:T(8,128)(2,1)}, bf16[2,128,896]{2,1,0:T(8,128)(2,1)}, bf16[2,128,896]{2,1,0:T(8,128)(2,1)}, bf16[2,128,768]{2,1,0:T(8,12...) custom-call(s32[19]{0:T(128)} %stack.69.starts_ref, bf16[2048,6656]{1,0:T(8,128)(2,1)} %refs_0_.35, ...), custom_call_target="tpu_custom_call" | custom-call | flops 1000 | bytes 1024 | tf_op jit(solution)/shard_map/step_gggggd/pallas_call | solution.py:340
  148.3 2.5 collective-permute-start.18
  158.5 8.4 %step_g.14.refs_6_.refs_3_ = bf16[256,896]{1,0:T(8,128)(2,1)} custom-call(s32[3]{0:T(128)} %add_add_fusion.1.starts_ref, bf16[2048,6656]{1,0:T(8,128)(2,1)} %refs_0_.35, bf16[2048,6656]{1,0:T(8,128)(2,1)} %refs_1_.35, bf16[6656,2048]{1,0:T(8,128)(2,1)} %refs_2_.35, bf16[512,2048]{1,0:T(8,128)(2,1)} %all-gather.2.cloned.1.call-done.refs_3_, ...), custom_call_target="tpu_custom_call" | custom-call | flops 1000 | bytes 1024 | tf_op jit(solution)/shard_map/step_g/pallas_call | solution.py:340
  168.3 7.8 %step_g.15.refs_6_.refs_7_ = bf16[256,768]{1,0:T(8,128)(2,1)} custom-call(s32[3]{0:T(128)} %add_add_fusion.2.starts_ref, bf16[2048,6656]{1,0:T(8,128)(2,1)} %refs_0_.35, bf16[2048,6656]{1,0:T(8,128)(2,1)} %refs_1_.35, bf16[6656,2048]{1,0:T(8,128)(2,1)} %refs_2_.35, bf16[512,2048]{1,0:T(8,128)(2,1)} %all-gather.2.cloned.1.call-done.refs_3_, ...), custom_call_target="tpu_custom_call" | custom-call | flops 1000 | bytes 1024 | tf_op jit(solution)/shard_map/step_g/pallas_call | solution.py:340
  179.2 10.1 %step_gg.9 = (bf16[2,128,896]{2,1,0:T(8,128)(2,1)}, bf16[2,128,768]{2,1,0:T(8,128)(2,1)}) custom-call(s32[4]{0:T(128)} %pad_add_fusion.8.starts_ref, bf16[2048,6656]{1,0:T(8,128)(2,1)} %refs_0_.35, bf16[2048,6656]{1,0:T(8,128)(2,1)} %refs_1_.35, bf16[6656,2048]{1,0:T(8,128)(2,1)} %refs_2_.35, bf16[512,2048]{1,0:T(8,128)(2,1)} %all-gather.2.cloned.1.call-done.refs_3_, ...), custom_call_target="tpu_custom_call" | custom-call | flops 1000 | bytes 1024 | tf_op jit(solution)/shard_map/step_gg/pallas_call | solution.py:340
  192.6 25.3 %step_d.3 = (bf16[128,2048]{1,0:T(8,128)(2,1)}, bf16[128,2048]{1,0:T(8,128)(2,1)}) custom-call(s32[8]{0:T(128)} %stack.79.starts_ref, bf16[2048,6656]{1,0:T(8,128)(2,1)} %refs_0_.35, bf16[2048,6656]{1,0:T(8,128)(2,1)} %refs_1_.35, bf16[6656,2048]{1,0:T(8,128)(2,1)} %refs_2_.35, bf16[256,896]{1,0:T(8,128)(2,1)} %step_g.14.refs_6_.refs_3_, ...), custom_call_target="tpu_custom_call" | custom-call | flops 1000 | bytes 1024 | tf_op jit(solution)/shard_map/step_d/pallas_call | solution.py:340
  221.6 6.8 %step_g.16.refs_6_.refs_3_ = bf16[128,896]{1,0:T(8,128)(2,1)} custom-call(s32[2]{0:T(128)} %pad_add_fusion.12.starts_ref, bf16[2048,6656]{1,0:T(8,128)(2,1)} %refs_0_.35, bf16[2048,6656]{1,0:T(8,128)(2,1)} %refs_1_.35, bf16[6656,2048]{1,0:T(8,128)(2,1)} %refs_2_.35, bf16[512,2048]{1,0:T(8,128)(2,1)} %all-gather.2.cloned.1.call-done.refs_3_, ...), custom_call_target="tpu_custom_call" | custom-call | flops 1000 | bytes 1024 | tf_op jit(solution)/shard_map/step_g/pallas_call | solution.py:340
  230.5 6.4 %step_g.17.refs_7_.refs_3_ = bf16[128,768]{1,0:T(8,128)(2,1)} custom-call(s32[2]{0:T(128)} %pad_add_fusion.11.starts_ref, bf16[2048,6656]{1,0:T(8,128)(2,1)} %refs_0_.35, bf16[2048,6656]{1,0:T(8,128)(2,1)} %refs_1_.35, bf16[6656,2048]{1,0:T(8,128)(2,1)} %refs_2_.35, bf16[512,2048]{1,0:T(8,128)(2,1)} %all-gather.2.cloned.1.call-done.refs_3_, ...), custom_call_target="tpu_custom_call" | custom-call | flops 1000 | bytes 1024 | tf_op jit(solution)/shard_map/step_g/pallas_call | solution.py:340
  239.2 11.4 %step_d.4.refs_7_.refs_8_ = f32[128,2048]{1,0:T(8,128)} custom-call(s32[4]{0:T(128)} %pad_add_fusion.10.starts_ref, bf16[2048,6656]{1,0:T(8,128)(2,1)} %refs_0_.35, bf16[2048,6656]{1,0:T(8,128)(2,1)} %refs_1_.35, bf16[6656,2048]{1,0:T(8,128)(2,1)} %refs_2_.35, bf16[128,896]{1,0:T(8,128)(2,1)} %step_g.16.refs_6_.refs_3_, ...), custom_call_target="tpu_custom_call" | custom-call | flops 1000 | bytes 1024 | tf_op jit(solution)/shard_map/step_d/pallas_call | solution.py:340
  253.3 2.6 collective-permute-start.31
  256.0 10.5 %step_d.5 = bf16[128,2048]{1,0:T(8,128)(2,1)} custom-call(s32[4]{0:T(128)} %pad_add_fusion.9.starts_ref, bf16[2048,6656]{1,0:T(8,128)(2,1)} %refs_0_.35, bf16[2048,6656]{1,0:T(8,128)(2,1)} %refs_1_.35, bf16[6656,2048]{1,0:T(8,128)(2,1)} %refs_2_.35, bf16[128,768]{1,0:T(8,128)(2,1)} %step_g.17.refs_7_.refs_3_, ...), custom_call_target="tpu_custom_call" | custom-call | flops 1000 | bytes 1024 | tf_op jit(solution)/shard_map/step_d/pallas_call | solution.py:340
  267.0 12.7 %collective-permute-done.31 = bf16[128,2048]{1,0:T(8,128)(2,1)} collective-permute-done((bf16[128,2048]{1,0:T(8,128)(2,1)}, bf16[128,2048]{1,0:T(8,128)(2,1)}, u32[]{:S(2)}, u32[]{:S(2)}) %collective-permute-start.31) | collective-permute-done | bytes 524320 | tf_op jit(solution)/shard_map/ppermute | solution.py:23
  279.7 11.0 %collective-permute-done.42 = bf16[128,2048]{1,0:T(8,128)(2,1)S(1)} collective-permute-done((bf16[128,2048]{1,0:T(8,128)(2,1)}, bf16[128,2048]{1,0:T(8,128)(2,1)S(1)}, u32[]{:S(2)}, u32[]{:S(2)}) %collective-permute-start.42) | collective-permute-done | bytes 524320 | tf_op jit(solution)/shard_map/ppermute | solution.py:23
  (113 shorter events, 49.9 us)
Async XLA Ops:
  6.5 60.6 %all-gather.2.cloned.1.call-start = ((), (), s32[]{:S(2)}) async-start(), calls=%async_computation | async-start | bytes 2621440 | tf_op jit(solution)/shard_map/all_gather | solution.py:405
  27.5 13.6 %collective-permute-start.1 = (bf16[2,128,768]{2,1,0:T(8,128)(2,1)}, bf16[2,128,768]{2,1,0:T(8,128)(2,1)}, u32[]{:S(2)}, u32[]{:S(2)}) collective-permute-start(bf16[2,128,768]{2,1,0:T(8,128)(2,1)} %get-tuple-element.37.refs_5_), channel_id=1, source_target_pairs={{0,4},{4,0},{8,12},{12,8},{1,5},{5,1},{9,13},{13,9},{2,6},{6,2},{1... | collective-permute-start | bytes 1179656 | tf_op jit(solution)/shard_map/ppermute | solution.py:23
  27.7 23.2 %collective-permute-start.4 = (bf16[2,128,896]{2,1,0:T(8,128)(2,1)}, bf16[2,128,896]{2,1,0:T(8,128)(2,1)}, u32[]{:S(2)}, u32[]{:S(2)}) collective-permute-start(bf16[2,128,896]{2,1,0:T(8,128)(2,1)} %get-tuple-element.38), channel_id=1, source_target_pairs={{0,4},{4,0},{8,12},{12,8},{1,5},{5,1},{9,13},{13,9},{2,6},{6,2},{1... | collective-permute-start | bytes 1376264 | tf_op jit(solution)/shard_map/ppermute | solution.py:23
  34.9 15.9 %collective-permute-start.5 = (bf16[2,128,896]{2,1,0:T(8,128)(2,1)}, bf16[2,128,896]{2,1,0:T(8,128)(2,1)}, u32[]{:S(2)}, u32[]{:S(2)}) collective-permute-start(bf16[2,128,896]{2,1,0:T(8,128)(2,1)} %step_g.9.refs_5_), channel_id=1, source_target_pairs={{0,8},{4,12},{8,0},{12,4},{1,9},{5,13},{9,1},{13,5},{2,10},{6,14},... | collective-permute-start | bytes 1376264 | tf_op jit(solution)/shard_map/ppermute | solution.py:23
  38.8 21.9 %collective-permute-start = (bf16[2,128,768]{2,1,0:T(8,128)(2,1)}, bf16[2,128,768]{2,1,0:T(8,128)(2,1)}, u32[]{:S(2)}, u32[]{:S(2)}) collective-permute-start(bf16[2,128,768]{2,1,0:T(8,128)(2,1)} %get-tuple-element.36), channel_id=1, source_target_pairs={{0,4},{4,0},{8,12},{12,8},{1,5},{5,1},{9,13},{13,9},{2,6},{6,2},{1... | collective-permute-start | bytes 1179656 | tf_op jit(solution)/shard_map/ppermute | solution.py:23
  46.8 13.9 %collective-permute-start.3 = (bf16[2,128,768]{2,1,0:T(8,128)(2,1)}, bf16[2,128,768]{2,1,0:T(8,128)(2,1)}, u32[]{:S(2)}, u32[]{:S(2)}) collective-permute-start(bf16[2,128,768]{2,1,0:T(8,128)(2,1)} %step_g.10.refs_6_), channel_id=1, source_target_pairs={{0,8},{4,12},{8,0},{12,4},{1,9},{5,13},{9,1},{13,5},{2,10},{6,14},... | collective-permute-start | bytes 1179656 | tf_op jit(solution)/shard_map/ppermute | solution.py:23
  79.1 20.4 %collective-permute-start.15 = (bf16[2,256,896]{2,1,0:T(8,128)(2,1)}, bf16[2,256,896]{2,1,0:T(8,128)(2,1)}, u32[]{:S(2)}, u32[]{:S(2)}) collective-permute-start(bf16[2,256,896]{2,1,0:T(8,128)(2,1)} %get-tuple-element.41.refs_4_), channel_id=1, source_target_pairs={{0,4},{4,0},{8,12},{12,8},{1,5},{5,1},{9,13},{13,9},{2,6},{6,2},{1... | collective-permute-start | bytes 2752520 | tf_op jit(solution)/shard_map/ppermute | solution.py:23
  99.1 59.3 %collective-permute-start.16 = (bf16[2,256,896]{2,1,0:T(8,128)(2,1)}, bf16[2,256,896]{2,1,0:T(8,128)(2,1)}, u32[]{:S(2)}, u32[]{:S(2)}) collective-permute-start(bf16[2,256,896]{2,1,0:T(8,128)(2,1)} %get-tuple-element.46), channel_id=1, source_target_pairs={{0,4},{4,0},{8,12},{12,8},{1,5},{5,1},{9,13},{13,9},{2,6},{6,2},{1... | collective-permute-start | bytes 2752520 | tf_op jit(solution)/shard_map/ppermute | solution.py:23
  106.8 51.6 %collective-permute-start.17 = (bf16[2,256,896]{2,1,0:T(8,128)(2,1)}, bf16[2,256,896]{2,1,0:T(8,128)(2,1)}, u32[]{:S(2)}, u32[]{:S(2)}) collective-permute-start(bf16[2,256,896]{2,1,0:T(8,128)(2,1)} %step_g.13.refs_13_), channel_id=1, source_target_pairs={{0,8},{4,12},{8,0},{12,4},{1,9},{5,13},{9,1},{13,5},{2,10},{6,14},... | collective-permute-start | bytes 2752520 | tf_op jit(solution)/shard_map/ppermute | solution.py:23
  108.9 59.3 %collective-permute-start.22 = (bf16[2,256,768]{2,1,0:T(8,128)(2,1)}, bf16[2,256,768]{2,1,0:T(8,128)(2,1)}, u32[]{:S(2)}, u32[]{:S(2)}) collective-permute-start(bf16[2,256,768]{2,1,0:T(8,128)(2,1)} %get-tuple-element.48), channel_id=1, source_target_pairs={{0,4},{4,0},{8,12},{12,8},{1,5},{5,1},{9,13},{13,9},{2,6},{6,2},{1... | collective-permute-start | bytes 2359304 | tf_op jit(solution)/shard_map/ppermute | solution.py:23
  146.4 21.8 %collective-permute-start.23 = (bf16[2,256,768]{2,1,0:T(8,128)(2,1)}, bf16[2,256,768]{2,1,0:T(8,128)(2,1)}, u32[]{:S(2)}, u32[]{:S(2)}) collective-permute-start(bf16[2,256,768]{2,1,0:T(8,128)(2,1)} %get-tuple-element.47.refs_6_), channel_id=1, source_target_pairs={{0,8},{4,12},{8,0},{12,4},{1,9},{5,13},{9,1},{13,5},{2,10},{6,14},... | collective-permute-start | bytes 2359304 | tf_op jit(solution)/shard_map/ppermute | solution.py:23
  167.2 12.0 %collective-permute-start.27 = (bf16[2,128,896]{2,1,0:T(8,128)(2,1)}, bf16[2,128,896]{2,1,0:T(8,128)(2,1)}, u32[]{:S(2)}, u32[]{:S(2)}) collective-permute-start(bf16[2,128,896]{2,1,0:T(8,128)(2,1)} %get-tuple-element.50), channel_id=1, source_target_pairs={{0,4},{4,0},{8,12},{12,8},{1,5},{5,1},{9,13},{13,9},{2,6},{6,2},{1... | collective-permute-start | bytes 1376264 | tf_op jit(solution)/shard_map/ppermute | solution.py:23
  176.1 13.2 %collective-permute-start.26 = (bf16[256,768]{1,0:T(8,128)(2,1)}, bf16[256,768]{1,0:T(8,128)(2,1)}, u32[]{:S(2)}, u32[]{:S(2)}) collective-permute-start(bf16[256,768]{1,0:T(8,128)(2,1)} %step_g.15.refs_6_.refs_7_), channel_id=1, source_target_pairs={{0,8},{4,12},{8,0},{12,4},{1,9},{5,13},{9,1},{13,5},{2,10},{6,14},... | collective-permute-start | bytes 1179656 | tf_op jit(solution)/shard_map/ppermute | solution.py:23
  177.9 12.4 %collective-permute-start.20 = (bf16[256,896]{1,0:T(8,128)(2,1)}, bf16[256,896]{1,0:T(8,128)(2,1)}, u32[]{:S(2)}, u32[]{:S(2)}) collective-permute-start(bf16[256,896]{1,0:T(8,128)(2,1)} %step_g.14.refs_6_.refs_3_), channel_id=1, source_target_pairs={{0,4},{4,0},{8,12},{12,8},{1,5},{5,1},{9,13},{13,9},{2,6},{6,2},{1... | collective-permute-start | bytes 1376264 | tf_op jit(solution)/shard_map/ppermute | solution.py:23
  178.5 14.2 %collective-permute-start.24 = (bf16[256,896]{1,0:T(8,128)(2,1)}, bf16[256,896]{1,0:T(8,128)(2,1)}, u32[]{:S(2)}, u32[]{:S(2)}) collective-permute-start(bf16[256,896]{1,0:T(8,128)(2,1)} %collective-permute-done.21.refs_5_), channel_id=1, source_target_pairs={{0,4},{4,0},{8,12},{12,8},{1,5},{5,1},{9,13},{13,9},{2,6},{6,2},{1... | collective-permute-start | bytes 1376264 | tf_op jit(solution)/shard_map/ppermute | solution.py:23
  189.8 31.8 %collective-permute-start.34 = (bf16[2,128,896]{2,1,0:T(8,128)(2,1)}, bf16[2,128,896]{2,1,0:T(8,128)(2,1)}, u32[]{:S(2)}, u32[]{:S(2)}) collective-permute-start(bf16[2,128,896]{2,1,0:T(8,128)(2,1)} %get-tuple-element.60), channel_id=1, source_target_pairs={{0,4},{4,0},{8,12},{12,8},{1,5},{5,1},{9,13},{13,9},{2,6},{6,2},{1... | collective-permute-start | bytes 1376264 | tf_op jit(solution)/shard_map/ppermute | solution.py:23
  189.8 31.7 %collective-permute-start.35 = (bf16[2,128,896]{2,1,0:T(8,128)(2,1)}, bf16[2,128,896]{2,1,0:T(8,128)(2,1)}, u32[]{:S(2)}, u32[]{:S(2)}) collective-permute-start(bf16[2,128,896]{2,1,0:T(8,128)(2,1)} %get-tuple-element.55.refs_11_), channel_id=1, source_target_pairs={{0,8},{4,12},{8,0},{12,4},{1,9},{5,13},{9,1},{13,5},{2,10},{6,14},... | collective-permute-start | bytes 1376264 | tf_op jit(solution)/shard_map/ppermute | solution.py:23
  190.4 40.2 %collective-permute-start.32 = (bf16[2,128,768]{2,1,0:T(8,128)(2,1)}, bf16[2,128,768]{2,1,0:T(8,128)(2,1)}, u32[]{:S(2)}, u32[]{:S(2)}) collective-permute-start(bf16[2,128,768]{2,1,0:T(8,128)(2,1)} %get-tuple-element.58), channel_id=1, source_target_pairs={{0,4},{4,0},{8,12},{12,8},{1,5},{5,1},{9,13},{13,9},{2,6},{6,2},{1... | collective-permute-start | bytes 1179656 | tf_op jit(solution)/shard_map/ppermute | solution.py:23
  191.5 39.1 %collective-permute-start.33 = (bf16[2,128,768]{2,1,0:T(8,128)(2,1)}, bf16[2,128,768]{2,1,0:T(8,128)(2,1)}, u32[]{:S(2)}, u32[]{:S(2)}) collective-permute-start(bf16[2,128,768]{2,1,0:T(8,128)(2,1)} %get-tuple-element.59), channel_id=1, source_target_pairs={{0,8},{4,12},{8,0},{12,4},{1,9},{5,13},{9,1},{13,5},{2,10},{6,14},... | collective-permute-start | bytes 1179656 | tf_op jit(solution)/shard_map/ppermute | solution.py:23
  218.0 33.2 %collective-permute-start.30 = (bf16[128,2048]{1,0:T(8,128)(2,1)}, bf16[128,2048]{1,0:T(8,128)(2,1)}, u32[]{:S(2)}, u32[]{:S(2)}) collective-permute-start(bf16[128,2048]{1,0:T(8,128)(2,1)} %get-tuple-element.57), channel_id=1, source_target_pairs={{0,1},{1,0},{2,3},{3,2},{4,5},{5,4},{6,7},{7,6},{8,9},{9,8},{10,11... | collective-permute-start | bytes 1572872 | tf_op jit(solution)/shard_map/ppermute | solution.py:23
  237.5 13.1 %collective-permute-start.37 = (bf16[128,768]{1,0:T(8,128)(2,1)}, bf16[128,768]{1,0:T(8,128)(2,1)}, u32[]{:S(2)}, u32[]{:S(2)}) collective-permute-start(bf16[128,768]{1,0:T(8,128)(2,1)} %step_g.17.refs_7_.refs_3_), channel_id=1, source_target_pairs={{0,8},{4,12},{8,0},{12,4},{1,9},{5,13},{9,1},{13,5},{2,10},{6,14},... | collective-permute-start | bytes 589832 | tf_op jit(solution)/shard_map/ppermute | solution.py:23
  239.2 16.7 %collective-permute-start.36 = (bf16[128,768]{1,0:T(8,128)(2,1)}, bf16[128,768]{1,0:T(8,128)(2,1)}, u32[]{:S(2)}, u32[]{:S(2)}) collective-permute-start(bf16[128,768]{1,0:T(8,128)(2,1)} %step_g.17.refs_7_.refs_3_), channel_id=1, source_target_pairs={{0,4},{4,0},{8,12},{12,8},{1,5},{5,1},{9,13},{13,9},{2,6},{6,2},{1... | collective-permute-start | bytes 589832 | tf_op jit(solution)/shard_map/ppermute | solution.py:23
  253.3 26.3 %collective-permute-start.31 = (bf16[128,2048]{1,0:T(8,128)(2,1)}, bf16[128,2048]{1,0:T(8,128)(2,1)}, u32[]{:S(2)}, u32[]{:S(2)}) collective-permute-start(bf16[128,2048]{1,0:T(8,128)(2,1)} %add_convert_fusion.1), channel_id=1, source_target_pairs={{0,2},{1,3},{2,0},{3,1},{4,6},{5,7},{6,4},{7,5},{8,10},{9,11},{10,... | collective-permute-start | bytes 1572872 | tf_op jit(solution)/shard_map/ppermute | solution.py:23
  266.5 24.2 %collective-permute-start.42 = (bf16[128,2048]{1,0:T(8,128)(2,1)}, bf16[128,2048]{1,0:T(8,128)(2,1)S(1)}, u32[]{:S(2)}, u32[]{:S(2)}) collective-permute-start(bf16[128,2048]{1,0:T(8,128)(2,1)} %step_d.5), channel_id=1, source_target_pairs={{0,1},{1,0},{2,3},{3,2},{4,5},{5,4},{6,7},{7,6},{8,9},{9,8},{10,11... | collective-permute-start | bytes 1572872 | tf_op jit(solution)/shard_map/ppermute | solution.py:23
  (21 other events, 141.1 us)
Sparse Core Ops, SparseCore 0:
  8.9 48.8 all-gather.1

commit v3 on v0

v3 whole, which is shorter than its diff:
```python
import functools

import jax
import jax.numpy as jnp
from jax import lax
from jax.experimental import pallas as pl
from jax.experimental.pallas import tpu as pltpu
from jax.sharding import PartitionSpec as P

EPS = 1e-05
LANES = 128
DEPTH = 512
BREADTH = 2048
UNIT = 128
AHEAD = 4
SLOTS = AHEAD + 1
COST = pl.CostEstimate(flops=1000, bytes_accessed=1000, transcendentals=0)
VMEM_LIMIT = 64 * 1024 * 1024 - 64 * 1024
ANY = pl.BlockSpec(memory_space=pl.ANY)
SMEM = pl.BlockSpec(memory_space=pltpu.SMEM)


def swap(value, axis, size, mask):
    return lax.ppermute(value, axis, [(i, i ^ mask) for i in range(size)])


def silu_product(gate, up, scale):
    gate = gate * scale
    return gate / (1.0 + jnp.exp(-gate)) * (up * scale)


def multiple(value, of):
    return value if isinstance(value, int) else pl.multiple_of(value, of)


class Group:
    def __init__(self, toks, block):
        self.toks, self.block, self.rows = toks, block, block * len(toks)

    def plain(self, table):
        return jnp.concatenate([lax.dynamic_slice_in_dim(t, table[i], self.block, 0) for t, i in self.toks], axis=0)


class GateUp:
    def __init__(self, group, place, low, width, recvs=(), squares=(), finish=False, emit=False, features=1):
        self.group, self.place, self.low, self.width, self.recvs = group, place, low, width, list(recvs)
        self.squares, self.finish, self.emit, self.features = list(squares), finish, emit, features
        rows = group.rows
        self.outs = [jax.ShapeDtypeStruct((rows, width) if finish else (2, rows, width), jnp.bfloat16)]
        if emit:
            self.outs.append(jax.ShapeDtypeStruct((rows, LANES), jnp.float32))

    def fits(self, depth, columns):
        return self.width % LANES == 0 and 2 * self.width <= BREADTH and depth % DEPTH == 0 and self.group.block % 16 == 0

    def arrays(self):
        return [*self.recvs, *[s for s in self.squares if s is not None]]

    def plain(self, table, gate_matrix, up_matrix, down_matrix):
        tok = self.group.plain(table)
        gate, up = (
            jnp.dot(
                tok,
                lax.dynamic_slice_in_dim(m, table[self.place] + self.low, self.width, 1),
                preferred_element_type=jnp.float32,
            )
            for m in (gate_matrix, up_matrix)
        )
        for r in self.recvs:
            gate, up = gate + r[0].astype(jnp.float32), up + r[1].astype(jnp.float32)
        values = tok.astype(jnp.float32)
        own = jnp.broadcast_to(jnp.sum(values * values, axis=1, keepdims=True), (tok.shape[0], LANES))
        squares = sum(own if s is None else s for s in self.squares)
        if self.finish:
            scale = lax.rsqrt(squares[:, :1] / self.features + EPS)
            return [silu_product(gate, up, scale).astype(jnp.bfloat16)]
        return [jnp.stack([gate, up]).astype(jnp.bfloat16)] + ([squares] if self.emit else [])

    def scratch(self):
        rows, n, s = self.group.rows, self.width, len(self.arrays()) - len(self.recvs)
        return [
            pltpu.VMEM((max(len(self.recvs), 1), 2, rows, n) if self.recvs else (1, 2, 16, LANES), jnp.bfloat16),
            pltpu.VMEM((max(s, 1), rows, LANES), jnp.float32),
            pltpu.VMEM((1 if self.finish else 2, rows, n), jnp.bfloat16),
            pltpu.VMEM((rows, LANES), jnp.float32),
            pltpu.SemaphoreType.DMA((len(self.recvs) + s + 1,)),
            pltpu.SemaphoreType.DMA((2,)),
        ]

    def bind(self, refs, table, arrays, outs, scratch):
        rbuf, sbuf, obuf, qbuf, rsem, osem = scratch
        n, rows, n_recv = self.width, self.group.rows, len(self.recvs)
        xbuf, acc = refs["x"][id(self.group)], refs["acc"]
        self.count = xbuf.shape[1] // DEPTH
        columns = pl.ds(pl.multiple_of(table[self.place] + self.low, LANES), n)

        def weights(k, slot):
            part = pl.ds(multiple(k * DEPTH, DEPTH), DEPTH)
            return [
                pltpu.make_async_copy(m.at[part, columns], refs["w"].at[slot, :, pl.ds(i * n, n)], refs["wsem"].at[slot, i])
                for i, m in enumerate((refs["gate"], refs["up"]))
            ]

        copies = [pltpu.make_async_copy(a, rbuf.at[i], rsem.at[i]) for i, a in enumerate(arrays[:n_recv])]
        copies += [pltpu.make_async_copy(a, sbuf.at[i], rsem.at[n_recv + i]) for i, a in enumerate(arrays[n_recv:])]
        writes = [pltpu.make_async_copy(obuf.at[0] if self.finish else obuf, outs[0], osem.at[0])]
        if self.emit:
            writes.append(pltpu.make_async_copy(qbuf, outs[1], osem.at[1]))

        def multiply(k, slot):
            part = pl.ds(multiple(k * DEPTH, LANES), DEPTH)
            acc[:rows, : 2 * n] += jnp.dot(
                xbuf[:, part], refs["w"][slot, :, : 2 * n], preferred_element_type=jnp.float32
            )

        def sums():
            held, total = 0, None
            for s in self.squares:
                if s is None:
                    values = xbuf[...].astype(jnp.float32)
                    term = jnp.broadcast_to(jnp.sum(values * values, axis=1, keepdims=True), (rows, LANES))
                else:
                    term, held = sbuf[held], held + 1
                total = term if total is None else total + term
            return total

        def end():
            for copy in copies:
                copy.wait()
            if self.emit:
                qbuf[...] = sums()
            if self.finish:
                scale = lax.rsqrt(sums()[:, :1] / self.features + EPS)
            for low in range(0, n, LANES):
                gate, up = acc[:rows, low : low + LANES], acc[:rows, n + low : n + low + LANES]
                for r in range(n_recv):
                    gate = gate + rbuf[r, 0, :, low : low + LANES].astype(jnp.float32)
                    up = up + rbuf[r, 1, :, low : low + LANES].astype(jnp.float32)
                if self.finish:
                    obuf[0, :, low : low + LANES] = silu_product(gate, up, scale).astype(jnp.bfloat16)
                else:
                    obuf[0, :, low : low + LANES] = gate.astype(jnp.bfloat16)
                    obuf[1, :, low : low + LANES] = up.astype(jnp.bfloat16)
            for copy in writes:
                copy.start()

        self.weights, self.copies, self.multiply, self.end, self.writes = weights, copies, multiply, end, writes

    def clear(self, acc):
        acc[: self.group.rows, : 2 * self.width] = jnp.zeros((self.group.rows, 2 * self.width), jnp.float32)


class Down:
    def __init__(self, pieces, places, lows, total, block, columns, dtype):
        self.pieces, self.places, self.lows, self.total, self.block, self.dtype = pieces, places, lows, total, block, dtype
        self.rows, self.columns, self.group = pieces[0].shape[0], columns, None
        self.outs = [jax.ShapeDtypeStruct((block, columns), dtype) for _ in range(self.rows // block)]

    def fits(self, depth, columns):
        whole = sum(p.shape[1] for p in self.pieces) % DEPTH == 0
        return all(p.shape[1] % UNIT == 0 for p in self.pieces) and whole and columns <= BREADTH and columns % LANES == 0

    def arrays(self):
        return [*self.pieces, *(self.total or [])]

    def plain(self, table, gate_matrix, up_matrix, down_matrix):
        result = sum(
            jnp.dot(
                p, lax.dynamic_slice_in_dim(down_matrix, table[i] + low, p.shape[1], 0), preferred_element_type=jnp.float32
            )
            for p, i, low in zip(self.pieces, self.places, self.lows)
        )
        if self.total is not None:
            result = result + jnp.concatenate(self.total, axis=0)
        return jnp.split(result.astype(self.dtype), len(self.outs))

    def scratch(self):
        return [
            pltpu.VMEM((self.rows, sum(p.shape[1] for p in self.pieces)), jnp.bfloat16),
            pltpu.VMEM((self.rows if self.total else 8, self.columns), jnp.float32),
            pltpu.VMEM((self.rows, self.columns), self.dtype),
            pltpu.SemaphoreType.DMA((len(self.pieces) + len(self.outs),)),
            pltpu.SemaphoreType.DMA((len(self.outs),)),
        ]

    def bind(self, refs, table, arrays, outs, scratch):
        hbuf, tbuf, obuf, hsem, osem = scratch
        n, rows, block, columns, acc = len(self.pieces), self.rows, self.block, self.columns, refs["acc"]
        sizes = [p.shape[1] for p in self.pieces]
        self.count = sum(sizes) // DEPTH
        firsts = [sum(sizes[:p]) // UNIT for p in range(n)]
        starts = [table[i] + low for i, low in zip(self.places, self.lows)]

        def weights(k, slot):
            copies = []
            for i in range(DEPTH // UNIT):
                unit = k * (DEPTH // UNIT) + i
                row = starts[0] + unit * UNIT
                for p in range(1, n):
                    row = jnp.where(unit >= firsts[p], starts[p] + (unit - firsts[p]) * UNIT, row)
                copies.append(
                    pltpu.make_async_copy(
                        refs["down"].at[pl.ds(pl.multiple_of(row, UNIT), UNIT)],
                        refs["w"].at[slot, pl.ds(i * UNIT, UNIT), pl.ds(0, columns)],
                        refs["wsem"].at[slot, i],
                    )
                )
            return copies

        copies = [
            pltpu.make_async_copy(a, hbuf.at[:, pl.ds(first * UNIT, size)], hsem.at[i])
            for i, (a, first, size) in enumerate(zip(arrays, firsts, sizes))
        ]
        copies += [
            pltpu.make_async_copy(a, tbuf.at[pl.ds(i * block, block)], hsem.at[n + i]) for i, a in enumerate(arrays[n:])
        ]
        writes = [
            pltpu.make_async_copy(obuf.at[pl.ds(i * block, block)], out, osem.at[i]) for i, out in enumerate(outs)
        ]

        def multiply(k, slot):
            part = pl.ds(multiple(k * DEPTH, LANES), DEPTH)
            acc[:rows, :columns] += jnp.dot(
                hbuf[:, part], refs["w"][slot, :, :columns], preferred_element_type=jnp.float32
            )

        def end():
            obuf[...] = acc[:rows, :columns].astype(obuf.dtype)
            for copy in writes:
                copy.start()

        self.tbuf = tbuf
        self.weights, self.copies, self.multiply, self.end, self.writes = weights, copies, multiply, end, writes

    def clear(self, acc):
        acc[: self.rows, : self.columns] = (
            self.tbuf[...] if self.total else jnp.zeros((self.rows, self.columns), jnp.float32)
        )


def run(phases, table, gate_matrix, up_matrix, down_matrix, dep):
    depth, columns = gate_matrix.shape[0], down_matrix.shape[1]
    if not all(p.fits(depth, columns) for p in phases):
        return [p.plain(table, gate_matrix, up_matrix, down_matrix) for p in phases]
    operands = [gate_matrix, up_matrix, down_matrix]

    def index(array):
        for i, known in enumerate(operands):
            if known is array:
                return i
        operands.append(array)
        return len(operands) - 1

    groups = []
    for p in phases:
        if p.group is not None and all(p.group is not g for g in groups):
            groups.append(p.group)
    tok_places = [[index(t) for t, _ in g.toks] for g in groups]
    where = [[index(a) for a in p.arrays()] for p in phases]
    index(dep)
    outs = [o for p in phases for o in p.outs]
    scratch = [p.scratch() for p in phases]
    rows = max(p.group.rows if p.group is not None else p.rows for p in phases)

    def kernel(table_ref, *args):
        args = list(args)
        arrays = [args.pop(0) for _ in operands]
        out_refs = [args.pop(0) for _ in outs]
        refs = {"gate": arrays[0], "up": arrays[1], "down": arrays[2], "x": {}}
        refs["w"], refs["wsem"], refs["acc"] = args.pop(0), args.pop(0), args.pop(0)
        ready = {}
        for g, places in zip(groups, tok_places):
            xbuf, xsem = args.pop(0), args.pop(0)
            refs["x"][id(g)] = xbuf
            ready[id(g)] = [
                pltpu.make_async_copy(
                    arrays[place].at[pl.ds(pl.multiple_of(table_ref[i], 16), g.block)],
                    xbuf.at[pl.ds(j * g.block, g.block)],
                    xsem.at[j],
                )
                for j, (place, (_, i)) in enumerate(zip(places, g.toks))
            ]
        for p, places, buffers in zip(phases, where, scratch):
            mine = [out_refs.pop(0) for _ in p.outs]
            held = [args.pop(0) for _ in buffers]
            p.bind(refs, table_ref, [arrays[i] for i in places], mine, held)

        def begin(i, k, slot):
            for copy in phases[i].weights(k, slot):
                copy.start()

        offsets = [sum(q.count for q in phases[:i]) for i in range(len(phases) + 1)]
        for g in groups[:1]:
            for copy in ready[id(g)]:
                copy.start()
        for t in range(min(AHEAD, offsets[-1])):
            i = max(j for j in range(len(phases)) if offsets[j] <= t)
            begin(i, t - offsets[i], t % SLOTS)
        for g in groups[1:]:
            for copy in ready[id(g)]:
                copy.start()
        for p in phases:
            for copy in p.copies:
                copy.start()
        for i, p in enumerate(phases):
            if p.group is not None:
                for copy in ready.pop(id(p.group), []):
                    copy.wait()
            else:
                for copy in p.copies:
                    copy.wait()
            p.clear(refs["acc"])

            @pl.loop(0, p.count)
            def _(k):
                t = offsets[i] + k
                slot = lax.rem(t, SLOTS)
                for copy in p.weights(k, slot):
                    copy.wait()
                later = lax.rem(t + AHEAD, SLOTS)
                for j in range(i, len(phases)):
                    if offsets[j] < offsets[i + 1] + AHEAD:
                        @pl.when((t + AHEAD >= offsets[j]) & (t + AHEAD < offsets[j + 1]))
                        def _():
                            begin(j, t + AHEAD - offsets[j], later)
                p.multiply(k, slot)

            p.end()
        for p in phases:
            for copy in p.writes:
                copy.wait()

    results = list(
        pl.pallas_call(
            kernel,
            out_shape=outs,
            in_specs=[SMEM] + [ANY] * len(operands),
            out_specs=[ANY] * len(outs),
            scratch_shapes=[
                pltpu.VMEM((SLOTS, DEPTH, BREADTH), jnp.bfloat16),
                pltpu.SemaphoreType.DMA((SLOTS, DEPTH // UNIT)),
                pltpu.VMEM((rows, BREADTH), jnp.float32),
                *[
                    buffer
                    for g in groups
                    for buffer in (pltpu.VMEM((g.rows, depth), jnp.bfloat16), pltpu.SemaphoreType.DMA((len(g.toks),)))
                ],
                *[buffer for buffers in scratch for buffer in buffers],
            ],
            compiler_params=pltpu.CompilerParams(vmem_limit_bytes=VMEM_LIMIT),
            cost_estimate=COST,
            name="step_" + "".join("g" if p.group is not None else "d" for p in phases),
        )(table, *operands)
    )
    return [[results.pop(0) for _ in p.outs] for p in phases]


STEPS = (
    ("s0", "s1"),
    ("x0",),
    ("x1",),
    ("h0",),
    ("h1",),
    ("r0", "s2"),
    ("r1", "s3"),
    ("x2",),
    ("x3", "s4", "s5", "d0", "d1"),
    ("h2",),
    ("h3",),
    ("r2", "x4", "x5"),
    ("r3", "d2", "d3"),
    ("h4",),
    ("h5",),
    ("r4", "d4"),
    ("r5", "d5"),
)


def cut(width, part, parts):
    unit = LANES if width % LANES == 0 else 1
    return width // unit * part // parts * unit


def on_device(n_gx, n_gy, tokens, gate_matrix, up_matrix, down_matrix):
    features = tokens.shape[1] * n_gx
    width = gate_matrix.shape[1] // n_gx
    block, columns = tokens.shape[0], down_matrix.shape[1]
    far = [2 * k for k in range(1, n_gx // 2)]

    def core(value):
        return swap(value, "gx", n_gx, 1)

    gathered = lax.all_gather(tokens, "gy", axis=0, tiled=True)
    table = jnp.concatenate(
        [
            (lax.axis_index("gx") ^ jnp.arange(n_gx, dtype=jnp.int32)) * width,
            (lax.axis_index("gy") ^ jnp.arange(n_gy, dtype=jnp.int32)) * block,
            jnp.zeros((1,), jnp.int32),
        ]
    )
    sets = [[0], list(range(2, n_gy)), [1]]
    groups = [Group([(gathered, n_gx + j) if j else (tokens, n_gx + n_gy) for j in js], block) for js in sets]
    squares = [None] * len(groups)
    half = cut(width, 7, 13)
    jobs = [(g, low, high - low) for g in range(len(groups)) for low, high in ((0, half), (half, width))]
    state = [dict() for _ in jobs]
    totals = {}
    chain = tokens

    def phases_of(kind, job):
        g, low, n = jobs[job]
        group, st, first = groups[g], state[job], low == 0
        if kind == "s":
            return [
                GateUp(group, k ^ 1, low, n, squares=[None], emit=first and k == 0) for k in [*far, 0]
            ]
        if kind == "x":
            return [
                GateUp(group, k, low, n, [st["lent"][i]], squares=[None, squares[g]] if first else [], emit=first and i == 0)
                for i, k in enumerate(far)
            ]
        if kind == "h":
            return [GateUp(group, 0, low, n, [st["lent"][-1], *st["far"]], squares[g], finish=True, features=features)]
        pieces = [(st["hidden"], 0), (st["sibling"], 1)] + st["over"]
        return [
            Down(
                [h for h, _ in pieces], [q for _, q in pieces], [low] * len(pieces), totals.get(g), block, columns,
                jnp.bfloat16 if not first and g else jnp.float32,
            )
        ]

    def deliver(kind, job, outs):
        g, st = jobs[job][0], state[job]
        if kind == "s":
            st["lent"] = [core(o[0]) for o in outs]
            if jobs[job][1] == 0:
                squares[g] = core(outs[-1][1])
        elif kind == "x":
            st["far"] = [swap(o[0], "gx", n_gx, k) for o, k in zip(outs, far)]
            if jobs[job][1] == 0:
                squares[g] = [outs[0][1], *[swap(outs[0][1], "gx", n_gx, k) for k in far]]
        elif kind == "h":
            st["hidden"], st["sibling"] = outs[0][0], core(outs[0][0])
            st["crossed"] = [swap(outs[0][0], "gx", n_gx, k) for k in far]
        else:
            totals[g] = outs[0]

    def forward(job):
        nonlocal chain
        crossed, chain = lax.optimization_barrier((state[job]["crossed"], chain))
        state[job]["over"] = [(h, k) for h, k in zip(crossed, far)]
        state[job]["over"] += [(core(h), k ^ 1) for h, k in zip(crossed, far)]

    for names in STEPS:
        items = []
        for kind, job in [(name[0], int(name[1:])) for name in names]:
            if kind == "r":
                forward(job)
                continue
            found = phases_of(kind, job)
            if kind == "d" and items and items[-1][0] == "d" and jobs[items[-1][1]][0] == jobs[job][0]:
                before, after = items.pop()[2][0], found[0]
                found = [
                    Down(
                        before.pieces + after.pieces, before.places + after.places, before.lows + after.lows, before.total,
                        block, columns, after.dtype,
                    )
                ]
            items.append((kind, job, found))
        results = run([p for _, _, ps in items for p in ps], table, gate_matrix, up_matrix, down_matrix, chain)
        chain = results[0][0]
        for kind, job, ps in items:
            deliver(kind, job, [results.pop(0) for _ in ps])

    parts = dict(zip(sets[1], totals[1]))
    parts[0] = totals[0][0]
    mask = 1
    while mask < n_gy:
        for j in [j for j in parts if j & mask]:
            arrived = swap(parts.pop(j), "gy", n_gy, mask).astype(jnp.float32)
            total = parts[j ^ mask].astype(jnp.float32) + arrived
            parts[j ^ mask] = total if j == mask else total.astype(jnp.bfloat16)
        mask *= 2
    last = swap(totals[2][0], "gy", n_gy, 1).astype(jnp.float32)
    return (parts[0] + last).astype(jnp.bfloat16)


def solution(mesh):
    n_gx, n_gy = mesh.shape["gx"], mesh.shape["gy"]
    placed = (P(("groups", "gy"), "gx"), P("gx", "gy"), P("gx", "gy"), P("gy", "gx"))
    return jax.shard_map(
        functools.partial(on_device, n_gx, n_gy),
        mesh=mesh,
        in_specs=placed,
        out_specs=P(("groups", "gy"), "gx"),
        check_vma=False,
    )
```

time: 350 us -> 290 us (0.83)
  Pallas kernels: 0 us -> 169 us
  waiting for transfers between devices: 228 us -> 72.7 us
  matrix products: 66.5 us -> 0 us
  starting transfers between devices: 0.35 us -> 29.9 us
  local copies, waits for them, and re-layouts: 26.9 us -> 0 us
  blocking collectives: 8.34 us -> 0 us
    pallas_call x0 -> x17, Pallas kernels: none -> 169 us  [run(): pl.pallas_call(kernel, out_shape=outs, in_specs=[SMEM] + [ANY] * len(oper...]
    all_gather x2 -> x1, waiting for transfers between devices: 95.8 us -> 0.02 us  [on_device(): gathered = lax.all_gather(tokens, 'gy', axis=0, tiled=True)]
    unnamed x7 -> x1, waiting for transfers between devices: 88.3 us -> 0.71 us
    ppermute x0 -> x45, waiting for transfers between devices: none -> 72 us  [swap(): return lax.ppermute(value, axis, [(i, i ^ mask) for i in range(size)])]
    dot_general x3 -> x0, matrix products: 66.5 us -> none  [the longest x1 22.6 us: on_device(): jnp.dot(gathered, gate_matrix, preferred_element_type=jnp.float32)]
    reduce_scatter x1 -> x0, waiting for transfers between devices: 44 us -> none  [on_device(): lax.psum_scatter(partial_out.astype(jnp.bfloat16), 'gy', scatter_dimensio...]
    ppermute x0 -> x45, starting transfers between devices: none -> 29.9 us  [swap(): return lax.ppermute(value, axis, [(i, i ^ mask) for i in range(size)])]
    unnamed x6 -> x0, local copies, waits for them, and re-layouts: 26.9 us -> none
  transfers between devices with their start and end apart: 5 -> 46, of which waited for: 5 -> 12; matrix products, arithmetic and copies ran while one was open for 10% -> 1% of each run, Pallas kernels for 0% -> 54%
where the time goes in v3:
time: 290 us
  Pallas kernels  169 us (58%)
  waiting for transfers between devices  72.7 us (25%)
  starting transfers between devices  29.9 us (10%)
  between operations  13.7 us (5%)
  other arithmetic  5.13 us (2%)
    pallas_call x17, Pallas kernels, run(): pl.pallas_call(kernel, out_shape=outs, in_specs=[SMEM] + [ANY] * len(oper...  169 us
    ppermute x45, waiting for transfers between devices, swap(): return lax.ppermute(value, axis, [(i, i ^ mask) for i in range(size)])  72 us
    ppermute x45, starting transfers between devices, swap(): return lax.ppermute(value, axis, [(i, i ^ mask) for i in range(size)])  29.9 us
  transfers between devices with their start and end apart: 46, of which 12 were waited for; matrix products, arithmetic and copies ran while one was open for 1% of the time, Pallas kernels for 54%

profile of v3, /device:TPU:0, one launch (start us, length us, event | category | flops | bytes accessed | tf_op | source)
XLA Modules:
  0.0 290.0 jit_solution(3939889257196668657)
XLA Ops:
  7.9 13.4 %step_gggg.1 = (bf16[2,128,896]{2,1,0:T(8,128)(2,1)}, bf16[2,128,896]{2,1,0:T(8,128)(2,1)}, f32[128,128]{1,0:T(8,128)}, bf16[2,128,768]{2,1,0:T(8,128)(2,1)}, bf16[2,128,768]{2,1,0:T(8,128)(2,1)}) custom-call(s32[9]{0:T(128)} %pad_add_fusion.table_ref, bf16[2048,6656]{1,0:T(8,128)(2,1)} %args_0_.36, bf16[2048,6656]{1,0:T(8,128)(2,1)} %args_1_.36, ...), custom_call_target="tpu_custom_call" | custom-call | flops 1000 | bytes 1000 | tf_op jit(solution)/shard_map/step_gggg/pallas_call | solution.py:334
  24.3 6.8 %step_g.9 = (bf16[2,128,896]{2,1,0:T(8,128)(2,1)}, f32[128,128]{1,0:T(8,128)}) custom-call(s32[9]{0:T(128)} %pad_add_fusion.table_ref, bf16[2048,6656]{1,0:T(8,128)(2,1)} %args_0_.36, bf16[2048,6656]{1,0:T(8,128)(2,1)} %args_1_.36, bf16[6656,2048]{1,0:T(8,128)(2,1)} %args_2_.36, bf16[128,2048]{1,0:T(8,128)(2,1)} %args_3_.12, ...), custom_call_target="tpu_custom_call" | custom-call | flops 1000 | bytes 1000 | tf_op jit(solution)/shard_map/step_g/pallas_call | solution.py:334
  31.1 3.1 %collective-permute-start.7 = (bf16[2,128,896]{2,1,0:T(8,128)(2,1)}, bf16[2,128,896]{2,1,0:T(8,128)(2,1)}, u32[]{:S(2)}, u32[]{:S(2)}) collective-permute-start(bf16[2,128,896]{2,1,0:T(8,128)(2,1)} %get-tuple-element.47.args_5_), channel_id=1, source_target_pairs={{0,8},{4,12},{8,0},{12,4},{1,9},{5,13},{9,1},{13,5},{2,10},{6,14},... | collective-permute-start | bytes 1376264 | tf_op jit(solution)/shard_map/ppermute | solution.py:24
  34.2 6.2 %step_g.10.args_8_ = bf16[2,128,768]{2,1,0:T(8,128)(2,1)} custom-call(s32[9]{0:T(128)} %pad_add_fusion.table_ref, bf16[2048,6656]{1,0:T(8,128)(2,1)} %args_0_.36, bf16[2048,6656]{1,0:T(8,128)(2,1)} %args_1_.36, bf16[6656,2048]{1,0:T(8,128)(2,1)} %args_2_.36, bf16[128,2048]{1,0:T(8,128)(2,1)} %args_3_.12, ...), custom_call_target="tpu_custom_call" | custom-call | flops 1000 | bytes 1000 | tf_op jit(solution)/shard_map/step_g/pallas_call | solution.py:334
  42.6 12.5 %collective-permute-done.5.args_7_ = f32[128,128]{1,0:T(8,128)} collective-permute-done((f32[128,128]{1,0:T(8,128)}, f32[128,128]{1,0:T(8,128)}, u32[]{:S(2)}, u32[]{:S(2)}) %collective-permute-start.5) | collective-permute-done | bytes 65568 | tf_op jit(solution)/shard_map/ppermute | solution.py:24
  55.1 7.1 %step_g.11.args_8_.args_5_ = bf16[128,896]{1,0:T(8,128)(2,1)} custom-call(s32[9]{0:T(128)} %pad_add_fusion.table_ref, bf16[2048,6656]{1,0:T(8,128)(2,1)} %args_0_.36, bf16[2048,6656]{1,0:T(8,128)(2,1)} %args_1_.36, bf16[6656,2048]{1,0:T(8,128)(2,1)} %args_2_.36, bf16[128,2048]{1,0:T(8,128)(2,1)} %args_3_.12, ...), custom_call_target="tpu_custom_call" | custom-call | flops 1000 | bytes 1000 | tf_op jit(solution)/shard_map/step_g/pallas_call | solution.py:334
  63.9 6.7 %step_g.12.args_4_.args_9_ = bf16[128,768]{1,0:T(8,128)(2,1)} custom-call(s32[9]{0:T(128)} %pad_add_fusion.table_ref, bf16[2048,6656]{1,0:T(8,128)(2,1)} %args_0_.36, bf16[2048,6656]{1,0:T(8,128)(2,1)} %args_1_.36, bf16[6656,2048]{1,0:T(8,128)(2,1)} %args_2_.36, bf16[128,2048]{1,0:T(8,128)(2,1)} %args_3_.12, ...), custom_call_target="tpu_custom_call" | custom-call | flops 1000 | bytes 1000 | tf_op jit(solution)/shard_map/step_g/pallas_call | solution.py:334
  70.7 11.1 %step_gg.3 = (bf16[2,256,896]{2,1,0:T(8,128)(2,1)}, bf16[2,256,896]{2,1,0:T(8,128)(2,1)}, f32[256,128]{1,0:T(8,128)}) custom-call(s32[9]{0:T(128)} %pad_add_fusion.table_ref, bf16[2048,6656]{1,0:T(8,128)(2,1)} %args_0_.36, bf16[2048,6656]{1,0:T(8,128)(2,1)} %args_1_.36, bf16[6656,2048]{1,0:T(8,128)(2,1)} %args_2_.36, ...), custom_call_target="tpu_custom_call" | custom-call | flops 1000 | bytes 1000 | tf_op jit(solution)/shard_map/step_gg/pallas_call | solution.py:334
  82.3 7.2 %collective-permute-done.8.args_11_ = bf16[128,768]{1,0:T(8,128)(2,1)} collective-permute-done((bf16[128,768]{1,0:T(8,128)(2,1)}, bf16[128,768]{1,0:T(8,128)(2,1)}, u32[]{:S(2)}, u32[]{:S(2)}) %collective-permute-start.8) | collective-permute-done | bytes 196640 | tf_op jit(solution)/shard_map/ppermute | solution.py:24
  89.5 10.0 %step_gg.4 = (bf16[2,256,768]{2,1,0:T(8,128)(2,1)}, bf16[2,256,768]{2,1,0:T(8,128)(2,1)}) custom-call(s32[9]{0:T(128)} %pad_add_fusion.table_ref, bf16[2048,6656]{1,0:T(8,128)(2,1)} %args_0_.36, bf16[2048,6656]{1,0:T(8,128)(2,1)} %args_1_.36, bf16[6656,2048]{1,0:T(8,128)(2,1)} %args_2_.36, bf16[512,2048]{1,0:T(8,128)(2,1)} %all-gather.2.cloned.1.call-done.args_3_, ...), custom_call_target="tpu_custom_call" | custom-call | flops 1000 | bytes 1000 | tf_op jit(solution)/shard_map/step_gg/pallas_call | solution.py:334
  103.1 8.8 %step_g.13 = (bf16[2,256,896]{2,1,0:T(8,128)(2,1)}, f32[256,128]{1,0:T(8,128)}) custom-call(s32[9]{0:T(128)} %pad_add_fusion.table_ref, bf16[2048,6656]{1,0:T(8,128)(2,1)} %args_0_.36, bf16[2048,6656]{1,0:T(8,128)(2,1)} %args_1_.36, bf16[6656,2048]{1,0:T(8,128)(2,1)} %args_2_.36, bf16[512,2048]{1,0:T(8,128)(2,1)} %all-gather.2.cloned.1.call-done.args_3_, ...), custom_call_target="tpu_custom_call" | custom-call | flops 1000 | bytes 1000 | tf_op jit(solution)/shard_map/step_g/pallas_call | solution.py:334
  114.6 24.6 %step_gggggd.1 = (bf16[2,256,768]{2,1,0:T(8,128)(2,1)}, bf16[2,128,896]{2,1,0:T(8,128)(2,1)}, bf16[2,128,896]{2,1,0:T(8,128)(2,1)}, f32[128,128]{1,0:T(8,128)}, ...) custom-call(s32[9]{0:T(128)} %pad_add_fusion.table_ref, ...), custom_call_target="tpu_custom_call" | custom-call | flops 1000 | bytes 1000 | tf_op jit(solution)/shard_map/step_gggggd/pallas_call | solution.py:334
  141.3 20.7 %collective-permute-done.19.args_7_ = f32[256,128]{1,0:T(8,128)} collective-permute-done((f32[256,128]{1,0:T(8,128)}, f32[256,128]{1,0:T(8,128)}, u32[]{:S(2)}, u32[]{:S(2)}) %collective-permute-start.19) | collective-permute-done | bytes 131104 | tf_op jit(solution)/shard_map/ppermute | solution.py:24
  162.0 8.9 %step_g.14.args_8_.args_3_ = bf16[256,896]{1,0:T(8,128)(2,1)} custom-call(s32[9]{0:T(128)} %pad_add_fusion.table_ref, bf16[2048,6656]{1,0:T(8,128)(2,1)} %args_0_.36, bf16[2048,6656]{1,0:T(8,128)(2,1)} %args_1_.36, bf16[6656,2048]{1,0:T(8,128)(2,1)} %args_2_.36, bf16[512,2048]{1,0:T(8,128)(2,1)} %all-gather.2.cloned.1.call-done.args_3_, ...), custom_call_target="tpu_custom_call" | custom-call | flops 1000 | bytes 1000 | tf_op jit(solution)/shard_map/step_g/pallas_call | solution.py:334
  173.1 8.2 %step_g.15.args_7_ = bf16[256,768]{1,0:T(8,128)(2,1)} custom-call(s32[9]{0:T(128)} %pad_add_fusion.table_ref, bf16[2048,6656]{1,0:T(8,128)(2,1)} %args_0_.36, bf16[2048,6656]{1,0:T(8,128)(2,1)} %args_1_.36, bf16[6656,2048]{1,0:T(8,128)(2,1)} %args_2_.36, bf16[512,2048]{1,0:T(8,128)(2,1)} %all-gather.2.cloned.1.call-done.args_3_, ...), custom_call_target="tpu_custom_call" | custom-call | flops 1000 | bytes 1000 | tf_op jit(solution)/shard_map/step_g/pallas_call | solution.py:334
  184.0 8.7 %step_gg.5 = (bf16[2,128,896]{2,1,0:T(8,128)(2,1)}, f32[128,128]{1,0:T(8,128)}, bf16[2,128,768]{2,1,0:T(8,128)(2,1)}) custom-call(s32[9]{0:T(128)} %pad_add_fusion.table_ref, bf16[2048,6656]{1,0:T(8,128)(2,1)} %args_0_.36, bf16[2048,6656]{1,0:T(8,128)(2,1)} %args_1_.36, bf16[6656,2048]{1,0:T(8,128)(2,1)} %args_2_.36, ...), custom_call_target="tpu_custom_call" | custom-call | flops 1000 | bytes 1000 | tf_op jit(solution)/shard_map/step_gg/pallas_call | solution.py:334
  197.2 16.4 %step_d.3 = (bf16[128,2048]{1,0:T(8,128)(2,1)}, bf16[128,2048]{1,0:T(8,128)(2,1)}) custom-call(s32[9]{0:T(128)} %pad_add_fusion.table_ref, bf16[2048,6656]{1,0:T(8,128)(2,1)} %args_0_.36, bf16[2048,6656]{1,0:T(8,128)(2,1)} %args_1_.36, bf16[6656,2048]{1,0:T(8,128)(2,1)} %args_2_.36, bf16[256,896]{1,0:T(8,128)(2,1)} %step_g.14.args_8_.args_3_, ...), custom_call_target="tpu_custom_call" | custom-call | flops 1000 | bytes 1000 | tf_op jit(solution)/shard_map/step_d/pallas_call | solution.py:334
  216.4 7.1 %step_g.16.args_8_.args_3_ = bf16[128,896]{1,0:T(8,128)(2,1)} custom-call(s32[9]{0:T(128)} %pad_add_fusion.table_ref, bf16[2048,6656]{1,0:T(8,128)(2,1)} %args_0_.36, bf16[2048,6656]{1,0:T(8,128)(2,1)} %args_1_.36, bf16[6656,2048]{1,0:T(8,128)(2,1)} %args_2_.36, bf16[512,2048]{1,0:T(8,128)(2,1)} %all-gather.2.cloned.1.call-done.args_3_, ...), custom_call_target="tpu_custom_call" | custom-call | flops 1000 | bytes 1000 | tf_op jit(solution)/shard_map/step_g/pallas_call | solution.py:334
  225.0 6.7 %step_g.17.args_7_.args_3_ = bf16[128,768]{1,0:T(8,128)(2,1)} custom-call(s32[9]{0:T(128)} %pad_add_fusion.table_ref, bf16[2048,6656]{1,0:T(8,128)(2,1)} %args_0_.36, bf16[2048,6656]{1,0:T(8,128)(2,1)} %args_1_.36, bf16[6656,2048]{1,0:T(8,128)(2,1)} %args_2_.36, bf16[512,2048]{1,0:T(8,128)(2,1)} %all-gather.2.cloned.1.call-done.args_3_, ...), custom_call_target="tpu_custom_call" | custom-call | flops 1000 | bytes 1000 | tf_op jit(solution)/shard_map/step_g/pallas_call | solution.py:334
  233.8 9.1 %step_d.4.args_7_.args_8_ = f32[128,2048]{1,0:T(8,128)} custom-call(s32[9]{0:T(128)} %pad_add_fusion.table_ref, bf16[2048,6656]{1,0:T(8,128)(2,1)} %args_0_.36, bf16[2048,6656]{1,0:T(8,128)(2,1)} %args_1_.36, bf16[6656,2048]{1,0:T(8,128)(2,1)} %args_2_.36, bf16[128,896]{1,0:T(8,128)(2,1)} %step_g.16.args_8_.args_3_, ...), custom_call_target="tpu_custom_call" | custom-call | flops 1000 | bytes 1000 | tf_op jit(solution)/shard_map/step_d/pallas_call | solution.py:334
  245.5 2.6 collective-permute-start.32
  248.1 8.7 %step_d.5 = bf16[128,2048]{1,0:T(8,128)(2,1)} custom-call(s32[9]{0:T(128)} %pad_add_fusion.table_ref, bf16[2048,6656]{1,0:T(8,128)(2,1)} %args_0_.36, bf16[2048,6656]{1,0:T(8,128)(2,1)} %args_1_.36, bf16[6656,2048]{1,0:T(8,128)(2,1)} %args_2_.36, bf16[128,768]{1,0:T(8,128)(2,1)} %step_g.17.args_7_.args_3_, bf16[128,768]{1,0:T(8,128)(2,1)} %collective-permute-done.38.args_4_, ...), custom_call_target="tpu_custom_call" | custom-call | flops 1000 | bytes 1000 | tf_op jit(solution)/shard_map/step_d/pallas_call | solution.py:334
  258.5 13.5 %collective-permute-done.32 = bf16[128,2048]{1,0:T(8,128)(2,1)} collective-permute-done((bf16[128,2048]{1,0:T(8,128)(2,1)}, bf16[128,2048]{1,0:T(8,128)(2,1)}, u32[]{:S(2)}, u32[]{:S(2)}) %collective-permute-start.32) | collective-permute-done | bytes 524320 | tf_op jit(solution)/shard_map/ppermute | solution.py:24
  272.0 8.8 %collective-permute-done.44 = bf16[128,2048]{1,0:T(8,128)(2,1)S(1)} collective-permute-done((bf16[128,2048]{1,0:T(8,128)(2,1)}, bf16[128,2048]{1,0:T(8,128)(2,1)S(1)}, u32[]{:S(2)}, u32[]{:S(2)}) %collective-permute-start.44) | collective-permute-done | bytes 524320 | tf_op jit(solution)/shard_map/ppermute | solution.py:24
  (90 shorter events, 39.3 us)
Async XLA Ops:
  6.5 64.1 %all-gather.2.cloned.1.call-start = ((), (), s32[]{:S(2)}) async-start(), calls=%async_computation | async-start | bytes 2621440 | tf_op jit(solution)/shard_map/all_gather | solution.py:393
  22.3 20.3 %collective-permute-start.6 = (bf16[2,128,896]{2,1,0:T(8,128)(2,1)}, bf16[2,128,896]{2,1,0:T(8,128)(2,1)}, u32[]{:S(2)}, u32[]{:S(2)}) collective-permute-start(bf16[2,128,896]{2,1,0:T(8,128)(2,1)} %get-tuple-element.49), channel_id=1, source_target_pairs={{0,4},{4,0},{8,12},{12,8},{1,5},{5,1},{9,13},{13,9},{2,6},{6,2},{1... | collective-permute-start | bytes 1376264 | tf_op jit(solution)/shard_map/ppermute | solution.py:24
  31.1 24.0 %collective-permute-start.7 = (bf16[2,128,896]{2,1,0:T(8,128)(2,1)}, bf16[2,128,896]{2,1,0:T(8,128)(2,1)}, u32[]{:S(2)}, u32[]{:S(2)}) collective-permute-start(bf16[2,128,896]{2,1,0:T(8,128)(2,1)} %get-tuple-element.47.args_5_), channel_id=1, source_target_pairs={{0,8},{4,12},{8,0},{12,4},{1,9},{5,13},{9,1},{13,5},{2,10},{6,14},... | collective-permute-start | bytes 1376264 | tf_op jit(solution)/shard_map/ppermute | solution.py:24
  34.2 29.7 %collective-permute-start = (bf16[2,128,768]{2,1,0:T(8,128)(2,1)}, bf16[2,128,768]{2,1,0:T(8,128)(2,1)}, u32[]{:S(2)}, u32[]{:S(2)}) collective-permute-start(bf16[2,128,768]{2,1,0:T(8,128)(2,1)} %get-tuple-element.43), channel_id=1, source_target_pairs={{0,4},{4,0},{8,12},{12,8},{1,5},{5,1},{9,13},{13,9},{2,6},{6,2},{1... | collective-permute-start | bytes 1179656 | tf_op jit(solution)/shard_map/ppermute | solution.py:24
  40.5 23.4 %collective-permute-start.4 = (bf16[2,128,768]{2,1,0:T(8,128)(2,1)}, bf16[2,128,768]{2,1,0:T(8,128)(2,1)}, u32[]{:S(2)}, u32[]{:S(2)}) collective-permute-start(bf16[2,128,768]{2,1,0:T(8,128)(2,1)} %step_g.10.args_8_), channel_id=1, source_target_pairs={{0,8},{4,12},{8,0},{12,4},{1,9},{5,13},{9,1},{13,5},{2,10},{6,14},... | collective-permute-start | bytes 1179656 | tf_op jit(solution)/shard_map/ppermute | solution.py:24
  40.6 14.5 %collective-permute-start.5 = (f32[128,128]{1,0:T(8,128)}, f32[128,128]{1,0:T(8,128)}, u32[]{:S(2)}, u32[]{:S(2)}) collective-permute-start(f32[128,128]{1,0:T(8,128)} %get-tuple-element.48.args_6_), channel_id=1, source_target_pairs={{0,8},{4,12},{8,0},{12,4},{1,9},{5,13},{9,1},{13,5},{2,10},{6,14},... | collective-permute-start | bytes 196616 | tf_op jit(solution)/shard_map/ppermute | solution.py:24
  81.8 21.4 %collective-permute-start.15 = (bf16[2,256,896]{2,1,0:T(8,128)(2,1)}, bf16[2,256,896]{2,1,0:T(8,128)(2,1)}, u32[]{:S(2)}, u32[]{:S(2)}) collective-permute-start(bf16[2,256,896]{2,1,0:T(8,128)(2,1)} %get-tuple-element.52.args_4_), channel_id=1, source_target_pairs={{0,4},{4,0},{8,12},{12,8},{1,5},{5,1},{9,13},{13,9},{2,6},{6,2},{1... | collective-permute-start | bytes 2752520 | tf_op jit(solution)/shard_map/ppermute | solution.py:24
  99.5 15.1 %collective-permute-start.10 = (bf16[2,256,768]{2,1,0:T(8,128)(2,1)}, bf16[2,256,768]{2,1,0:T(8,128)(2,1)}, u32[]{:S(2)}, u32[]{:S(2)}) collective-permute-start(bf16[2,256,768]{2,1,0:T(8,128)(2,1)} %get-tuple-element.53.args_6_), channel_id=1, source_target_pairs={{0,4},{4,0},{8,12},{12,8},{1,5},{5,1},{9,13},{13,9},{2,6},{6,2},{1... | collective-permute-start | bytes 2359304 | tf_op jit(solution)/shard_map/ppermute | solution.py:24
  99.6 12.9 %collective-permute-start.13 = (bf16[128,768]{1,0:T(8,128)(2,1)}, bf16[128,768]{1,0:T(8,128)(2,1)}, u32[]{:S(2)}, u32[]{:S(2)}) collective-permute-start(bf16[128,768]{1,0:T(8,128)(2,1)} %step_g.12.args_4_.args_9_), channel_id=1, source_target_pairs={{0,4},{4,0},{8,12},{12,8},{1,5},{5,1},{9,13},{13,9},{2,6},{6,2},{1... | collective-permute-start | bytes 589832 | tf_op jit(solution)/shard_map/ppermute | solution.py:24
  103.0 38.3 %collective-permute-start.17 = (bf16[2,256,896]{2,1,0:T(8,128)(2,1)}, bf16[2,256,896]{2,1,0:T(8,128)(2,1)}, u32[]{:S(2)}, u32[]{:S(2)}) collective-permute-start(bf16[2,256,896]{2,1,0:T(8,128)(2,1)} %get-tuple-element.59), channel_id=1, source_target_pairs={{0,4},{4,0},{8,12},{12,8},{1,5},{5,1},{9,13},{13,9},{2,6},{6,2},{1... | collective-permute-start | bytes 2752520 | tf_op jit(solution)/shard_map/ppermute | solution.py:24
  112.0 50.1 %collective-permute-start.18 = (bf16[2,256,896]{2,1,0:T(8,128)(2,1)}, bf16[2,256,896]{2,1,0:T(8,128)(2,1)}, u32[]{:S(2)}, u32[]{:S(2)}) collective-permute-start(bf16[2,256,896]{2,1,0:T(8,128)(2,1)} %get-tuple-element.57.args_13_), channel_id=1, source_target_pairs={{0,8},{4,12},{8,0},{12,4},{1,9},{5,13},{9,1},{13,5},{2,10},{6,14},... | collective-permute-start | bytes 2752520 | tf_op jit(solution)/shard_map/ppermute | solution.py:24
  114.3 58.8 %collective-permute-start.22 = (bf16[2,256,768]{2,1,0:T(8,128)(2,1)}, bf16[2,256,768]{2,1,0:T(8,128)(2,1)}, u32[]{:S(2)}, u32[]{:S(2)}) collective-permute-start(bf16[2,256,768]{2,1,0:T(8,128)(2,1)} %get-tuple-element.62), channel_id=1, source_target_pairs={{0,4},{4,0},{8,12},{12,8},{1,5},{5,1},{9,13},{13,9},{2,6},{6,2},{1... | collective-permute-start | bytes 2359304 | tf_op jit(solution)/shard_map/ppermute | solution.py:24
  139.2 33.8 %collective-permute-start.23 = (bf16[2,256,768]{2,1,0:T(8,128)(2,1)}, bf16[2,256,768]{2,1,0:T(8,128)(2,1)}, u32[]{:S(2)}, u32[]{:S(2)}) collective-permute-start(bf16[2,256,768]{2,1,0:T(8,128)(2,1)} %get-tuple-element.61.args_8_), channel_id=1, source_target_pairs={{0,8},{4,12},{8,0},{12,4},{1,9},{5,13},{9,1},{13,5},{2,10},{6,14},... | collective-permute-start | bytes 2359304 | tf_op jit(solution)/shard_map/ppermute | solution.py:24
  140.9 21.1 %collective-permute-start.19 = (f32[256,128]{1,0:T(8,128)}, f32[256,128]{1,0:T(8,128)}, u32[]{:S(2)}, u32[]{:S(2)}) collective-permute-start(f32[256,128]{1,0:T(8,128)} %get-tuple-element.60.args_6_), channel_id=1, source_target_pairs={{0,8},{4,12},{8,0},{12,4},{1,9},{5,13},{9,1},{13,5},{2,10},{6,14},... | collective-permute-start | bytes 393224 | tf_op jit(solution)/shard_map/ppermute | solution.py:24
  170.9 12.7 %collective-permute-start.21 = (bf16[256,896]{1,0:T(8,128)(2,1)}, bf16[256,896]{1,0:T(8,128)(2,1)}, u32[]{:S(2)}, u32[]{:S(2)}) collective-permute-start(bf16[256,896]{1,0:T(8,128)(2,1)} %step_g.14.args_8_.args_3_), channel_id=1, source_target_pairs={{0,8},{4,12},{8,0},{12,4},{1,9},{5,13},{9,1},{13,5},{2,10},{6,14},... | collective-permute-start | bytes 1376264 | tf_op jit(solution)/shard_map/ppermute | solution.py:24
  193.3 20.2 %collective-permute-start.36 = (bf16[2,128,896]{2,1,0:T(8,128)(2,1)}, bf16[2,128,896]{2,1,0:T(8,128)(2,1)}, u32[]{:S(2)}, u32[]{:S(2)}) collective-permute-start(bf16[2,128,896]{2,1,0:T(8,128)(2,1)} %get-tuple-element.76), channel_id=1, source_target_pairs={{0,4},{4,0},{8,12},{12,8},{1,5},{5,1},{9,13},{13,9},{2,6},{6,2},{1... | collective-permute-start | bytes 1376264 | tf_op jit(solution)/shard_map/ppermute | solution.py:24
  193.5 22.9 %collective-permute-start.37 = (bf16[2,128,896]{2,1,0:T(8,128)(2,1)}, bf16[2,128,896]{2,1,0:T(8,128)(2,1)}, u32[]{:S(2)}, u32[]{:S(2)}) collective-permute-start(bf16[2,128,896]{2,1,0:T(8,128)(2,1)} %get-tuple-element.70.args_11_), channel_id=1, source_target_pairs={{0,8},{4,12},{8,0},{12,4},{1,9},{5,13},{9,1},{13,5},{2,10},{6,14},... | collective-permute-start | bytes 1376264 | tf_op jit(solution)/shard_map/ppermute | solution.py:24
  195.0 30.0 %collective-permute-start.33 = (bf16[2,128,768]{2,1,0:T(8,128)(2,1)}, bf16[2,128,768]{2,1,0:T(8,128)(2,1)}, u32[]{:S(2)}, u32[]{:S(2)}) collective-permute-start(bf16[2,128,768]{2,1,0:T(8,128)(2,1)} %get-tuple-element.73), channel_id=1, source_target_pairs={{0,4},{4,0},{8,12},{12,8},{1,5},{5,1},{9,13},{13,9},{2,6},{6,2},{1... | collective-permute-start | bytes 1179656 | tf_op jit(solution)/shard_map/ppermute | solution.py:24
  195.1 29.9 %collective-permute-start.34 = (bf16[2,128,768]{2,1,0:T(8,128)(2,1)}, bf16[2,128,768]{2,1,0:T(8,128)(2,1)}, u32[]{:S(2)}, u32[]{:S(2)}) collective-permute-start(bf16[2,128,768]{2,1,0:T(8,128)(2,1)} %get-tuple-element.74), channel_id=1, source_target_pairs={{0,8},{4,12},{8,0},{12,4},{1,9},{5,13},{9,1},{13,5},{2,10},{6,14},... | collective-permute-start | bytes 1179656 | tf_op jit(solution)/shard_map/ppermute | solution.py:24
  196.4 20.0 %collective-permute-start.35 = (f32[128,128]{1,0:T(8,128)}, f32[128,128]{1,0:T(8,128)}, u32[]{:S(2)}, u32[]{:S(2)}) collective-permute-start(f32[128,128]{1,0:T(8,128)} %get-tuple-element.75.args_6_), channel_id=1, source_target_pairs={{0,8},{4,12},{8,0},{12,4},{1,9},{5,13},{9,1},{13,5},{2,10},{6,14},... | collective-permute-start | bytes 196616 | tf_op jit(solution)/shard_map/ppermute | solution.py:24
  213.6 29.8 %collective-permute-start.31 = (bf16[128,2048]{1,0:T(8,128)(2,1)}, bf16[128,2048]{1,0:T(8,128)(2,1)}, u32[]{:S(2)}, u32[]{:S(2)}) collective-permute-start(bf16[128,2048]{1,0:T(8,128)(2,1)} %get-tuple-element.72), channel_id=1, source_target_pairs={{0,1},{1,0},{2,3},{3,2},{4,5},{5,4},{6,7},{7,6},{8,9},{9,8},{10,11... | collective-permute-start | bytes 1572872 | tf_op jit(solution)/shard_map/ppermute | solution.py:24
  232.9 15.1 %collective-permute-start.38 = (bf16[128,768]{1,0:T(8,128)(2,1)}, bf16[128,768]{1,0:T(8,128)(2,1)}, u32[]{:S(2)}, u32[]{:S(2)}) collective-permute-start(bf16[128,768]{1,0:T(8,128)(2,1)} %step_g.17.args_7_.args_3_), channel_id=1, source_target_pairs={{0,4},{4,0},{8,12},{12,8},{1,5},{5,1},{9,13},{13,9},{2,6},{6,2},{1... | collective-permute-start | bytes 589832 | tf_op jit(solution)/shard_map/ppermute | solution.py:24
  245.5 26.5 %collective-permute-start.32 = (bf16[128,2048]{1,0:T(8,128)(2,1)}, bf16[128,2048]{1,0:T(8,128)(2,1)}, u32[]{:S(2)}, u32[]{:S(2)}) collective-permute-start(bf16[128,2048]{1,0:T(8,128)(2,1)} %add_convert_fusion.1), channel_id=1, source_target_pairs={{0,2},{1,3},{2,0},{3,1},{4,6},{5,7},{6,4},{7,5},{8,10},{9,11},{10,... | collective-permute-start | bytes 1572872 | tf_op jit(solution)/shard_map/ppermute | solution.py:24
  256.8 24.0 %collective-permute-start.44 = (bf16[128,2048]{1,0:T(8,128)(2,1)}, bf16[128,2048]{1,0:T(8,128)(2,1)S(1)}, u32[]{:S(2)}, u32[]{:S(2)}) collective-permute-start(bf16[128,2048]{1,0:T(8,128)(2,1)} %step_d.5), channel_id=1, source_target_pairs={{0,1},{1,0},{2,3},{3,2},{4,5},{5,4},{6,7},{7,6},{8,9},{9,8},{10,11... | collective-permute-start | bytes 1572872 | tf_op jit(solution)/shard_map/ppermute | solution.py:24
  (22 other events, 150.1 us)
Sparse Core Ops, SparseCore 0:
  8.9 48.6 all-gather.1

commit v4 on v3

--- a/solution.py
+++ b/solution.py
@@ -9,10 +9,9 @@
 
 EPS = 1e-05
 LANES = 128
-DEPTH = 512
-BREADTH = 2048
+DEPTH = 256
 UNIT = 128
-AHEAD = 4
+AHEAD = 5
 SLOTS = AHEAD + 1
 COST = pl.CostEstimate(flops=1000, bytes_accessed=1000, transcendentals=0)
 VMEM_LIMIT = 64 * 1024 * 1024 - 64 * 1024
@@ -42,19 +41,19 @@
 
 
 class GateUp:
-    def __init__(self, group, place, low, width, recvs=(), squares=(), finish=False, emit=False, features=1):
+    def __init__(self, group, place, low, width, recvs=(), squares=(), emit=False, features=1):
         self.group, self.place, self.low, self.width, self.recvs = group, place, low, width, list(recvs)
-        self.squares, self.finish, self.emit, self.features = list(squares), finish, emit, features
+        self.squares, self.finish, self.emit, self.features = list(squares), bool(squares), emit, features
         rows = group.rows
-        self.outs = [jax.ShapeDtypeStruct((rows, width) if finish else (2, rows, width), jnp.bfloat16)]
+        self.outs = [jax.ShapeDtypeStruct((rows, width) if self.finish else (2, rows, width), jnp.bfloat16)]
         if emit:
             self.outs.append(jax.ShapeDtypeStruct((rows, LANES), jnp.float32))
 
     def fits(self, depth, columns):
-        return self.width % LANES == 0 and 2 * self.width <= BREADTH and depth % DEPTH == 0 and self.group.block % 16 == 0
+        return self.width % LANES == 0 and depth % DEPTH == 0 and self.group.block % 16 == 0
 
     def arrays(self):
-        return [*self.recvs, *[s for s in self.squares if s is not None]]
+        return [*self.recvs, *[s for s, _ in self.squares]]
 
     def plain(self, table, gate_matrix, up_matrix, down_matrix):
         tok = self.group.plain(table)
@@ -68,19 +67,19 @@
         )
         for r in self.recvs:
             gate, up = gate + r[0].astype(jnp.float32), up + r[1].astype(jnp.float32)
+        if self.finish:
+            squares = Group(self.squares, self.group.block).plain(table)
+            scale = lax.rsqrt(squares[:, :1] / self.features + EPS)
+            return [silu_product(gate, up, scale).astype(jnp.bfloat16)]
         values = tok.astype(jnp.float32)
         own = jnp.broadcast_to(jnp.sum(values * values, axis=1, keepdims=True), (tok.shape[0], LANES))
-        squares = sum(own if s is None else s for s in self.squares)
-        if self.finish:
-            scale = lax.rsqrt(squares[:, :1] / self.features + EPS)
-            return [silu_product(gate, up, scale).astype(jnp.bfloat16)]
-        return [jnp.stack([gate, up]).astype(jnp.bfloat16)] + ([squares] if self.emit else [])
+        return [jnp.stack([gate, up]).astype(jnp.bfloat16)] + ([own] if self.emit else [])
 
     def scratch(self):
-        rows, n, s = self.group.rows, self.width, len(self.arrays()) - len(self.recvs)
+        rows, n, s = self.group.rows, self.width, len(self.squares)
         return [
             pltpu.VMEM((max(len(self.recvs), 1), 2, rows, n) if self.recvs else (1, 2, 16, LANES), jnp.bfloat16),
-            pltpu.VMEM((max(s, 1), rows, LANES), jnp.float32),
+            pltpu.VMEM((rows if s else 8, LANES), jnp.float32),
             pltpu.VMEM((1 if self.finish else 2, rows, n), jnp.bfloat16),
             pltpu.VMEM((rows, LANES), jnp.float32),
             pltpu.SemaphoreType.DMA((len(self.recvs) + s + 1,)),
@@ -102,7 +101,13 @@
             ]
 
         copies = [pltpu.make_async_copy(a, rbuf.at[i], rsem.at[i]) for i, a in enumerate(arrays[:n_recv])]
-        copies += [pltpu.make_async_copy(a, sbuf.at[i], rsem.at[n_recv + i]) for i, a in enumerate(arrays[n_recv:])]
+        block = self.group.block
+        copies += [
+            pltpu.make_async_copy(
+                a.at[pl.ds(pl.multiple_of(table[place], 16), block)], sbuf.at[pl.ds(i * block, block)], rsem.at[n_recv + i]
+            )
+            for i, (a, (_, place)) in enumerate(zip(arrays[n_recv:], self.squares))
+        ]
         writes = [pltpu.make_async_copy(obuf.at[0] if self.finish else obuf, outs[0], osem.at[0])]
         if self.emit:
             writes.append(pltpu.make_async_copy(qbuf, outs[1], osem.at[1]))
@@ -113,24 +118,14 @@
                 xbuf[:, part], refs["w"][slot, :, : 2 * n], preferred_element_type=jnp.float32
             )
 
-        def sums():
-            held, total = 0, None
-            for s in self.squares:
-                if s is None:
-                    values = xbuf[...].astype(jnp.float32)
-                    term = jnp.broadcast_to(jnp.sum(values * values, axis=1, keepdims=True), (rows, LANES))
-                else:
-                    term, held = sbuf[held], held + 1
-                total = term if total is None else total + term
-            return total
-
         def end():
             for copy in copies:
                 copy.wait()
             if self.emit:
-                qbuf[...] = sums()
+                values = xbuf[...].astype(jnp.float32)
+                qbuf[...] = jnp.broadcast_to(jnp.sum(values * values, axis=1, keepdims=True), (rows, LANES))
             if self.finish:
-                scale = lax.rsqrt(sums()[:, :1] / self.features + EPS)
+                scale = lax.rsqrt(sbuf[:, :1] / self.features + EPS)
             for low in range(0, n, LANES):
                 gate, up = acc[:rows, low : low + LANES], acc[:rows, n + low : n + low + LANES]
                 for r in range(n_recv):
@@ -158,7 +153,7 @@
 
     def fits(self, depth, columns):
         whole = sum(p.shape[1] for p in self.pieces) % DEPTH == 0
-        return all(p.shape[1] % UNIT == 0 for p in self.pieces) and whole and columns <= BREADTH and columns % LANES == 0
+        return all(p.shape[1] % UNIT == 0 for p in self.pieces) and whole and columns % LANES == 0
 
     def arrays(self):
         return [*self.pieces, *(self.total or [])]
@@ -171,13 +166,13 @@
             for p, i, low in zip(self.pieces, self.places, self.lows)
         )
         if self.total is not None:
-            result = result + jnp.concatenate(self.total, axis=0)
+            result = result + jnp.concatenate(self.total, axis=0).astype(jnp.float32)
         return jnp.split(result.astype(self.dtype), len(self.outs))
 
     def scratch(self):
         return [
             pltpu.VMEM((self.rows, sum(p.shape[1] for p in self.pieces)), jnp.bfloat16),
-            pltpu.VMEM((self.rows if self.total else 8, self.columns), jnp.float32),
+            pltpu.VMEM((self.rows if self.total else 16, self.columns), self.total[0].dtype if self.total else jnp.float32),
             pltpu.VMEM((self.rows, self.columns), self.dtype),
             pltpu.SemaphoreType.DMA((len(self.pieces) + len(self.outs),)),
             pltpu.SemaphoreType.DMA((len(self.outs),)),
@@ -234,7 +229,7 @@
 
     def clear(self, acc):
         acc[: self.rows, : self.columns] = (
-            self.tbuf[...] if self.total else jnp.zeros((self.rows, self.columns), jnp.float32)
+            self.tbuf[...].astype(jnp.float32) if self.total else jnp.zeros((self.rows, self.columns), jnp.float32)
         )
 
 
@@ -261,6 +256,7 @@
     outs = [o for p in phases for o in p.outs]
     scratch = [p.scratch() for p in phases]
     rows = max(p.group.rows if p.group is not None else p.rows for p in phases)
+    breadth = max(2 * p.width if p.group is not None else columns for p in phases)
 
     def kernel(table_ref, *args):
         args = list(args)
@@ -337,9 +333,9 @@
             in_specs=[SMEM] + [ANY] * len(operands),
             out_specs=[ANY] * len(outs),
             scratch_shapes=[
-                pltpu.VMEM((SLOTS, DEPTH, BREADTH), jnp.bfloat16),
+                pltpu.VMEM((SLOTS, DEPTH, breadth), jnp.bfloat16),
                 pltpu.SemaphoreType.DMA((SLOTS, DEPTH // UNIT)),
-                pltpu.VMEM((rows, BREADTH), jnp.float32),
+                pltpu.VMEM((rows, breadth), jnp.float32),
                 *[
                     buffer
                     for g in groups
@@ -357,22 +353,20 @@
 
 STEPS = (
     ("s0", "s1"),
-    ("x0",),
-    ("x1",),
+    ("q", "x0", "x1"),
     ("h0",),
     ("h1",),
-    ("r0", "s2"),
-    ("r1", "s3"),
+    ("r0", "r1", "s2", "s3"),
     ("x2",),
-    ("x3", "s4", "s5", "d0", "d1"),
+    ("x3",),
     ("h2",),
+    ("s4",),
     ("h3",),
-    ("r2", "x4", "x5"),
-    ("r3", "d2", "d3"),
+    ("x4",),
+    ("r2", "r3", "d2", "d3"),
     ("h4",),
-    ("h5",),
+    ("z", "d0", "d1"),
     ("r4", "d4"),
-    ("r5", "d5"),
 )
 
 
@@ -400,9 +394,9 @@
     )
     sets = [[0], list(range(2, n_gy)), [1]]
     groups = [Group([(gathered, n_gx + j) if j else (tokens, n_gx + n_gy) for j in js], block) for js in sets]
-    squares = [None] * len(groups)
+    squares = gathered_squares = None
     half = cut(width, 7, 13)
-    jobs = [(g, low, high - low) for g in range(len(groups)) for low, high in ((0, half), (half, width))]
+    jobs = [(0, 0, half), (0, half, width - half), (1, 0, half), (1, half, width - half), (2, 0, width)]
     state = [dict() for _ in jobs]
     totals = {}
     chain = tokens
@@ -412,50 +406,76 @@
         group, st, first = groups[g], state[job], low == 0
         if kind == "s":
             return [
-                GateUp(group, k ^ 1, low, n, squares=[None], emit=first and k == 0) for k in [*far, 0]
+                GateUp(group, k ^ 1, low, n, emit=job == 0 and k == 0) for k in [*far, 0]
             ]
         if kind == "x":
-            return [
-                GateUp(group, k, low, n, [st["lent"][i]], squares=[None, squares[g]] if first else [], emit=first and i == 0)
-                for i, k in enumerate(far)
-            ]
+            return [GateUp(group, k, low, n, [st["lent"][i]]) for i, k in enumerate(far)]
         if kind == "h":
-            return [GateUp(group, 0, low, n, [st["lent"][-1], *st["far"]], squares[g], finish=True, features=features)]
+            known = [(gathered_squares, n_gx + j) if j else (squares, n_gx + n_gy) for j in sets[g]]
+            return [GateUp(group, 0, low, n, [st["lent"][-1], *st["far"]], known, features=features)]
         pieces = [(st["hidden"], 0), (st["sibling"], 1)] + st["over"]
         return [
             Down(
                 [h for h, _ in pieces], [q for _, q in pieces], [low] * len(pieces), totals.get(g), block, columns,
-                jnp.bfloat16 if not first and g else jnp.float32,
+                jnp.bfloat16 if g and low + n == width else jnp.float32,
             )
         ]
 
     def deliver(kind, job, outs):
+        nonlocal squares
         g, st = jobs[job][0], state[job]
         if kind == "s":
             st["lent"] = [core(o[0]) for o in outs]
-            if jobs[job][1] == 0:
-                squares[g] = core(outs[-1][1])
+            if job == 0:
+                squares = [outs[-1][1], *[swap(outs[-1][1], "gx", n_gx, k) for k in range(1, n_gx)]]
         elif kind == "x":
             st["far"] = [swap(o[0], "gx", n_gx, k) for o, k in zip(outs, far)]
-            if jobs[job][1] == 0:
-                squares[g] = [outs[0][1], *[swap(outs[0][1], "gx", n_gx, k) for k in far]]
         elif kind == "h":
             st["hidden"], st["sibling"] = outs[0][0], core(outs[0][0])
             st["crossed"] = [swap(outs[0][0], "gx", n_gx, k) for k in far]
         else:
             totals[g] = outs[0]
 
+    def tied(values):
+        nonlocal chain
+        values, chain = lax.optimization_barrier((values, chain))
+        return values
+
     def forward(job):
-        nonlocal chain
-        crossed, chain = lax.optimization_barrier((state[job]["crossed"], chain))
+        crossed = tied(state[job]["crossed"])
         state[job]["over"] = [(h, k) for h, k in zip(crossed, far)]
         state[job]["over"] += [(core(h), k ^ 1) for h, k in zip(crossed, far)]
 
+    def reduce_over_gy():
+        parts = dict(zip(sets[1], totals[1]))
+        mask = 1
+        while mask < n_gy:
+            for j in [j for j in parts if j & mask]:
+                arrived = swap(parts.pop(j), "gy", n_gy, mask)
+                if j == mask:
+                    landed.append(arrived)
+                    continue
+                arrived = tied(arrived).astype(jnp.float32)
+                parts[j ^ mask] = (parts[j ^ mask].astype(jnp.float32) + arrived).astype(jnp.bfloat16)
+            mask *= 2
+
+    landed = []
     for names in STEPS:
         items = []
-        for kind, job in [(name[0], int(name[1:])) for name in names]:
+        for name in names:
+            kind, job = name[0], int(name[1:] or 0)
             if kind == "r":
                 forward(job)
+                continue
+            if kind == "q":
+                squares = sum(tied(squares))
+                gathered_squares = lax.all_gather(squares, "gy", axis=0, tiled=True)
+                continue
+            if kind == "z":
+                reduce_over_gy()
+                continue
+            if kind == "e":
+                totals[0] = [landed.pop(0)]
                 continue
             found = phases_of(kind, job)
             if kind == "d" and items and items[-1][0] == "d" and jobs[items[-1][1]][0] == jobs[job][0]:
@@ -472,17 +492,8 @@
         for kind, job, ps in items:
             deliver(kind, job, [results.pop(0) for _ in ps])
 
-    parts = dict(zip(sets[1], totals[1]))
-    parts[0] = totals[0][0]
-    mask = 1
-    while mask < n_gy:
-        for j in [j for j in parts if j & mask]:
-            arrived = swap(parts.pop(j), "gy", n_gy, mask).astype(jnp.float32)
-            total = parts[j ^ mask].astype(jnp.float32) + arrived
-            parts[j ^ mask] = total if j == mask else total.astype(jnp.bfloat16)
-        mask *= 2
-    last = swap(totals[2][0], "gy", n_gy, 1).astype(jnp.float32)
-    return (parts[0] + last).astype(jnp.bfloat16)
+    landed.append(swap(totals[2][0], "gy", n_gy, 1))
+    return sum((part.astype(jnp.float32) for part in landed), totals[0][0]).astype(jnp.bfloat16)
 
 
 def solution(mesh):

time: 290 us -> 274 us (0.945)
  waiting for transfers between devices: 72.7 us -> 50.8 us
  blocking collectives: 0 us -> 16.4 us
  starting transfers between devices: 29.9 us -> 21.2 us
  Pallas kernels: 169 us -> 165 us
    ppermute x45 -> x36, waiting for transfers between devices: 72 us -> 50.1 us  [swap(): return lax.ppermute(value, axis, [(i, i ^ mask) for i in range(size)])]
    all_gather x0 -> x1, blocking collectives: none -> 16.4 us  [on_device(): gathered_squares = lax.all_gather(squares, 'gy', axis=0, tiled=True)]
    ppermute x45 -> x36, starting transfers between devices: 29.9 us -> 21.2 us  [swap(): return lax.ppermute(value, axis, [(i, i ^ mask) for i in range(size)])]
    pallas_call x17 -> x15, Pallas kernels: 169 us -> 165 us  [run(): pl.pallas_call(kernel, out_shape=outs, in_specs=[SMEM] + [ANY] * len(oper...]
  transfers between devices with their start and end apart: 46 -> 37, of which waited for: 12 -> 12; matrix products, arithmetic and copies ran while one was open for 1% -> 2% of each run, Pallas kernels for 54% -> 54%
where the time goes in v4:
time: 274 us
  Pallas kernels  165 us (60%)
  waiting for transfers between devices  50.8 us (19%)
  starting transfers between devices  21.2 us (8%)
  blocking collectives  16.4 us (6%)
  between operations  13.6 us (5%)
  other arithmetic  6.65 us (2%)
    pallas_call x15, Pallas kernels, run(): pl.pallas_call(kernel, out_shape=outs, in_specs=[SMEM] + [ANY] * len(oper...  165 us
    ppermute x36, waiting for transfers between devices, swap(): return lax.ppermute(value, axis, [(i, i ^ mask) for i in range(size)])  50.1 us
    ppermute x36, starting transfers between devices, swap(): return lax.ppermute(value, axis, [(i, i ^ mask) for i in range(size)])  21.2 us
    all_gather x1, blocking collectives, on_device(): gathered_squares = lax.all_gather(squares, 'gy', axis=0, tiled=True)  16.4 us
  transfers between devices with their start and end apart: 37, of which 12 were waited for; matrix products, arithmetic and copies ran while one was open for 2% of the time, Pallas kernels for 54%

profile of v4, /device:TPU:0, one launch (start us, length us, event | category | flops | bytes accessed | tf_op | source)
XLA Modules:
  0.0 273.9 jit_solution(11686746011288329844)
XLA Ops:
  7.9 14.5 %step_gggg.2 = (bf16[2,128,896]{2,1,0:T(8,128)(2,1)}, bf16[2,128,896]{2,1,0:T(8,128)(2,1)}, f32[128,128]{1,0:T(8,128)}, bf16[2,128,768]{2,1,0:T(8,128)(2,1)}, bf16[2,128,768]{2,1,0:T(8,128)(2,1)}) custom-call(s32[9]{0:T(128)} %pad_add_fusion.table_ref, bf16[2048,6656]{1,0:T(8,128)(2,1)} %args_0_.32, bf16[2048,6656]{1,0:T(8,128)(2,1)} %args_1_.32, ...), custom_call_target="tpu_custom_call" | custom-call | flops 1000 | bytes 1000 | tf_op jit(solution)/shard_map/step_gggg/pallas_call | solution.py:330
  23.3 2.6 collective-permute-start.4
  26.1 2.8 %collective-permute-done.4 = f32[128,128]{1,0:T(8,128)} collective-permute-done((f32[128,128]{1,0:T(8,128)}, f32[128,128]{1,0:T(8,128)}, u32[]{:S(2)}, u32[]{:S(2)}) %collective-permute-start.4) | collective-permute-done | bytes 65568 | tf_op jit(solution)/shard_map/ppermute | solution.py:23
  30.4 9.1 %step_gg.2 = (bf16[2,128,896]{2,1,0:T(8,128)(2,1)}, bf16[2,128,768]{2,1,0:T(8,128)(2,1)}) custom-call(s32[9]{0:T(128)} %pad_add_fusion.table_ref, bf16[2048,6656]{1,0:T(8,128)(2,1)} %args_0_.32, bf16[2048,6656]{1,0:T(8,128)(2,1)} %args_1_.32, bf16[6656,2048]{1,0:T(8,128)(2,1)} %args_2_.32, bf16[128,2048]{1,0:T(8,128)(2,1)} %args_3_.10, ...), custom_call_target="tpu_custom_call" | custom-call | flops 1000 | bytes 1000 | tf_op jit(solution)/shard_map/step_gg/pallas_call | solution.py:330
  43.4 9.8 %collective-permute-done.6.args_5_ = bf16[2,128,896]{2,1,0:T(8,128)(2,1)} collective-permute-done((bf16[2,128,896]{2,1,0:T(8,128)(2,1)}, bf16[2,128,896]{2,1,0:T(8,128)(2,1)}, u32[]{:S(2)}, u32[]{:S(2)}) %collective-permute-start.6) | collective-permute-done | bytes 458784 | tf_op jit(solution)/shard_map/ppermute | solution.py:23
  53.2 7.1 %step_g.8.args_7_.args_3_ = bf16[128,896]{1,0:T(8,128)(2,1)} custom-call(s32[9]{0:T(128)} %pad_add_fusion.table_ref, bf16[2048,6656]{1,0:T(8,128)(2,1)} %args_0_.32, bf16[2048,6656]{1,0:T(8,128)(2,1)} %args_1_.32, bf16[6656,2048]{1,0:T(8,128)(2,1)} %args_2_.32, bf16[128,2048]{1,0:T(8,128)(2,1)} %args_3_.10, ...), custom_call_target="tpu_custom_call" | custom-call | flops 1000 | bytes 1000 | tf_op jit(solution)/shard_map/step_g/pallas_call | solution.py:330
  61.6 6.6 %step_g.9.args_4_.args_7_ = bf16[128,768]{1,0:T(8,128)(2,1)} custom-call(s32[9]{0:T(128)} %pad_add_fusion.table_ref, bf16[2048,6656]{1,0:T(8,128)(2,1)} %args_0_.32, bf16[2048,6656]{1,0:T(8,128)(2,1)} %args_1_.32, bf16[6656,2048]{1,0:T(8,128)(2,1)} %args_2_.32, bf16[128,2048]{1,0:T(8,128)(2,1)} %args_3_.10, ...), custom_call_target="tpu_custom_call" | custom-call | flops 1000 | bytes 1000 | tf_op jit(solution)/shard_map/step_g/pallas_call | solution.py:330
  69.2 5.6 %collective-permute-done.13.args_9_ = bf16[128,768]{1,0:T(8,128)(2,1)} collective-permute-done((bf16[128,768]{1,0:T(8,128)(2,1)}, bf16[128,768]{1,0:T(8,128)(2,1)}, u32[]{:S(2)}, u32[]{:S(2)}) %collective-permute-start.13) | collective-permute-done | bytes 196640 | tf_op jit(solution)/shard_map/ppermute | solution.py:23
  74.7 18.5 %step_gggg.3 = (bf16[2,256,896]{2,1,0:T(8,128)(2,1)}, bf16[2,256,896]{2,1,0:T(8,128)(2,1)}, bf16[2,256,768]{2,1,0:T(8,128)(2,1)}, bf16[2,256,768]{2,1,0:T(8,128)(2,1)}) custom-call(s32[9]{0:T(128)} %pad_add_fusion.table_ref, bf16[2048,6656]{1,0:T(8,128)(2,1)} %args_0_.32, bf16[2048,6656]{1,0:T(8,128)(2,1)} %args_1_.32, bf16[6656,2048]{1,0:T(8,128)(2,1)} %args_2_.32, ...), custom_call_target="tpu_custom_call" | custom-call | flops 1000 | bytes 1000 | tf_op jit(solution)/shard_map/step_gggg/pallas_call | solution.py:330
  96.1 8.0 %step_g.10.args_5_ = bf16[2,256,896]{2,1,0:T(8,128)(2,1)} custom-call(s32[9]{0:T(128)} %pad_add_fusion.table_ref, bf16[2048,6656]{1,0:T(8,128)(2,1)} %args_0_.32, bf16[2048,6656]{1,0:T(8,128)(2,1)} %args_1_.32, bf16[6656,2048]{1,0:T(8,128)(2,1)} %args_2_.32, bf16[512,2048]{1,0:T(8,128)(2,1)} %all-gather.2.cloned.1.call-done.args_3_, ...), custom_call_target="tpu_custom_call" | custom-call | flops 1000 | bytes 1000 | tf_op jit(solution)/shard_map/step_g/pallas_call | solution.py:330
  105.7 7.3 %step_g.11.args_7_ = bf16[2,256,768]{2,1,0:T(8,128)(2,1)} custom-call(s32[9]{0:T(128)} %pad_add_fusion.table_ref, bf16[2048,6656]{1,0:T(8,128)(2,1)} %args_0_.32, bf16[2048,6656]{1,0:T(8,128)(2,1)} %args_1_.32, bf16[6656,2048]{1,0:T(8,128)(2,1)} %args_2_.32, bf16[512,2048]{1,0:T(8,128)(2,1)} %all-gather.2.cloned.1.call-done.args_3_, ...), custom_call_target="tpu_custom_call" | custom-call | flops 1000 | bytes 1000 | tf_op jit(solution)/shard_map/step_g/pallas_call | solution.py:330
  113.7 16.4 %all_gather.7.args_6_ = f32[512,128]{1,0:T(8,128)} all-gather(f32[128,128]{1,0:T(8,128)} %add_add_fusion.args_6_), channel_id=1, replica_groups=mesh['groups'=2,'gx'=4,'gy'=4] {'gy'}, dimensions={0}, use_global_device_ids=true | all-gather | bytes 327680 | tf_op jit(solution)/shard_map/all_gather | solution.py:472
  130.1 9.1 %step_g.12.args_4_.args_3_ = bf16[256,896]{1,0:T(8,128)(2,1)} custom-call(s32[9]{0:T(128)} %pad_add_fusion.table_ref, bf16[2048,6656]{1,0:T(8,128)(2,1)} %args_0_.32, bf16[2048,6656]{1,0:T(8,128)(2,1)} %args_1_.32, bf16[6656,2048]{1,0:T(8,128)(2,1)} %args_2_.32, bf16[512,2048]{1,0:T(8,128)(2,1)} %all-gather.2.cloned.1.call-done.args_3_, ...), custom_call_target="tpu_custom_call" | custom-call | flops 1000 | bytes 1000 | tf_op jit(solution)/shard_map/step_g/pallas_call | solution.py:330
  139.2 12.6 %step_gg.3 = (bf16[2,128,1664]{2,1,0:T(8,128)(2,1)}, bf16[2,128,1664]{2,1,0:T(8,128)(2,1)}) custom-call(s32[9]{0:T(128)} %pad_add_fusion.table_ref, bf16[2048,6656]{1,0:T(8,128)(2,1)} %args_0_.32, bf16[2048,6656]{1,0:T(8,128)(2,1)} %args_1_.32, bf16[6656,2048]{1,0:T(8,128)(2,1)} %args_2_.32, bf16[512,2048]{1,0:T(8,128)(2,1)} %all-gather.2.cloned.1.call-done.args_3_, ...), custom_call_target="tpu_custom_call" | custom-call | flops 1000 | bytes 1000 | tf_op jit(solution)/shard_map/step_gg/pallas_call | solution.py:330
  153.1 8.2 %step_g.13.args_5_.args_7_ = bf16[256,768]{1,0:T(8,128)(2,1)} custom-call(s32[9]{0:T(128)} %pad_add_fusion.table_ref, bf16[2048,6656]{1,0:T(8,128)(2,1)} %args_0_.32, bf16[2048,6656]{1,0:T(8,128)(2,1)} %args_1_.32, bf16[6656,2048]{1,0:T(8,128)(2,1)} %args_2_.32, bf16[512,2048]{1,0:T(8,128)(2,1)} %all-gather.2.cloned.1.call-done.args_3_, ...), custom_call_target="tpu_custom_call" | custom-call | flops 1000 | bytes 1000 | tf_op jit(solution)/shard_map/step_g/pallas_call | solution.py:330
  162.7 8.7 %step_g.14.args_11_ = bf16[2,128,1664]{2,1,0:T(8,128)(2,1)} custom-call(s32[9]{0:T(128)} %pad_add_fusion.table_ref, bf16[2048,6656]{1,0:T(8,128)(2,1)} %args_0_.32, bf16[2048,6656]{1,0:T(8,128)(2,1)} %args_1_.32, bf16[6656,2048]{1,0:T(8,128)(2,1)} %args_2_.32, bf16[512,2048]{1,0:T(8,128)(2,1)} %all-gather.2.cloned.1.call-done.args_3_, ...), custom_call_target="tpu_custom_call" | custom-call | flops 1000 | bytes 1000 | tf_op jit(solution)/shard_map/step_g/pallas_call | solution.py:330
  176.3 18.2 %step_d.3 = (bf16[128,2048]{1,0:T(8,128)(2,1)}, bf16[128,2048]{1,0:T(8,128)(2,1)}) custom-call(s32[9]{0:T(128)} %pad_add_fusion.table_ref, bf16[2048,6656]{1,0:T(8,128)(2,1)} %args_0_.32, bf16[2048,6656]{1,0:T(8,128)(2,1)} %args_1_.32, bf16[6656,2048]{1,0:T(8,128)(2,1)} %args_2_.32, bf16[256,896]{1,0:T(8,128)(2,1)} %step_g.12.args_4_.args_3_, ...), custom_call_target="tpu_custom_call" | custom-call | flops 1000 | bytes 1000 | tf_op jit(solution)/shard_map/step_d/pallas_call | solution.py:330
  195.0 9.6 %step_g.15.args_11_.args_3_ = bf16[128,1664]{1,0:T(8,128)(2,1)} custom-call(s32[9]{0:T(128)} %pad_add_fusion.table_ref, bf16[2048,6656]{1,0:T(8,128)(2,1)} %args_0_.32, bf16[2048,6656]{1,0:T(8,128)(2,1)} %args_1_.32, bf16[6656,2048]{1,0:T(8,128)(2,1)} %args_2_.32, bf16[512,2048]{1,0:T(8,128)(2,1)} %all-gather.2.cloned.1.call-done.args_3_, ...), custom_call_target="tpu_custom_call" | custom-call | flops 1000 | bytes 1000 | tf_op jit(solution)/shard_map/step_g/pallas_call | solution.py:330
  206.2 2.6 collective-permute-done.28
  210.6 14.1 %step_d.4.args_7_ = f32[128,2048]{1,0:T(8,128)} custom-call(s32[9]{0:T(128)} %pad_add_fusion.table_ref, bf16[2048,6656]{1,0:T(8,128)(2,1)} %args_0_.32, bf16[2048,6656]{1,0:T(8,128)(2,1)} %args_1_.32, bf16[6656,2048]{1,0:T(8,128)(2,1)} %args_2_.32, bf16[128,896]{1,0:T(8,128)(2,1)} %step_g.8.args_7_.args_3_, bf16[128,896]{1,0:T(8,128)(2,1)} %collective-permute-done.7.args_4_, ...), custom_call_target="tpu_custom_call" | custom-call | flops 1000 | bytes 1000 | tf_op jit(solution)/shard_map/step_d/pallas_call | solution.py:330
  228.1 13.6 %step_d.5 = bf16[128,2048]{1,0:T(8,128)(2,1)} custom-call(s32[9]{0:T(128)} %pad_add_fusion.table_ref, bf16[2048,6656]{1,0:T(8,128)(2,1)} %args_0_.32, bf16[2048,6656]{1,0:T(8,128)(2,1)} %args_1_.32, bf16[6656,2048]{1,0:T(8,128)(2,1)} %args_2_.32, bf16[128,1664]{1,0:T(8,128)(2,1)} %step_g.15.args_11_.args_3_, ...), custom_call_target="tpu_custom_call" | custom-call | flops 1000 | bytes 1000 | tf_op jit(solution)/shard_map/step_d/pallas_call | solution.py:330
  243.5 10.2 %collective-permute-done.31 = bf16[128,2048]{1,0:T(8,128)(2,1)} collective-permute-done((bf16[128,2048]{1,0:T(8,128)(2,1)}, bf16[128,2048]{1,0:T(8,128)(2,1)}, u32[]{:S(2)}, u32[]{:S(2)}) %collective-permute-start.31) | collective-permute-done | bytes 524320 | tf_op jit(solution)/shard_map/ppermute | solution.py:23
  253.7 11.0 %collective-permute-done.35 = bf16[128,2048]{1,0:T(8,128)(2,1)S(1)} collective-permute-done((bf16[128,2048]{1,0:T(8,128)(2,1)}, bf16[128,2048]{1,0:T(8,128)(2,1)S(1)}, u32[]{:S(2)}, u32[]{:S(2)}) %collective-permute-start.35) | collective-permute-done | bytes 524320 | tf_op jit(solution)/shard_map/ppermute | solution.py:23
  264.7 2.3 add_convert_fusion
  (72 shorter events, 31.8 us)
Async XLA Ops:
  6.5 68.2 %all-gather.2.cloned.1.call-start = ((), (), s32[]{:S(2)}) async-start(), calls=%async_computation | async-start | bytes 2621440 | tf_op jit(solution)/shard_map/all_gather | solution.py:387
  22.4 8.0 %collective-permute-start.1 = (bf16[2,128,896]{2,1,0:T(8,128)(2,1)}, bf16[2,128,896]{2,1,0:T(8,128)(2,1)}, u32[]{:S(2)}, u32[]{:S(2)}) collective-permute-start(bf16[2,128,896]{2,1,0:T(8,128)(2,1)} %get-tuple-element.41.args_6_), channel_id=1, source_target_pairs={{0,4},{4,0},{8,12},{12,8},{1,5},{5,1},{9,13},{13,9},{2,6},{6,2},{1... | collective-permute-start | bytes 1376264 | tf_op jit(solution)/shard_map/ppermute | solution.py:23
  22.8 7.5 %collective-permute-start.2 = (bf16[2,128,768]{2,1,0:T(8,128)(2,1)}, bf16[2,128,768]{2,1,0:T(8,128)(2,1)}, u32[]{:S(2)}, u32[]{:S(2)}) collective-permute-start(bf16[2,128,768]{2,1,0:T(8,128)(2,1)} %get-tuple-element.39), channel_id=1, source_target_pairs={{0,4},{4,0},{8,12},{12,8},{1,5},{5,1},{9,13},{13,9},{2,6},{6,2},{1... | collective-permute-start | bytes 1179656 | tf_op jit(solution)/shard_map/ppermute | solution.py:23
  26.0 17.4 %collective-permute-start = (bf16[2,128,896]{2,1,0:T(8,128)(2,1)}, bf16[2,128,896]{2,1,0:T(8,128)(2,1)}, u32[]{:S(2)}, u32[]{:S(2)}) collective-permute-start(bf16[2,128,896]{2,1,0:T(8,128)(2,1)} %get-tuple-element.37), channel_id=1, source_target_pairs={{0,4},{4,0},{8,12},{12,8},{1,5},{5,1},{9,13},{13,9},{2,6},{6,2},{1... | collective-permute-start | bytes 1376264 | tf_op jit(solution)/shard_map/ppermute | solution.py:23
  39.5 13.7 %collective-permute-start.6 = (bf16[2,128,896]{2,1,0:T(8,128)(2,1)}, bf16[2,128,896]{2,1,0:T(8,128)(2,1)}, u32[]{:S(2)}, u32[]{:S(2)}) collective-permute-start(bf16[2,128,896]{2,1,0:T(8,128)(2,1)} %get-tuple-element.42.args_7_), channel_id=1, source_target_pairs={{0,8},{4,12},{8,0},{12,4},{1,9},{5,13},{9,1},{13,5},{2,10},{6,14},... | collective-permute-start | bytes 1376264 | tf_op jit(solution)/shard_map/ppermute | solution.py:23
  40.8 20.8 %collective-permute-start.9 = (bf16[2,128,768]{2,1,0:T(8,128)(2,1)}, bf16[2,128,768]{2,1,0:T(8,128)(2,1)}, u32[]{:S(2)}, u32[]{:S(2)}) collective-permute-start(bf16[2,128,768]{2,1,0:T(8,128)(2,1)} %get-tuple-element.47), channel_id=1, source_target_pairs={{0,4},{4,0},{8,12},{12,8},{1,5},{5,1},{9,13},{13,9},{2,6},{6,2},{1... | collective-permute-start | bytes 1179656 | tf_op jit(solution)/shard_map/ppermute | solution.py:23
  41.1 20.5 %collective-permute-start.10 = (bf16[2,128,768]{2,1,0:T(8,128)(2,1)}, bf16[2,128,768]{2,1,0:T(8,128)(2,1)}, u32[]{:S(2)}, u32[]{:S(2)}) collective-permute-start(bf16[2,128,768]{2,1,0:T(8,128)(2,1)} %get-tuple-element.48), channel_id=1, source_target_pairs={{0,8},{4,12},{8,0},{12,4},{1,9},{5,13},{9,1},{13,5},{2,10},{6,14},... | collective-permute-start | bytes 1179656 | tf_op jit(solution)/shard_map/ppermute | solution.py:23
  60.3 8.9 %collective-permute-start.8 = (bf16[128,896]{1,0:T(8,128)(2,1)}, bf16[128,896]{1,0:T(8,128)(2,1)}, u32[]{:S(2)}, u32[]{:S(2)}) collective-permute-start(bf16[128,896]{1,0:T(8,128)(2,1)} %step_g.8.args_7_.args_3_), channel_id=1, source_target_pairs={{0,8},{4,12},{8,0},{12,4},{1,9},{5,13},{9,1},{13,5},{2,10},{6,14},... | collective-permute-start | bytes 688136 | tf_op jit(solution)/shard_map/ppermute | solution.py:23
  93.3 12.3 %collective-permute-start.18 = (bf16[2,256,768]{2,1,0:T(8,128)(2,1)}, bf16[2,256,768]{2,1,0:T(8,128)(2,1)}, u32[]{:S(2)}, u32[]{:S(2)}) collective-permute-start(bf16[2,256,768]{2,1,0:T(8,128)(2,1)} %get-tuple-element.55), channel_id=1, source_target_pairs={{0,4},{4,0},{8,12},{12,8},{1,5},{5,1},{9,13},{13,9},{2,6},{6,2},{1... | collective-permute-start | bytes 2359304 | tf_op jit(solution)/shard_map/ppermute | solution.py:23
  93.8 36.2 %collective-permute-start.15 = (bf16[2,256,896]{2,1,0:T(8,128)(2,1)}, bf16[2,256,896]{2,1,0:T(8,128)(2,1)}, u32[]{:S(2)}, u32[]{:S(2)}) collective-permute-start(bf16[2,256,896]{2,1,0:T(8,128)(2,1)} %get-tuple-element.53), channel_id=1, source_target_pairs={{0,4},{4,0},{8,12},{12,8},{1,5},{5,1},{9,13},{13,9},{2,6},{6,2},{1... | collective-permute-start | bytes 2752520 | tf_op jit(solution)/shard_map/ppermute | solution.py:23
  104.1 25.9 %collective-permute-start.17 = (bf16[2,256,896]{2,1,0:T(8,128)(2,1)}, bf16[2,256,896]{2,1,0:T(8,128)(2,1)}, u32[]{:S(2)}, u32[]{:S(2)}) collective-permute-start(bf16[2,256,896]{2,1,0:T(8,128)(2,1)} %step_g.10.args_5_), channel_id=1, source_target_pairs={{0,8},{4,12},{8,0},{12,4},{1,9},{5,13},{9,1},{13,5},{2,10},{6,14},... | collective-permute-start | bytes 2752520 | tf_op jit(solution)/shard_map/ppermute | solution.py:23
  105.7 47.4 %collective-permute-start.22 = (bf16[2,256,768]{2,1,0:T(8,128)(2,1)}, bf16[2,256,768]{2,1,0:T(8,128)(2,1)}, u32[]{:S(2)}, u32[]{:S(2)}) collective-permute-start(bf16[2,256,768]{2,1,0:T(8,128)(2,1)} %get-tuple-element.57), channel_id=1, source_target_pairs={{0,4},{4,0},{8,12},{12,8},{1,5},{5,1},{9,13},{13,9},{2,6},{6,2},{1... | collective-permute-start | bytes 2359304 | tf_op jit(solution)/shard_map/ppermute | solution.py:23
  113.0 40.0 %collective-permute-start.23 = (bf16[2,256,768]{2,1,0:T(8,128)(2,1)}, bf16[2,256,768]{2,1,0:T(8,128)(2,1)}, u32[]{:S(2)}, u32[]{:S(2)}) collective-permute-start(bf16[2,256,768]{2,1,0:T(8,128)(2,1)} %step_g.11.args_7_), channel_id=1, source_target_pairs={{0,8},{4,12},{8,0},{12,4},{1,9},{5,13},{9,1},{13,5},{2,10},{6,14},... | collective-permute-start | bytes 2359304 | tf_op jit(solution)/shard_map/ppermute | solution.py:23
  151.8 10.9 %collective-permute-start.21 = (bf16[2,128,1664]{2,1,0:T(8,128)(2,1)}, bf16[2,128,1664]{2,1,0:T(8,128)(2,1)}, u32[]{:S(2)}, u32[]{:S(2)}) collective-permute-start(bf16[2,128,1664]{2,1,0:T(8,128)(2,1)} %get-tuple-element.56.args_7_), channel_id=1, source_target_pairs={{0,4},{4,0},{8,12},{12,8},{1,5},{5,1},{9,13},{13,9},{2,6},{6,2},{1... | collective-permute-start | bytes 2555912 | tf_op jit(solution)/shard_map/ppermute | solution.py:23
  151.9 20.8 %collective-permute-start.20 = (bf16[256,896]{1,0:T(8,128)(2,1)}, bf16[256,896]{1,0:T(8,128)(2,1)}, u32[]{:S(2)}, u32[]{:S(2)}) collective-permute-start(bf16[256,896]{1,0:T(8,128)(2,1)} %step_g.12.args_4_.args_3_), channel_id=1, source_target_pairs={{0,8},{4,12},{8,0},{12,4},{1,9},{5,13},{9,1},{13,5},{2,10},{6,14},... | collective-permute-start | bytes 1376264 | tf_op jit(solution)/shard_map/ppermute | solution.py:23
  161.3 12.3 %collective-permute-start.26 = (bf16[256,768]{1,0:T(8,128)(2,1)}, bf16[256,768]{1,0:T(8,128)(2,1)}, u32[]{:S(2)}, u32[]{:S(2)}) collective-permute-start(bf16[256,768]{1,0:T(8,128)(2,1)} %step_g.13.args_5_.args_7_), channel_id=1, source_target_pairs={{0,8},{4,12},{8,0},{12,4},{1,9},{5,13},{9,1},{13,5},{2,10},{6,14},... | collective-permute-start | bytes 1179656 | tf_op jit(solution)/shard_map/ppermute | solution.py:23
  162.2 11.3 %collective-permute-start.25 = (bf16[256,768]{1,0:T(8,128)(2,1)}, bf16[256,768]{1,0:T(8,128)(2,1)}, u32[]{:S(2)}, u32[]{:S(2)}) collective-permute-start(bf16[256,768]{1,0:T(8,128)(2,1)} %step_g.13.args_5_.args_7_), channel_id=1, source_target_pairs={{0,4},{4,0},{8,12},{12,8},{1,5},{5,1},{9,13},{13,9},{2,6},{6,2},{1... | collective-permute-start | bytes 1179656 | tf_op jit(solution)/shard_map/ppermute | solution.py:23
  162.2 32.8 %collective-permute-start.29 = (bf16[2,128,1664]{2,1,0:T(8,128)(2,1)}, bf16[2,128,1664]{2,1,0:T(8,128)(2,1)}, u32[]{:S(2)}, u32[]{:S(2)}) collective-permute-start(bf16[2,128,1664]{2,1,0:T(8,128)(2,1)} %get-tuple-element.63), channel_id=1, source_target_pairs={{0,4},{4,0},{8,12},{12,8},{1,5},{5,1},{9,13},{13,9},{2,6},{6,2},{1... | collective-permute-start | bytes 2555912 | tf_op jit(solution)/shard_map/ppermute | solution.py:23
  171.4 23.5 %collective-permute-start.30 = (bf16[2,128,1664]{2,1,0:T(8,128)(2,1)}, bf16[2,128,1664]{2,1,0:T(8,128)(2,1)}, u32[]{:S(2)}, u32[]{:S(2)}) collective-permute-start(bf16[2,128,1664]{2,1,0:T(8,128)(2,1)} %step_g.14.args_11_), channel_id=1, source_target_pairs={{0,8},{4,12},{8,0},{12,4},{1,9},{5,13},{9,1},{13,5},{2,10},{6,14},... | collective-permute-start | bytes 2555912 | tf_op jit(solution)/shard_map/ppermute | solution.py:23
  194.4 14.3 %collective-permute-start.28 = (bf16[128,2048]{1,0:T(8,128)(2,1)}, bf16[128,2048]{1,0:T(8,128)(2,1)}, u32[]{:S(2)}, u32[]{:S(2)}) collective-permute-start(bf16[128,2048]{1,0:T(8,128)(2,1)} %get-tuple-element.62), channel_id=1, source_target_pairs={{0,1},{1,0},{2,3},{3,2},{4,5},{5,4},{6,7},{7,6},{8,9},{9,8},{10,11... | collective-permute-start | bytes 1572872 | tf_op jit(solution)/shard_map/ppermute | solution.py:23
  204.6 20.1 %collective-permute-start.33 = (bf16[128,1664]{1,0:T(8,128)(2,1)}, bf16[128,1664]{1,0:T(8,128)(2,1)}, u32[]{:S(2)}, u32[]{:S(2)}) collective-permute-start(bf16[128,1664]{1,0:T(8,128)(2,1)} %step_g.15.args_11_.args_3_), channel_id=1, source_target_pairs={{0,8},{4,12},{8,0},{12,4},{1,9},{5,13},{9,1},{13,5},{2,10},{6,14},... | collective-permute-start | bytes 1277960 | tf_op jit(solution)/shard_map/ppermute | solution.py:23
  208.8 19.3 %collective-permute-start.32 = (bf16[128,1664]{1,0:T(8,128)(2,1)}, bf16[128,1664]{1,0:T(8,128)(2,1)}, u32[]{:S(2)}, u32[]{:S(2)}) collective-permute-start(bf16[128,1664]{1,0:T(8,128)(2,1)} %step_g.15.args_11_.args_3_), channel_id=1, source_target_pairs={{0,4},{4,0},{8,12},{12,8},{1,5},{5,1},{9,13},{13,9},{2,6},{6,2},{1... | collective-permute-start | bytes 1277960 | tf_op jit(solution)/shard_map/ppermute | solution.py:23
  227.0 26.7 %collective-permute-start.31 = (bf16[128,2048]{1,0:T(8,128)(2,1)}, bf16[128,2048]{1,0:T(8,128)(2,1)}, u32[]{:S(2)}, u32[]{:S(2)}) collective-permute-start(bf16[128,2048]{1,0:T(8,128)(2,1)} %add_convert_fusion.1), channel_id=1, source_target_pairs={{0,2},{1,3},{2,0},{3,1},{4,6},{5,7},{6,4},{7,5},{8,10},{9,11},{10,... | collective-permute-start | bytes 1572872 | tf_op jit(solution)/shard_map/ppermute | solution.py:23
  241.7 23.0 %collective-permute-start.35 = (bf16[128,2048]{1,0:T(8,128)(2,1)}, bf16[128,2048]{1,0:T(8,128)(2,1)S(1)}, u32[]{:S(2)}, u32[]{:S(2)}) collective-permute-start(bf16[128,2048]{1,0:T(8,128)(2,1)} %step_d.5), channel_id=1, source_target_pairs={{0,1},{1,0},{2,3},{3,2},{4,5},{5,4},{6,7},{7,6},{8,9},{9,8},{10,11... | collective-permute-start | bytes 1572872 | tf_op jit(solution)/shard_map/ppermute | solution.py:23
  (13 other events, 46.4 us)
Sparse Core Ops, SparseCore 0:
  8.9 48.6 all-gather.1

commit v5 on v4

v5 whole, which is shorter than its diff:
```python
import functools

import jax
import jax.numpy as jnp
from jax import lax
from jax.experimental import pallas as pl
from jax.experimental.pallas import tpu as pltpu
from jax.sharding import PartitionSpec as P

EPS = 1e-05
LANES = 128
GU_TILE = 256
OUT_TILE = 512
COST = pl.CostEstimate(flops=1000, bytes_accessed=1000, transcendentals=0)
VMEM_LIMIT = 64 * 1024 * 1024 - 64 * 1024
ANY = pl.BlockSpec(memory_space=pl.ANY)
SMEM = pl.BlockSpec(memory_space=pltpu.SMEM)


def swap(value, axis, size, mask):
    return lax.ppermute(value, axis, [(i, i ^ mask) for i in range(size)])


def silu_product(gate, up, scale):
    gate = gate * scale
    return gate / (1.0 + jnp.exp(-gate)) * (up * scale)


class Group:
    def __init__(self, toks, block):
        self.toks, self.block, self.rows = toks, block, block * len(toks)

    def plain(self, table):
        return jnp.concatenate([lax.dynamic_slice_in_dim(t, table[i], self.block, 0) for t, i in self.toks], axis=0)


class GateUp:
    def __init__(self, group, place, low, width, recvs=(), carry=False, emit=False, squares=None, at=0, features=1):
        self.group, self.place, self.low, self.width, self.recvs = group, place, low, width, list(recvs)
        self.carry, self.emit, self.squares, self.at, self.features = carry, emit, squares, at, features
        rows, wide = group.rows, width + (LANES if carry else 0)
        self.outs = [jax.ShapeDtypeStruct((2, rows, wide) if squares is None else (rows, width), jnp.bfloat16)]
        if emit:
            self.outs.append(jax.ShapeDtypeStruct((rows, LANES), jnp.float32))

    def fits(self, depth, columns):
        return self.width % LANES == 0 and depth % LANES == 0 and self.group.block % 16 == 0

    def arrays(self):
        return [*self.recvs, *([self.squares[0], *self.squares[1]] if self.squares else [])]

    def plain(self, table, gate_matrix, up_matrix, down_matrix):
        tok, n = self.group.plain(table), self.width
        gate, up = (
            jnp.dot(
                tok, lax.dynamic_slice_in_dim(m, table[self.place] + self.low, n, 1), preferred_element_type=jnp.float32
            )
            for m in (gate_matrix, up_matrix)
        )
        for r in self.recvs:
            gate, up = gate + r[0, :, :n].astype(jnp.float32), up + r[1, :, :n].astype(jnp.float32)
        if self.squares:
            total = self.squares[0]
            for part in self.squares[1]:
                part = part[:, :, self.at : self.at + LANES].astype(jnp.float32)
                total = total + part[0] + part[1]
            return [silu_product(gate, up, lax.rsqrt(total[:, :1] / self.features + EPS)).astype(jnp.bfloat16)]
        if not self.carry:
            return [jnp.stack([gate, up]).astype(jnp.bfloat16)]
        values = tok.astype(jnp.float32)
        total = jnp.broadcast_to(jnp.sum(values * values, axis=1, keepdims=True), (tok.shape[0], LANES))
        for r in self.recvs:
            part = r[:, :, n : n + LANES].astype(jnp.float32)
            total = total + part[0] + part[1]
        high = total.astype(jnp.bfloat16).astype(jnp.float32)
        both = jnp.stack([jnp.concatenate([gate, high], axis=1), jnp.concatenate([up, total - high], axis=1)])
        return [both.astype(jnp.bfloat16)] + ([total] if self.emit else [])

    def scratch(self, depth):
        rows, n, tiles, n_recv = self.group.rows, self.width, pl.cdiv(self.width, GU_TILE), len(self.recvs)
        extra = len(self.squares[1]) if self.squares else n_recv if self.carry else 0
        return [
            pltpu.VMEM((tiles, depth, 2 * GU_TILE), jnp.bfloat16),
            pltpu.VMEM((n_recv, 2, rows, n) if n_recv else (1, 2, 16, LANES), jnp.bfloat16),
            pltpu.VMEM((extra, 2, rows, LANES) if extra else (1, 2, 16, LANES), jnp.bfloat16),
            pltpu.VMEM((rows, LANES) if self.squares or self.emit else (8, LANES), jnp.float32),
            pltpu.VMEM((tiles, 1 if self.squares else 2, rows, GU_TILE), jnp.bfloat16),
            pltpu.VMEM((2, rows, LANES) if self.carry else (2, 16, LANES), jnp.bfloat16),
            pltpu.SemaphoreType.DMA((2, tiles)),
            pltpu.SemaphoreType.DMA((n_recv + extra + 1,)),
            pltpu.SemaphoreType.DMA((tiles + 2,)),
        ]

    def bind(self, refs, table, arrays, outs, scratch):
        wbuf, rbuf, ebuf, qbuf, obuf, cbuf, wsem, rsem, osem = scratch
        n, rows, n_recv = self.width, self.group.rows, len(self.recvs)
        xbuf, hidden = refs["x"][id(self.group)], self.squares is not None
        full, rest = divmod(n, GU_TILE)
        tiles = full + (rest > 0)
        start = table[self.place] + self.low

        def weights(j, m):
            columns = pl.ds(pl.multiple_of(start + j * GU_TILE, LANES), m)
            return [
                pltpu.make_async_copy(refs[name].at[:, columns], wbuf.at[j, :, pl.ds(i * m, m)], wsem.at[i, j])
                for i, name in enumerate(("gate", "up"))
            ]

        def write(j, m):
            columns = pl.ds(pl.multiple_of(j * GU_TILE, LANES), m)
            if hidden:
                return pltpu.make_async_copy(obuf.at[j, 0, :, pl.ds(0, m)], outs[0].at[:, columns], osem.at[j])
            return pltpu.make_async_copy(obuf.at[j, :, :, pl.ds(0, m)], outs[0].at[:, :, columns], osem.at[j])

        def over_tiles(step):
            if full:
                @pl.loop(0, full)
                def _(j):
                    step(j, GU_TILE)
            if rest:
                step(full, rest)

        copies = [
            pltpu.make_async_copy(a.at[:, :, pl.ds(0, n)], rbuf.at[i], rsem.at[i]) for i, a in enumerate(arrays[:n_recv])
        ]
        extras = arrays[n_recv + 1 :] if hidden else arrays[:n_recv] if self.carry else []
        copies += [
            pltpu.make_async_copy(a.at[:, :, pl.ds(self.at if hidden else n, LANES)], ebuf.at[i], rsem.at[n_recv + i])
            for i, a in enumerate(extras)
        ]
        if hidden:
            copies.append(pltpu.make_async_copy(arrays[n_recv], qbuf, rsem.at[n_recv + len(extras)]))
        writes = []
        if self.carry:
            writes.append(pltpu.make_async_copy(cbuf, outs[0].at[:, :, pl.ds(n, LANES)], osem.at[tiles]))
        if self.emit:
            writes.append(pltpu.make_async_copy(qbuf, outs[1], osem.at[tiles + 1]))

        def begin():
            def step(j, m):
                for copy in weights(j, m):
                    copy.start()

            over_tiles(step)

        def compute():
            for copy in copies:
                copy.wait()
            extra = None
            for i in range(len(extras)):
                term = ebuf[i, 0].astype(jnp.float32) + ebuf[i, 1].astype(jnp.float32)
                extra = term if extra is None else extra + term
            if self.carry:
                values = xbuf[...].astype(jnp.float32)
                total = jnp.broadcast_to(jnp.sum(values * values, axis=1, keepdims=True), (rows, LANES))
                total = total if extra is None else total + extra
                high = total.astype(jnp.bfloat16)
                cbuf[0] = high
                cbuf[1] = (total - high.astype(jnp.float32)).astype(jnp.bfloat16)
                if self.emit:
                    qbuf[...] = total
                for copy in writes:
                    copy.start()
            if hidden:
                total = qbuf[...] if extra is None else qbuf[...] + extra
                qbuf[...] = lax.rsqrt(total / self.features + EPS)

            def step(j, m):
                for copy in weights(j, m):
                    copy.wait()
                both = jnp.dot(xbuf[...], wbuf[j, :, pl.ds(0, 2 * m)], preferred_element_type=jnp.float32)
                gate, up = both[:, :m], both[:, m:]
                columns = pl.ds(pl.multiple_of(j * GU_TILE, LANES), m)
                for r in range(n_recv):
                    gate = gate + rbuf[r, 0, :, columns].astype(jnp.float32)
                    up = up + rbuf[r, 1, :, columns].astype(jnp.float32)
                if hidden:
                    obuf[j, 0, :, pl.ds(0, m)] = silu_product(gate, up, qbuf[:, :1]).astype(jnp.bfloat16)
                else:
                    obuf[j, 0, :, pl.ds(0, m)] = gate.astype(jnp.bfloat16)
                    obuf[j, 1, :, pl.ds(0, m)] = up.astype(jnp.bfloat16)
                write(j, m).start()

            over_tiles(step)

        def drain():
            over_tiles(lambda j, m: write(j, m).wait())
            for copy in writes:
                copy.wait()

        return copies, begin, compute, drain


class Down:
    def __init__(self, pieces, places, lows, total, block, columns, dtype):
        self.pieces, self.places, self.lows, self.total, self.block, self.dtype = pieces, places, lows, total, block, dtype
        self.rows, self.columns, self.group = pieces[0].shape[0], columns, None
        self.outs = [jax.ShapeDtypeStruct((block, columns), dtype) for _ in range(self.rows // block)]

    def fits(self, depth, columns):
        return all(p.shape[1] % LANES == 0 for p in self.pieces) and columns % OUT_TILE == 0 and self.block % 16 == 0

    def arrays(self):
        return [*self.pieces, *(self.total or [])]

    def plain(self, table, gate_matrix, up_matrix, down_matrix):
        result = sum(
            jnp.dot(
                p, lax.dynamic_slice_in_dim(down_matrix, table[i] + low, p.shape[1], 0), preferred_element_type=jnp.float32
            )
            for p, i, low in zip(self.pieces, self.places, self.lows)
        )
        if self.total is not None:
            result = result + jnp.concatenate(self.total, axis=0).astype(jnp.float32)
        return jnp.split(result.astype(self.dtype), len(self.outs))

    def scratch(self, depth):
        tiles, whole = self.columns // OUT_TILE, sum(p.shape[1] for p in self.pieces)
        return [
            pltpu.VMEM((self.rows, whole), jnp.bfloat16),
            pltpu.VMEM((tiles, whole, OUT_TILE), jnp.bfloat16),
            pltpu.VMEM(
                (self.rows if self.total else 16, self.columns), self.total[0].dtype if self.total else jnp.float32
            ),
            pltpu.VMEM((tiles, self.rows, OUT_TILE), self.dtype),
            pltpu.SemaphoreType.DMA((len(self.pieces) + len(self.outs),)),
            pltpu.SemaphoreType.DMA((len(self.pieces), tiles)),
            pltpu.SemaphoreType.DMA((len(self.outs), tiles)),
        ]

    def bind(self, refs, table, arrays, outs, scratch):
        hbuf, dbuf, tbuf, obuf, hsem, dsem, osem = scratch
        n, block, tiles = len(self.pieces), self.block, self.columns // OUT_TILE
        sizes = [p.shape[1] for p in self.pieces]
        firsts = [sum(sizes[:p]) for p in range(n)]
        starts = [table[i] + low for i, low in zip(self.places, self.lows)]

        def columns(j):
            return pl.ds(pl.multiple_of(j * OUT_TILE, LANES), OUT_TILE)

        def weights(p, j):
            return pltpu.make_async_copy(
                refs["down"].at[pl.ds(pl.multiple_of(starts[p], LANES), sizes[p]), columns(j)],
                dbuf.at[j, pl.ds(firsts[p], sizes[p])],
                dsem.at[p, j],
            )

        def write(i, j):
            return pltpu.make_async_copy(
                obuf.at[j, pl.ds(i * block, block)], outs[i].at[:, columns(j)], osem.at[i, j]
            )

        copies = [
            pltpu.make_async_copy(a, hbuf.at[:, pl.ds(firsts[i], sizes[i])], hsem.at[i]) for i, a in enumerate(arrays[:n])
        ]
        copies += [
            pltpu.make_async_copy(a, tbuf.at[pl.ds(i * block, block)], hsem.at[n + i]) for i, a in enumerate(arrays[n:])
        ]

        def begin():
            @pl.loop(0, tiles)
            def _(j):
                for p in range(n):
                    weights(p, j).start()

        def compute():
            for copy in copies:
                copy.wait()

            @pl.loop(0, tiles)
            def _(j):
                for p in range(n):
                    weights(p, j).wait()
                result = jnp.dot(hbuf[...], dbuf[j], preferred_element_type=jnp.float32)
                if self.total:
                    result = result + tbuf[:, columns(j)].astype(jnp.float32)
                obuf[j] = result.astype(obuf.dtype)
                for i in range(len(outs)):
                    write(i, j).start()

        def drain():
            @pl.loop(0, tiles)
            def _(j):
                for i in range(len(outs)):
                    write(i, j).wait()

        return copies, begin, compute, drain


def run(phases, table, gate_matrix, up_matrix, down_matrix, dep):
    depth, columns = gate_matrix.shape[0], down_matrix.shape[1]
    if not all(p.fits(depth, columns) for p in phases):
        return [p.plain(table, gate_matrix, up_matrix, down_matrix) for p in phases]
    operands = [gate_matrix, up_matrix, down_matrix]

    def index(array):
        for i, known in enumerate(operands):
            if known is array:
                return i
        operands.append(array)
        return len(operands) - 1

    groups = []
    for p in phases:
        if p.group is not None and all(p.group is not g for g in groups):
            groups.append(p.group)
    tok_places = [[index(t) for t, _ in g.toks] for g in groups]
    where = [[index(a) for a in p.arrays()] for p in phases]
    index(dep)
    outs = [o for p in phases for o in p.outs]
    scratch = [p.scratch(depth) for p in phases]

    def kernel(table_ref, *args):
        args = list(args)
        arrays = [args.pop(0) for _ in operands]
        out_refs = [args.pop(0) for _ in outs]
        refs = {"gate": arrays[0], "up": arrays[1], "down": arrays[2], "x": {}}
        ready = {}
        for g, places in zip(groups, tok_places):
            xbuf, xsem = args.pop(0), args.pop(0)
            refs["x"][id(g)] = xbuf
            ready[id(g)] = [
                pltpu.make_async_copy(
                    arrays[place].at[pl.ds(pl.multiple_of(table_ref[i], 16), g.block)],
                    xbuf.at[pl.ds(j * g.block, g.block)],
                    xsem.at[j],
                )
                for j, (place, (_, i)) in enumerate(zip(places, g.toks))
            ]
        bound = []
        for p, places, buffers in zip(phases, where, scratch):
            mine = [out_refs.pop(0) for _ in p.outs]
            held = [args.pop(0) for _ in buffers]
            bound.append(p.bind(refs, table_ref, [arrays[i] for i in places], mine, held))
        for copies in ready.values():
            for copy in copies:
                copy.start()
        for copies, begin, _, _ in bound:
            for copy in copies:
                copy.start()
            begin()
        for p, (_, _, compute, _) in zip(phases, bound):
            for copy in ready.pop(id(p.group), []):
                copy.wait()
            compute()
        for _, _, _, drain in bound:
            drain()

    results = list(
        pl.pallas_call(
            kernel,
            out_shape=outs,
            in_specs=[SMEM] + [ANY] * len(operands),
            out_specs=[ANY] * len(outs),
            scratch_shapes=[
                *[
                    buffer
                    for g in groups
                    for buffer in (pltpu.VMEM((g.rows, depth), jnp.bfloat16), pltpu.SemaphoreType.DMA((len(g.toks),)))
                ],
                *[buffer for buffers in scratch for buffer in buffers],
            ],
            compiler_params=pltpu.CompilerParams(vmem_limit_bytes=VMEM_LIMIT),
            cost_estimate=COST,
            name="step_" + "".join("g" if p.group is not None else "d" for p in phases),
        )(table, *operands)
    )
    return [[results.pop(0) for _ in p.outs] for p in phases]


STEPS = (
    ("s0", "s1"),
    ("x0", "x1"),
    ("h0",),
    ("h1",),
    ("r0", "r1", "s2", "s3"),
    ("x2",),
    ("x3",),
    ("s4",),
    ("h2",),
    ("h3",),
    ("x4",),
    ("r2", "r3", "d2", "d3"),
    ("h4",),
    ("z", "d0", "d1"),
    ("r4", "d4"),
)


def cut(width, part, parts):
    unit = LANES if width % LANES == 0 else 1
    return width // unit * part // parts * unit


def on_device(n_gx, n_gy, tokens, gate_matrix, up_matrix, down_matrix):
    features = tokens.shape[1] * n_gx
    width = gate_matrix.shape[1] // n_gx
    block, columns = tokens.shape[0], down_matrix.shape[1]
    far = [2 * k for k in range(1, n_gx // 2)]

    def core(value):
        return swap(value, "gx", n_gx, 1)

    gathered = lax.all_gather(tokens, "gy", axis=0, tiled=True)
    table = jnp.concatenate(
        [
            (lax.axis_index("gx") ^ jnp.arange(n_gx, dtype=jnp.int32)) * width,
            (lax.axis_index("gy") ^ jnp.arange(n_gy, dtype=jnp.int32)) * block,
            jnp.zeros((1,), jnp.int32),
        ]
    )
    sets = [[0], list(range(2, n_gy)), [1]]
    groups = [Group([(gathered, n_gx + j) if j else (tokens, n_gx + n_gy) for j in js], block) for js in sets]
    squares = {}
    half = cut(width, 7, 13)
    jobs = [(0, 0, half), (0, half, width - half), (1, 0, half), (1, half, width - half), (2, 0, width)]
    firsts = [min(i for i, job in enumerate(jobs) if job[0] == g) for g in range(len(groups))]
    state = [dict() for _ in jobs]
    totals = {}
    chain = tokens

    def phases_of(kind, job):
        g, low, n = jobs[job]
        group, st, first = groups[g], state[job], low == 0
        if kind == "s":
            return [GateUp(group, k ^ 1, low, n, carry=first and k > 0) for k in [*far, 0]]
        if kind == "x":
            return [
                GateUp(group, k, low, n, [st["lent"][i]], carry=first, emit=first and i == 0)
                for i, k in enumerate(far)
            ]
        if kind == "h":
            recvs = [st["lent"][-1], *st["far"]]
            return [GateUp(group, 0, low, n, recvs, squares=squares[g], at=jobs[firsts[g]][2], features=features)]
        pieces = [(st["hidden"], 0), (st["sibling"], 1)] + st["over"]
        return [
            Down(
                [h for h, _ in pieces], [q for _, q in pieces], [low] * len(pieces), totals.get(g), block, columns,
                jnp.bfloat16 if g and low + n == width else jnp.float32,
            )
        ]

    def deliver(kind, job, outs):
        g, st = jobs[job][0], state[job]
        if kind == "s":
            st["lent"] = [core(o[0]) for o in outs]
        elif kind == "x":
            st["far"] = [swap(o[0], "gx", n_gx, k) for o, k in zip(outs, far)]
            if job == firsts[g]:
                squares[g] = (outs[0][1], st["far"])
        elif kind == "h":
            st["hidden"], st["sibling"] = outs[0][0], core(outs[0][0])
            st["crossed"] = [swap(outs[0][0], "gx", n_gx, k) for k in far]
        else:
            totals[g] = outs[0]

    def tied(values):
        nonlocal chain
        values, chain = lax.optimization_barrier((values, chain))
        return values

    def forward(job):
        crossed = tied(state[job]["crossed"])
        state[job]["over"] = [(h, k) for h, k in zip(crossed, far)]
        state[job]["over"] += [(core(h), k ^ 1) for h, k in zip(crossed, far)]

    def reduce_over_gy():
        parts = dict(zip(sets[1], totals[1]))
        mask = 1
        while mask < n_gy:
            for j in [j for j in parts if j & mask]:
                arrived = swap(parts.pop(j), "gy", n_gy, mask)
                if j == mask:
                    landed.append(arrived)
                    continue
                arrived = tied(arrived).astype(jnp.float32)
                parts[j ^ mask] = (parts[j ^ mask].astype(jnp.float32) + arrived).astype(jnp.bfloat16)
            mask *= 2

    landed = []
    for names in STEPS:
        items = []
        for name in names:
            kind, job = name[0], int(name[1:] or 0)
            if kind == "r":
                forward(job)
                continue
            if kind == "z":
                reduce_over_gy()
                continue
            found = phases_of(kind, job)
            if kind == "d" and items and items[-1][0] == "d" and jobs[items[-1][1]][0] == jobs[job][0]:
                before, after = items.pop()[2][0], found[0]
                found = [
                    Down(
                        before.pieces + after.pieces, before.places + after.places, before.lows + after.lows, before.total,
                        block, columns, after.dtype,
                    )
                ]
            items.append((kind, job, found))
        results = run([p for _, _, ps in items for p in ps], table, gate_matrix, up_matrix, down_matrix, chain)
        chain = results[0][0]
        for kind, job, ps in items:
            deliver(kind, job, [results.pop(0) for _ in ps])

    landed.append(swap(totals[2][0], "gy", n_gy, 1))
    return sum((part.astype(jnp.float32) for part in landed), totals[0][0]).astype(jnp.bfloat16)


def solution(mesh):
    n_gx, n_gy = mesh.shape["gx"], mesh.shape["gy"]
    placed = (P(("groups", "gy"), "gx"), P("gx", "gy"), P("gx", "gy"), P("gy", "gx"))
    return jax.shard_map(
        functools.partial(on_device, n_gx, n_gy),
        mesh=mesh,
        in_specs=placed,
        out_specs=P(("groups", "gy"), "gx"),
        check_vma=False,
    )
```

time: 274 us -> 246 us (0.90)
  Pallas kernels: 165 us -> 136 us
  waiting for transfers between devices: 50.8 us -> 67.6 us
  blocking collectives: 16.4 us -> 0 us
    pallas_call x15, Pallas kernels: 165 us -> 136 us  [run(): pl.pallas_call(kernel, out_shape=outs, in_specs=[SMEM] + [ANY] * len(oper...]
    ppermute x36 -> x33, waiting for transfers between devices: 50.1 us -> 66.9 us  [swap(): return lax.ppermute(value, axis, [(i, i ^ mask) for i in range(size)])]
    all_gather x1 -> x0, blocking collectives: 16.4 us -> none  [on_device(): gathered_squares = lax.all_gather(squares, 'gy', axis=0, tiled=True)]
    ppermute x36 -> x33, starting transfers between devices: 21.2 us -> 23.8 us  [swap(): return lax.ppermute(value, axis, [(i, i ^ mask) for i in range(size)])]
  transfers between devices with their start and end apart: 37 -> 34, of which waited for: 12 -> 17; matrix products, arithmetic and copies ran while one was open for 2% -> 1% of each run, Pallas kernels for 54% -> 50%
where the time goes in v5:
time: 246 us
  Pallas kernels  136 us (55%)
  waiting for transfers between devices  67.6 us (27%)
  starting transfers between devices  23.8 us (10%)
  between operations  13.6 us (6%)
  other arithmetic  5.12 us (2%)
    pallas_call x15, Pallas kernels, run(): pl.pallas_call(kernel, out_shape=outs, in_specs=[SMEM] + [ANY] * len(oper...  136 us
    ppermute x33, waiting for transfers between devices, swap(): return lax.ppermute(value, axis, [(i, i ^ mask) for i in range(size)])  66.9 us
    ppermute x33, starting transfers between devices, swap(): return lax.ppermute(value, axis, [(i, i ^ mask) for i in range(size)])  23.8 us
  transfers between devices with their start and end apart: 34, of which 17 were waited for; matrix products, arithmetic and copies ran while one was open for 1% of the time, Pallas kernels for 50%

profile of v5, /device:TPU:0, one launch (start us, length us, event | category | flops | bytes accessed | tf_op | source)
XLA Modules:
  0.0 246.0 jit_solution(17253942988287400685)
XLA Ops:
  7.9 12.3 %step_gggg.2 = (bf16[2,128,1024]{2,1,0:T(8,128)(2,1)}, bf16[2,128,896]{2,1,0:T(8,128)(2,1)}, bf16[2,128,768]{2,1,0:T(8,128)(2,1)}, bf16[2,128,768]{2,1,0:T(8,128)(2,1)}) custom-call(s32[9]{0:T(128)} %pad_add_fusion.table_ref, bf16[2048,6656]{1,0:T(8,128)(2,1)} %args_0_.32, bf16[2048,6656]{1,0:T(8,128)(2,1)} %args_1_.32, bf16[6656,2048]{1,0:T(8,128)(2,1)} %args_2_.32, ...), custom_call_target="tpu_custom_call" | custom-call | flops 1000 | bytes 1000 | tf_op jit(solution)/shard_map/step_gggg/pallas_call | solution.py:350
  23.3 7.9 %step_gg.2 = (bf16[2,128,1024]{2,1,0:T(8,128)(2,1)}, f32[128,128]{1,0:T(8,128)}, bf16[2,128,768]{2,1,0:T(8,128)(2,1)}) custom-call(s32[9]{0:T(128)} %pad_add_fusion.table_ref, bf16[2048,6656]{1,0:T(8,128)(2,1)} %args_0_.32, bf16[2048,6656]{1,0:T(8,128)(2,1)} %args_1_.32, bf16[6656,2048]{1,0:T(8,128)(2,1)} %args_2_.32, bf16[128,2048]{1,0:T(8,128)(2,1)} %args_3_.10, ...), custom_call_target="tpu_custom_call" | custom-call | flops 1000 | bytes 1000 | tf_op jit(solution)/shard_map/step_gg/pallas_call | solution.py:350
  31.2 3.1 %collective-permute-start.3 = (bf16[2,128,1024]{2,1,0:T(8,128)(2,1)}, bf16[2,128,1024]{2,1,0:T(8,128)(2,1)}, u32[]{:S(2)}, u32[]{:S(2)}) collective-permute-start(bf16[2,128,1024]{2,1,0:T(8,128)(2,1)} %get-tuple-element.39.args_7_), channel_id=1, source_target_pairs={{0,8},{4,12},{8,0},{12,4},{1,9},{5,13},{9,1},{13,5},{2,10},{6,14},... | collective-permute-start | bytes 1572872 | tf_op jit(solution)/shard_map/ppermute | solution.py:21
  36.4 10.9 %collective-permute-done.3.args_5_.args_7_ = bf16[2,128,1024]{2,1,0:T(8,128)(2,1)} collective-permute-done((bf16[2,128,1024]{2,1,0:T(8,128)(2,1)}, bf16[2,128,1024]{2,1,0:T(8,128)(2,1)}, u32[]{:S(2)}, u32[]{:S(2)}) %collective-permute-start.3) | collective-permute-done | bytes 524320 | tf_op jit(solution)/shard_map/ppermute | solution.py:21
  47.3 5.7 %step_g.8.args_8_.args_3_ = bf16[128,896]{1,0:T(8,128)(2,1)} custom-call(s32[9]{0:T(128)} %pad_add_fusion.table_ref, bf16[2048,6656]{1,0:T(8,128)(2,1)} %args_0_.32, bf16[2048,6656]{1,0:T(8,128)(2,1)} %args_1_.32, bf16[6656,2048]{1,0:T(8,128)(2,1)} %args_2_.32, bf16[128,2048]{1,0:T(8,128)(2,1)} %args_3_.10, ...), custom_call_target="tpu_custom_call" | custom-call | flops 1000 | bytes 1000 | tf_op jit(solution)/shard_map/step_g/pallas_call | solution.py:350
  55.4 5.2 %step_g.9.args_4_.args_7_ = bf16[128,768]{1,0:T(8,128)(2,1)} custom-call(s32[9]{0:T(128)} %pad_add_fusion.table_ref, bf16[2048,6656]{1,0:T(8,128)(2,1)} %args_0_.32, bf16[2048,6656]{1,0:T(8,128)(2,1)} %args_1_.32, bf16[6656,2048]{1,0:T(8,128)(2,1)} %args_2_.32, bf16[128,2048]{1,0:T(8,128)(2,1)} %args_3_.10, ...), custom_call_target="tpu_custom_call" | custom-call | flops 1000 | bytes 1000 | tf_op jit(solution)/shard_map/step_g/pallas_call | solution.py:350
  62.7 4.6 %collective-permute-done.10.args_9_ = bf16[128,768]{1,0:T(8,128)(2,1)} collective-permute-done((bf16[128,768]{1,0:T(8,128)(2,1)}, bf16[128,768]{1,0:T(8,128)(2,1)}, u32[]{:S(2)}, u32[]{:S(2)}) %collective-permute-start.10) | collective-permute-done | bytes 196640 | tf_op jit(solution)/shard_map/ppermute | solution.py:21
  67.4 13.2 %step_gggg.3 = (bf16[2,256,1024]{2,1,0:T(8,128)(2,1)}, bf16[2,256,896]{2,1,0:T(8,128)(2,1)}, bf16[2,256,768]{2,1,0:T(8,128)(2,1)}, bf16[2,256,768]{2,1,0:T(8,128)(2,1)}) custom-call(s32[9]{0:T(128)} %pad_add_fusion.table_ref, bf16[2048,6656]{1,0:T(8,128)(2,1)} %args_0_.32, bf16[2048,6656]{1,0:T(8,128)(2,1)} %args_1_.32, bf16[6656,2048]{1,0:T(8,128)(2,1)} %args_2_.32, ...), custom_call_target="tpu_custom_call" | custom-call | flops 1000 | bytes 1000 | tf_op jit(solution)/shard_map/step_gggg/pallas_call | solution.py:350
  81.1 2.5 %collective-permute-done.13.args_4_ = bf16[2,256,1024]{2,1,0:T(8,128)(2,1)} collective-permute-done((bf16[2,256,1024]{2,1,0:T(8,128)(2,1)}, bf16[2,256,1024]{2,1,0:T(8,128)(2,1)}, u32[]{:S(2)}, u32[]{:S(2)}) %collective-permute-start.13) | collective-permute-done | bytes 1048608 | tf_op jit(solution)/shard_map/ppermute | solution.py:21
  83.6 6.3 %step_g.10 = (bf16[2,256,1024]{2,1,0:T(8,128)(2,1)}, f32[256,128]{1,0:T(8,128)}) custom-call(s32[9]{0:T(128)} %pad_add_fusion.table_ref, bf16[2048,6656]{1,0:T(8,128)(2,1)} %args_0_.32, bf16[2048,6656]{1,0:T(8,128)(2,1)} %args_1_.32, bf16[6656,2048]{1,0:T(8,128)(2,1)} %args_2_.32, bf16[512,2048]{1,0:T(8,128)(2,1)} %all-gather.2.cloned.1.call-done.args_3_, ...), custom_call_target="tpu_custom_call" | custom-call | flops 1000 | bytes 1000 | tf_op jit(solution)/shard_map/step_g/pallas_call | solution.py:350
  91.9 5.8 %step_g.11.args_4_ = bf16[2,256,768]{2,1,0:T(8,128)(2,1)} custom-call(s32[9]{0:T(128)} %pad_add_fusion.table_ref, bf16[2048,6656]{1,0:T(8,128)(2,1)} %args_0_.32, bf16[2048,6656]{1,0:T(8,128)(2,1)} %args_1_.32, bf16[6656,2048]{1,0:T(8,128)(2,1)} %args_2_.32, bf16[512,2048]{1,0:T(8,128)(2,1)} %all-gather.2.cloned.1.call-done.args_3_, ...), custom_call_target="tpu_custom_call" | custom-call | flops 1000 | bytes 1000 | tf_op jit(solution)/shard_map/step_g/pallas_call | solution.py:350
  98.4 12.0 %step_gg.3 = (bf16[2,128,1792]{2,1,0:T(8,128)(2,1)}, bf16[2,128,1664]{2,1,0:T(8,128)(2,1)}) custom-call(s32[9]{0:T(128)} %pad_add_fusion.table_ref, bf16[2048,6656]{1,0:T(8,128)(2,1)} %args_0_.32, bf16[2048,6656]{1,0:T(8,128)(2,1)} %args_1_.32, bf16[6656,2048]{1,0:T(8,128)(2,1)} %args_2_.32, bf16[512,2048]{1,0:T(8,128)(2,1)} %all-gather.2.cloned.1.call-done.args_3_, ...), custom_call_target="tpu_custom_call" | custom-call | flops 1000 | bytes 1000 | tf_op jit(solution)/shard_map/step_gg/pallas_call | solution.py:350
  110.5 5.8 %collective-permute-done.14.args_5_.args_7_ = bf16[2,256,1024]{2,1,0:T(8,128)(2,1)} collective-permute-done((bf16[2,256,1024]{2,1,0:T(8,128)(2,1)}, bf16[2,256,1024]{2,1,0:T(8,128)(2,1)}, u32[]{:S(2)}, u32[]{:S(2)}) %collective-permute-start.14) | collective-permute-done | bytes 1048608 | tf_op jit(solution)/shard_map/ppermute | solution.py:21
  116.3 6.8 %step_g.12.args_8_.args_3_ = bf16[256,896]{1,0:T(8,128)(2,1)} custom-call(s32[9]{0:T(128)} %pad_add_fusion.table_ref, bf16[2048,6656]{1,0:T(8,128)(2,1)} %args_0_.32, bf16[2048,6656]{1,0:T(8,128)(2,1)} %args_1_.32, bf16[6656,2048]{1,0:T(8,128)(2,1)} %args_2_.32, bf16[512,2048]{1,0:T(8,128)(2,1)} %all-gather.2.cloned.1.call-done.args_3_, ...), custom_call_target="tpu_custom_call" | custom-call | flops 1000 | bytes 1000 | tf_op jit(solution)/shard_map/step_g/pallas_call | solution.py:350
  124.6 8.5 %collective-permute-done.20.args_5_ = bf16[2,256,768]{2,1,0:T(8,128)(2,1)} collective-permute-done((bf16[2,256,768]{2,1,0:T(8,128)(2,1)}, bf16[2,256,768]{2,1,0:T(8,128)(2,1)}, u32[]{:S(2)}, u32[]{:S(2)}) %collective-permute-start.20) | collective-permute-done | bytes 786464 | tf_op jit(solution)/shard_map/ppermute | solution.py:21
  133.2 6.3 %step_g.13.args_5_.args_7_ = bf16[256,768]{1,0:T(8,128)(2,1)} custom-call(s32[9]{0:T(128)} %pad_add_fusion.table_ref, bf16[2048,6656]{1,0:T(8,128)(2,1)} %args_0_.32, bf16[2048,6656]{1,0:T(8,128)(2,1)} %args_1_.32, bf16[6656,2048]{1,0:T(8,128)(2,1)} %args_2_.32, bf16[512,2048]{1,0:T(8,128)(2,1)} %all-gather.2.cloned.1.call-done.args_3_, ...), custom_call_target="tpu_custom_call" | custom-call | flops 1000 | bytes 1000 | tf_op jit(solution)/shard_map/step_g/pallas_call | solution.py:350
  140.9 7.7 %step_g.14 = (bf16[2,128,1792]{2,1,0:T(8,128)(2,1)}, f32[128,128]{1,0:T(8,128)}) custom-call(s32[9]{0:T(128)} %pad_add_fusion.table_ref, bf16[2048,6656]{1,0:T(8,128)(2,1)} %args_0_.32, bf16[2048,6656]{1,0:T(8,128)(2,1)} %args_1_.32, bf16[6656,2048]{1,0:T(8,128)(2,1)} %args_2_.32, bf16[512,2048]{1,0:T(8,128)(2,1)} %all-gather.2.cloned.1.call-done.args_3_, ...), custom_call_target="tpu_custom_call" | custom-call | flops 1000 | bytes 1000 | tf_op jit(solution)/shard_map/step_g/pallas_call | solution.py:350
  153.9 13.9 %step_d.3 = (bf16[128,2048]{1,0:T(8,128)(2,1)}, bf16[128,2048]{1,0:T(8,128)(2,1)}) custom-call(s32[9]{0:T(128)} %pad_add_fusion.table_ref, bf16[2048,6656]{1,0:T(8,128)(2,1)} %args_0_.32, bf16[2048,6656]{1,0:T(8,128)(2,1)} %args_1_.32, bf16[6656,2048]{1,0:T(8,128)(2,1)} %args_2_.32, bf16[256,896]{1,0:T(8,128)(2,1)} %step_g.12.args_8_.args_3_, ...), custom_call_target="tpu_custom_call" | custom-call | flops 1000 | bytes 1000 | tf_op jit(solution)/shard_map/step_d/pallas_call | solution.py:350
  171.8 7.9 %step_g.15.args_11_.args_3_ = bf16[128,1664]{1,0:T(8,128)(2,1)} custom-call(s32[9]{0:T(128)} %pad_add_fusion.table_ref, bf16[2048,6656]{1,0:T(8,128)(2,1)} %args_0_.32, bf16[2048,6656]{1,0:T(8,128)(2,1)} %args_1_.32, bf16[6656,2048]{1,0:T(8,128)(2,1)} %args_2_.32, bf16[512,2048]{1,0:T(8,128)(2,1)} %all-gather.2.cloned.1.call-done.args_3_, ...), custom_call_target="tpu_custom_call" | custom-call | flops 1000 | bytes 1000 | tf_op jit(solution)/shard_map/step_g/pallas_call | solution.py:350
  184.0 12.7 %step_d.4.args_7_ = f32[128,2048]{1,0:T(8,128)} custom-call(s32[9]{0:T(128)} %pad_add_fusion.table_ref, bf16[2048,6656]{1,0:T(8,128)(2,1)} %args_0_.32, bf16[2048,6656]{1,0:T(8,128)(2,1)} %args_1_.32, bf16[6656,2048]{1,0:T(8,128)(2,1)} %args_2_.32, bf16[128,896]{1,0:T(8,128)(2,1)} %step_g.8.args_8_.args_3_, bf16[128,896]{1,0:T(8,128)(2,1)} %collective-permute-done.4.args_4_, ...), custom_call_target="tpu_custom_call" | custom-call | flops 1000 | bytes 1000 | tf_op jit(solution)/shard_map/step_d/pallas_call | solution.py:350
  199.0 2.5 %collective-permute-start.28 = (bf16[128,2048]{1,0:T(8,128)(2,1)}, bf16[128,2048]{1,0:T(8,128)(2,1)}, u32[]{:S(2)}, u32[]{:S(2)}) collective-permute-start(bf16[128,2048]{1,0:T(8,128)(2,1)} %add_convert_fusion.1), channel_id=1, source_target_pairs={{0,2},{1,3},{2,0},{3,1},{4,6},{5,7},{6,4},{7,5},{8,10},{9,11},{10,... | collective-permute-start | bytes 1572872 | tf_op jit(solution)/shard_map/ppermute | solution.py:21
  201.6 12.2 %step_d.5 = bf16[128,2048]{1,0:T(8,128)(2,1)} custom-call(s32[9]{0:T(128)} %pad_add_fusion.table_ref, bf16[2048,6656]{1,0:T(8,128)(2,1)} %args_0_.32, bf16[2048,6656]{1,0:T(8,128)(2,1)} %args_1_.32, bf16[6656,2048]{1,0:T(8,128)(2,1)} %args_2_.32, bf16[128,1664]{1,0:T(8,128)(2,1)} %step_g.15.args_11_.args_3_, ...), custom_call_target="tpu_custom_call" | custom-call | flops 1000 | bytes 1000 | tf_op jit(solution)/shard_map/step_d/pallas_call | solution.py:350
  215.4 10.3 %collective-permute-done.28 = bf16[128,2048]{1,0:T(8,128)(2,1)} collective-permute-done((bf16[128,2048]{1,0:T(8,128)(2,1)}, bf16[128,2048]{1,0:T(8,128)(2,1)}, u32[]{:S(2)}, u32[]{:S(2)}) %collective-permute-start.28) | collective-permute-done | bytes 524320 | tf_op jit(solution)/shard_map/ppermute | solution.py:21
  225.8 11.0 %collective-permute-done.32 = bf16[128,2048]{1,0:T(8,128)(2,1)S(1)} collective-permute-done((bf16[128,2048]{1,0:T(8,128)(2,1)}, bf16[128,2048]{1,0:T(8,128)(2,1)S(1)}, u32[]{:S(2)}, u32[]{:S(2)}) %collective-permute-start.32) | collective-permute-done | bytes 524320 | tf_op jit(solution)/shard_map/ppermute | solution.py:21
  (64 shorter events, 37.2 us)
Async XLA Ops:
  6.5 60.8 %all-gather.2.cloned.1.call-start = ((), (), s32[]{:S(2)}) async-start(), calls=%async_computation | async-start | bytes 2621440 | tf_op jit(solution)/shard_map/all_gather | solution.py:404
  31.2 16.1 %collective-permute-start.3 = (bf16[2,128,1024]{2,1,0:T(8,128)(2,1)}, bf16[2,128,1024]{2,1,0:T(8,128)(2,1)}, u32[]{:S(2)}, u32[]{:S(2)}) collective-permute-start(bf16[2,128,1024]{2,1,0:T(8,128)(2,1)} %get-tuple-element.39.args_7_), channel_id=1, source_target_pairs={{0,8},{4,12},{8,0},{12,4},{1,9},{5,13},{9,1},{13,5},{2,10},{6,14},... | collective-permute-start | bytes 1572872 | tf_op jit(solution)/shard_map/ppermute | solution.py:21
  34.3 20.8 %collective-permute-start.6 = (bf16[2,128,768]{2,1,0:T(8,128)(2,1)}, bf16[2,128,768]{2,1,0:T(8,128)(2,1)}, u32[]{:S(2)}, u32[]{:S(2)}) collective-permute-start(bf16[2,128,768]{2,1,0:T(8,128)(2,1)} %get-tuple-element.41), channel_id=1, source_target_pairs={{0,4},{4,0},{8,12},{12,8},{1,5},{5,1},{9,13},{13,9},{2,6},{6,2},{1... | collective-permute-start | bytes 1179656 | tf_op jit(solution)/shard_map/ppermute | solution.py:21
  34.8 20.6 %collective-permute-start.7 = (bf16[2,128,768]{2,1,0:T(8,128)(2,1)}, bf16[2,128,768]{2,1,0:T(8,128)(2,1)}, u32[]{:S(2)}, u32[]{:S(2)}) collective-permute-start(bf16[2,128,768]{2,1,0:T(8,128)(2,1)} %get-tuple-element.42), channel_id=1, source_target_pairs={{0,8},{4,12},{8,0},{12,4},{1,9},{5,13},{9,1},{13,5},{2,10},{6,14},... | collective-permute-start | bytes 1179656 | tf_op jit(solution)/shard_map/ppermute | solution.py:21
  53.0 9.8 %collective-permute-start.5 = (bf16[128,896]{1,0:T(8,128)(2,1)}, bf16[128,896]{1,0:T(8,128)(2,1)}, u32[]{:S(2)}, u32[]{:S(2)}) collective-permute-start(bf16[128,896]{1,0:T(8,128)(2,1)} %step_g.8.args_8_.args_3_), channel_id=1, source_target_pairs={{0,8},{4,12},{8,0},{12,4},{1,9},{5,13},{9,1},{13,5},{2,10},{6,14},... | collective-permute-start | bytes 688136 | tf_op jit(solution)/shard_map/ppermute | solution.py:21
  60.6 6.8 %collective-permute-start.10 = (bf16[128,768]{1,0:T(8,128)(2,1)}, bf16[128,768]{1,0:T(8,128)(2,1)}, u32[]{:S(2)}, u32[]{:S(2)}) collective-permute-start(bf16[128,768]{1,0:T(8,128)(2,1)} %step_g.9.args_4_.args_7_), channel_id=1, source_target_pairs={{0,8},{4,12},{8,0},{12,4},{1,9},{5,13},{9,1},{13,5},{2,10},{6,14},... | collective-permute-start | bytes 589832 | tf_op jit(solution)/shard_map/ppermute | solution.py:21
  80.6 11.3 %collective-permute-start.15 = (bf16[2,256,768]{2,1,0:T(8,128)(2,1)}, bf16[2,256,768]{2,1,0:T(8,128)(2,1)}, u32[]{:S(2)}, u32[]{:S(2)}) collective-permute-start(bf16[2,256,768]{2,1,0:T(8,128)(2,1)} %get-tuple-element.51), channel_id=1, source_target_pairs={{0,4},{4,0},{8,12},{12,8},{1,5},{5,1},{9,13},{13,9},{2,6},{6,2},{1... | collective-permute-start | bytes 2359304 | tf_op jit(solution)/shard_map/ppermute | solution.py:21
  89.9 26.4 %collective-permute-start.14 = (bf16[2,256,1024]{2,1,0:T(8,128)(2,1)}, bf16[2,256,1024]{2,1,0:T(8,128)(2,1)}, u32[]{:S(2)}, u32[]{:S(2)}) collective-permute-start(bf16[2,256,1024]{2,1,0:T(8,128)(2,1)} %get-tuple-element.49.args_5_), channel_id=1, source_target_pairs={{0,8},{4,12},{8,0},{12,4},{1,9},{5,13},{9,1},{13,5},{2,10},{6,14},... | collective-permute-start | bytes 3145736 | tf_op jit(solution)/shard_map/ppermute | solution.py:21
  91.4 19.1 %collective-permute-start.12 = (bf16[2,256,896]{2,1,0:T(8,128)(2,1)}, bf16[2,256,896]{2,1,0:T(8,128)(2,1)}, u32[]{:S(2)}, u32[]{:S(2)}) collective-permute-start(bf16[2,256,896]{2,1,0:T(8,128)(2,1)} %get-tuple-element.47), channel_id=1, source_target_pairs={{0,4},{4,0},{8,12},{12,8},{1,5},{5,1},{9,13},{13,9},{2,6},{6,2},{1... | collective-permute-start | bytes 2752520 | tf_op jit(solution)/shard_map/ppermute | solution.py:21
  91.4 33.2 %collective-permute-start.19 = (bf16[2,256,768]{2,1,0:T(8,128)(2,1)}, bf16[2,256,768]{2,1,0:T(8,128)(2,1)}, u32[]{:S(2)}, u32[]{:S(2)}) collective-permute-start(bf16[2,256,768]{2,1,0:T(8,128)(2,1)} %get-tuple-element.53), channel_id=1, source_target_pairs={{0,4},{4,0},{8,12},{12,8},{1,5},{5,1},{9,13},{13,9},{2,6},{6,2},{1... | collective-permute-start | bytes 2359304 | tf_op jit(solution)/shard_map/ppermute | solution.py:21
  97.7 35.4 %collective-permute-start.20 = (bf16[2,256,768]{2,1,0:T(8,128)(2,1)}, bf16[2,256,768]{2,1,0:T(8,128)(2,1)}, u32[]{:S(2)}, u32[]{:S(2)}) collective-permute-start(bf16[2,256,768]{2,1,0:T(8,128)(2,1)} %step_g.11.args_4_), channel_id=1, source_target_pairs={{0,8},{4,12},{8,0},{12,4},{1,9},{5,13},{9,1},{13,5},{2,10},{6,14},... | collective-permute-start | bytes 2359304 | tf_op jit(solution)/shard_map/ppermute | solution.py:21
  110.4 30.5 %collective-permute-start.18 = (bf16[2,128,1792]{2,1,0:T(8,128)(2,1)}, bf16[2,128,1792]{2,1,0:T(8,128)(2,1)}, u32[]{:S(2)}, u32[]{:S(2)}) collective-permute-start(bf16[2,128,1792]{2,1,0:T(8,128)(2,1)} %get-tuple-element.52.args_7_), channel_id=1, source_target_pairs={{0,4},{4,0},{8,12},{12,8},{1,5},{5,1},{9,13},{13,9},{2,6},{6,2},{1... | collective-permute-start | bytes 2752520 | tf_op jit(solution)/shard_map/ppermute | solution.py:21
  123.2 26.4 %collective-permute-start.17 = (bf16[256,896]{1,0:T(8,128)(2,1)}, bf16[256,896]{1,0:T(8,128)(2,1)}, u32[]{:S(2)}, u32[]{:S(2)}) collective-permute-start(bf16[256,896]{1,0:T(8,128)(2,1)} %step_g.12.args_8_.args_3_), channel_id=1, source_target_pairs={{0,8},{4,12},{8,0},{12,4},{1,9},{5,13},{9,1},{13,5},{2,10},{6,14},... | collective-permute-start | bytes 1376264 | tf_op jit(solution)/shard_map/ppermute | solution.py:21
  139.4 11.2 %collective-permute-start.23 = (bf16[256,768]{1,0:T(8,128)(2,1)}, bf16[256,768]{1,0:T(8,128)(2,1)}, u32[]{:S(2)}, u32[]{:S(2)}) collective-permute-start(bf16[256,768]{1,0:T(8,128)(2,1)} %step_g.13.args_5_.args_7_), channel_id=1, source_target_pairs={{0,8},{4,12},{8,0},{12,4},{1,9},{5,13},{9,1},{13,5},{2,10},{6,14},... | collective-permute-start | bytes 1179656 | tf_op jit(solution)/shard_map/ppermute | solution.py:21
  140.9 9.7 %collective-permute-start.22 = (bf16[256,768]{1,0:T(8,128)(2,1)}, bf16[256,768]{1,0:T(8,128)(2,1)}, u32[]{:S(2)}, u32[]{:S(2)}) collective-permute-start(bf16[256,768]{1,0:T(8,128)(2,1)} %step_g.13.args_5_.args_7_), channel_id=1, source_target_pairs={{0,4},{4,0},{8,12},{12,8},{1,5},{5,1},{9,13},{13,9},{2,6},{6,2},{1... | collective-permute-start | bytes 1179656 | tf_op jit(solution)/shard_map/ppermute | solution.py:21
  148.6 23.1 %collective-permute-start.27 = (bf16[2,128,1792]{2,1,0:T(8,128)(2,1)}, bf16[2,128,1792]{2,1,0:T(8,128)(2,1)}, u32[]{:S(2)}, u32[]{:S(2)}) collective-permute-start(bf16[2,128,1792]{2,1,0:T(8,128)(2,1)} %get-tuple-element.58.args_11_), channel_id=1, source_target_pairs={{0,8},{4,12},{8,0},{12,4},{1,9},{5,13},{9,1},{13,5},{2,10},{6,14},... | collective-permute-start | bytes 2752520 | tf_op jit(solution)/shard_map/ppermute | solution.py:21
  149.3 20.0 %collective-permute-start.26 = (bf16[2,128,1664]{2,1,0:T(8,128)(2,1)}, bf16[2,128,1664]{2,1,0:T(8,128)(2,1)}, u32[]{:S(2)}, u32[]{:S(2)}) collective-permute-start(bf16[2,128,1664]{2,1,0:T(8,128)(2,1)} %get-tuple-element.60), channel_id=1, source_target_pairs={{0,4},{4,0},{8,12},{12,8},{1,5},{5,1},{9,13},{13,9},{2,6},{6,2},{1... | collective-permute-start | bytes 2555912 | tf_op jit(solution)/shard_map/ppermute | solution.py:21
  167.8 14.4 %collective-permute-start.25 = (bf16[128,2048]{1,0:T(8,128)(2,1)}, bf16[128,2048]{1,0:T(8,128)(2,1)}, u32[]{:S(2)}, u32[]{:S(2)}) collective-permute-start(bf16[128,2048]{1,0:T(8,128)(2,1)} %get-tuple-element.59), channel_id=1, source_target_pairs={{0,1},{1,0},{2,3},{3,2},{4,5},{5,4},{6,7},{7,6},{8,9},{9,8},{10,11... | collective-permute-start | bytes 1572872 | tf_op jit(solution)/shard_map/ppermute | solution.py:21
  179.7 17.0 %collective-permute-start.30 = (bf16[128,1664]{1,0:T(8,128)(2,1)}, bf16[128,1664]{1,0:T(8,128)(2,1)}, u32[]{:S(2)}, u32[]{:S(2)}) collective-permute-start(bf16[128,1664]{1,0:T(8,128)(2,1)} %step_g.15.args_11_.args_3_), channel_id=1, source_target_pairs={{0,8},{4,12},{8,0},{12,4},{1,9},{5,13},{9,1},{13,5},{2,10},{6,14},... | collective-permute-start | bytes 1277960 | tf_op jit(solution)/shard_map/ppermute | solution.py:21
  180.4 3.7 %collective-permute-start.8 = (bf16[128,896]{1,0:T(8,128)(2,1)}, bf16[128,896]{1,0:T(8,128)(2,1)}, u32[]{:S(2)}, u32[]{:S(2)}) collective-permute-start(bf16[128,896]{1,0:T(8,128)(2,1)} %collective-permute-done.5.args_5_), channel_id=1, source_target_pairs={{0,4},{4,0},{8,12},{12,8},{1,5},{5,1},{9,13},{13,9},{2,6},{6,2},{1... | collective-permute-start | bytes 688136 | tf_op jit(solution)/shard_map/ppermute | solution.py:21
  182.8 18.8 %collective-permute-start.29 = (bf16[128,1664]{1,0:T(8,128)(2,1)}, bf16[128,1664]{1,0:T(8,128)(2,1)}, u32[]{:S(2)}, u32[]{:S(2)}) collective-permute-start(bf16[128,1664]{1,0:T(8,128)(2,1)} %step_g.15.args_11_.args_3_), channel_id=1, source_target_pairs={{0,4},{4,0},{8,12},{12,8},{1,5},{5,1},{9,13},{13,9},{2,6},{6,2},{1... | collective-permute-start | bytes 1277960 | tf_op jit(solution)/shard_map/ppermute | solution.py:21
  196.7 4.9 %collective-permute-start.31 = (bf16[128,1664]{1,0:T(8,128)(2,1)}, bf16[128,1664]{1,0:T(8,128)(2,1)}, u32[]{:S(2)}, u32[]{:S(2)}) collective-permute-start(bf16[128,1664]{1,0:T(8,128)(2,1)} %collective-permute-done.30.args_5_), channel_id=1, source_target_pairs={{0,4},{4,0},{8,12},{12,8},{1,5},{5,1},{9,13},{13,9},{2,6},{6,2},{1... | collective-permute-start | bytes 1277960 | tf_op jit(solution)/shard_map/ppermute | solution.py:21
  199.0 26.8 %collective-permute-start.28 = (bf16[128,2048]{1,0:T(8,128)(2,1)}, bf16[128,2048]{1,0:T(8,128)(2,1)}, u32[]{:S(2)}, u32[]{:S(2)}) collective-permute-start(bf16[128,2048]{1,0:T(8,128)(2,1)} %add_convert_fusion.1), channel_id=1, source_target_pairs={{0,2},{1,3},{2,0},{3,1},{4,6},{5,7},{6,4},{7,5},{8,10},{9,11},{10,... | collective-permute-start | bytes 1572872 | tf_op jit(solution)/shard_map/ppermute | solution.py:21
  213.8 23.0 %collective-permute-start.32 = (bf16[128,2048]{1,0:T(8,128)(2,1)}, bf16[128,2048]{1,0:T(8,128)(2,1)S(1)}, u32[]{:S(2)}, u32[]{:S(2)}) collective-permute-start(bf16[128,2048]{1,0:T(8,128)(2,1)} %step_d.5), channel_id=1, source_target_pairs={{0,1},{1,0},{2,3},{3,2},{4,5},{5,4},{6,7},{7,6},{8,9},{9,8},{10,11... | collective-permute-start | bytes 1572872 | tf_op jit(solution)/shard_map/ppermute | solution.py:21
  (10 other events, 26.7 us)
Sparse Core Ops, SparseCore 0:
  8.9 48.6 all-gather.1

commit v6 on v5

--- a/solution.py
+++ b/solution.py
@@ -192,56 +192,57 @@
 
 
 class Down:
-    def __init__(self, pieces, places, lows, total, block, columns, dtype):
-        self.pieces, self.places, self.lows, self.total, self.block, self.dtype = pieces, places, lows, total, block, dtype
-        self.rows, self.columns, self.group = pieces[0].shape[0], columns, None
-        self.outs = [jax.ShapeDtypeStruct((block, columns), dtype) for _ in range(self.rows // block)]
+    def __init__(self, parts, places, width, block, columns):
+        self.parts, self.places, self.width, self.block, self.columns = parts, places, width, block, columns
+        self.group, self.rows = None, sum(part[0][0].shape[0] for part in parts)
+        self.outs = [jax.ShapeDtypeStruct((block, columns), jnp.bfloat16) for _ in range(self.rows // block)]
 
     def fits(self, depth, columns):
-        return all(p.shape[1] % LANES == 0 for p in self.pieces) and columns % OUT_TILE == 0 and self.block % 16 == 0
+        sizes = [a.shape[1] for part in self.parts for a, _, _ in part]
+        return all(n % LANES == 0 for n in sizes) and columns % OUT_TILE == 0 and self.block % 16 == 0
 
     def arrays(self):
-        return [*self.pieces, *(self.total or [])]
+        return [a for part in self.parts for a, _, _ in part]
 
     def plain(self, table, gate_matrix, up_matrix, down_matrix):
-        result = sum(
-            jnp.dot(
-                p, lax.dynamic_slice_in_dim(down_matrix, table[i] + low, p.shape[1], 0), preferred_element_type=jnp.float32
-            )
-            for p, i, low in zip(self.pieces, self.places, self.lows)
+        result = jnp.concatenate(
+            [
+                sum(
+                    jnp.dot(
+                        a,
+                        lax.dynamic_slice_in_dim(down_matrix, table[place] + low, a.shape[1], 0),
+                        preferred_element_type=jnp.float32,
+                    )
+                    for a, place, low in part
+                )
+                for part in self.parts
+            ],
+            axis=0,
         )
-        if self.total is not None:
-            result = result + jnp.concatenate(self.total, axis=0).astype(jnp.float32)
-        return jnp.split(result.astype(self.dtype), len(self.outs))
+        return jnp.split(result.astype(jnp.bfloat16), len(self.outs))
 
     def scratch(self, depth):
-        tiles, whole = self.columns // OUT_TILE, sum(p.shape[1] for p in self.pieces)
+        tiles, whole = self.columns // OUT_TILE, len(self.places) * self.width
         return [
             pltpu.VMEM((self.rows, whole), jnp.bfloat16),
             pltpu.VMEM((tiles, whole, OUT_TILE), jnp.bfloat16),
-            pltpu.VMEM(
-                (self.rows if self.total else 16, self.columns), self.total[0].dtype if self.total else jnp.float32
-            ),
-            pltpu.VMEM((tiles, self.rows, OUT_TILE), self.dtype),
-            pltpu.SemaphoreType.DMA((len(self.pieces) + len(self.outs),)),
-            pltpu.SemaphoreType.DMA((len(self.pieces), tiles)),
+            pltpu.VMEM((tiles, self.rows, OUT_TILE), jnp.bfloat16),
+            pltpu.SemaphoreType.DMA((len(self.arrays()),)),
+            pltpu.SemaphoreType.DMA((len(self.places), tiles)),
             pltpu.SemaphoreType.DMA((len(self.outs), tiles)),
         ]
 
     def bind(self, refs, table, arrays, outs, scratch):
-        hbuf, dbuf, tbuf, obuf, hsem, dsem, osem = scratch
-        n, block, tiles = len(self.pieces), self.block, self.columns // OUT_TILE
-        sizes = [p.shape[1] for p in self.pieces]
-        firsts = [sum(sizes[:p]) for p in range(n)]
-        starts = [table[i] + low for i, low in zip(self.places, self.lows)]
+        hbuf, dbuf, obuf, hsem, dsem, osem = scratch
+        block, width, tiles = self.block, self.width, self.columns // OUT_TILE
 
         def columns(j):
             return pl.ds(pl.multiple_of(j * OUT_TILE, LANES), OUT_TILE)
 
         def weights(p, j):
             return pltpu.make_async_copy(
-                refs["down"].at[pl.ds(pl.multiple_of(starts[p], LANES), sizes[p]), columns(j)],
-                dbuf.at[j, pl.ds(firsts[p], sizes[p])],
+                refs["down"].at[pl.ds(pl.multiple_of(table[self.places[p]], LANES), width), columns(j)],
+                dbuf.at[j, pl.ds(p * width, width)],
                 dsem.at[p, j],
             )
 
@@ -250,17 +251,19 @@
                 obuf.at[j, pl.ds(i * block, block)], outs[i].at[:, columns(j)], osem.at[i, j]
             )
 
-        copies = [
-            pltpu.make_async_copy(a, hbuf.at[:, pl.ds(firsts[i], sizes[i])], hsem.at[i]) for i, a in enumerate(arrays[:n])
-        ]
-        copies += [
-            pltpu.make_async_copy(a, tbuf.at[pl.ds(i * block, block)], hsem.at[n + i]) for i, a in enumerate(arrays[n:])
-        ]
+        copies, row = [], 0
+        for part in self.parts:
+            rows = part[0][0].shape[0]
+            for a, place, low in part:
+                units = pl.ds(self.places.index(place) * width + low, a.shape[1])
+                i = len(copies)
+                copies.append(pltpu.make_async_copy(arrays[i], hbuf.at[pl.ds(row, rows), units], hsem.at[i]))
+            row += rows
 
         def begin():
             @pl.loop(0, tiles)
             def _(j):
-                for p in range(n):
+                for p in range(len(self.places)):
                     weights(p, j).start()
 
         def compute():
@@ -269,12 +272,10 @@
 
             @pl.loop(0, tiles)
             def _(j):
-                for p in range(n):
+                for p in range(len(self.places)):
                     weights(p, j).wait()
                 result = jnp.dot(hbuf[...], dbuf[j], preferred_element_type=jnp.float32)
-                if self.total:
-                    result = result + tbuf[:, columns(j)].astype(jnp.float32)
-                obuf[j] = result.astype(obuf.dtype)
+                obuf[j] = result.astype(jnp.bfloat16)
                 for i in range(len(outs)):
                     write(i, j).start()
 
@@ -369,8 +370,10 @@
 
 
 STEPS = (
-    ("s0", "s1"),
-    ("x0", "x1"),
+    ("s0",),
+    ("s1",),
+    ("x0",),
+    ("x1",),
     ("h0",),
     ("h1",),
     ("r0", "r1", "s2", "s3"),
@@ -380,10 +383,9 @@
     ("h2",),
     ("h3",),
     ("x4",),
-    ("r2", "r3", "d2", "d3"),
+    ("r2", "r3", "d1"),
     ("h4",),
-    ("z", "d0", "d1"),
-    ("r4", "d4"),
+    ("z", "r4", "d02"),
 )
 
 
@@ -432,13 +434,12 @@
         if kind == "h":
             recvs = [st["lent"][-1], *st["far"]]
             return [GateUp(group, 0, low, n, recvs, squares=squares[g], at=jobs[firsts[g]][2], features=features)]
-        pieces = [(st["hidden"], 0), (st["sibling"], 1)] + st["over"]
-        return [
-            Down(
-                [h for h, _ in pieces], [q for _, q in pieces], [low] * len(pieces), totals.get(g), block, columns,
-                jnp.bfloat16 if g and low + n == width else jnp.float32,
-            )
+
+    def down(gs):
+        parts = [
+            [(h, q, jobs[i][1]) for i, st in enumerate(state) if jobs[i][0] == g for h, q in st["pieces"]] for g in gs
         ]
+        return Down(parts, list(range(n_gx)), width, block, columns)
 
     def deliver(kind, job, outs):
         g, st = jobs[job][0], state[job]
@@ -449,10 +450,8 @@
             if job == firsts[g]:
                 squares[g] = (outs[0][1], st["far"])
         elif kind == "h":
-            st["hidden"], st["sibling"] = outs[0][0], core(outs[0][0])
+            st["pieces"] = [(outs[0][0], 0), (core(outs[0][0]), 1)]
             st["crossed"] = [swap(outs[0][0], "gx", n_gx, k) for k in far]
-        else:
-            totals[g] = outs[0]
 
     def tied(values):
         nonlocal chain
@@ -461,8 +460,8 @@
 
     def forward(job):
         crossed = tied(state[job]["crossed"])
-        state[job]["over"] = [(h, k) for h, k in zip(crossed, far)]
-        state[job]["over"] += [(core(h), k ^ 1) for h, k in zip(crossed, far)]
+        state[job]["pieces"] += [(h, k) for h, k in zip(crossed, far)]
+        state[job]["pieces"] += [(core(h), k ^ 1) for h, k in zip(crossed, far)]
 
     def reduce_over_gy():
         parts = dict(zip(sets[1], totals[1]))
@@ -488,23 +487,22 @@
             if kind == "z":
                 reduce_over_gy()
                 continue
-            found = phases_of(kind, job)
-            if kind == "d" and items and items[-1][0] == "d" and jobs[items[-1][1]][0] == jobs[job][0]:
-                before, after = items.pop()[2][0], found[0]
-                found = [
-                    Down(
-                        before.pieces + after.pieces, before.places + after.places, before.lows + after.lows, before.total,
-                        block, columns, after.dtype,
-                    )
-                ]
-            items.append((kind, job, found))
+            if kind == "d":
+                items.append((kind, [int(g) for g in name[1:]], [down([int(g) for g in name[1:]])]))
+            else:
+                items.append((kind, job, phases_of(kind, job)))
         results = run([p for _, _, ps in items for p in ps], table, gate_matrix, up_matrix, down_matrix, chain)
         chain = results[0][0]
         for kind, job, ps in items:
-            deliver(kind, job, [results.pop(0) for _ in ps])
+            outs = [results.pop(0) for _ in ps]
+            if kind != "d":
+                deliver(kind, job, outs)
+                continue
+            for g in job:
+                totals[g] = [outs[0].pop(0) for _ in sets[g]]
 
     landed.append(swap(totals[2][0], "gy", n_gy, 1))
-    return sum((part.astype(jnp.float32) for part in landed), totals[0][0]).astype(jnp.bfloat16)
+    return sum(part.astype(jnp.float32) for part in [totals[0][0], *landed]).astype(jnp.bfloat16)
 
 
 def solution(mesh):

time: 246 us -> 238 us (0.967)
  Pallas kernels: 136 us -> 131 us
  waiting for transfers between devices: 67.6 us -> 63.9 us
    pallas_call x15 -> x16, Pallas kernels: 136 us -> 131 us  [run(): pl.pallas_call(kernel, out_shape=outs, in_specs=[SMEM] + [ANY] * len(oper...]
    ppermute x33, waiting for transfers between devices: 66.9 us -> 63.2 us  [swap(): return lax.ppermute(value, axis, [(i, i ^ mask) for i in range(size)])]
  transfers between devices with their start and end apart: 34 -> 34, of which waited for: 17 -> 15; matrix products, arithmetic and copies ran while one was open for 1% -> 1% of each run, Pallas kernels for 50% -> 49%
where the time goes in v6:
time: 238 us
  Pallas kernels  131 us (55%)
  waiting for transfers between devices  63.9 us (27%)
  starting transfers between devices  23.7 us (10%)
  between operations  13.6 us (6%)
  other arithmetic  4.95 us (2%)
    pallas_call x16, Pallas kernels, run(): pl.pallas_call(kernel, out_shape=outs, in_specs=[SMEM] + [ANY] * len(oper...  131 us
    ppermute x33, waiting for transfers between devices, swap(): return lax.ppermute(value, axis, [(i, i ^ mask) for i in range(size)])  63.2 us
    ppermute x33, starting transfers between devices, swap(): return lax.ppermute(value, axis, [(i, i ^ mask) for i in range(size)])  23.7 us
  transfers between devices with their start and end apart: 34, of which 15 were waited for; matrix products, arithmetic and copies ran while one was open for 1% of the time, Pallas kernels for 49%

profile of v6, /device:TPU:0, one launch (start us, length us, event | category | flops | bytes accessed | tf_op | source)
XLA Modules:
  0.0 237.5 jit_solution(18280664809316314024)
XLA Ops:
  7.9 7.8 %step_gg.3 = (bf16[2,128,1024]{2,1,0:T(8,128)(2,1)}, bf16[2,128,896]{2,1,0:T(8,128)(2,1)}) custom-call(s32[9]{0:T(128)} %pad_add_fusion.table_ref, bf16[2048,6656]{1,0:T(8,128)(2,1)} %args_0_.34, bf16[2048,6656]{1,0:T(8,128)(2,1)} %args_1_.34, bf16[6656,2048]{1,0:T(8,128)(2,1)} %args_2_.34, bf16[128,2048]{1,0:T(8,128)(2,1)} %args_3_.14), custom_call_target="tpu_custom_call" | custom-call | flops 1000 | bytes 1000 | tf_op jit(solution)/shard_map/step_gg/pallas_call | solution.py:351
  16.2 7.6 %step_gg.4 = (bf16[2,128,768]{2,1,0:T(8,128)(2,1)}, bf16[2,128,768]{2,1,0:T(8,128)(2,1)}) custom-call(s32[9]{0:T(128)} %pad_add_fusion.table_ref, bf16[2048,6656]{1,0:T(8,128)(2,1)} %args_0_.34, bf16[2048,6656]{1,0:T(8,128)(2,1)} %args_1_.34, bf16[6656,2048]{1,0:T(8,128)(2,1)} %args_2_.34, bf16[128,2048]{1,0:T(8,128)(2,1)} %args_3_.14, ...), custom_call_target="tpu_custom_call" | custom-call | flops 1000 | bytes 1000 | tf_op jit(solution)/shard_map/step_gg/pallas_call | solution.py:351
  23.9 5.5 %step_g.10 = (bf16[2,128,1024]{2,1,0:T(8,128)(2,1)}, f32[128,128]{1,0:T(8,128)}) custom-call(s32[9]{0:T(128)} %pad_add_fusion.table_ref, bf16[2048,6656]{1,0:T(8,128)(2,1)} %args_0_.34, bf16[2048,6656]{1,0:T(8,128)(2,1)} %args_1_.34, bf16[6656,2048]{1,0:T(8,128)(2,1)} %args_2_.34, bf16[128,2048]{1,0:T(8,128)(2,1)} %args_3_.14, ...), custom_call_target="tpu_custom_call" | custom-call | flops 1000 | bytes 1000 | tf_op jit(solution)/shard_map/step_g/pallas_call | solution.py:351
  29.4 2.9 %collective-permute-start.2 = (bf16[2,128,1024]{2,1,0:T(8,128)(2,1)}, bf16[2,128,1024]{2,1,0:T(8,128)(2,1)}, u32[]{:S(2)}, u32[]{:S(2)}) collective-permute-start(bf16[2,128,1024]{2,1,0:T(8,128)(2,1)} %get-tuple-element.40.args_5_), channel_id=1, source_target_pairs={{0,8},{4,12},{8,0},{12,4},{1,9},{5,13},{9,1},{13,5},{2,10},{6,14},... | collective-permute-start | bytes 1572872 | tf_op jit(solution)/shard_map/ppermute | solution.py:21
  32.9 5.1 %step_g.11.args_7_ = bf16[2,128,768]{2,1,0:T(8,128)(2,1)} custom-call(s32[9]{0:T(128)} %pad_add_fusion.table_ref, bf16[2048,6656]{1,0:T(8,128)(2,1)} %args_0_.34, bf16[2048,6656]{1,0:T(8,128)(2,1)} %args_1_.34, bf16[6656,2048]{1,0:T(8,128)(2,1)} %args_2_.34, bf16[128,2048]{1,0:T(8,128)(2,1)} %args_3_.14, ...), custom_call_target="tpu_custom_call" | custom-call | flops 1000 | bytes 1000 | tf_op jit(solution)/shard_map/step_g/pallas_call | solution.py:351
  38.1 7.3 %collective-permute-done.2.args_5_.args_7_ = bf16[2,128,1024]{2,1,0:T(8,128)(2,1)} collective-permute-done((bf16[2,128,1024]{2,1,0:T(8,128)(2,1)}, bf16[2,128,1024]{2,1,0:T(8,128)(2,1)}, u32[]{:S(2)}, u32[]{:S(2)}) %collective-permute-start.2) | collective-permute-done | bytes 524320 | tf_op jit(solution)/shard_map/ppermute | solution.py:21
  45.4 5.6 %step_g.12.args_8_.args_3_ = bf16[128,896]{1,0:T(8,128)(2,1)} custom-call(s32[9]{0:T(128)} %pad_add_fusion.table_ref, bf16[2048,6656]{1,0:T(8,128)(2,1)} %args_0_.34, bf16[2048,6656]{1,0:T(8,128)(2,1)} %args_1_.34, bf16[6656,2048]{1,0:T(8,128)(2,1)} %args_2_.34, bf16[128,2048]{1,0:T(8,128)(2,1)} %args_3_.14, ...), custom_call_target="tpu_custom_call" | custom-call | flops 1000 | bytes 1000 | tf_op jit(solution)/shard_map/step_g/pallas_call | solution.py:351
  53.5 5.2 %step_g.13.args_4_.args_7_ = bf16[128,768]{1,0:T(8,128)(2,1)} custom-call(s32[9]{0:T(128)} %pad_add_fusion.table_ref, bf16[2048,6656]{1,0:T(8,128)(2,1)} %args_0_.34, bf16[2048,6656]{1,0:T(8,128)(2,1)} %args_1_.34, bf16[6656,2048]{1,0:T(8,128)(2,1)} %args_2_.34, bf16[128,2048]{1,0:T(8,128)(2,1)} %args_3_.14, ...), custom_call_target="tpu_custom_call" | custom-call | flops 1000 | bytes 1000 | tf_op jit(solution)/shard_map/step_g/pallas_call | solution.py:351
  60.8 4.3 %collective-permute-done.10.args_9_ = bf16[128,768]{1,0:T(8,128)(2,1)} collective-permute-done((bf16[128,768]{1,0:T(8,128)(2,1)}, bf16[128,768]{1,0:T(8,128)(2,1)}, u32[]{:S(2)}, u32[]{:S(2)}) %collective-permute-start.10) | collective-permute-done | bytes 196640 | tf_op jit(solution)/shard_map/ppermute | solution.py:21
  65.2 13.2 %step_gggg.1 = (bf16[2,256,1024]{2,1,0:T(8,128)(2,1)}, bf16[2,256,896]{2,1,0:T(8,128)(2,1)}, bf16[2,256,768]{2,1,0:T(8,128)(2,1)}, bf16[2,256,768]{2,1,0:T(8,128)(2,1)}) custom-call(s32[9]{0:T(128)} %pad_add_fusion.table_ref, bf16[2048,6656]{1,0:T(8,128)(2,1)} %args_0_.34, bf16[2048,6656]{1,0:T(8,128)(2,1)} %args_1_.34, bf16[6656,2048]{1,0:T(8,128)(2,1)} %args_2_.34, ...), custom_call_target="tpu_custom_call" | custom-call | flops 1000 | bytes 1000 | tf_op jit(solution)/shard_map/step_gggg/pallas_call | solution.py:351
  81.4 6.3 %step_g.14 = (bf16[2,256,1024]{2,1,0:T(8,128)(2,1)}, f32[256,128]{1,0:T(8,128)}) custom-call(s32[9]{0:T(128)} %pad_add_fusion.table_ref, bf16[2048,6656]{1,0:T(8,128)(2,1)} %args_0_.34, bf16[2048,6656]{1,0:T(8,128)(2,1)} %args_1_.34, bf16[6656,2048]{1,0:T(8,128)(2,1)} %args_2_.34, bf16[512,2048]{1,0:T(8,128)(2,1)} %all-gather.2.cloned.1.call-done.args_3_, ...), custom_call_target="tpu_custom_call" | custom-call | flops 1000 | bytes 1000 | tf_op jit(solution)/shard_map/step_g/pallas_call | solution.py:351
  89.5 5.8 %step_g.15.args_4_ = bf16[2,256,768]{2,1,0:T(8,128)(2,1)} custom-call(s32[9]{0:T(128)} %pad_add_fusion.table_ref, bf16[2048,6656]{1,0:T(8,128)(2,1)} %args_0_.34, bf16[2048,6656]{1,0:T(8,128)(2,1)} %args_1_.34, bf16[6656,2048]{1,0:T(8,128)(2,1)} %args_2_.34, bf16[512,2048]{1,0:T(8,128)(2,1)} %all-gather.2.cloned.1.call-done.args_3_, ...), custom_call_target="tpu_custom_call" | custom-call | flops 1000 | bytes 1000 | tf_op jit(solution)/shard_map/step_g/pallas_call | solution.py:351
  95.2 12.1 %step_gg.5 = (bf16[2,128,1792]{2,1,0:T(8,128)(2,1)}, bf16[2,128,1664]{2,1,0:T(8,128)(2,1)}) custom-call(s32[9]{0:T(128)} %pad_add_fusion.table_ref, bf16[2048,6656]{1,0:T(8,128)(2,1)} %args_0_.34, bf16[2048,6656]{1,0:T(8,128)(2,1)} %args_1_.34, bf16[6656,2048]{1,0:T(8,128)(2,1)} %args_2_.34, bf16[512,2048]{1,0:T(8,128)(2,1)} %all-gather.2.cloned.1.call-done.args_3_, ...), custom_call_target="tpu_custom_call" | custom-call | flops 1000 | bytes 1000 | tf_op jit(solution)/shard_map/step_gg/pallas_call | solution.py:351
  108.4 5.8 %collective-permute-done.18.args_5_.args_7_ = bf16[2,256,1024]{2,1,0:T(8,128)(2,1)} collective-permute-done((bf16[2,256,1024]{2,1,0:T(8,128)(2,1)}, bf16[2,256,1024]{2,1,0:T(8,128)(2,1)}, u32[]{:S(2)}, u32[]{:S(2)}) %collective-permute-start.18) | collective-permute-done | bytes 1048608 | tf_op jit(solution)/shard_map/ppermute | solution.py:21
  114.1 6.8 %step_g.16.args_8_.args_3_ = bf16[256,896]{1,0:T(8,128)(2,1)} custom-call(s32[9]{0:T(128)} %pad_add_fusion.table_ref, bf16[2048,6656]{1,0:T(8,128)(2,1)} %args_0_.34, bf16[2048,6656]{1,0:T(8,128)(2,1)} %args_1_.34, bf16[6656,2048]{1,0:T(8,128)(2,1)} %args_2_.34, bf16[512,2048]{1,0:T(8,128)(2,1)} %all-gather.2.cloned.1.call-done.args_3_, ...), custom_call_target="tpu_custom_call" | custom-call | flops 1000 | bytes 1000 | tf_op jit(solution)/shard_map/step_g/pallas_call | solution.py:351
  122.7 8.3 %collective-permute-done.17.args_5_ = bf16[2,256,768]{2,1,0:T(8,128)(2,1)} collective-permute-done((bf16[2,256,768]{2,1,0:T(8,128)(2,1)}, bf16[2,256,768]{2,1,0:T(8,128)(2,1)}, u32[]{:S(2)}, u32[]{:S(2)}) %collective-permute-start.17) | collective-permute-done | bytes 786464 | tf_op jit(solution)/shard_map/ppermute | solution.py:21
  131.0 6.3 %step_g.17.args_5_.args_7_ = bf16[256,768]{1,0:T(8,128)(2,1)} custom-call(s32[9]{0:T(128)} %pad_add_fusion.table_ref, bf16[2048,6656]{1,0:T(8,128)(2,1)} %args_0_.34, bf16[2048,6656]{1,0:T(8,128)(2,1)} %args_1_.34, bf16[6656,2048]{1,0:T(8,128)(2,1)} %args_2_.34, bf16[512,2048]{1,0:T(8,128)(2,1)} %all-gather.2.cloned.1.call-done.args_3_, ...), custom_call_target="tpu_custom_call" | custom-call | flops 1000 | bytes 1000 | tf_op jit(solution)/shard_map/step_g/pallas_call | solution.py:351
  139.0 7.7 %step_g.18 = (bf16[2,128,1792]{2,1,0:T(8,128)(2,1)}, f32[128,128]{1,0:T(8,128)}) custom-call(s32[9]{0:T(128)} %pad_add_fusion.table_ref, bf16[2048,6656]{1,0:T(8,128)(2,1)} %args_0_.34, bf16[2048,6656]{1,0:T(8,128)(2,1)} %args_1_.34, bf16[6656,2048]{1,0:T(8,128)(2,1)} %args_2_.34, bf16[512,2048]{1,0:T(8,128)(2,1)} %all-gather.2.cloned.1.call-done.args_3_, ...), custom_call_target="tpu_custom_call" | custom-call | flops 1000 | bytes 1000 | tf_op jit(solution)/shard_map/step_g/pallas_call | solution.py:351
  152.3 13.8 %step_d.2 = (bf16[128,2048]{1,0:T(8,128)(2,1)}, bf16[128,2048]{1,0:T(8,128)(2,1)}) custom-call(s32[9]{0:T(128)} %pad_add_fusion.table_ref, bf16[2048,6656]{1,0:T(8,128)(2,1)} %args_0_.34, bf16[2048,6656]{1,0:T(8,128)(2,1)} %args_1_.34, bf16[6656,2048]{1,0:T(8,128)(2,1)} %args_2_.34, bf16[256,896]{1,0:T(8,128)(2,1)} %step_g.16.args_8_.args_3_, ...), custom_call_target="tpu_custom_call" | custom-call | flops 1000 | bytes 1000 | tf_op jit(solution)/shard_map/step_d/pallas_call | solution.py:351
  168.1 7.9 %step_g.19.args_11_.args_15_ = bf16[128,1664]{1,0:T(8,128)(2,1)} custom-call(s32[9]{0:T(128)} %pad_add_fusion.table_ref, bf16[2048,6656]{1,0:T(8,128)(2,1)} %args_0_.34, bf16[2048,6656]{1,0:T(8,128)(2,1)} %args_1_.34, bf16[6656,2048]{1,0:T(8,128)(2,1)} %args_2_.34, bf16[512,2048]{1,0:T(8,128)(2,1)} %all-gather.2.cloned.1.call-done.args_3_, ...), custom_call_target="tpu_custom_call" | custom-call | flops 1000 | bytes 1000 | tf_op jit(solution)/shard_map/step_g/pallas_call | solution.py:351
  180.4 7.2 %collective-permute-done.28.args_13_ = bf16[128,1664]{1,0:T(8,128)(2,1)S(1)} collective-permute-done((bf16[128,1664]{1,0:T(8,128)(2,1)}, bf16[128,1664]{1,0:T(8,128)(2,1)S(1)}, u32[]{:S(2)}, u32[]{:S(2)}) %collective-permute-start.28) | collective-permute-done | bytes 426016 | tf_op jit(solution)/shard_map/ppermute | solution.py:21
  193.2 13.9 %step_d.3 = (bf16[128,2048]{1,0:T(8,128)(2,1)}, bf16[128,2048]{1,0:T(8,128)(2,1)}) custom-call(s32[9]{0:T(128)} %pad_add_fusion.table_ref, bf16[2048,6656]{1,0:T(8,128)(2,1)} %args_0_.34, bf16[2048,6656]{1,0:T(8,128)(2,1)} %args_1_.34, bf16[6656,2048]{1,0:T(8,128)(2,1)} %args_2_.34, bf16[128,896]{1,0:T(8,128)(2,1)} %step_g.12.args_8_.args_3_, ...), custom_call_target="tpu_custom_call" | custom-call | flops 1000 | bytes 1000 | tf_op jit(solution)/shard_map/step_d/pallas_call | solution.py:351
  207.8 9.6 %collective-permute-done.31 = bf16[128,2048]{1,0:T(8,128)(2,1)} collective-permute-done((bf16[128,2048]{1,0:T(8,128)(2,1)}, bf16[128,2048]{1,0:T(8,128)(2,1)}, u32[]{:S(2)}, u32[]{:S(2)}) %collective-permute-start.31) | collective-permute-done | bytes 524320 | tf_op jit(solution)/shard_map/ppermute | solution.py:21
  217.4 11.0 %collective-permute-done.32 = bf16[128,2048]{1,0:T(8,128)(2,1)S(1)} collective-permute-done((bf16[128,2048]{1,0:T(8,128)(2,1)}, bf16[128,2048]{1,0:T(8,128)(2,1)S(1)}, u32[]{:S(2)}, u32[]{:S(2)}) %collective-permute-start.32) | collective-permute-done | bytes 524320 | tf_op jit(solution)/shard_map/ppermute | solution.py:21
  (67 shorter events, 36.9 us)
Async XLA Ops:
  6.5 58.6 %all-gather.2.cloned.1.call-start = ((), (), s32[]{:S(2)}) async-start(), calls=%async_computation | async-start | bytes 2621440 | tf_op jit(solution)/shard_map/all_gather | solution.py:406
  23.8 9.1 %collective-permute-start.3 = (bf16[2,128,768]{2,1,0:T(8,128)(2,1)}, bf16[2,128,768]{2,1,0:T(8,128)(2,1)}, u32[]{:S(2)}, u32[]{:S(2)}) collective-permute-start(bf16[2,128,768]{2,1,0:T(8,128)(2,1)} %get-tuple-element.39.args_5_), channel_id=1, source_target_pairs={{0,4},{4,0},{8,12},{12,8},{1,5},{5,1},{9,13},{13,9},{2,6},{6,2},{1... | collective-permute-start | bytes 1179656 | tf_op jit(solution)/shard_map/ppermute | solution.py:21
  29.4 16.0 %collective-permute-start.2 = (bf16[2,128,1024]{2,1,0:T(8,128)(2,1)}, bf16[2,128,1024]{2,1,0:T(8,128)(2,1)}, u32[]{:S(2)}, u32[]{:S(2)}) collective-permute-start(bf16[2,128,1024]{2,1,0:T(8,128)(2,1)} %get-tuple-element.40.args_5_), channel_id=1, source_target_pairs={{0,8},{4,12},{8,0},{12,4},{1,9},{5,13},{9,1},{13,5},{2,10},{6,14},... | collective-permute-start | bytes 1572872 | tf_op jit(solution)/shard_map/ppermute | solution.py:21
  32.4 20.8 %collective-permute-start.6 = (bf16[2,128,768]{2,1,0:T(8,128)(2,1)}, bf16[2,128,768]{2,1,0:T(8,128)(2,1)}, u32[]{:S(2)}, u32[]{:S(2)}) collective-permute-start(bf16[2,128,768]{2,1,0:T(8,128)(2,1)} %get-tuple-element.42), channel_id=1, source_target_pairs={{0,4},{4,0},{8,12},{12,8},{1,5},{5,1},{9,13},{13,9},{2,6},{6,2},{1... | collective-permute-start | bytes 1179656 | tf_op jit(solution)/shard_map/ppermute | solution.py:21
  38.0 15.5 %collective-permute-start.7 = (bf16[2,128,768]{2,1,0:T(8,128)(2,1)}, bf16[2,128,768]{2,1,0:T(8,128)(2,1)}, u32[]{:S(2)}, u32[]{:S(2)}) collective-permute-start(bf16[2,128,768]{2,1,0:T(8,128)(2,1)} %step_g.11.args_7_), channel_id=1, source_target_pairs={{0,8},{4,12},{8,0},{12,4},{1,9},{5,13},{9,1},{13,5},{2,10},{6,14},... | collective-permute-start | bytes 1179656 | tf_op jit(solution)/shard_map/ppermute | solution.py:21
  51.1 9.8 %collective-permute-start.5 = (bf16[128,896]{1,0:T(8,128)(2,1)}, bf16[128,896]{1,0:T(8,128)(2,1)}, u32[]{:S(2)}, u32[]{:S(2)}) collective-permute-start(bf16[128,896]{1,0:T(8,128)(2,1)} %step_g.12.args_8_.args_3_), channel_id=1, source_target_pairs={{0,8},{4,12},{8,0},{12,4},{1,9},{5,13},{9,1},{13,5},{2,10},{6,14},... | collective-permute-start | bytes 688136 | tf_op jit(solution)/shard_map/ppermute | solution.py:21
  78.5 11.0 %collective-permute-start.12 = (bf16[2,256,768]{2,1,0:T(8,128)(2,1)}, bf16[2,256,768]{2,1,0:T(8,128)(2,1)}, u32[]{:S(2)}, u32[]{:S(2)}) collective-permute-start(bf16[2,256,768]{2,1,0:T(8,128)(2,1)} %get-tuple-element.47), channel_id=1, source_target_pairs={{0,4},{4,0},{8,12},{12,8},{1,5},{5,1},{9,13},{13,9},{2,6},{6,2},{1... | collective-permute-start | bytes 2359304 | tf_op jit(solution)/shard_map/ppermute | solution.py:21
  87.8 26.4 %collective-permute-start.18 = (bf16[2,256,1024]{2,1,0:T(8,128)(2,1)}, bf16[2,256,1024]{2,1,0:T(8,128)(2,1)}, u32[]{:S(2)}, u32[]{:S(2)}) collective-permute-start(bf16[2,256,1024]{2,1,0:T(8,128)(2,1)} %get-tuple-element.49.args_5_), channel_id=1, source_target_pairs={{0,8},{4,12},{8,0},{12,4},{1,9},{5,13},{9,1},{13,5},{2,10},{6,14},... | collective-permute-start | bytes 3145736 | tf_op jit(solution)/shard_map/ppermute | solution.py:21
  89.5 18.9 %collective-permute-start.19 = (bf16[2,256,896]{2,1,0:T(8,128)(2,1)}, bf16[2,256,896]{2,1,0:T(8,128)(2,1)}, u32[]{:S(2)}, u32[]{:S(2)}) collective-permute-start(bf16[2,256,896]{2,1,0:T(8,128)(2,1)} %get-tuple-element.54), channel_id=1, source_target_pairs={{0,4},{4,0},{8,12},{12,8},{1,5},{5,1},{9,13},{13,9},{2,6},{6,2},{1... | collective-permute-start | bytes 2752520 | tf_op jit(solution)/shard_map/ppermute | solution.py:21
  107.3 31.7 %collective-permute-start.15 = (bf16[2,128,1792]{2,1,0:T(8,128)(2,1)}, bf16[2,128,1792]{2,1,0:T(8,128)(2,1)}, u32[]{:S(2)}, u32[]{:S(2)}) collective-permute-start(bf16[2,128,1792]{2,1,0:T(8,128)(2,1)} %get-tuple-element.51.args_7_), channel_id=1, source_target_pairs={{0,4},{4,0},{8,12},{12,8},{1,5},{5,1},{9,13},{13,9},{2,6},{6,2},{1... | collective-permute-start | bytes 2752520 | tf_op jit(solution)/shard_map/ppermute | solution.py:21
  107.9 14.8 %collective-permute-start.16 = (bf16[2,256,768]{2,1,0:T(8,128)(2,1)}, bf16[2,256,768]{2,1,0:T(8,128)(2,1)}, u32[]{:S(2)}, u32[]{:S(2)}) collective-permute-start(bf16[2,256,768]{2,1,0:T(8,128)(2,1)} %get-tuple-element.52), channel_id=1, source_target_pairs={{0,4},{4,0},{8,12},{12,8},{1,5},{5,1},{9,13},{13,9},{2,6},{6,2},{1... | collective-permute-start | bytes 2359304 | tf_op jit(solution)/shard_map/ppermute | solution.py:21
  108.0 23.0 %collective-permute-start.17 = (bf16[2,256,768]{2,1,0:T(8,128)(2,1)}, bf16[2,256,768]{2,1,0:T(8,128)(2,1)}, u32[]{:S(2)}, u32[]{:S(2)}) collective-permute-start(bf16[2,256,768]{2,1,0:T(8,128)(2,1)} %step_g.15.args_4_), channel_id=1, source_target_pairs={{0,8},{4,12},{8,0},{12,4},{1,9},{5,13},{9,1},{13,5},{2,10},{6,14},... | collective-permute-start | bytes 2359304 | tf_op jit(solution)/shard_map/ppermute | solution.py:21
  121.0 26.7 %collective-permute-start.22 = (bf16[256,896]{1,0:T(8,128)(2,1)}, bf16[256,896]{1,0:T(8,128)(2,1)}, u32[]{:S(2)}, u32[]{:S(2)}) collective-permute-start(bf16[256,896]{1,0:T(8,128)(2,1)} %step_g.16.args_8_.args_3_), channel_id=1, source_target_pairs={{0,8},{4,12},{8,0},{12,4},{1,9},{5,13},{9,1},{13,5},{2,10},{6,14},... | collective-permute-start | bytes 1376264 | tf_op jit(solution)/shard_map/ppermute | solution.py:21
  137.3 11.7 %collective-permute-start.25 = (bf16[256,768]{1,0:T(8,128)(2,1)}, bf16[256,768]{1,0:T(8,128)(2,1)}, u32[]{:S(2)}, u32[]{:S(2)}) collective-permute-start(bf16[256,768]{1,0:T(8,128)(2,1)} %step_g.17.args_5_.args_7_), channel_id=1, source_target_pairs={{0,8},{4,12},{8,0},{12,4},{1,9},{5,13},{9,1},{13,5},{2,10},{6,14},... | collective-permute-start | bytes 1179656 | tf_op jit(solution)/shard_map/ppermute | solution.py:21
  146.7 21.4 %collective-permute-start.20 = (bf16[2,128,1792]{2,1,0:T(8,128)(2,1)}, bf16[2,128,1792]{2,1,0:T(8,128)(2,1)}, u32[]{:S(2)}, u32[]{:S(2)}) collective-permute-start(bf16[2,128,1792]{2,1,0:T(8,128)(2,1)} %get-tuple-element.60.args_11_), channel_id=1, source_target_pairs={{0,8},{4,12},{8,0},{12,4},{1,9},{5,13},{9,1},{13,5},{2,10},{6,14},... | collective-permute-start | bytes 2752520 | tf_op jit(solution)/shard_map/ppermute | solution.py:21
  147.1 20.7 %collective-permute-start.14 = (bf16[2,128,1664]{2,1,0:T(8,128)(2,1)}, bf16[2,128,1664]{2,1,0:T(8,128)(2,1)}, u32[]{:S(2)}, u32[]{:S(2)}) collective-permute-start(bf16[2,128,1664]{2,1,0:T(8,128)(2,1)} %get-tuple-element.50), channel_id=1, source_target_pairs={{0,4},{4,0},{8,12},{12,8},{1,5},{5,1},{9,13},{13,9},{2,6},{6,2},{1... | collective-permute-start | bytes 2555912 | tf_op jit(solution)/shard_map/ppermute | solution.py:21
  166.1 14.3 %collective-permute-start.29 = (bf16[128,2048]{1,0:T(8,128)(2,1)}, bf16[128,2048]{1,0:T(8,128)(2,1)}, u32[]{:S(2)}, u32[]{:S(2)}) collective-permute-start(bf16[128,2048]{1,0:T(8,128)(2,1)} %get-tuple-element.62), channel_id=1, source_target_pairs={{0,1},{1,0},{2,3},{3,2},{4,5},{5,4},{6,7},{7,6},{8,9},{9,8},{10,11... | collective-permute-start | bytes 1572872 | tf_op jit(solution)/shard_map/ppermute | solution.py:21
  176.0 11.6 %collective-permute-start.28 = (bf16[128,1664]{1,0:T(8,128)(2,1)}, bf16[128,1664]{1,0:T(8,128)(2,1)S(1)}, u32[]{:S(2)}, u32[]{:S(2)}) collective-permute-start(bf16[128,1664]{1,0:T(8,128)(2,1)} %step_g.19.args_11_.args_15_), channel_id=1, source_target_pairs={{0,8},{4,12},{8,0},{12,4},{1,9},{5,13},{9,1},{13,5},{2,10},{6,14},... | collective-permute-start | bytes 1277960 | tf_op jit(solution)/shard_map/ppermute | solution.py:21
  177.7 9.9 %collective-permute-start.9 = (bf16[128,768]{1,0:T(8,128)(2,1)}, bf16[128,768]{1,0:T(8,128)(2,1)}, u32[]{:S(2)}, u32[]{:S(2)}) collective-permute-start(bf16[128,768]{1,0:T(8,128)(2,1)} %step_g.13.args_4_.args_7_), channel_id=1, source_target_pairs={{0,4},{4,0},{8,12},{12,8},{1,5},{5,1},{9,13},{13,9},{2,6},{6,2},{1... | collective-permute-start | bytes 589832 | tf_op jit(solution)/shard_map/ppermute | solution.py:21
  177.7 12.8 %collective-permute-start.4 = (bf16[128,896]{1,0:T(8,128)(2,1)}, bf16[128,896]{1,0:T(8,128)(2,1)}, u32[]{:S(2)}, u32[]{:S(2)}) collective-permute-start(bf16[128,896]{1,0:T(8,128)(2,1)} %step_g.12.args_8_.args_3_), channel_id=1, source_target_pairs={{0,4},{4,0},{8,12},{12,8},{1,5},{5,1},{9,13},{13,9},{2,6},{6,2},{1... | collective-permute-start | bytes 688136 | tf_op jit(solution)/shard_map/ppermute | solution.py:21
  178.3 14.9 %collective-permute-start.11 = (bf16[128,768]{1,0:T(8,128)(2,1)}, bf16[128,768]{1,0:T(8,128)(2,1)}, u32[]{:S(2)}, u32[]{:S(2)}) collective-permute-start(bf16[128,768]{1,0:T(8,128)(2,1)} %collective-permute-done.10.args_9_), channel_id=1, source_target_pairs={{0,4},{4,0},{8,12},{12,8},{1,5},{5,1},{9,13},{13,9},{2,6},{6,2},{1... | collective-permute-start | bytes 589832 | tf_op jit(solution)/shard_map/ppermute | solution.py:21
  180.4 12.7 %collective-permute-start.8 = (bf16[128,896]{1,0:T(8,128)(2,1)}, bf16[128,896]{1,0:T(8,128)(2,1)}, u32[]{:S(2)}, u32[]{:S(2)}) collective-permute-start(bf16[128,896]{1,0:T(8,128)(2,1)} %collective-permute-done.5.args_5_), channel_id=1, source_target_pairs={{0,4},{4,0},{8,12},{12,8},{1,5},{5,1},{9,13},{13,9},{2,6},{6,2},{1... | collective-permute-start | bytes 688136 | tf_op jit(solution)/shard_map/ppermute | solution.py:21
  190.5 26.9 %collective-permute-start.31 = (bf16[128,2048]{1,0:T(8,128)(2,1)}, bf16[128,2048]{1,0:T(8,128)(2,1)}, u32[]{:S(2)}, u32[]{:S(2)}) collective-permute-start(bf16[128,2048]{1,0:T(8,128)(2,1)} %add_convert_fusion.1), channel_id=1, source_target_pairs={{0,2},{1,3},{2,0},{3,1},{4,6},{5,7},{6,4},{7,5},{8,10},{9,11},{10,... | collective-permute-start | bytes 1572872 | tf_op jit(solution)/shard_map/ppermute | solution.py:21
  207.1 21.3 %collective-permute-start.32 = (bf16[128,2048]{1,0:T(8,128)(2,1)}, bf16[128,2048]{1,0:T(8,128)(2,1)S(1)}, u32[]{:S(2)}, u32[]{:S(2)}) collective-permute-start(bf16[128,2048]{1,0:T(8,128)(2,1)} %get-tuple-element.68), channel_id=1, source_target_pairs={{0,1},{1,0},{2,3},{3,2},{4,5},{5,4},{6,7},{7,6},{8,9},{9,8},{10,11... | collective-permute-start | bytes 1572872 | tf_op jit(solution)/shard_map/ppermute | solution.py:21
  (11 other events, 46.6 us)
Sparse Core Ops, SparseCore 0:
  8.9 48.6 all-gather.1

commit v7 on v6

--- a/solution.py
+++ b/solution.py
@@ -27,11 +27,11 @@
 
 
 class Group:
-    def __init__(self, toks, block):
-        self.toks, self.block, self.rows = toks, block, block * len(toks)
-
-    def plain(self, table):
-        return jnp.concatenate([lax.dynamic_slice_in_dim(t, table[i], self.block, 0) for t, i in self.toks], axis=0)
+    def __init__(self, blocks, names, block):
+        self.blocks, self.names, self.block, self.rows = blocks, names, block, block * len(names)
+
+    def arrays(self):
+        return [self.blocks[name] for name in self.names]
 
 
 class GateUp:
@@ -50,7 +50,7 @@
         return [*self.recvs, *([self.squares[0], *self.squares[1]] if self.squares else [])]
 
     def plain(self, table, gate_matrix, up_matrix, down_matrix):
-        tok, n = self.group.plain(table), self.width
+        tok, n = jnp.concatenate(self.group.arrays(), axis=0), self.width
         gate, up = (
             jnp.dot(
                 tok, lax.dynamic_slice_in_dim(m, table[self.place] + self.low, n, 1), preferred_element_type=jnp.float32
@@ -305,7 +305,7 @@
     for p in phases:
         if p.group is not None and all(p.group is not g for g in groups):
             groups.append(p.group)
-    tok_places = [[index(t) for t, _ in g.toks] for g in groups]
+    tok_places = [[index(t) for t in g.arrays()] for g in groups]
     where = [[index(a) for a in p.arrays()] for p in phases]
     index(dep)
     outs = [o for p in phases for o in p.outs]
@@ -321,12 +321,8 @@
             xbuf, xsem = args.pop(0), args.pop(0)
             refs["x"][id(g)] = xbuf
             ready[id(g)] = [
-                pltpu.make_async_copy(
-                    arrays[place].at[pl.ds(pl.multiple_of(table_ref[i], 16), g.block)],
-                    xbuf.at[pl.ds(j * g.block, g.block)],
-                    xsem.at[j],
-                )
-                for j, (place, (_, i)) in enumerate(zip(places, g.toks))
+                pltpu.make_async_copy(arrays[place], xbuf.at[pl.ds(j * g.block, g.block)], xsem.at[j])
+                for j, place in enumerate(places)
             ]
         bound = []
         for p, places, buffers in zip(phases, where, scratch):
@@ -357,7 +353,7 @@
                 *[
                     buffer
                     for g in groups
-                    for buffer in (pltpu.VMEM((g.rows, depth), jnp.bfloat16), pltpu.SemaphoreType.DMA((len(g.toks),)))
+                    for buffer in (pltpu.VMEM((g.rows, depth), jnp.bfloat16), pltpu.SemaphoreType.DMA((len(g.names),)))
                 ],
                 *[buffer for buffers in scratch for buffer in buffers],
             ],
@@ -375,11 +371,11 @@
     ("x0",),
     ("x1",),
     ("h0",),
-    ("h1",),
+    ("t", "h1"),
     ("r0", "r1", "s2", "s3"),
     ("x2",),
     ("x3",),
-    ("s4",),
+    ("b", "s4"),
     ("h2",),
     ("h3",),
     ("x4",),
@@ -403,16 +399,12 @@
     def core(value):
         return swap(value, "gx", n_gx, 1)
 
-    gathered = lax.all_gather(tokens, "gy", axis=0, tiled=True)
     table = jnp.concatenate(
-        [
-            (lax.axis_index("gx") ^ jnp.arange(n_gx, dtype=jnp.int32)) * width,
-            (lax.axis_index("gy") ^ jnp.arange(n_gy, dtype=jnp.int32)) * block,
-            jnp.zeros((1,), jnp.int32),
-        ]
+        [(lax.axis_index("gx") ^ jnp.arange(n_gx, dtype=jnp.int32)) * width, jnp.zeros((1,), jnp.int32)]
     )
+    blocks = {0: tokens}
     sets = [[0], list(range(2, n_gy)), [1]]
-    groups = [Group([(gathered, n_gx + j) if j else (tokens, n_gx + n_gy) for j in js], block) for js in sets]
+    groups = [Group(blocks, js, block) for js in sets]
     squares = {}
     half = cut(width, 7, 13)
     jobs = [(0, 0, half), (0, half, width - half), (1, 0, half), (1, half, width - half), (2, 0, width)]
@@ -476,7 +468,15 @@
                 parts[j ^ mask] = (parts[j ^ mask].astype(jnp.float32) + arrived).astype(jnp.bfloat16)
             mask *= 2
 
+    def gather_over_gy(mask):
+        got = [j for j in blocks if j]
+        blocks.update(zip(got, tied([blocks[j] for j in got])))
+        for j in list(blocks) if mask > 1 else got:
+            blocks[j ^ mask] = swap(blocks[j], "gy", n_gy, mask)
+
     landed = []
+    mask = n_gy // 2
+    gather_over_gy(mask)
     for names in STEPS:
         items = []
         for name in names:
@@ -484,8 +484,14 @@
             if kind == "r":
                 forward(job)
                 continue
+            while kind == "t" and mask > 1:
+                mask //= 2
+                gather_over_gy(mask)
+            if kind == "b":
+                blocks[1] = tied(swap(tokens, "gy", n_gy, 1))
             if kind == "z":
                 reduce_over_gy()
+            if kind in "tbz":
                 continue
             if kind == "d":
                 items.append((kind, [int(g) for g in name[1:]], [down([int(g) for g in name[1:]])]))
@@ -501,7 +507,8 @@
             for g in job:
                 totals[g] = [outs[0].pop(0) for _ in sets[g]]
 
-    landed.append(swap(totals[2][0], "gy", n_gy, 1))
+    landed, last = lax.optimization_barrier((landed, totals[2][0]))
+    landed.append(swap(last, "gy", n_gy, 1))
     return sum(part.astype(jnp.float32) for part in [totals[0][0], *landed]).astype(jnp.bfloat16)
 
 

time: 238 us -> 223 us (0.937)
  between operations: 13.6 us -> 0.22 us
  waiting for transfers between devices: 63.9 us -> 60.6 us
    ppermute x33 -> x36, waiting for transfers between devices: 63.2 us -> 60.6 us  [swap(): return lax.ppermute(value, axis, [(i, i ^ mask) for i in range(size)])]
    ppermute x33 -> x36, starting transfers between devices: 23.7 us -> 25.8 us  [swap(): return lax.ppermute(value, axis, [(i, i ^ mask) for i in range(size)])]
  transfers between devices with their start and end apart: 34 -> 36, of which waited for: 15 -> 15; matrix products, arithmetic and copies ran while one was open for 1% -> 1% of each run, Pallas kernels for 49% -> 47%
where the time goes in v7:
time: 223 us; the launch traced here: 222 us
  Pallas kernels  130 us (58%)
  waiting for transfers between devices  60.6 us (27%)
  starting transfers between devices  25.8 us (12%)
  other arithmetic  4.95 us (2%)
    pallas_call x16, Pallas kernels, run(): pl.pallas_call(kernel, out_shape=outs, in_specs=[SMEM] + [ANY] * len(oper...  130 us
    ppermute x36, waiting for transfers between devices, swap(): return lax.ppermute(value, axis, [(i, i ^ mask) for i in range(size)])  60.6 us
    ppermute x36, starting transfers between devices, swap(): return lax.ppermute(value, axis, [(i, i ^ mask) for i in range(size)])  25.8 us
  transfers between devices with their start and end apart: 36, of which 15 were waited for; matrix products, arithmetic and copies ran while one was open for 1% of the time, Pallas kernels for 47%

profile of v7, /device:TPU:0, one launch (start us, length us, event | category | flops | bytes accessed | tf_op | source)
XLA Modules:
  0.0 222.4 jit_solution(5003239625589293991)
XLA Ops:
  0.6 7.8 %step_gg.3 = (bf16[2,128,1024]{2,1,0:T(8,128)(2,1)}, bf16[2,128,896]{2,1,0:T(8,128)(2,1)}) custom-call(s32[5]{0:T(128)} %pad_add_fusion.table_ref, bf16[2048,6656]{1,0:T(8,128)(2,1)} %args_0_.34, bf16[2048,6656]{1,0:T(8,128)(2,1)} %args_1_.34, bf16[6656,2048]{1,0:T(8,128)(2,1)} %args_2_.34, bf16[128,2048]{1,0:T(8,128)(2,1)} %args_3_.14, ...), custom_call_target="tpu_custom_call" | custom-call | flops 1000 | bytes 1000 | tf_op jit(solution)/shard_map/step_gg/pallas_call | solution.py:347
  8.9 7.1 %step_gg.4 = (bf16[2,128,768]{2,1,0:T(8,128)(2,1)}, bf16[2,128,768]{2,1,0:T(8,128)(2,1)}) custom-call(s32[5]{0:T(128)} %pad_add_fusion.table_ref, bf16[2048,6656]{1,0:T(8,128)(2,1)} %args_0_.34, bf16[2048,6656]{1,0:T(8,128)(2,1)} %args_1_.34, bf16[6656,2048]{1,0:T(8,128)(2,1)} %args_2_.34, bf16[128,2048]{1,0:T(8,128)(2,1)} %args_3_.14, ...), custom_call_target="tpu_custom_call" | custom-call | flops 1000 | bytes 1000 | tf_op jit(solution)/shard_map/step_gg/pallas_call | solution.py:347
  16.0 5.5 %step_g.10 = (bf16[2,128,1024]{2,1,0:T(8,128)(2,1)}, f32[128,128]{1,0:T(8,128)}) custom-call(s32[5]{0:T(128)} %pad_add_fusion.table_ref, bf16[2048,6656]{1,0:T(8,128)(2,1)} %args_0_.34, bf16[2048,6656]{1,0:T(8,128)(2,1)} %args_1_.34, bf16[6656,2048]{1,0:T(8,128)(2,1)} %args_2_.34, bf16[128,2048]{1,0:T(8,128)(2,1)} %args_3_.14, ...), custom_call_target="tpu_custom_call" | custom-call | flops 1000 | bytes 1000 | tf_op jit(solution)/shard_map/step_g/pallas_call | solution.py:347
  28.7 5.1 %step_g.11.args_7_ = bf16[2,128,768]{2,1,0:T(8,128)(2,1)} custom-call(s32[5]{0:T(128)} %pad_add_fusion.table_ref, bf16[2048,6656]{1,0:T(8,128)(2,1)} %args_0_.34, bf16[2048,6656]{1,0:T(8,128)(2,1)} %args_1_.34, bf16[6656,2048]{1,0:T(8,128)(2,1)} %args_2_.34, bf16[128,2048]{1,0:T(8,128)(2,1)} %args_3_.14, ...), custom_call_target="tpu_custom_call" | custom-call | flops 1000 | bytes 1000 | tf_op jit(solution)/shard_map/step_g/pallas_call | solution.py:347
  37.1 5.6 %step_g.12.args_8_.args_3_ = bf16[128,896]{1,0:T(8,128)(2,1)} custom-call(s32[5]{0:T(128)} %pad_add_fusion.table_ref, bf16[2048,6656]{1,0:T(8,128)(2,1)} %args_0_.34, bf16[2048,6656]{1,0:T(8,128)(2,1)} %args_1_.34, bf16[6656,2048]{1,0:T(8,128)(2,1)} %args_2_.34, bf16[128,2048]{1,0:T(8,128)(2,1)} %args_3_.14, ...), custom_call_target="tpu_custom_call" | custom-call | flops 1000 | bytes 1000 | tf_op jit(solution)/shard_map/step_g/pallas_call | solution.py:347
  42.8 7.9 %collective-permute-done.8.args_3_ = bf16[128,2048]{1,0:T(8,128)(2,1)} collective-permute-done((bf16[128,2048]{1,0:T(8,128)(2,1)}, bf16[128,2048]{1,0:T(8,128)(2,1)}, u32[]{:S(2)}, u32[]{:S(2)}) %collective-permute-start.8) | collective-permute-done | bytes 524320 | tf_op jit(solution)/shard_map/ppermute | solution.py:21
  51.9 5.3 %step_g.13.args_5_.args_7_ = bf16[128,768]{1,0:T(8,128)(2,1)} custom-call(s32[5]{0:T(128)} %pad_add_fusion.table_ref, bf16[2048,6656]{1,0:T(8,128)(2,1)} %args_0_.34, bf16[2048,6656]{1,0:T(8,128)(2,1)} %args_1_.34, bf16[6656,2048]{1,0:T(8,128)(2,1)} %args_2_.34, bf16[128,2048]{1,0:T(8,128)(2,1)} %args_3_.14, ...), custom_call_target="tpu_custom_call" | custom-call | flops 1000 | bytes 1000 | tf_op jit(solution)/shard_map/step_g/pallas_call | solution.py:347
  59.0 4.9 %collective-permute-done.11.args_9_ = bf16[128,768]{1,0:T(8,128)(2,1)} collective-permute-done((bf16[128,768]{1,0:T(8,128)(2,1)}, bf16[128,768]{1,0:T(8,128)(2,1)}, u32[]{:S(2)}, u32[]{:S(2)}) %collective-permute-start.11) | collective-permute-done | bytes 196640 | tf_op jit(solution)/shard_map/ppermute | solution.py:21
  64.4 13.2 %step_gggg.1 = (bf16[2,256,1024]{2,1,0:T(8,128)(2,1)}, bf16[2,256,896]{2,1,0:T(8,128)(2,1)}, bf16[2,256,768]{2,1,0:T(8,128)(2,1)}, bf16[2,256,768]{2,1,0:T(8,128)(2,1)}) custom-call(s32[5]{0:T(128)} %pad_add_fusion.table_ref, bf16[2048,6656]{1,0:T(8,128)(2,1)} %args_0_.34, bf16[2048,6656]{1,0:T(8,128)(2,1)} %args_1_.34, bf16[6656,2048]{1,0:T(8,128)(2,1)} %args_2_.34, ...), custom_call_target="tpu_custom_call" | custom-call | flops 1000 | bytes 1000 | tf_op jit(solution)/shard_map/step_gggg/pallas_call | solution.py:347
  80.6 6.3 %step_g.14 = (bf16[2,256,1024]{2,1,0:T(8,128)(2,1)}, f32[256,128]{1,0:T(8,128)}) custom-call(s32[5]{0:T(128)} %pad_add_fusion.table_ref, bf16[2048,6656]{1,0:T(8,128)(2,1)} %args_0_.34, bf16[2048,6656]{1,0:T(8,128)(2,1)} %args_1_.34, bf16[6656,2048]{1,0:T(8,128)(2,1)} %args_2_.34, bf16[128,2048]{1,0:T(8,128)(2,1)} %collective-permute-done.8.args_3_, ...), custom_call_target="tpu_custom_call" | custom-call | flops 1000 | bytes 1000 | tf_op jit(solution)/shard_map/step_g/pallas_call | solution.py:347
  89.4 5.8 %step_g.15.args_4_ = bf16[2,256,768]{2,1,0:T(8,128)(2,1)} custom-call(s32[5]{0:T(128)} %pad_add_fusion.table_ref, bf16[2048,6656]{1,0:T(8,128)(2,1)} %args_0_.34, bf16[2048,6656]{1,0:T(8,128)(2,1)} %args_1_.34, bf16[6656,2048]{1,0:T(8,128)(2,1)} %args_2_.34, bf16[128,2048]{1,0:T(8,128)(2,1)} %collective-permute-done.8.args_3_, ...), custom_call_target="tpu_custom_call" | custom-call | flops 1000 | bytes 1000 | tf_op jit(solution)/shard_map/step_g/pallas_call | solution.py:347
  96.6 5.4 %collective-permute-done.13.args_3_ = bf16[128,2048]{1,0:T(8,128)(2,1)} collective-permute-done((bf16[128,2048]{1,0:T(8,128)(2,1)}, bf16[128,2048]{1,0:T(8,128)(2,1)}, u32[]{:S(2)}, u32[]{:S(2)}) %collective-permute-start.13) | collective-permute-done | bytes 524320 | tf_op jit(solution)/shard_map/ppermute | solution.py:21
  102.0 12.1 %step_gg.5 = (bf16[2,128,1792]{2,1,0:T(8,128)(2,1)}, bf16[2,128,1664]{2,1,0:T(8,128)(2,1)}) custom-call(s32[5]{0:T(128)} %pad_add_fusion.table_ref, bf16[2048,6656]{1,0:T(8,128)(2,1)} %args_0_.34, bf16[2048,6656]{1,0:T(8,128)(2,1)} %args_1_.34, bf16[6656,2048]{1,0:T(8,128)(2,1)} %args_2_.34, bf16[128,2048]{1,0:T(8,128)(2,1)} %collective-permute-done.13.args_3_, ...), custom_call_target="tpu_custom_call" | custom-call | flops 1000 | bytes 1000 | tf_op jit(solution)/shard_map/step_gg/pallas_call | solution.py:347
  114.2 6.8 %step_g.16.args_9_.args_3_ = bf16[256,896]{1,0:T(8,128)(2,1)} custom-call(s32[5]{0:T(128)} %pad_add_fusion.table_ref, bf16[2048,6656]{1,0:T(8,128)(2,1)} %args_0_.34, bf16[2048,6656]{1,0:T(8,128)(2,1)} %args_1_.34, bf16[6656,2048]{1,0:T(8,128)(2,1)} %args_2_.34, bf16[128,2048]{1,0:T(8,128)(2,1)} %collective-permute-done.8.args_3_, ...), custom_call_target="tpu_custom_call" | custom-call | flops 1000 | bytes 1000 | tf_op jit(solution)/shard_map/step_g/pallas_call | solution.py:347
  122.1 8.1 %collective-permute-done.20.args_6_ = bf16[2,256,768]{2,1,0:T(8,128)(2,1)} collective-permute-done((bf16[2,256,768]{2,1,0:T(8,128)(2,1)}, bf16[2,256,768]{2,1,0:T(8,128)(2,1)}, u32[]{:S(2)}, u32[]{:S(2)}) %collective-permute-start.20) | collective-permute-done | bytes 786464 | tf_op jit(solution)/shard_map/ppermute | solution.py:21
  130.2 6.3 %step_g.17.args_5_.args_7_ = bf16[256,768]{1,0:T(8,128)(2,1)} custom-call(s32[5]{0:T(128)} %pad_add_fusion.table_ref, bf16[2048,6656]{1,0:T(8,128)(2,1)} %args_0_.34, bf16[2048,6656]{1,0:T(8,128)(2,1)} %args_1_.34, bf16[6656,2048]{1,0:T(8,128)(2,1)} %args_2_.34, bf16[128,2048]{1,0:T(8,128)(2,1)} %collective-permute-done.8.args_3_, ...), custom_call_target="tpu_custom_call" | custom-call | flops 1000 | bytes 1000 | tf_op jit(solution)/shard_map/step_g/pallas_call | solution.py:347
  138.0 7.7 %step_g.18 = (bf16[2,128,1792]{2,1,0:T(8,128)(2,1)}, f32[128,128]{1,0:T(8,128)}) custom-call(s32[5]{0:T(128)} %pad_add_fusion.table_ref, bf16[2048,6656]{1,0:T(8,128)(2,1)} %args_0_.34, bf16[2048,6656]{1,0:T(8,128)(2,1)} %args_1_.34, bf16[6656,2048]{1,0:T(8,128)(2,1)} %args_2_.34, bf16[128,2048]{1,0:T(8,128)(2,1)} %collective-permute-done.13.args_3_, ...), custom_call_target="tpu_custom_call" | custom-call | flops 1000 | bytes 1000 | tf_op jit(solution)/shard_map/step_g/pallas_call | solution.py:347
  149.7 13.8 %step_d.2 = (bf16[128,2048]{1,0:T(8,128)(2,1)}, bf16[128,2048]{1,0:T(8,128)(2,1)}) custom-call(s32[5]{0:T(128)} %pad_add_fusion.table_ref, bf16[2048,6656]{1,0:T(8,128)(2,1)} %args_0_.34, bf16[2048,6656]{1,0:T(8,128)(2,1)} %args_1_.34, bf16[6656,2048]{1,0:T(8,128)(2,1)} %args_2_.34, bf16[256,896]{1,0:T(8,128)(2,1)} %step_g.16.args_9_.args_3_, ...), custom_call_target="tpu_custom_call" | custom-call | flops 1000 | bytes 1000 | tf_op jit(solution)/shard_map/step_d/pallas_call | solution.py:347
  164.8 4.1 %collective-permute-done.23.args_5_ = bf16[2,128,1792]{2,1,0:T(8,128)(2,1)} collective-permute-done((bf16[2,128,1792]{2,1,0:T(8,128)(2,1)}, bf16[2,128,1792]{2,1,0:T(8,128)(2,1)}, u32[]{:S(2)}, u32[]{:S(2)}) %collective-permute-start.23) | collective-permute-done | bytes 917536 | tf_op jit(solution)/shard_map/ppermute | solution.py:21
  168.9 7.9 %step_g.19.args_11_.args_15_ = bf16[128,1664]{1,0:T(8,128)(2,1)} custom-call(s32[5]{0:T(128)} %pad_add_fusion.table_ref, bf16[2048,6656]{1,0:T(8,128)(2,1)} %args_0_.34, bf16[2048,6656]{1,0:T(8,128)(2,1)} %args_1_.34, bf16[6656,2048]{1,0:T(8,128)(2,1)} %args_2_.34, bf16[128,2048]{1,0:T(8,128)(2,1)} %collective-permute-done.13.args_3_, ...), custom_call_target="tpu_custom_call" | custom-call | flops 1000 | bytes 1000 | tf_op jit(solution)/shard_map/step_g/pallas_call | solution.py:347
  180.1 2.9 %collective-permute-start.34 = (bf16[128,2048]{1,0:T(8,128)(2,1)}, bf16[128,2048]{1,0:T(8,128)(2,1)}, u32[]{:S(2)}, u32[]{:S(2)}) collective-permute-start(bf16[128,2048]{1,0:T(8,128)(2,1)} %add_convert_fusion.1), channel_id=1, source_target_pairs={{0,2},{1,3},{2,0},{3,1},{4,6},{5,7},{6,4},{7,5},{8,10},{9,11},{10,... | collective-permute-start | bytes 1572872 | tf_op jit(solution)/shard_map/ppermute | solution.py:21
  183.5 5.0 %collective-permute-done.31.args_13_ = bf16[128,1664]{1,0:T(8,128)(2,1)S(1)} collective-permute-done((bf16[128,1664]{1,0:T(8,128)(2,1)}, bf16[128,1664]{1,0:T(8,128)(2,1)S(1)}, u32[]{:S(2)}, u32[]{:S(2)}) %collective-permute-start.31) | collective-permute-done | bytes 426016 | tf_op jit(solution)/shard_map/ppermute | solution.py:21
  192.0 14.0 %step_d.3 = (bf16[128,2048]{1,0:T(8,128)(2,1)}, bf16[128,2048]{1,0:T(8,128)(2,1)}) custom-call(s32[5]{0:T(128)} %pad_add_fusion.table_ref, bf16[2048,6656]{1,0:T(8,128)(2,1)} %args_0_.34, bf16[2048,6656]{1,0:T(8,128)(2,1)} %args_1_.34, bf16[6656,2048]{1,0:T(8,128)(2,1)} %args_2_.34, bf16[128,896]{1,0:T(8,128)(2,1)} %step_g.12.args_8_.args_3_, ...), custom_call_target="tpu_custom_call" | custom-call | flops 1000 | bytes 1000 | tf_op jit(solution)/shard_map/step_d/pallas_call | solution.py:347
  206.9 13.3 %collective-permute-done.35 = bf16[128,2048]{1,0:T(8,128)(2,1)S(1)} collective-permute-done((bf16[128,2048]{1,0:T(8,128)(2,1)}, bf16[128,2048]{1,0:T(8,128)(2,1)S(1)}, u32[]{:S(2)}, u32[]{:S(2)}) %collective-permute-start.35) | collective-permute-done | bytes 524320 | tf_op jit(solution)/shard_map/ppermute | solution.py:21
  (70 shorter events, 40.5 us)
Async XLA Ops:
  21.5 15.7 %collective-permute-start.2 = (bf16[2,128,1024]{2,1,0:T(8,128)(2,1)}, bf16[2,128,1024]{2,1,0:T(8,128)(2,1)}, u32[]{:S(2)}, u32[]{:S(2)}) collective-permute-start(bf16[2,128,1024]{2,1,0:T(8,128)(2,1)} %get-tuple-element.46.args_5_), channel_id=1, source_target_pairs={{0,8},{4,12},{8,0},{12,4},{1,9},{5,13},{9,1},{13,5},{2,10},{6,14},... | collective-permute-start | bytes 1572872 | tf_op jit(solution)/shard_map/ppermute | solution.py:21
  24.1 26.6 %collective-permute-start.8 = (bf16[128,2048]{1,0:T(8,128)(2,1)}, bf16[128,2048]{1,0:T(8,128)(2,1)}, u32[]{:S(2)}, u32[]{:S(2)}) collective-permute-start(bf16[128,2048]{1,0:T(8,128)(2,1)} %args_3_.14), channel_id=1, source_target_pairs={{0,2},{1,3},{2,0},{3,1},{4,6},{5,7},{6,4},{7,5},{8,10},{9,11},{10,... | collective-permute-start | bytes 1572872 | tf_op jit(solution)/shard_map/ppermute | solution.py:21
  26.7 7.7 %collective-permute-start = (bf16[2,128,896]{2,1,0:T(8,128)(2,1)}, bf16[2,128,896]{2,1,0:T(8,128)(2,1)}, u32[]{:S(2)}, u32[]{:S(2)}) collective-permute-start(bf16[2,128,896]{2,1,0:T(8,128)(2,1)} %get-tuple-element.43), channel_id=1, source_target_pairs={{0,4},{4,0},{8,12},{12,8},{1,5},{5,1},{9,13},{13,9},{2,6},{6,2},{1... | collective-permute-start | bytes 1376264 | tf_op jit(solution)/shard_map/ppermute | solution.py:21
  27.2 24.8 %collective-permute-start.6 = (bf16[2,128,768]{2,1,0:T(8,128)(2,1)}, bf16[2,128,768]{2,1,0:T(8,128)(2,1)}, u32[]{:S(2)}, u32[]{:S(2)}) collective-permute-start(bf16[2,128,768]{2,1,0:T(8,128)(2,1)} %get-tuple-element.48), channel_id=1, source_target_pairs={{0,4},{4,0},{8,12},{12,8},{1,5},{5,1},{9,13},{13,9},{2,6},{6,2},{1... | collective-permute-start | bytes 1179656 | tf_op jit(solution)/shard_map/ppermute | solution.py:21
  33.9 18.1 %collective-permute-start.7 = (bf16[2,128,768]{2,1,0:T(8,128)(2,1)}, bf16[2,128,768]{2,1,0:T(8,128)(2,1)}, u32[]{:S(2)}, u32[]{:S(2)}) collective-permute-start(bf16[2,128,768]{2,1,0:T(8,128)(2,1)} %step_g.11.args_7_), channel_id=1, source_target_pairs={{0,8},{4,12},{8,0},{12,4},{1,9},{5,13},{9,1},{13,5},{2,10},{6,14},... | collective-permute-start | bytes 1179656 | tf_op jit(solution)/shard_map/ppermute | solution.py:21
  50.7 13.7 %collective-permute-start.14 = (bf16[128,2048]{1,0:T(8,128)(2,1)}, bf16[128,2048]{1,0:T(8,128)(2,1)}, u32[]{:S(2)}, u32[]{:S(2)}) collective-permute-start(bf16[128,2048]{1,0:T(8,128)(2,1)} %collective-permute-done.8.args_3_), channel_id=1, source_target_pairs={{0,1},{1,0},{2,3},{3,2},{4,5},{5,4},{6,7},{7,6},{8,9},{9,8},{10,11... | collective-permute-start | bytes 1572872 | tf_op jit(solution)/shard_map/ppermute | solution.py:21
  77.6 11.7 %collective-permute-start.15 = (bf16[2,256,768]{2,1,0:T(8,128)(2,1)}, bf16[2,256,768]{2,1,0:T(8,128)(2,1)}, u32[]{:S(2)}, u32[]{:S(2)}) collective-permute-start(bf16[2,256,768]{2,1,0:T(8,128)(2,1)} %get-tuple-element.55), channel_id=1, source_target_pairs={{0,4},{4,0},{8,12},{12,8},{1,5},{5,1},{9,13},{13,9},{2,6},{6,2},{1... | collective-permute-start | bytes 2359304 | tf_op jit(solution)/shard_map/ppermute | solution.py:21
  87.0 27.2 %collective-permute-start.21 = (bf16[2,256,1024]{2,1,0:T(8,128)(2,1)}, bf16[2,256,1024]{2,1,0:T(8,128)(2,1)}, u32[]{:S(2)}, u32[]{:S(2)}) collective-permute-start(bf16[2,256,1024]{2,1,0:T(8,128)(2,1)} %get-tuple-element.57.args_6_), channel_id=1, source_target_pairs={{0,8},{4,12},{8,0},{12,4},{1,9},{5,13},{9,1},{13,5},{2,10},{6,14},... | collective-permute-start | bytes 3145736 | tf_op jit(solution)/shard_map/ppermute | solution.py:21
  88.0 14.0 %collective-permute-start.13 = (bf16[128,2048]{1,0:T(8,128)(2,1)}, bf16[128,2048]{1,0:T(8,128)(2,1)}, u32[]{:S(2)}, u32[]{:S(2)}) collective-permute-start(bf16[128,2048]{1,0:T(8,128)(2,1)} %args_3_.14), channel_id=1, source_target_pairs={{0,1},{1,0},{2,3},{3,2},{4,5},{5,4},{6,7},{7,6},{8,9},{9,8},{10,11... | collective-permute-start | bytes 1572872 | tf_op jit(solution)/shard_map/ppermute | solution.py:21
  88.9 25.3 %collective-permute-start.22 = (bf16[2,256,896]{2,1,0:T(8,128)(2,1)}, bf16[2,256,896]{2,1,0:T(8,128)(2,1)}, u32[]{:S(2)}, u32[]{:S(2)}) collective-permute-start(bf16[2,256,896]{2,1,0:T(8,128)(2,1)} %get-tuple-element.64), channel_id=1, source_target_pairs={{0,4},{4,0},{8,12},{12,8},{1,5},{5,1},{9,13},{13,9},{2,6},{6,2},{1... | collective-permute-start | bytes 2752520 | tf_op jit(solution)/shard_map/ppermute | solution.py:21
  88.9 33.3 %collective-permute-start.19 = (bf16[2,256,768]{2,1,0:T(8,128)(2,1)}, bf16[2,256,768]{2,1,0:T(8,128)(2,1)}, u32[]{:S(2)}, u32[]{:S(2)}) collective-permute-start(bf16[2,256,768]{2,1,0:T(8,128)(2,1)} %get-tuple-element.62), channel_id=1, source_target_pairs={{0,4},{4,0},{8,12},{12,8},{1,5},{5,1},{9,13},{13,9},{2,6},{6,2},{1... | collective-permute-start | bytes 2359304 | tf_op jit(solution)/shard_map/ppermute | solution.py:21
  95.2 35.0 %collective-permute-start.20 = (bf16[2,256,768]{2,1,0:T(8,128)(2,1)}, bf16[2,256,768]{2,1,0:T(8,128)(2,1)}, u32[]{:S(2)}, u32[]{:S(2)}) collective-permute-start(bf16[2,256,768]{2,1,0:T(8,128)(2,1)} %step_g.15.args_4_), channel_id=1, source_target_pairs={{0,8},{4,12},{8,0},{12,4},{1,9},{5,13},{9,1},{13,5},{2,10},{6,14},... | collective-permute-start | bytes 2359304 | tf_op jit(solution)/shard_map/ppermute | solution.py:21
  114.1 23.9 %collective-permute-start.18 = (bf16[2,128,1792]{2,1,0:T(8,128)(2,1)}, bf16[2,128,1792]{2,1,0:T(8,128)(2,1)}, u32[]{:S(2)}, u32[]{:S(2)}) collective-permute-start(bf16[2,128,1792]{2,1,0:T(8,128)(2,1)} %get-tuple-element.61.args_8_), channel_id=1, source_target_pairs={{0,4},{4,0},{8,12},{12,8},{1,5},{5,1},{9,13},{13,9},{2,6},{6,2},{1... | collective-permute-start | bytes 2752520 | tf_op jit(solution)/shard_map/ppermute | solution.py:21
  121.0 24.7 %collective-permute-start.25 = (bf16[256,896]{1,0:T(8,128)(2,1)}, bf16[256,896]{1,0:T(8,128)(2,1)}, u32[]{:S(2)}, u32[]{:S(2)}) collective-permute-start(bf16[256,896]{1,0:T(8,128)(2,1)} %step_g.16.args_9_.args_3_), channel_id=1, source_target_pairs={{0,8},{4,12},{8,0},{12,4},{1,9},{5,13},{9,1},{13,5},{2,10},{6,14},... | collective-permute-start | bytes 1376264 | tf_op jit(solution)/shard_map/ppermute | solution.py:21
  136.5 11.2 %collective-permute-start.28 = (bf16[256,768]{1,0:T(8,128)(2,1)}, bf16[256,768]{1,0:T(8,128)(2,1)}, u32[]{:S(2)}, u32[]{:S(2)}) collective-permute-start(bf16[256,768]{1,0:T(8,128)(2,1)} %step_g.17.args_5_.args_7_), channel_id=1, source_target_pairs={{0,8},{4,12},{8,0},{12,4},{1,9},{5,13},{9,1},{13,5},{2,10},{6,14},... | collective-permute-start | bytes 1179656 | tf_op jit(solution)/shard_map/ppermute | solution.py:21
  137.5 10.2 %collective-permute-start.27 = (bf16[256,768]{1,0:T(8,128)(2,1)}, bf16[256,768]{1,0:T(8,128)(2,1)}, u32[]{:S(2)}, u32[]{:S(2)}) collective-permute-start(bf16[256,768]{1,0:T(8,128)(2,1)} %step_g.17.args_5_.args_7_), channel_id=1, source_target_pairs={{0,4},{4,0},{8,12},{12,8},{1,5},{5,1},{9,13},{13,9},{2,6},{6,2},{1... | collective-permute-start | bytes 1179656 | tf_op jit(solution)/shard_map/ppermute | solution.py:21
  137.5 10.7 %collective-permute-start.24 = (bf16[256,896]{1,0:T(8,128)(2,1)}, bf16[256,896]{1,0:T(8,128)(2,1)}, u32[]{:S(2)}, u32[]{:S(2)}) collective-permute-start(bf16[256,896]{1,0:T(8,128)(2,1)} %step_g.16.args_9_.args_3_), channel_id=1, source_target_pairs={{0,4},{4,0},{8,12},{12,8},{1,5},{5,1},{9,13},{13,9},{2,6},{6,2},{1... | collective-permute-start | bytes 1376264 | tf_op jit(solution)/shard_map/ppermute | solution.py:21
  145.8 23.1 %collective-permute-start.23 = (bf16[2,128,1792]{2,1,0:T(8,128)(2,1)}, bf16[2,128,1792]{2,1,0:T(8,128)(2,1)}, u32[]{:S(2)}, u32[]{:S(2)}) collective-permute-start(bf16[2,128,1792]{2,1,0:T(8,128)(2,1)} %get-tuple-element.70.args_11_), channel_id=1, source_target_pairs={{0,8},{4,12},{8,0},{12,4},{1,9},{5,13},{9,1},{13,5},{2,10},{6,14},... | collective-permute-start | bytes 2752520 | tf_op jit(solution)/shard_map/ppermute | solution.py:21
  147.7 17.1 %collective-permute-start.17 = (bf16[2,128,1664]{2,1,0:T(8,128)(2,1)}, bf16[2,128,1664]{2,1,0:T(8,128)(2,1)}, u32[]{:S(2)}, u32[]{:S(2)}) collective-permute-start(bf16[2,128,1664]{2,1,0:T(8,128)(2,1)} %get-tuple-element.60), channel_id=1, source_target_pairs={{0,4},{4,0},{8,12},{12,8},{1,5},{5,1},{9,13},{13,9},{2,6},{6,2},{1... | collective-permute-start | bytes 2555912 | tf_op jit(solution)/shard_map/ppermute | solution.py:21
  163.6 14.4 %collective-permute-start.32 = (bf16[128,2048]{1,0:T(8,128)(2,1)}, bf16[128,2048]{1,0:T(8,128)(2,1)}, u32[]{:S(2)}, u32[]{:S(2)}) collective-permute-start(bf16[128,2048]{1,0:T(8,128)(2,1)} %get-tuple-element.72), channel_id=1, source_target_pairs={{0,1},{1,0},{2,3},{3,2},{4,5},{5,4},{6,7},{7,6},{8,9},{9,8},{10,11... | collective-permute-start | bytes 1572872 | tf_op jit(solution)/shard_map/ppermute | solution.py:21
  176.8 11.7 %collective-permute-start.31 = (bf16[128,1664]{1,0:T(8,128)(2,1)}, bf16[128,1664]{1,0:T(8,128)(2,1)S(1)}, u32[]{:S(2)}, u32[]{:S(2)}) collective-permute-start(bf16[128,1664]{1,0:T(8,128)(2,1)} %step_g.19.args_11_.args_15_), channel_id=1, source_target_pairs={{0,8},{4,12},{8,0},{12,4},{1,9},{5,13},{9,1},{13,5},{2,10},{6,14},... | collective-permute-start | bytes 1277960 | tf_op jit(solution)/shard_map/ppermute | solution.py:21
  180.1 25.9 %collective-permute-start.34 = (bf16[128,2048]{1,0:T(8,128)(2,1)}, bf16[128,2048]{1,0:T(8,128)(2,1)}, u32[]{:S(2)}, u32[]{:S(2)}) collective-permute-start(bf16[128,2048]{1,0:T(8,128)(2,1)} %add_convert_fusion.1), channel_id=1, source_target_pairs={{0,2},{1,3},{2,0},{3,1},{4,6},{5,7},{6,4},{7,5},{8,10},{9,11},{10,... | collective-permute-start | bytes 1572872 | tf_op jit(solution)/shard_map/ppermute | solution.py:21
  183.4 8.5 %collective-permute-start.30 = (bf16[128,1664]{1,0:T(8,128)(2,1)}, bf16[128,1664]{1,0:T(8,128)(2,1)}, u32[]{:S(2)}, u32[]{:S(2)}) collective-permute-start(bf16[128,1664]{1,0:T(8,128)(2,1)} %step_g.19.args_11_.args_15_), channel_id=1, source_target_pairs={{0,4},{4,0},{8,12},{12,8},{1,5},{5,1},{9,13},{13,9},{2,6},{6,2},{1... | collective-permute-start | bytes 1277960 | tf_op jit(solution)/shard_map/ppermute | solution.py:21
  206.0 14.2 %collective-permute-start.35 = (bf16[128,2048]{1,0:T(8,128)(2,1)}, bf16[128,2048]{1,0:T(8,128)(2,1)S(1)}, u32[]{:S(2)}, u32[]{:S(2)}) collective-permute-start(bf16[128,2048]{1,0:T(8,128)(2,1)} %get-tuple-element.80), channel_id=1, source_target_pairs={{0,1},{1,0},{2,3},{3,2},{4,5},{5,4},{6,7},{7,6},{8,9},{9,8},{10,11... | collective-permute-start | bytes 1572872 | tf_op jit(solution)/shard_map/ppermute | solution.py:21
  (13 other events, 54.6 us)

commit v8 on v7

--- a/solution.py
+++ b/solution.py
@@ -11,7 +11,7 @@
 LANES = 128
 GU_TILE = 256
 OUT_TILE = 512
-COST = pl.CostEstimate(flops=1000, bytes_accessed=1000, transcendentals=0)
+SHORT, LONG = 1000, 10**11
 VMEM_LIMIT = 64 * 1024 * 1024 - 64 * 1024
 ANY = pl.BlockSpec(memory_space=pl.ANY)
 SMEM = pl.BlockSpec(memory_space=pltpu.SMEM)
@@ -288,7 +288,7 @@
         return copies, begin, compute, drain
 
 
-def run(phases, table, gate_matrix, up_matrix, down_matrix, dep):
+def run(phases, table, gate_matrix, up_matrix, down_matrix, dep, work):
     depth, columns = gate_matrix.shape[0], down_matrix.shape[1]
     if not all(p.fits(depth, columns) for p in phases):
         return [p.plain(table, gate_matrix, up_matrix, down_matrix) for p in phases]
@@ -358,7 +358,7 @@
                 *[buffer for buffers in scratch for buffer in buffers],
             ],
             compiler_params=pltpu.CompilerParams(vmem_limit_bytes=VMEM_LIMIT),
-            cost_estimate=COST,
+            cost_estimate=pl.CostEstimate(flops=work, bytes_accessed=1000, transcendentals=0),
             name="step_" + "".join("g" if p.group is not None else "d" for p in phases),
         )(table, *operands)
     )
@@ -370,14 +370,14 @@
     ("s1",),
     ("x0",),
     ("x1",),
-    ("h0",),
-    ("t", "h1"),
-    ("r0", "r1", "s2", "s3"),
-    ("x2",),
+    ("t", "h0"),
+    ("h1",),
+    ("r0", "s2", "s3"),
+    ("r1", "x2"),
     ("x3",),
     ("b", "s4"),
     ("h2",),
-    ("h3",),
+    ("f0", "f1", "h3"),
     ("x4",),
     ("r2", "r3", "d1"),
     ("h4",),
@@ -407,7 +407,8 @@
     groups = [Group(blocks, js, block) for js in sets]
     squares = {}
     half = cut(width, 7, 13)
-    jobs = [(0, 0, half), (0, half, width - half), (1, 0, half), (1, half, width - half), (2, 0, width)]
+    early = cut(width, 7, 13)
+    jobs = [(0, 0, early), (0, early, width - early), (1, 0, half), (1, half, width - half), (2, 0, width)]
     firsts = [min(i for i, job in enumerate(jobs) if job[0] == g) for g in range(len(groups))]
     state = [dict() for _ in jobs]
     totals = {}
@@ -478,8 +479,10 @@
     mask = n_gy // 2
     gather_over_gy(mask)
     for names in STEPS:
-        items = []
+        items, work = [], LONG if "long" in names else SHORT
         for name in names:
+            if name == "long":
+                continue
             kind, job = name[0], int(name[1:] or 0)
             if kind == "r":
                 forward(job)
@@ -487,17 +490,20 @@
             while kind == "t" and mask > 1:
                 mask //= 2
                 gather_over_gy(mask)
+            if kind == "f":
+                held, places = zip(*state[job]["pieces"])
+                state[job]["pieces"] = list(zip(tied(list(held)), places))
             if kind == "b":
                 blocks[1] = tied(swap(tokens, "gy", n_gy, 1))
             if kind == "z":
                 reduce_over_gy()
-            if kind in "tbz":
+            if kind in "tfbz":
                 continue
             if kind == "d":
                 items.append((kind, [int(g) for g in name[1:]], [down([int(g) for g in name[1:]])]))
             else:
                 items.append((kind, job, phases_of(kind, job)))
-        results = run([p for _, _, ps in items for p in ps], table, gate_matrix, up_matrix, down_matrix, chain)
+        results = run([p for _, _, ps in items for p in ps], table, gate_matrix, up_matrix, down_matrix, chain, work)
         chain = results[0][0]
         for kind, job, ps in items:
             outs = [results.pop(0) for _ in ps]

time: 223 us -> 218 us (0.978)
  waiting for transfers between devices: 60.6 us -> 54.4 us
    ppermute x36, waiting for transfers between devices: 60.6 us -> 54.4 us  [swap(): return lax.ppermute(value, axis, [(i, i ^ mask) for i in range(size)])]
  transfers between devices with their start and end apart: 36 -> 36, of which waited for: 15 -> 12; matrix products, arithmetic and copies ran while one was open for 1% -> 1% of each run, Pallas kernels for 47% -> 50%
where the time goes in v8:
time: 218 us
  Pallas kernels  130 us (60%)
  waiting for transfers between devices  54.4 us (25%)
  starting transfers between devices  27.5 us (13%)
  other arithmetic  5 us (2%)
    pallas_call x16, Pallas kernels, run(): pl.pallas_call(kernel, out_shape=outs, in_specs=[SMEM] + [ANY] * len(oper...  130 us
    ppermute x36, waiting for transfers between devices, swap(): return lax.ppermute(value, axis, [(i, i ^ mask) for i in range(size)])  54.4 us
    ppermute x36, starting transfers between devices, swap(): return lax.ppermute(value, axis, [(i, i ^ mask) for i in range(size)])  27.5 us
  transfers between devices with their start and end apart: 36, of which 12 were waited for; matrix products, arithmetic and copies ran while one was open for 1% of the time, Pallas kernels for 50%

profile of v8, /device:TPU:0, one launch (start us, length us, event | category | flops | bytes accessed | tf_op | source)
XLA Modules:
  0.0 218.1 jit_solution(12202138372151338089)
XLA Ops:
  0.6 7.8 %step_gg.3 = (bf16[2,128,1024]{2,1,0:T(8,128)(2,1)}, bf16[2,128,896]{2,1,0:T(8,128)(2,1)}) custom-call(s32[5]{0:T(128)} %pad_add_fusion.table_ref, bf16[2048,6656]{1,0:T(8,128)(2,1)} %args_0_.34, bf16[2048,6656]{1,0:T(8,128)(2,1)} %args_1_.34, bf16[6656,2048]{1,0:T(8,128)(2,1)} %args_2_.34, bf16[128,2048]{1,0:T(8,128)(2,1)} %args_3_.14, ...), custom_call_target="tpu_custom_call" | custom-call | flops 1000 | bytes 1000 | tf_op jit(solution)/shard_map/step_gg/pallas_call | solution.py:347
  9.0 3.7 %collective-permute-start.3 = (bf16[128,2048]{1,0:T(8,128)(2,1)}, bf16[128,2048]{1,0:T(8,128)(2,1)}, u32[]{:S(2)}, u32[]{:S(2)}) collective-permute-start(bf16[128,2048]{1,0:T(8,128)(2,1)} %args_3_.14), channel_id=1, source_target_pairs={{0,2},{1,3},{2,0},{3,1},{4,6},{5,7},{6,4},{7,5},{8,10},{9,11},{10,... | collective-permute-start | bytes 1572872 | tf_op jit(solution)/shard_map/ppermute | solution.py:21
  12.6 7.1 %step_gg.4 = (bf16[2,128,768]{2,1,0:T(8,128)(2,1)}, bf16[2,128,768]{2,1,0:T(8,128)(2,1)}) custom-call(s32[5]{0:T(128)} %pad_add_fusion.table_ref, bf16[2048,6656]{1,0:T(8,128)(2,1)} %args_0_.34, bf16[2048,6656]{1,0:T(8,128)(2,1)} %args_1_.34, bf16[6656,2048]{1,0:T(8,128)(2,1)} %args_2_.34, bf16[128,2048]{1,0:T(8,128)(2,1)} %args_3_.14, ...), custom_call_target="tpu_custom_call" | custom-call | flops 1000 | bytes 1000 | tf_op jit(solution)/shard_map/step_gg/pallas_call | solution.py:347
  20.1 5.5 %step_g.10 = (bf16[2,128,1024]{2,1,0:T(8,128)(2,1)}, f32[128,128]{1,0:T(8,128)}) custom-call(s32[5]{0:T(128)} %pad_add_fusion.table_ref, bf16[2048,6656]{1,0:T(8,128)(2,1)} %args_0_.34, bf16[2048,6656]{1,0:T(8,128)(2,1)} %args_1_.34, bf16[6656,2048]{1,0:T(8,128)(2,1)} %args_2_.34, bf16[128,2048]{1,0:T(8,128)(2,1)} %args_3_.14, ...), custom_call_target="tpu_custom_call" | custom-call | flops 1000 | bytes 1000 | tf_op jit(solution)/shard_map/step_g/pallas_call | solution.py:347
  27.1 5.1 %step_g.11.args_7_ = bf16[2,128,768]{2,1,0:T(8,128)(2,1)} custom-call(s32[5]{0:T(128)} %pad_add_fusion.table_ref, bf16[2048,6656]{1,0:T(8,128)(2,1)} %args_0_.34, bf16[2048,6656]{1,0:T(8,128)(2,1)} %args_1_.34, bf16[6656,2048]{1,0:T(8,128)(2,1)} %args_2_.34, bf16[128,2048]{1,0:T(8,128)(2,1)} %args_3_.14, ...), custom_call_target="tpu_custom_call" | custom-call | flops 1000 | bytes 1000 | tf_op jit(solution)/shard_map/step_g/pallas_call | solution.py:347
  32.2 4.5 %collective-permute-done.3.args_3_ = bf16[128,2048]{1,0:T(8,128)(2,1)} collective-permute-done((bf16[128,2048]{1,0:T(8,128)(2,1)}, bf16[128,2048]{1,0:T(8,128)(2,1)}, u32[]{:S(2)}, u32[]{:S(2)}) %collective-permute-start.3) | collective-permute-done | bytes 524320 | tf_op jit(solution)/shard_map/ppermute | solution.py:21
  40.0 5.6 %step_g.12.args_8_.args_3_ = bf16[128,896]{1,0:T(8,128)(2,1)} custom-call(s32[5]{0:T(128)} %pad_add_fusion.table_ref, bf16[2048,6656]{1,0:T(8,128)(2,1)} %args_0_.34, bf16[2048,6656]{1,0:T(8,128)(2,1)} %args_1_.34, bf16[6656,2048]{1,0:T(8,128)(2,1)} %args_2_.34, bf16[128,2048]{1,0:T(8,128)(2,1)} %args_3_.14, ...), custom_call_target="tpu_custom_call" | custom-call | flops 1000 | bytes 1000 | tf_op jit(solution)/shard_map/step_g/pallas_call | solution.py:347
  49.7 5.3 %step_g.13.args_5_.args_7_ = bf16[128,768]{1,0:T(8,128)(2,1)} custom-call(s32[5]{0:T(128)} %pad_add_fusion.table_ref, bf16[2048,6656]{1,0:T(8,128)(2,1)} %args_0_.34, bf16[2048,6656]{1,0:T(8,128)(2,1)} %args_1_.34, bf16[6656,2048]{1,0:T(8,128)(2,1)} %args_2_.34, bf16[128,2048]{1,0:T(8,128)(2,1)} %args_3_.14, ...), custom_call_target="tpu_custom_call" | custom-call | flops 1000 | bytes 1000 | tf_op jit(solution)/shard_map/step_g/pallas_call | solution.py:347
  55.0 13.2 %step_gggg.1 = (bf16[2,256,1024]{2,1,0:T(8,128)(2,1)}, bf16[2,256,896]{2,1,0:T(8,128)(2,1)}, bf16[2,256,768]{2,1,0:T(8,128)(2,1)}, bf16[2,256,768]{2,1,0:T(8,128)(2,1)}) custom-call(s32[5]{0:T(128)} %pad_add_fusion.table_ref, bf16[2048,6656]{1,0:T(8,128)(2,1)} %args_0_.34, bf16[2048,6656]{1,0:T(8,128)(2,1)} %args_1_.34, bf16[6656,2048]{1,0:T(8,128)(2,1)} %args_2_.34, ...), custom_call_target="tpu_custom_call" | custom-call | flops 1000 | bytes 1000 | tf_op jit(solution)/shard_map/step_gggg/pallas_call | solution.py:347
  71.6 4.3 %collective-permute-done.13.args_9_ = bf16[128,768]{1,0:T(8,128)(2,1)} collective-permute-done((bf16[128,768]{1,0:T(8,128)(2,1)}, bf16[128,768]{1,0:T(8,128)(2,1)}, u32[]{:S(2)}, u32[]{:S(2)}) %collective-permute-start.13) | collective-permute-done | bytes 196640 | tf_op jit(solution)/shard_map/ppermute | solution.py:21
  75.9 6.3 %step_g.14 = (bf16[2,256,1024]{2,1,0:T(8,128)(2,1)}, f32[256,128]{1,0:T(8,128)}) custom-call(s32[5]{0:T(128)} %pad_add_fusion.table_ref, bf16[2048,6656]{1,0:T(8,128)(2,1)} %args_0_.34, bf16[2048,6656]{1,0:T(8,128)(2,1)} %args_1_.34, bf16[6656,2048]{1,0:T(8,128)(2,1)} %args_2_.34, bf16[128,2048]{1,0:T(8,128)(2,1)} %collective-permute-done.3.args_3_, ...), custom_call_target="tpu_custom_call" | custom-call | flops 1000 | bytes 1000 | tf_op jit(solution)/shard_map/step_g/pallas_call | solution.py:347
  84.4 5.8 %step_g.15.args_4_ = bf16[2,256,768]{2,1,0:T(8,128)(2,1)} custom-call(s32[5]{0:T(128)} %pad_add_fusion.table_ref, bf16[2048,6656]{1,0:T(8,128)(2,1)} %args_0_.34, bf16[2048,6656]{1,0:T(8,128)(2,1)} %args_1_.34, bf16[6656,2048]{1,0:T(8,128)(2,1)} %args_2_.34, bf16[128,2048]{1,0:T(8,128)(2,1)} %collective-permute-done.3.args_3_, ...), custom_call_target="tpu_custom_call" | custom-call | flops 1000 | bytes 1000 | tf_op jit(solution)/shard_map/step_g/pallas_call | solution.py:347
  90.8 12.0 %step_gg.5 = (bf16[2,128,1792]{2,1,0:T(8,128)(2,1)}, bf16[2,128,1664]{2,1,0:T(8,128)(2,1)}) custom-call(s32[5]{0:T(128)} %pad_add_fusion.table_ref, bf16[2048,6656]{1,0:T(8,128)(2,1)} %args_0_.34, bf16[2048,6656]{1,0:T(8,128)(2,1)} %args_1_.34, bf16[6656,2048]{1,0:T(8,128)(2,1)} %args_2_.34, bf16[128,2048]{1,0:T(8,128)(2,1)} %collective-permute-done.15.args_3_, ...), custom_call_target="tpu_custom_call" | custom-call | flops 1000 | bytes 1000 | tf_op jit(solution)/shard_map/step_gg/pallas_call | solution.py:347
  103.5 5.3 %collective-permute-done.14.args_6_.args_8_ = bf16[2,256,1024]{2,1,0:T(8,128)(2,1)} collective-permute-done((bf16[2,256,1024]{2,1,0:T(8,128)(2,1)}, bf16[2,256,1024]{2,1,0:T(8,128)(2,1)}, u32[]{:S(2)}, u32[]{:S(2)}) %collective-permute-start.14) | collective-permute-done | bytes 1048608 | tf_op jit(solution)/shard_map/ppermute | solution.py:21
  108.8 7.0 %step_g.16.args_9_.args_3_ = bf16[256,896]{1,0:T(8,128)(2,1)} custom-call(s32[5]{0:T(128)} %pad_add_fusion.table_ref, bf16[2048,6656]{1,0:T(8,128)(2,1)} %args_0_.34, bf16[2048,6656]{1,0:T(8,128)(2,1)} %args_1_.34, bf16[6656,2048]{1,0:T(8,128)(2,1)} %args_2_.34, bf16[128,2048]{1,0:T(8,128)(2,1)} %collective-permute-done.3.args_3_, ...), custom_call_target="tpu_custom_call" | custom-call | flops 1000 | bytes 1000 | tf_op jit(solution)/shard_map/step_g/pallas_call | solution.py:347
  117.4 8.3 %collective-permute-done.22.args_6_ = bf16[2,256,768]{2,1,0:T(8,128)(2,1)} collective-permute-done((bf16[2,256,768]{2,1,0:T(8,128)(2,1)}, bf16[2,256,768]{2,1,0:T(8,128)(2,1)}, u32[]{:S(2)}, u32[]{:S(2)}) %collective-permute-start.22) | collective-permute-done | bytes 786464 | tf_op jit(solution)/shard_map/ppermute | solution.py:21
  125.6 6.3 %step_g.17.args_5_.args_7_ = bf16[256,768]{1,0:T(8,128)(2,1)} custom-call(s32[5]{0:T(128)} %pad_add_fusion.table_ref, bf16[2048,6656]{1,0:T(8,128)(2,1)} %args_0_.34, bf16[2048,6656]{1,0:T(8,128)(2,1)} %args_1_.34, bf16[6656,2048]{1,0:T(8,128)(2,1)} %args_2_.34, bf16[128,2048]{1,0:T(8,128)(2,1)} %collective-permute-done.3.args_3_, ...), custom_call_target="tpu_custom_call" | custom-call | flops 1000 | bytes 1000 | tf_op jit(solution)/shard_map/step_g/pallas_call | solution.py:347
  134.0 7.7 %step_g.18 = (bf16[2,128,1792]{2,1,0:T(8,128)(2,1)}, f32[128,128]{1,0:T(8,128)}) custom-call(s32[5]{0:T(128)} %pad_add_fusion.table_ref, bf16[2048,6656]{1,0:T(8,128)(2,1)} %args_0_.34, bf16[2048,6656]{1,0:T(8,128)(2,1)} %args_1_.34, bf16[6656,2048]{1,0:T(8,128)(2,1)} %args_2_.34, bf16[128,2048]{1,0:T(8,128)(2,1)} %collective-permute-done.15.args_3_, ...), custom_call_target="tpu_custom_call" | custom-call | flops 1000 | bytes 1000 | tf_op jit(solution)/shard_map/step_g/pallas_call | solution.py:347
  144.5 13.8 %step_d.2 = (bf16[128,2048]{1,0:T(8,128)(2,1)}, bf16[128,2048]{1,0:T(8,128)(2,1)}) custom-call(s32[5]{0:T(128)} %pad_add_fusion.table_ref, bf16[2048,6656]{1,0:T(8,128)(2,1)} %args_0_.34, bf16[2048,6656]{1,0:T(8,128)(2,1)} %args_1_.34, bf16[6656,2048]{1,0:T(8,128)(2,1)} %args_2_.34, bf16[256,896]{1,0:T(8,128)(2,1)} %step_g.16.args_9_.args_3_, ...), custom_call_target="tpu_custom_call" | custom-call | flops 1000 | bytes 1000 | tf_op jit(solution)/shard_map/step_d/pallas_call | solution.py:347
  159.7 5.1 %collective-permute-done.23.args_5_ = bf16[2,128,1792]{2,1,0:T(8,128)(2,1)} collective-permute-done((bf16[2,128,1792]{2,1,0:T(8,128)(2,1)}, bf16[2,128,1792]{2,1,0:T(8,128)(2,1)}, u32[]{:S(2)}, u32[]{:S(2)}) %collective-permute-start.23) | collective-permute-done | bytes 917536 | tf_op jit(solution)/shard_map/ppermute | solution.py:21
  164.9 7.9 %step_g.19.args_11_.args_15_ = bf16[128,1664]{1,0:T(8,128)(2,1)} custom-call(s32[5]{0:T(128)} %pad_add_fusion.table_ref, bf16[2048,6656]{1,0:T(8,128)(2,1)} %args_0_.34, bf16[2048,6656]{1,0:T(8,128)(2,1)} %args_1_.34, bf16[6656,2048]{1,0:T(8,128)(2,1)} %args_2_.34, bf16[128,2048]{1,0:T(8,128)(2,1)} %collective-permute-done.15.args_3_, ...), custom_call_target="tpu_custom_call" | custom-call | flops 1000 | bytes 1000 | tf_op jit(solution)/shard_map/step_g/pallas_call | solution.py:347
  178.8 5.6 %collective-permute-done.31.args_13_ = bf16[128,1664]{1,0:T(8,128)(2,1)S(1)} collective-permute-done((bf16[128,1664]{1,0:T(8,128)(2,1)}, bf16[128,1664]{1,0:T(8,128)(2,1)S(1)}, u32[]{:S(2)}, u32[]{:S(2)}) %collective-permute-start.31) | collective-permute-done | bytes 426016 | tf_op jit(solution)/shard_map/ppermute | solution.py:21
  187.1 14.0 %step_d.3 = (bf16[128,2048]{1,0:T(8,128)(2,1)}, bf16[128,2048]{1,0:T(8,128)(2,1)}) custom-call(s32[5]{0:T(128)} %pad_add_fusion.table_ref, bf16[2048,6656]{1,0:T(8,128)(2,1)} %args_0_.34, bf16[2048,6656]{1,0:T(8,128)(2,1)} %args_1_.34, bf16[6656,2048]{1,0:T(8,128)(2,1)} %args_2_.34, bf16[128,896]{1,0:T(8,128)(2,1)} %step_g.12.args_8_.args_3_, ...), custom_call_target="tpu_custom_call" | custom-call | flops 1000 | bytes 1000 | tf_op jit(solution)/shard_map/step_d/pallas_call | solution.py:347
  202.5 13.4 %collective-permute-done.35 = bf16[128,2048]{1,0:T(8,128)(2,1)S(1)} collective-permute-done((bf16[128,2048]{1,0:T(8,128)(2,1)}, bf16[128,2048]{1,0:T(8,128)(2,1)S(1)}, u32[]{:S(2)}, u32[]{:S(2)}) %collective-permute-start.35) | collective-permute-done | bytes 524320 | tf_op jit(solution)/shard_map/ppermute | solution.py:21
  (70 shorter events, 37.5 us)
Async XLA Ops:
  8.4 11.6 %collective-permute-start.1 = (bf16[2,128,1024]{2,1,0:T(8,128)(2,1)}, bf16[2,128,1024]{2,1,0:T(8,128)(2,1)}, u32[]{:S(2)}, u32[]{:S(2)}) collective-permute-start(bf16[2,128,1024]{2,1,0:T(8,128)(2,1)} %get-tuple-element.54.args_4_), channel_id=1, source_target_pairs={{0,4},{4,0},{8,12},{12,8},{1,5},{5,1},{9,13},{13,9},{2,6},{6,2},{1... | collective-permute-start | bytes 1572872 | tf_op jit(solution)/shard_map/ppermute | solution.py:21
  9.0 27.7 %collective-permute-start.3 = (bf16[128,2048]{1,0:T(8,128)(2,1)}, bf16[128,2048]{1,0:T(8,128)(2,1)}, u32[]{:S(2)}, u32[]{:S(2)}) collective-permute-start(bf16[128,2048]{1,0:T(8,128)(2,1)} %args_3_.14), channel_id=1, source_target_pairs={{0,2},{1,3},{2,0},{3,1},{4,6},{5,7},{6,4},{7,5},{8,10},{9,11},{10,... | collective-permute-start | bytes 1572872 | tf_op jit(solution)/shard_map/ppermute | solution.py:21
  25.6 14.4 %collective-permute-start.2 = (bf16[2,128,1024]{2,1,0:T(8,128)(2,1)}, bf16[2,128,1024]{2,1,0:T(8,128)(2,1)}, u32[]{:S(2)}, u32[]{:S(2)}) collective-permute-start(bf16[2,128,1024]{2,1,0:T(8,128)(2,1)} %get-tuple-element.56.args_5_), channel_id=1, source_target_pairs={{0,8},{4,12},{8,0},{12,4},{1,9},{5,13},{9,1},{13,5},{2,10},{6,14},... | collective-permute-start | bytes 1572872 | tf_op jit(solution)/shard_map/ppermute | solution.py:21
  27.1 11.8 %collective-permute-start = (bf16[2,128,896]{2,1,0:T(8,128)(2,1)}, bf16[2,128,896]{2,1,0:T(8,128)(2,1)}, u32[]{:S(2)}, u32[]{:S(2)}) collective-permute-start(bf16[2,128,896]{2,1,0:T(8,128)(2,1)} %get-tuple-element.53), channel_id=1, source_target_pairs={{0,4},{4,0},{8,12},{12,8},{1,5},{5,1},{9,13},{13,9},{2,6},{6,2},{1... | collective-permute-start | bytes 1376264 | tf_op jit(solution)/shard_map/ppermute | solution.py:21
  36.7 18.2 %collective-permute-start.10 = (bf16[128,2048]{1,0:T(8,128)(2,1)}, bf16[128,2048]{1,0:T(8,128)(2,1)}, u32[]{:S(2)}, u32[]{:S(2)}) collective-permute-start(bf16[128,2048]{1,0:T(8,128)(2,1)} %collective-permute-done.3.args_3_), channel_id=1, source_target_pairs={{0,1},{1,0},{2,3},{3,2},{4,5},{5,4},{6,7},{7,6},{8,9},{9,8},{10,11... | collective-permute-start | bytes 1572872 | tf_op jit(solution)/shard_map/ppermute | solution.py:21
  37.4 9.7 %collective-permute-start.7 = (bf16[2,128,768]{2,1,0:T(8,128)(2,1)}, bf16[2,128,768]{2,1,0:T(8,128)(2,1)}, u32[]{:S(2)}, u32[]{:S(2)}) collective-permute-start(bf16[2,128,768]{2,1,0:T(8,128)(2,1)} %get-tuple-element.59), channel_id=1, source_target_pairs={{0,4},{4,0},{8,12},{12,8},{1,5},{5,1},{9,13},{13,9},{2,6},{6,2},{1... | collective-permute-start | bytes 1179656 | tf_op jit(solution)/shard_map/ppermute | solution.py:21
  37.4 12.2 %collective-permute-start.8 = (bf16[2,128,768]{2,1,0:T(8,128)(2,1)}, bf16[2,128,768]{2,1,0:T(8,128)(2,1)}, u32[]{:S(2)}, u32[]{:S(2)}) collective-permute-start(bf16[2,128,768]{2,1,0:T(8,128)(2,1)} %step_g.11.args_7_), channel_id=1, source_target_pairs={{0,8},{4,12},{8,0},{12,4},{1,9},{5,13},{9,1},{13,5},{2,10},{6,14},... | collective-permute-start | bytes 1179656 | tf_op jit(solution)/shard_map/ppermute | solution.py:21
  68.2 15.6 %collective-permute-start.16 = (bf16[2,256,768]{2,1,0:T(8,128)(2,1)}, bf16[2,256,768]{2,1,0:T(8,128)(2,1)}, u32[]{:S(2)}, u32[]{:S(2)}) collective-permute-start(bf16[2,256,768]{2,1,0:T(8,128)(2,1)} %get-tuple-element.68), channel_id=1, source_target_pairs={{0,4},{4,0},{8,12},{12,8},{1,5},{5,1},{9,13},{13,9},{2,6},{6,2},{1... | collective-permute-start | bytes 2359304 | tf_op jit(solution)/shard_map/ppermute | solution.py:21
  70.3 19.9 %collective-permute-start.15 = (bf16[128,2048]{1,0:T(8,128)(2,1)}, bf16[128,2048]{1,0:T(8,128)(2,1)}, u32[]{:S(2)}, u32[]{:S(2)}) collective-permute-start(bf16[128,2048]{1,0:T(8,128)(2,1)} %args_3_.14), channel_id=1, source_target_pairs={{0,1},{1,0},{2,3},{3,2},{4,5},{5,4},{6,7},{7,6},{8,9},{9,8},{10,11... | collective-permute-start | bytes 1572872 | tf_op jit(solution)/shard_map/ppermute | solution.py:21
  71.6 31.5 %collective-permute-start.11 = (bf16[2,256,896]{2,1,0:T(8,128)(2,1)}, bf16[2,256,896]{2,1,0:T(8,128)(2,1)}, u32[]{:S(2)}, u32[]{:S(2)}) collective-permute-start(bf16[2,256,896]{2,1,0:T(8,128)(2,1)} %get-tuple-element.63), channel_id=1, source_target_pairs={{0,4},{4,0},{8,12},{12,8},{1,5},{5,1},{9,13},{13,9},{2,6},{6,2},{1... | collective-permute-start | bytes 2752520 | tf_op jit(solution)/shard_map/ppermute | solution.py:21
  82.3 26.5 %collective-permute-start.14 = (bf16[2,256,1024]{2,1,0:T(8,128)(2,1)}, bf16[2,256,1024]{2,1,0:T(8,128)(2,1)}, u32[]{:S(2)}, u32[]{:S(2)}) collective-permute-start(bf16[2,256,1024]{2,1,0:T(8,128)(2,1)} %get-tuple-element.66.args_6_), channel_id=1, source_target_pairs={{0,8},{4,12},{8,0},{12,4},{1,9},{5,13},{9,1},{13,5},{2,10},{6,14},... | collective-permute-start | bytes 3145736 | tf_op jit(solution)/shard_map/ppermute | solution.py:21
  83.9 19.0 %collective-permute-start.5 = (bf16[128,896]{1,0:T(8,128)(2,1)}, bf16[128,896]{1,0:T(8,128)(2,1)}, u32[]{:S(2)}, u32[]{:S(2)}) collective-permute-start(bf16[128,896]{1,0:T(8,128)(2,1)} %step_g.12.args_8_.args_3_), channel_id=1, source_target_pairs={{0,4},{4,0},{8,12},{12,8},{1,5},{5,1},{9,13},{13,9},{2,6},{6,2},{1... | collective-permute-start | bytes 688136 | tf_op jit(solution)/shard_map/ppermute | solution.py:21
  90.2 27.2 %collective-permute-start.21 = (bf16[2,256,768]{2,1,0:T(8,128)(2,1)}, bf16[2,256,768]{2,1,0:T(8,128)(2,1)}, u32[]{:S(2)}, u32[]{:S(2)}) collective-permute-start(bf16[2,256,768]{2,1,0:T(8,128)(2,1)} %get-tuple-element.83), channel_id=1, source_target_pairs={{0,4},{4,0},{8,12},{12,8},{1,5},{5,1},{9,13},{13,9},{2,6},{6,2},{1... | collective-permute-start | bytes 2359304 | tf_op jit(solution)/shard_map/ppermute | solution.py:21
  90.3 35.3 %collective-permute-start.22 = (bf16[2,256,768]{2,1,0:T(8,128)(2,1)}, bf16[2,256,768]{2,1,0:T(8,128)(2,1)}, u32[]{:S(2)}, u32[]{:S(2)}) collective-permute-start(bf16[2,256,768]{2,1,0:T(8,128)(2,1)} %step_g.15.args_4_), channel_id=1, source_target_pairs={{0,8},{4,12},{8,0},{12,4},{1,9},{5,13},{9,1},{13,5},{2,10},{6,14},... | collective-permute-start | bytes 2359304 | tf_op jit(solution)/shard_map/ppermute | solution.py:21
  102.9 31.1 %collective-permute-start.20 = (bf16[2,128,1792]{2,1,0:T(8,128)(2,1)}, bf16[2,128,1792]{2,1,0:T(8,128)(2,1)}, u32[]{:S(2)}, u32[]{:S(2)}) collective-permute-start(bf16[2,128,1792]{2,1,0:T(8,128)(2,1)} %get-tuple-element.71.args_8_), channel_id=1, source_target_pairs={{0,4},{4,0},{8,12},{12,8},{1,5},{5,1},{9,13},{13,9},{2,6},{6,2},{1... | collective-permute-start | bytes 2752520 | tf_op jit(solution)/shard_map/ppermute | solution.py:21
  103.1 12.6 %collective-permute-start.9 = (bf16[128,896]{1,0:T(8,128)(2,1)}, bf16[128,896]{1,0:T(8,128)(2,1)}, u32[]{:S(2)}, u32[]{:S(2)}) collective-permute-start(bf16[128,896]{1,0:T(8,128)(2,1)} %collective-permute-done.6.args_5_), channel_id=1, source_target_pairs={{0,4},{4,0},{8,12},{12,8},{1,5},{5,1},{9,13},{13,9},{2,6},{6,2},{1... | collective-permute-start | bytes 688136 | tf_op jit(solution)/shard_map/ppermute | solution.py:21
  115.8 25.9 %collective-permute-start.25 = (bf16[256,896]{1,0:T(8,128)(2,1)}, bf16[256,896]{1,0:T(8,128)(2,1)}, u32[]{:S(2)}, u32[]{:S(2)}) collective-permute-start(bf16[256,896]{1,0:T(8,128)(2,1)} %step_g.16.args_9_.args_3_), channel_id=1, source_target_pairs={{0,8},{4,12},{8,0},{12,4},{1,9},{5,13},{9,1},{13,5},{2,10},{6,14},... | collective-permute-start | bytes 1376264 | tf_op jit(solution)/shard_map/ppermute | solution.py:21
  131.9 10.5 %collective-permute-start.28 = (bf16[256,768]{1,0:T(8,128)(2,1)}, bf16[256,768]{1,0:T(8,128)(2,1)}, u32[]{:S(2)}, u32[]{:S(2)}) collective-permute-start(bf16[256,768]{1,0:T(8,128)(2,1)} %step_g.17.args_5_.args_7_), channel_id=1, source_target_pairs={{0,8},{4,12},{8,0},{12,4},{1,9},{5,13},{9,1},{13,5},{2,10},{6,14},... | collective-permute-start | bytes 1179656 | tf_op jit(solution)/shard_map/ppermute | solution.py:21
  141.8 23.1 %collective-permute-start.23 = (bf16[2,128,1792]{2,1,0:T(8,128)(2,1)}, bf16[2,128,1792]{2,1,0:T(8,128)(2,1)}, u32[]{:S(2)}, u32[]{:S(2)}) collective-permute-start(bf16[2,128,1792]{2,1,0:T(8,128)(2,1)} %get-tuple-element.90.args_11_), channel_id=1, source_target_pairs={{0,8},{4,12},{8,0},{12,4},{1,9},{5,13},{9,1},{13,5},{2,10},{6,14},... | collective-permute-start | bytes 2752520 | tf_op jit(solution)/shard_map/ppermute | solution.py:21
  142.5 17.2 %collective-permute-start.19 = (bf16[2,128,1664]{2,1,0:T(8,128)(2,1)}, bf16[2,128,1664]{2,1,0:T(8,128)(2,1)}, u32[]{:S(2)}, u32[]{:S(2)}) collective-permute-start(bf16[2,128,1664]{2,1,0:T(8,128)(2,1)} %get-tuple-element.82), channel_id=1, source_target_pairs={{0,4},{4,0},{8,12},{12,8},{1,5},{5,1},{9,13},{13,9},{2,6},{6,2},{1... | collective-permute-start | bytes 2555912 | tf_op jit(solution)/shard_map/ppermute | solution.py:21
  158.3 15.0 %collective-permute-start.32 = (bf16[128,2048]{1,0:T(8,128)(2,1)}, bf16[128,2048]{1,0:T(8,128)(2,1)}, u32[]{:S(2)}, u32[]{:S(2)}) collective-permute-start(bf16[128,2048]{1,0:T(8,128)(2,1)} %get-tuple-element.92), channel_id=1, source_target_pairs={{0,1},{1,0},{2,3},{3,2},{4,5},{5,4},{6,7},{7,6},{8,9},{9,8},{10,11... | collective-permute-start | bytes 1572872 | tf_op jit(solution)/shard_map/ppermute | solution.py:21
  172.8 11.7 %collective-permute-start.31 = (bf16[128,1664]{1,0:T(8,128)(2,1)}, bf16[128,1664]{1,0:T(8,128)(2,1)S(1)}, u32[]{:S(2)}, u32[]{:S(2)}) collective-permute-start(bf16[128,1664]{1,0:T(8,128)(2,1)} %step_g.19.args_11_.args_15_), channel_id=1, source_target_pairs={{0,8},{4,12},{8,0},{12,4},{1,9},{5,13},{9,1},{13,5},{2,10},{6,14},... | collective-permute-start | bytes 1277960 | tf_op jit(solution)/shard_map/ppermute | solution.py:21
  175.4 26.4 %collective-permute-start.34 = (bf16[128,2048]{1,0:T(8,128)(2,1)}, bf16[128,2048]{1,0:T(8,128)(2,1)}, u32[]{:S(2)}, u32[]{:S(2)}) collective-permute-start(bf16[128,2048]{1,0:T(8,128)(2,1)} %add_convert_fusion.1), channel_id=1, source_target_pairs={{0,2},{1,3},{2,0},{3,1},{4,6},{5,7},{6,4},{7,5},{8,10},{9,11},{10,... | collective-permute-start | bytes 1572872 | tf_op jit(solution)/shard_map/ppermute | solution.py:21
  201.8 14.1 %collective-permute-start.35 = (bf16[128,2048]{1,0:T(8,128)(2,1)}, bf16[128,2048]{1,0:T(8,128)(2,1)S(1)}, u32[]{:S(2)}, u32[]{:S(2)}) collective-permute-start(bf16[128,2048]{1,0:T(8,128)(2,1)} %get-tuple-element.100), channel_id=1, source_target_pairs={{0,1},{1,0},{2,3},{3,2},{4,5},{5,4},{6,7},{7,6},{8,9},{9,8},{10,11... | collective-permute-start | bytes 1572872 | tf_op jit(solution)/shard_map/ppermute | solution.py:21
  (13 other events, 79.1 us)

commit v9 on v8

--- a/solution.py
+++ b/solution.py
@@ -192,14 +192,15 @@
 
 
 class Down:
-    def __init__(self, parts, places, width, block, columns):
-        self.parts, self.places, self.width, self.block, self.columns = parts, places, width, block, columns
+    def __init__(self, parts, places, width, block, first, columns):
+        self.parts, self.places, self.width, self.block = parts, places, width, block
+        self.first, self.columns = first, columns
         self.group, self.rows = None, sum(part[0][0].shape[0] for part in parts)
         self.outs = [jax.ShapeDtypeStruct((block, columns), jnp.bfloat16) for _ in range(self.rows // block)]
 
     def fits(self, depth, columns):
         sizes = [a.shape[1] for part in self.parts for a, _, _ in part]
-        return all(n % LANES == 0 for n in sizes) and columns % OUT_TILE == 0 and self.block % 16 == 0
+        return all(n % LANES == 0 for n in sizes) and self.columns % OUT_TILE == 0 and self.block % 16 == 0
 
     def arrays(self):
         return [a for part in self.parts for a, _, _ in part]
@@ -210,7 +211,9 @@
                 sum(
                     jnp.dot(
                         a,
-                        lax.dynamic_slice_in_dim(down_matrix, table[place] + low, a.shape[1], 0),
+                        lax.dynamic_slice_in_dim(
+                            down_matrix[:, self.first : self.first + self.columns], table[place] + low, a.shape[1], 0
+                        ),
                         preferred_element_type=jnp.float32,
                     )
                     for a, place, low in part
@@ -240,8 +243,9 @@
             return pl.ds(pl.multiple_of(j * OUT_TILE, LANES), OUT_TILE)
 
         def weights(p, j):
+            taken = pl.ds(pl.multiple_of(self.first + j * OUT_TILE, LANES), OUT_TILE)
             return pltpu.make_async_copy(
-                refs["down"].at[pl.ds(pl.multiple_of(table[self.places[p]], LANES), width), columns(j)],
+                refs["down"].at[pl.ds(pl.multiple_of(table[self.places[p]], LANES), width), taken],
                 dbuf.at[j, pl.ds(p * width, width)],
                 dsem.at[p, j],
             )
@@ -372,8 +376,9 @@
     ("x1",),
     ("t", "h0"),
     ("h1",),
-    ("r0", "s2", "s3"),
-    ("r1", "x2"),
+    ("r0", "s2"),
+    ("s3",),
+    ("r1", "x2", "long"),
     ("x3",),
     ("b", "s4"),
     ("h2",),
@@ -381,7 +386,8 @@
     ("x4",),
     ("r2", "r3", "d1"),
     ("h4",),
-    ("z", "r4", "d02"),
+    ("z", "r4", "d02l"),
+    ("d02r",),
 )
 
 
@@ -428,11 +434,12 @@
             recvs = [st["lent"][-1], *st["far"]]
             return [GateUp(group, 0, low, n, recvs, squares=squares[g], at=jobs[firsts[g]][2], features=features)]
 
-    def down(gs):
+    def down(gs, half):
         parts = [
             [(h, q, jobs[i][1]) for i, st in enumerate(state) if jobs[i][0] == g for h, q in st["pieces"]] for g in gs
         ]
-        return Down(parts, list(range(n_gx)), width, block, columns)
+        low, high = {"l": (0, columns // 2), "r": (columns // 2, columns)}.get(half, (0, columns))
+        return Down(parts, list(range(n_gx)), width, block, low, high - low)
 
     def deliver(kind, job, outs):
         g, st = jobs[job][0], state[job]
@@ -457,7 +464,7 @@
         state[job]["pieces"] += [(core(h), k ^ 1) for h, k in zip(crossed, far)]
 
     def reduce_over_gy():
-        parts = dict(zip(sets[1], totals[1]))
+        parts = dict(zip(sets[1], totals[1][0]))
         mask = 1
         while mask < n_gy:
             for j in [j for j in parts if j & mask]:
@@ -483,7 +490,7 @@
         for name in names:
             if name == "long":
                 continue
-            kind, job = name[0], int(name[1:] or 0)
+            kind, job = name[0], int(name[1:].rstrip("lr") or 0)
             if kind == "r":
                 forward(job)
                 continue
@@ -500,7 +507,8 @@
             if kind in "tfbz":
                 continue
             if kind == "d":
-                items.append((kind, [int(g) for g in name[1:]], [down([int(g) for g in name[1:]])]))
+                gs = [int(g) for g in name[1:] if g.isdigit()]
+                items.append((kind, gs, [down(gs, name[-1])]))
             else:
                 items.append((kind, job, phases_of(kind, job)))
         results = run([p for _, _, ps in items for p in ps], table, gate_matrix, up_matrix, down_matrix, chain, work)
@@ -511,11 +519,18 @@
                 deliver(kind, job, outs)
                 continue
             for g in job:
-                totals[g] = [outs[0].pop(0) for _ in sets[g]]
-
-    landed, last = lax.optimization_barrier((landed, totals[2][0]))
-    landed.append(swap(last, "gy", n_gy, 1))
-    return sum(part.astype(jnp.float32) for part in [totals[0][0], *landed]).astype(jnp.bfloat16)
+                totals.setdefault(g, []).append([outs[0].pop(0) for _ in sets[g]])
+
+    lefts, rights = ([total[i][0] for total in (totals[0], totals[2])] for i in (0, 1))
+    left = swap(lefts[1], "gy", n_gy, 1)
+    landed, last = lax.optimization_barrier((landed, rights[1]))
+    right = swap(last, "gy", n_gy, 1)
+    middle = columns // 2
+    halves = []
+    for low, parts in ((0, [lefts[0], left]), (middle, [rights[0], right])):
+        parts += [part[:, low : low + parts[0].shape[1]] for part in landed]
+        halves.append(sum(part.astype(jnp.float32) for part in parts).astype(jnp.bfloat16))
+    return jnp.concatenate(halves, axis=1)
 
 
 def solution(mesh):

time: 218 us -> 216 us (level)
  waiting for transfers between devices: 54.4 us -> 43.5 us
  Pallas kernels: 130 us -> 139 us
    ppermute x36 -> x37, waiting for transfers between devices: 54.4 us -> 43.5 us  [swap(): return lax.ppermute(value, axis, [(i, i ^ mask) for i in range(size)])]
    pallas_call x16 -> x18, Pallas kernels: 130 us -> 139 us  [run(): pl.pallas_call(kernel, out_shape=outs, in_specs=[SMEM] + [ANY] * len(oper...]
    ppermute x36 -> x37, starting transfers between devices: 27.5 us -> 27.2 us  [swap(): return lax.ppermute(value, axis, [(i, i ^ mask) for i in range(size)])]
  transfers between devices with their start and end apart: 36 -> 37, of which waited for: 12 -> 11; matrix products, arithmetic and copies ran while one was open for 1% -> 1% of each run, Pallas kernels for 50% -> 57%
where the time goes in v9:
time: 216 us
  Pallas kernels  139 us (64%)
  waiting for transfers between devices  43.5 us (20%)
  starting transfers between devices  27.2 us (13%)
  other arithmetic  4.31 us (2%)
    pallas_call x18, Pallas kernels, run(): pl.pallas_call(kernel, out_shape=outs, in_specs=[SMEM] + [ANY] * len(oper...  139 us
    ppermute x37, waiting for transfers between devices, swap(): return lax.ppermute(value, axis, [(i, i ^ mask) for i in range(size)])  43.5 us
    ppermute x37, starting transfers between devices, swap(): return lax.ppermute(value, axis, [(i, i ^ mask) for i in range(size)])  27.2 us
  transfers between devices with their start and end apart: 37, of which 11 were waited for; matrix products, arithmetic and copies ran while one was open for 1% of the time, Pallas kernels for 57%

profile of v9, /device:TPU:0, one launch (start us, length us, event | category | flops | bytes accessed | tf_op | source)
XLA Modules:
  0.0 215.9 jit_solution(16214632233560035270)
XLA Ops:
  0.7 7.8 %step_gg.5 = (bf16[2,128,1024]{2,1,0:T(8,128)(2,1)}, bf16[2,128,896]{2,1,0:T(8,128)(2,1)}) custom-call(s32[5]{0:T(128)} %pad_add_fusion.table_ref, bf16[2048,6656]{1,0:T(8,128)(2,1)} %args_0_.38, bf16[2048,6656]{1,0:T(8,128)(2,1)} %args_1_.38, bf16[6656,2048]{1,0:T(8,128)(2,1)} %args_2_.38, bf16[128,2048]{1,0:T(8,128)(2,1)} %args_3_.14, ...), custom_call_target="tpu_custom_call" | custom-call | flops 1000 | bytes 1000 | tf_op jit(solution)/shard_map/step_gg/pallas_call | solution.py:351
  12.6 7.1 %step_gg.6 = (bf16[2,128,768]{2,1,0:T(8,128)(2,1)}, bf16[2,128,768]{2,1,0:T(8,128)(2,1)}) custom-call(s32[5]{0:T(128)} %pad_add_fusion.table_ref, bf16[2048,6656]{1,0:T(8,128)(2,1)} %args_0_.38, bf16[2048,6656]{1,0:T(8,128)(2,1)} %args_1_.38, bf16[6656,2048]{1,0:T(8,128)(2,1)} %args_2_.38, bf16[128,2048]{1,0:T(8,128)(2,1)} %args_3_.14, ...), custom_call_target="tpu_custom_call" | custom-call | flops 1000 | bytes 1000 | tf_op jit(solution)/shard_map/step_gg/pallas_call | solution.py:351
  20.1 5.5 %step_g.10 = (bf16[2,128,1024]{2,1,0:T(8,128)(2,1)}, f32[128,128]{1,0:T(8,128)}) custom-call(s32[5]{0:T(128)} %pad_add_fusion.table_ref, bf16[2048,6656]{1,0:T(8,128)(2,1)} %args_0_.38, bf16[2048,6656]{1,0:T(8,128)(2,1)} %args_1_.38, bf16[6656,2048]{1,0:T(8,128)(2,1)} %args_2_.38, bf16[128,2048]{1,0:T(8,128)(2,1)} %args_3_.14, ...), custom_call_target="tpu_custom_call" | custom-call | flops 1000 | bytes 1000 | tf_op jit(solution)/shard_map/step_g/pallas_call | solution.py:351
  27.2 5.1 %step_g.11.args_7_ = bf16[2,128,768]{2,1,0:T(8,128)(2,1)} custom-call(s32[5]{0:T(128)} %pad_add_fusion.table_ref, bf16[2048,6656]{1,0:T(8,128)(2,1)} %args_0_.38, bf16[2048,6656]{1,0:T(8,128)(2,1)} %args_1_.38, bf16[6656,2048]{1,0:T(8,128)(2,1)} %args_2_.38, bf16[128,2048]{1,0:T(8,128)(2,1)} %args_3_.14, ...), custom_call_target="tpu_custom_call" | custom-call | flops 1000 | bytes 1000 | tf_op jit(solution)/shard_map/step_g/pallas_call | solution.py:351
  32.2 4.5 %collective-permute-done.3.args_3_ = bf16[128,2048]{1,0:T(8,128)(2,1)} collective-permute-done((bf16[128,2048]{1,0:T(8,128)(2,1)}, bf16[128,2048]{1,0:T(8,128)(2,1)}, u32[]{:S(2)}, u32[]{:S(2)}) %collective-permute-start.3) | collective-permute-done | bytes 524320 | tf_op jit(solution)/shard_map/ppermute | solution.py:21
  40.0 5.7 %step_g.12.args_8_.args_3_ = bf16[128,896]{1,0:T(8,128)(2,1)} custom-call(s32[5]{0:T(128)} %pad_add_fusion.table_ref, bf16[2048,6656]{1,0:T(8,128)(2,1)} %args_0_.38, bf16[2048,6656]{1,0:T(8,128)(2,1)} %args_1_.38, bf16[6656,2048]{1,0:T(8,128)(2,1)} %args_2_.38, bf16[128,2048]{1,0:T(8,128)(2,1)} %args_3_.14, ...), custom_call_target="tpu_custom_call" | custom-call | flops 1000 | bytes 1000 | tf_op jit(solution)/shard_map/step_g/pallas_call | solution.py:351
  49.7 5.2 %step_g.13.args_5_.args_7_ = bf16[128,768]{1,0:T(8,128)(2,1)} custom-call(s32[5]{0:T(128)} %pad_add_fusion.table_ref, bf16[2048,6656]{1,0:T(8,128)(2,1)} %args_0_.38, bf16[2048,6656]{1,0:T(8,128)(2,1)} %args_1_.38, bf16[6656,2048]{1,0:T(8,128)(2,1)} %args_2_.38, bf16[128,2048]{1,0:T(8,128)(2,1)} %args_3_.14, ...), custom_call_target="tpu_custom_call" | custom-call | flops 1000 | bytes 1000 | tf_op jit(solution)/shard_map/step_g/pallas_call | solution.py:351
  54.9 8.7 %step_gg.7 = (bf16[2,256,1024]{2,1,0:T(8,128)(2,1)}, bf16[2,256,896]{2,1,0:T(8,128)(2,1)}) custom-call(s32[5]{0:T(128)} %pad_add_fusion.table_ref, bf16[2048,6656]{1,0:T(8,128)(2,1)} %args_0_.38, bf16[2048,6656]{1,0:T(8,128)(2,1)} %args_1_.38, bf16[6656,2048]{1,0:T(8,128)(2,1)} %args_2_.38, bf16[128,2048]{1,0:T(8,128)(2,1)} %collective-permute-done.3.args_3_, ...), custom_call_target="tpu_custom_call" | custom-call | flops 1000 | bytes 1000 | tf_op jit(solution)/shard_map/step_gg/pallas_call | solution.py:351
  66.6 7.8 %step_gg.8 = (bf16[2,256,768]{2,1,0:T(8,128)(2,1)}, bf16[2,256,768]{2,1,0:T(8,128)(2,1)}) custom-call(s32[5]{0:T(128)} %pad_add_fusion.table_ref, bf16[2048,6656]{1,0:T(8,128)(2,1)} %args_0_.38, bf16[2048,6656]{1,0:T(8,128)(2,1)} %args_1_.38, bf16[6656,2048]{1,0:T(8,128)(2,1)} %args_2_.38, bf16[128,2048]{1,0:T(8,128)(2,1)} %collective-permute-done.3.args_3_, ...), custom_call_target="tpu_custom_call" | custom-call | flops 1000 | bytes 1000 | tf_op jit(solution)/shard_map/step_gg/pallas_call | solution.py:351
  75.0 6.4 %step_g.14 = (bf16[2,256,1024]{2,1,0:T(8,128)(2,1)}, f32[256,128]{1,0:T(8,128)}) custom-call(s32[5]{0:T(128)} %pad_add_fusion.table_ref, bf16[2048,6656]{1,0:T(8,128)(2,1)} %args_0_.38, bf16[2048,6656]{1,0:T(8,128)(2,1)} %args_1_.38, bf16[6656,2048]{1,0:T(8,128)(2,1)} %args_2_.38, bf16[128,2048]{1,0:T(8,128)(2,1)} %collective-permute-done.3.args_3_, ...), custom_call_target="tpu_custom_call" | custom-call | flops 99999997952 | bytes 1000 | tf_op jit(solution)/shard_map/step_g/pallas_call | solution.py:351
  82.4 5.8 %step_g.15.args_4_ = bf16[2,256,768]{2,1,0:T(8,128)(2,1)} custom-call(s32[5]{0:T(128)} %pad_add_fusion.table_ref, bf16[2048,6656]{1,0:T(8,128)(2,1)} %args_0_.38, bf16[2048,6656]{1,0:T(8,128)(2,1)} %args_1_.38, bf16[6656,2048]{1,0:T(8,128)(2,1)} %args_2_.38, bf16[128,2048]{1,0:T(8,128)(2,1)} %collective-permute-done.3.args_3_, ...), custom_call_target="tpu_custom_call" | custom-call | flops 1000 | bytes 1000 | tf_op jit(solution)/shard_map/step_g/pallas_call | solution.py:351
  89.9 12.0 %step_gg.9 = (bf16[2,128,1792]{2,1,0:T(8,128)(2,1)}, bf16[2,128,1664]{2,1,0:T(8,128)(2,1)}) custom-call(s32[5]{0:T(128)} %pad_add_fusion.table_ref, bf16[2048,6656]{1,0:T(8,128)(2,1)} %args_0_.38, bf16[2048,6656]{1,0:T(8,128)(2,1)} %args_1_.38, bf16[6656,2048]{1,0:T(8,128)(2,1)} %args_2_.38, bf16[128,2048]{1,0:T(8,128)(2,1)} %collective-permute-done.15.args_3_, ...), custom_call_target="tpu_custom_call" | custom-call | flops 1000 | bytes 1000 | tf_op jit(solution)/shard_map/step_gg/pallas_call | solution.py:351
  102.5 5.2 %collective-permute-done.14.args_6_.args_8_ = bf16[2,256,1024]{2,1,0:T(8,128)(2,1)} collective-permute-done((bf16[2,256,1024]{2,1,0:T(8,128)(2,1)}, bf16[2,256,1024]{2,1,0:T(8,128)(2,1)}, u32[]{:S(2)}, u32[]{:S(2)}) %collective-permute-start.14) | collective-permute-done | bytes 1048608 | tf_op jit(solution)/shard_map/ppermute | solution.py:21
  107.7 7.0 %step_g.16.args_9_.args_3_ = bf16[256,896]{1,0:T(8,128)(2,1)} custom-call(s32[5]{0:T(128)} %pad_add_fusion.table_ref, bf16[2048,6656]{1,0:T(8,128)(2,1)} %args_0_.38, bf16[2048,6656]{1,0:T(8,128)(2,1)} %args_1_.38, bf16[6656,2048]{1,0:T(8,128)(2,1)} %args_2_.38, bf16[128,2048]{1,0:T(8,128)(2,1)} %collective-permute-done.3.args_3_, ...), custom_call_target="tpu_custom_call" | custom-call | flops 1000 | bytes 1000 | tf_op jit(solution)/shard_map/step_g/pallas_call | solution.py:351
  115.3 9.3 %collective-permute-done.22.args_6_ = bf16[2,256,768]{2,1,0:T(8,128)(2,1)} collective-permute-done((bf16[2,256,768]{2,1,0:T(8,128)(2,1)}, bf16[2,256,768]{2,1,0:T(8,128)(2,1)}, u32[]{:S(2)}, u32[]{:S(2)}) %collective-permute-start.22) | collective-permute-done | bytes 786464 | tf_op jit(solution)/shard_map/ppermute | solution.py:21
  124.6 6.3 %step_g.17.args_5_.args_7_ = bf16[256,768]{1,0:T(8,128)(2,1)} custom-call(s32[5]{0:T(128)} %pad_add_fusion.table_ref, bf16[2048,6656]{1,0:T(8,128)(2,1)} %args_0_.38, bf16[2048,6656]{1,0:T(8,128)(2,1)} %args_1_.38, bf16[6656,2048]{1,0:T(8,128)(2,1)} %args_2_.38, bf16[128,2048]{1,0:T(8,128)(2,1)} %collective-permute-done.3.args_3_, ...), custom_call_target="tpu_custom_call" | custom-call | flops 1000 | bytes 1000 | tf_op jit(solution)/shard_map/step_g/pallas_call | solution.py:351
  131.9 7.7 %step_g.18 = (bf16[2,128,1792]{2,1,0:T(8,128)(2,1)}, f32[128,128]{1,0:T(8,128)}) custom-call(s32[5]{0:T(128)} %pad_add_fusion.table_ref, bf16[2048,6656]{1,0:T(8,128)(2,1)} %args_0_.38, bf16[2048,6656]{1,0:T(8,128)(2,1)} %args_1_.38, bf16[6656,2048]{1,0:T(8,128)(2,1)} %args_2_.38, bf16[128,2048]{1,0:T(8,128)(2,1)} %collective-permute-done.15.args_3_, ...), custom_call_target="tpu_custom_call" | custom-call | flops 1000 | bytes 1000 | tf_op jit(solution)/shard_map/step_g/pallas_call | solution.py:351
  144.0 13.8 %step_d.3 = (bf16[128,2048]{1,0:T(8,128)(2,1)}, bf16[128,2048]{1,0:T(8,128)(2,1)}) custom-call(s32[5]{0:T(128)} %pad_add_fusion.table_ref, bf16[2048,6656]{1,0:T(8,128)(2,1)} %args_0_.38, bf16[2048,6656]{1,0:T(8,128)(2,1)} %args_1_.38, bf16[6656,2048]{1,0:T(8,128)(2,1)} %args_2_.38, bf16[256,896]{1,0:T(8,128)(2,1)} %step_g.16.args_9_.args_3_, ...), custom_call_target="tpu_custom_call" | custom-call | flops 1000 | bytes 1000 | tf_op jit(solution)/shard_map/step_d/pallas_call | solution.py:351
  158.6 4.2 %collective-permute-done.23.args_5_ = bf16[2,128,1792]{2,1,0:T(8,128)(2,1)} collective-permute-done((bf16[2,128,1792]{2,1,0:T(8,128)(2,1)}, bf16[2,128,1792]{2,1,0:T(8,128)(2,1)}, u32[]{:S(2)}, u32[]{:S(2)}) %collective-permute-start.23) | collective-permute-done | bytes 917536 | tf_op jit(solution)/shard_map/ppermute | solution.py:21
  162.8 7.9 %step_g.19.args_11_.args_15_ = bf16[128,1664]{1,0:T(8,128)(2,1)} custom-call(s32[5]{0:T(128)} %pad_add_fusion.table_ref, bf16[2048,6656]{1,0:T(8,128)(2,1)} %args_0_.38, bf16[2048,6656]{1,0:T(8,128)(2,1)} %args_1_.38, bf16[6656,2048]{1,0:T(8,128)(2,1)} %args_2_.38, bf16[128,2048]{1,0:T(8,128)(2,1)} %collective-permute-done.15.args_3_, ...), custom_call_target="tpu_custom_call" | custom-call | flops 1000 | bytes 1000 | tf_op jit(solution)/shard_map/step_g/pallas_call | solution.py:351
  176.6 5.7 %collective-permute-done.31.args_13_ = bf16[128,1664]{1,0:T(8,128)(2,1)S(1)} collective-permute-done((bf16[128,1664]{1,0:T(8,128)(2,1)}, bf16[128,1664]{1,0:T(8,128)(2,1)S(1)}, u32[]{:S(2)}, u32[]{:S(2)}) %collective-permute-start.31) | collective-permute-done | bytes 426016 | tf_op jit(solution)/shard_map/ppermute | solution.py:21
  185.0 9.7 %step_d.4 = (bf16[128,1024]{1,0:T(8,128)(2,1)}, bf16[128,1024]{1,0:T(8,128)(2,1)}) custom-call(s32[5]{0:T(128)} %pad_add_fusion.table_ref, bf16[2048,6656]{1,0:T(8,128)(2,1)} %args_0_.38, bf16[2048,6656]{1,0:T(8,128)(2,1)} %args_1_.38, bf16[6656,2048]{1,0:T(8,128)(2,1)} %args_2_.38, bf16[128,896]{1,0:T(8,128)(2,1)} %step_g.12.args_8_.args_3_, ...), custom_call_target="tpu_custom_call" | custom-call | flops 1000 | bytes 1000 | tf_op jit(solution)/shard_map/step_d/pallas_call | solution.py:351
  195.5 9.7 %step_d.5 = (bf16[128,1024]{1,0:T(8,128)(2,1)}, bf16[128,1024]{1,0:T(8,128)(2,1)}) custom-call(s32[5]{0:T(128)} %pad_add_fusion.table_ref, bf16[2048,6656]{1,0:T(8,128)(2,1)} %args_0_.38, bf16[2048,6656]{1,0:T(8,128)(2,1)} %args_1_.38, bf16[6656,2048]{1,0:T(8,128)(2,1)} %args_2_.38, bf16[128,896]{1,0:T(8,128)(2,1)} %step_g.12.args_8_.args_3_, ...), custom_call_target="tpu_custom_call" | custom-call | flops 1000 | bytes 1000 | tf_op jit(solution)/shard_map/step_d/pallas_call | solution.py:351
  206.5 7.0 %collective-permute-done.36 = bf16[128,1024]{1,0:T(8,128)(2,1)S(1)} collective-permute-done((bf16[128,1024]{1,0:T(8,128)(2,1)}, bf16[128,1024]{1,0:T(8,128)(2,1)S(1)}, u32[]{:S(2)}, u32[]{:S(2)}) %collective-permute-start.36) | collective-permute-done | bytes 262176 | tf_op jit(solution)/shard_map/ppermute | solution.py:21
  (77 shorter events, 40.7 us)
Async XLA Ops:
  8.5 11.7 %collective-permute-start.1 = (bf16[2,128,1024]{2,1,0:T(8,128)(2,1)}, bf16[2,128,1024]{2,1,0:T(8,128)(2,1)}, u32[]{:S(2)}, u32[]{:S(2)}) collective-permute-start(bf16[2,128,1024]{2,1,0:T(8,128)(2,1)} %get-tuple-element.56.args_4_), channel_id=1, source_target_pairs={{0,4},{4,0},{8,12},{12,8},{1,5},{5,1},{9,13},{13,9},{2,6},{6,2},{1... | collective-permute-start | bytes 1572872 | tf_op jit(solution)/shard_map/ppermute | solution.py:21
  9.0 27.7 %collective-permute-start.3 = (bf16[128,2048]{1,0:T(8,128)(2,1)}, bf16[128,2048]{1,0:T(8,128)(2,1)}, u32[]{:S(2)}, u32[]{:S(2)}) collective-permute-start(bf16[128,2048]{1,0:T(8,128)(2,1)} %args_3_.14), channel_id=1, source_target_pairs={{0,2},{1,3},{2,0},{3,1},{4,6},{5,7},{6,4},{7,5},{8,10},{9,11},{10,... | collective-permute-start | bytes 1572872 | tf_op jit(solution)/shard_map/ppermute | solution.py:21
  25.6 14.4 %collective-permute-start.2 = (bf16[2,128,1024]{2,1,0:T(8,128)(2,1)}, bf16[2,128,1024]{2,1,0:T(8,128)(2,1)}, u32[]{:S(2)}, u32[]{:S(2)}) collective-permute-start(bf16[2,128,1024]{2,1,0:T(8,128)(2,1)} %get-tuple-element.58.args_5_), channel_id=1, source_target_pairs={{0,8},{4,12},{8,0},{12,4},{1,9},{5,13},{9,1},{13,5},{2,10},{6,14},... | collective-permute-start | bytes 1572872 | tf_op jit(solution)/shard_map/ppermute | solution.py:21
  27.2 11.8 %collective-permute-start = (bf16[2,128,896]{2,1,0:T(8,128)(2,1)}, bf16[2,128,896]{2,1,0:T(8,128)(2,1)}, u32[]{:S(2)}, u32[]{:S(2)}) collective-permute-start(bf16[2,128,896]{2,1,0:T(8,128)(2,1)} %get-tuple-element.55), channel_id=1, source_target_pairs={{0,4},{4,0},{8,12},{12,8},{1,5},{5,1},{9,13},{13,9},{2,6},{6,2},{1... | collective-permute-start | bytes 1376264 | tf_op jit(solution)/shard_map/ppermute | solution.py:21
  36.7 18.2 %collective-permute-start.10 = (bf16[128,2048]{1,0:T(8,128)(2,1)}, bf16[128,2048]{1,0:T(8,128)(2,1)}, u32[]{:S(2)}, u32[]{:S(2)}) collective-permute-start(bf16[128,2048]{1,0:T(8,128)(2,1)} %collective-permute-done.3.args_3_), channel_id=1, source_target_pairs={{0,1},{1,0},{2,3},{3,2},{4,5},{5,4},{6,7},{7,6},{8,9},{9,8},{10,11... | collective-permute-start | bytes 1572872 | tf_op jit(solution)/shard_map/ppermute | solution.py:21
  37.5 12.2 %collective-permute-start.8 = (bf16[2,128,768]{2,1,0:T(8,128)(2,1)}, bf16[2,128,768]{2,1,0:T(8,128)(2,1)}, u32[]{:S(2)}, u32[]{:S(2)}) collective-permute-start(bf16[2,128,768]{2,1,0:T(8,128)(2,1)} %step_g.11.args_7_), channel_id=1, source_target_pairs={{0,8},{4,12},{8,0},{12,4},{1,9},{5,13},{9,1},{13,5},{2,10},{6,14},... | collective-permute-start | bytes 1179656 | tf_op jit(solution)/shard_map/ppermute | solution.py:21
  63.6 11.3 %collective-permute-start.12 = (bf16[2,256,1024]{2,1,0:T(8,128)(2,1)}, bf16[2,256,1024]{2,1,0:T(8,128)(2,1)}, u32[]{:S(2)}, u32[]{:S(2)}) collective-permute-start(bf16[2,256,1024]{2,1,0:T(8,128)(2,1)} %get-tuple-element.66.args_5_), channel_id=1, source_target_pairs={{0,4},{4,0},{8,12},{12,8},{1,5},{5,1},{9,13},{13,9},{2,6},{6,2},{1... | collective-permute-start | bytes 3145736 | tf_op jit(solution)/shard_map/ppermute | solution.py:21
  65.3 22.9 %collective-permute-start.15 = (bf16[128,2048]{1,0:T(8,128)(2,1)}, bf16[128,2048]{1,0:T(8,128)(2,1)}, u32[]{:S(2)}, u32[]{:S(2)}) collective-permute-start(bf16[128,2048]{1,0:T(8,128)(2,1)} %args_3_.14), channel_id=1, source_target_pairs={{0,1},{1,0},{2,3},{3,2},{4,5},{5,4},{6,7},{7,6},{8,9},{9,8},{10,11... | collective-permute-start | bytes 1572872 | tf_op jit(solution)/shard_map/ppermute | solution.py:21
  74.5 27.7 %collective-permute-start.11 = (bf16[2,256,896]{2,1,0:T(8,128)(2,1)}, bf16[2,256,896]{2,1,0:T(8,128)(2,1)}, u32[]{:S(2)}, u32[]{:S(2)}) collective-permute-start(bf16[2,256,896]{2,1,0:T(8,128)(2,1)} %get-tuple-element.65), channel_id=1, source_target_pairs={{0,4},{4,0},{8,12},{12,8},{1,5},{5,1},{9,13},{13,9},{2,6},{6,2},{1... | collective-permute-start | bytes 2752520 | tf_op jit(solution)/shard_map/ppermute | solution.py:21
  81.3 26.4 %collective-permute-start.14 = (bf16[2,256,1024]{2,1,0:T(8,128)(2,1)}, bf16[2,256,1024]{2,1,0:T(8,128)(2,1)}, u32[]{:S(2)}, u32[]{:S(2)}) collective-permute-start(bf16[2,256,1024]{2,1,0:T(8,128)(2,1)} %get-tuple-element.69.args_6_), channel_id=1, source_target_pairs={{0,8},{4,12},{8,0},{12,4},{1,9},{5,13},{9,1},{13,5},{2,10},{6,14},... | collective-permute-start | bytes 3145736 | tf_op jit(solution)/shard_map/ppermute | solution.py:21
  81.9 20.1 %collective-permute-start.5 = (bf16[128,896]{1,0:T(8,128)(2,1)}, bf16[128,896]{1,0:T(8,128)(2,1)}, u32[]{:S(2)}, u32[]{:S(2)}) collective-permute-start(bf16[128,896]{1,0:T(8,128)(2,1)} %step_g.12.args_8_.args_3_), channel_id=1, source_target_pairs={{0,4},{4,0},{8,12},{12,8},{1,5},{5,1},{9,13},{13,9},{2,6},{6,2},{1... | collective-permute-start | bytes 688136 | tf_op jit(solution)/shard_map/ppermute | solution.py:21
  88.2 27.1 %collective-permute-start.21 = (bf16[2,256,768]{2,1,0:T(8,128)(2,1)}, bf16[2,256,768]{2,1,0:T(8,128)(2,1)}, u32[]{:S(2)}, u32[]{:S(2)}) collective-permute-start(bf16[2,256,768]{2,1,0:T(8,128)(2,1)} %get-tuple-element.85), channel_id=1, source_target_pairs={{0,4},{4,0},{8,12},{12,8},{1,5},{5,1},{9,13},{13,9},{2,6},{6,2},{1... | collective-permute-start | bytes 2359304 | tf_op jit(solution)/shard_map/ppermute | solution.py:21
  88.3 36.3 %collective-permute-start.22 = (bf16[2,256,768]{2,1,0:T(8,128)(2,1)}, bf16[2,256,768]{2,1,0:T(8,128)(2,1)}, u32[]{:S(2)}, u32[]{:S(2)}) collective-permute-start(bf16[2,256,768]{2,1,0:T(8,128)(2,1)} %step_g.15.args_4_), channel_id=1, source_target_pairs={{0,8},{4,12},{8,0},{12,4},{1,9},{5,13},{9,1},{13,5},{2,10},{6,14},... | collective-permute-start | bytes 2359304 | tf_op jit(solution)/shard_map/ppermute | solution.py:21
  101.9 29.9 %collective-permute-start.20 = (bf16[2,128,1792]{2,1,0:T(8,128)(2,1)}, bf16[2,128,1792]{2,1,0:T(8,128)(2,1)}, u32[]{:S(2)}, u32[]{:S(2)}) collective-permute-start(bf16[2,128,1792]{2,1,0:T(8,128)(2,1)} %get-tuple-element.73.args_8_), channel_id=1, source_target_pairs={{0,4},{4,0},{8,12},{12,8},{1,5},{5,1},{9,13},{13,9},{2,6},{6,2},{1... | collective-permute-start | bytes 2752520 | tf_op jit(solution)/shard_map/ppermute | solution.py:21
  102.2 12.6 %collective-permute-start.9 = (bf16[128,896]{1,0:T(8,128)(2,1)}, bf16[128,896]{1,0:T(8,128)(2,1)}, u32[]{:S(2)}, u32[]{:S(2)}) collective-permute-start(bf16[128,896]{1,0:T(8,128)(2,1)} %collective-permute-done.6.args_5_), channel_id=1, source_target_pairs={{0,4},{4,0},{8,12},{12,8},{1,5},{5,1},{9,13},{13,9},{2,6},{6,2},{1... | collective-permute-start | bytes 688136 | tf_op jit(solution)/shard_map/ppermute | solution.py:21
  114.7 24.9 %collective-permute-start.25 = (bf16[256,896]{1,0:T(8,128)(2,1)}, bf16[256,896]{1,0:T(8,128)(2,1)}, u32[]{:S(2)}, u32[]{:S(2)}) collective-permute-start(bf16[256,896]{1,0:T(8,128)(2,1)} %step_g.16.args_9_.args_3_), channel_id=1, source_target_pairs={{0,8},{4,12},{8,0},{12,4},{1,9},{5,13},{9,1},{13,5},{2,10},{6,14},... | collective-permute-start | bytes 1376264 | tf_op jit(solution)/shard_map/ppermute | solution.py:21
  130.9 11.1 %collective-permute-start.28 = (bf16[256,768]{1,0:T(8,128)(2,1)}, bf16[256,768]{1,0:T(8,128)(2,1)}, u32[]{:S(2)}, u32[]{:S(2)}) collective-permute-start(bf16[256,768]{1,0:T(8,128)(2,1)} %step_g.17.args_5_.args_7_), channel_id=1, source_target_pairs={{0,8},{4,12},{8,0},{12,4},{1,9},{5,13},{9,1},{13,5},{2,10},{6,14},... | collective-permute-start | bytes 1179656 | tf_op jit(solution)/shard_map/ppermute | solution.py:21
  131.4 11.1 %collective-permute-start.24 = (bf16[256,896]{1,0:T(8,128)(2,1)}, bf16[256,896]{1,0:T(8,128)(2,1)}, u32[]{:S(2)}, u32[]{:S(2)}) collective-permute-start(bf16[256,896]{1,0:T(8,128)(2,1)} %step_g.16.args_9_.args_3_), channel_id=1, source_target_pairs={{0,4},{4,0},{8,12},{12,8},{1,5},{5,1},{9,13},{13,9},{2,6},{6,2},{1... | collective-permute-start | bytes 1376264 | tf_op jit(solution)/shard_map/ppermute | solution.py:21
  139.7 23.1 %collective-permute-start.23 = (bf16[2,128,1792]{2,1,0:T(8,128)(2,1)}, bf16[2,128,1792]{2,1,0:T(8,128)(2,1)}, u32[]{:S(2)}, u32[]{:S(2)}) collective-permute-start(bf16[2,128,1792]{2,1,0:T(8,128)(2,1)} %get-tuple-element.92.args_11_), channel_id=1, source_target_pairs={{0,8},{4,12},{8,0},{12,4},{1,9},{5,13},{9,1},{13,5},{2,10},{6,14},... | collective-permute-start | bytes 2752520 | tf_op jit(solution)/shard_map/ppermute | solution.py:21
  142.0 16.6 %collective-permute-start.19 = (bf16[2,128,1664]{2,1,0:T(8,128)(2,1)}, bf16[2,128,1664]{2,1,0:T(8,128)(2,1)}, u32[]{:S(2)}, u32[]{:S(2)}) collective-permute-start(bf16[2,128,1664]{2,1,0:T(8,128)(2,1)} %get-tuple-element.84), channel_id=1, source_target_pairs={{0,4},{4,0},{8,12},{12,8},{1,5},{5,1},{9,13},{13,9},{2,6},{6,2},{1... | collective-permute-start | bytes 2555912 | tf_op jit(solution)/shard_map/ppermute | solution.py:21
  157.8 14.4 %collective-permute-start.32 = (bf16[128,2048]{1,0:T(8,128)(2,1)}, bf16[128,2048]{1,0:T(8,128)(2,1)}, u32[]{:S(2)}, u32[]{:S(2)}) collective-permute-start(bf16[128,2048]{1,0:T(8,128)(2,1)} %get-tuple-element.94), channel_id=1, source_target_pairs={{0,1},{1,0},{2,3},{3,2},{4,5},{5,4},{6,7},{7,6},{8,9},{9,8},{10,11... | collective-permute-start | bytes 1572872 | tf_op jit(solution)/shard_map/ppermute | solution.py:21
  170.7 11.7 %collective-permute-start.31 = (bf16[128,1664]{1,0:T(8,128)(2,1)}, bf16[128,1664]{1,0:T(8,128)(2,1)S(1)}, u32[]{:S(2)}, u32[]{:S(2)}) collective-permute-start(bf16[128,1664]{1,0:T(8,128)(2,1)} %step_g.19.args_11_.args_15_), channel_id=1, source_target_pairs={{0,8},{4,12},{8,0},{12,4},{1,9},{5,13},{9,1},{13,5},{2,10},{6,14},... | collective-permute-start | bytes 1277960 | tf_op jit(solution)/shard_map/ppermute | solution.py:21
  174.4 30.8 %collective-permute-start.35 = (bf16[128,2048]{1,0:T(8,128)(2,1)}, bf16[128,2048]{1,0:T(8,128)(2,1)}, u32[]{:S(2)}, u32[]{:S(2)}) collective-permute-start(bf16[128,2048]{1,0:T(8,128)(2,1)} %add_convert_fusion), channel_id=1, source_target_pairs={{0,2},{1,3},{2,0},{3,1},{4,6},{5,7},{6,4},{7,5},{8,10},{9,11},{10,... | collective-permute-start | bytes 1572872 | tf_op jit(solution)/shard_map/ppermute | solution.py:21
  194.7 11.9 %collective-permute-start.34 = (bf16[128,1024]{1,0:T(8,128)(2,1)}, bf16[128,1024]{1,0:T(8,128)(2,1)}, u32[]{:S(2)}, u32[]{:S(2)}) collective-permute-start(bf16[128,1024]{1,0:T(8,128)(2,1)} %get-tuple-element.99), channel_id=1, source_target_pairs={{0,1},{1,0},{2,3},{3,2},{4,5},{5,4},{6,7},{7,6},{8,9},{9,8},{10,11... | collective-permute-start | bytes 786440 | tf_op jit(solution)/shard_map/ppermute | solution.py:21
  (15 other events, 93.9 us)

commit v10 on v9

--- a/solution.py
+++ b/solution.py
@@ -373,21 +373,20 @@
     ("s0",),
     ("s1",),
     ("x0",),
-    ("x1",),
-    ("t", "h0"),
+    ("t", "x1"),
+    ("p0", "s2"),
+    ("p1", "s3", "long"),
+    ("x2",),
+    ("h0",),
     ("h1",),
-    ("r0", "s2"),
-    ("s3",),
-    ("r1", "x2", "long"),
     ("x3",),
     ("b", "s4"),
     ("h2",),
-    ("f0", "f1", "h3"),
-    ("x4",),
-    ("r2", "r3", "d1"),
+    ("h3",),
+    ("r0", "r1", "x4"),
+    ("f0", "f1", "r2", "r3", "d1"),
     ("h4",),
-    ("z", "r4", "d02l"),
-    ("d02r",),
+    ("z", "r4", "d02"),
 )
 
 
@@ -413,7 +412,7 @@
     groups = [Group(blocks, js, block) for js in sets]
     squares = {}
     half = cut(width, 7, 13)
-    early = cut(width, 7, 13)
+    early = cut(width, 6, 13)
     jobs = [(0, 0, early), (0, early, width - early), (1, 0, half), (1, half, width - half), (2, 0, width)]
     firsts = [min(i for i, job in enumerate(jobs) if job[0] == g) for g in range(len(groups))]
     state = [dict() for _ in jobs]
@@ -497,6 +496,10 @@
             while kind == "t" and mask > 1:
                 mask //= 2
                 gather_over_gy(mask)
+            if kind == "p":
+                state[job]["far"] = tied(state[job]["far"])
+                if job == firsts[jobs[job][0]]:
+                    squares[jobs[job][0]] = (squares[jobs[job][0]][0], state[job]["far"])
             if kind == "f":
                 held, places = zip(*state[job]["pieces"])
                 state[job]["pieces"] = list(zip(tied(list(held)), places))
@@ -504,7 +507,7 @@
                 blocks[1] = tied(swap(tokens, "gy", n_gy, 1))
             if kind == "z":
                 reduce_over_gy()
-            if kind in "tfbz":
+            if kind in "tpfbz":
                 continue
             if kind == "d":
                 gs = [int(g) for g in name[1:] if g.isdigit()]
@@ -521,16 +524,9 @@
             for g in job:
                 totals.setdefault(g, []).append([outs[0].pop(0) for _ in sets[g]])
 
-    lefts, rights = ([total[i][0] for total in (totals[0], totals[2])] for i in (0, 1))
-    left = swap(lefts[1], "gy", n_gy, 1)
-    landed, last = lax.optimization_barrier((landed, rights[1]))
-    right = swap(last, "gy", n_gy, 1)
-    middle = columns // 2
-    halves = []
-    for low, parts in ((0, [lefts[0], left]), (middle, [rights[0], right])):
-        parts += [part[:, low : low + parts[0].shape[1]] for part in landed]
-        halves.append(sum(part.astype(jnp.float32) for part in parts).astype(jnp.bfloat16))
-    return jnp.concatenate(halves, axis=1)
+    landed, last = lax.optimization_barrier((landed, totals[2][0][0]))
+    landed.append(swap(last, "gy", n_gy, 1))
+    return sum(part.astype(jnp.float32) for part in [totals[0][0][0], *landed]).astype(jnp.bfloat16)
 
 
 def solution(mesh):

time: 216 us -> 212 us (0.981)
  Pallas kernels: 139 us -> 133 us
  waiting for transfers between devices: 43.5 us -> 46.5 us
    pallas_call x18 -> x17, Pallas kernels: 139 us -> 133 us  [run(): pl.pallas_call(kernel, out_shape=outs, in_specs=[SMEM] + [ANY] * len(oper...]
    ppermute x37 -> x36, waiting for transfers between devices: 43.5 us -> 46.5 us  [swap(): return lax.ppermute(value, axis, [(i, i ^ mask) for i in range(size)])]
    ppermute x37 -> x36, starting transfers between devices: 27.2 us -> 25.6 us  [swap(): return lax.ppermute(value, axis, [(i, i ^ mask) for i in range(size)])]
  transfers between devices with their start and end apart: 37 -> 36, of which waited for: 11 -> 13; matrix products, arithmetic and copies ran while one was open for 1% -> 1% of each run, Pallas kernels for 57% -> 63%
where the time goes in v10:
time: 212 us; the launch traced here: 211 us
  Pallas kernels  133 us (63%)
  waiting for transfers between devices  46.5 us (22%)
  starting transfers between devices  25.6 us (12%)
  other arithmetic  4.95 us (2%)
    pallas_call x17, Pallas kernels, run(): pl.pallas_call(kernel, out_shape=outs, in_specs=[SMEM] + [ANY] * len(oper...  133 us
    ppermute x36, waiting for transfers between devices, swap(): return lax.ppermute(value, axis, [(i, i ^ mask) for i in range(size)])  46.5 us
    ppermute x36, starting transfers between devices, swap(): return lax.ppermute(value, axis, [(i, i ^ mask) for i in range(size)])  25.6 us
  transfers between devices with their start and end apart: 36, of which 13 were waited for; matrix products, arithmetic and copies ran while one was open for 1% of the time, Pallas kernels for 63%

profile of v10, /device:TPU:0, one launch (start us, length us, event | category | flops | bytes accessed | tf_op | source)
XLA Modules:
  0.0 211.3 jit_solution(13202282346199454306)
XLA Ops:
  0.0 4.0 %collective-permute-start.4 = (bf16[128,2048]{1,0:T(8,128)(2,1)}, bf16[128,2048]{1,0:T(8,128)(2,1)}, u32[]{:S(2)}, u32[]{:S(2)}) collective-permute-start(bf16[128,2048]{1,0:T(8,128)(2,1)} %args_3_.14), channel_id=1, source_target_pairs={{0,2},{1,3},{2,0},{3,1},{4,6},{5,7},{6,4},{7,5},{8,10},{9,11},{10,... | collective-permute-start | bytes 1572872 | tf_op jit(solution)/shard_map/ppermute | solution.py:21
  4.6 7.1 %step_gg.5 = (bf16[2,128,896]{2,1,0:T(8,128)(2,1)}, bf16[2,128,768]{2,1,0:T(8,128)(2,1)}) custom-call(s32[5]{0:T(128)} %pad_add_fusion.table_ref, bf16[2048,6656]{1,0:T(8,128)(2,1)} %args_0_.36, bf16[2048,6656]{1,0:T(8,128)(2,1)} %args_1_.36, bf16[6656,2048]{1,0:T(8,128)(2,1)} %args_2_.36, bf16[128,2048]{1,0:T(8,128)(2,1)} %args_3_.14, ...), custom_call_target="tpu_custom_call" | custom-call | flops 1000 | bytes 1000 | tf_op jit(solution)/shard_map/step_gg/pallas_call | solution.py:351
  11.8 7.8 %step_gg.6 = (bf16[2,128,896]{2,1,0:T(8,128)(2,1)}, bf16[2,128,896]{2,1,0:T(8,128)(2,1)}) custom-call(s32[5]{0:T(128)} %pad_add_fusion.table_ref, bf16[2048,6656]{1,0:T(8,128)(2,1)} %args_0_.36, bf16[2048,6656]{1,0:T(8,128)(2,1)} %args_1_.36, bf16[6656,2048]{1,0:T(8,128)(2,1)} %args_2_.36, bf16[128,2048]{1,0:T(8,128)(2,1)} %args_3_.14, ...), custom_call_target="tpu_custom_call" | custom-call | flops 1000 | bytes 1000 | tf_op jit(solution)/shard_map/step_gg/pallas_call | solution.py:351
  20.2 5.1 %step_g.10 = (bf16[2,128,896]{2,1,0:T(8,128)(2,1)}, f32[128,128]{1,0:T(8,128)}) custom-call(s32[5]{0:T(128)} %pad_add_fusion.table_ref, bf16[2048,6656]{1,0:T(8,128)(2,1)} %args_0_.36, bf16[2048,6656]{1,0:T(8,128)(2,1)} %args_1_.36, bf16[6656,2048]{1,0:T(8,128)(2,1)} %args_2_.36, bf16[128,2048]{1,0:T(8,128)(2,1)} %args_3_.14, ...), custom_call_target="tpu_custom_call" | custom-call | flops 1000 | bytes 1000 | tf_op jit(solution)/shard_map/step_g/pallas_call | solution.py:351
  29.7 5.4 %step_g.11.args_5_ = bf16[2,128,896]{2,1,0:T(8,128)(2,1)} custom-call(s32[5]{0:T(128)} %pad_add_fusion.table_ref, bf16[2048,6656]{1,0:T(8,128)(2,1)} %args_0_.36, bf16[2048,6656]{1,0:T(8,128)(2,1)} %args_1_.36, bf16[6656,2048]{1,0:T(8,128)(2,1)} %args_2_.36, bf16[128,2048]{1,0:T(8,128)(2,1)} %args_3_.14, ...), custom_call_target="tpu_custom_call" | custom-call | flops 1000 | bytes 1000 | tf_op jit(solution)/shard_map/step_g/pallas_call | solution.py:351
  35.8 6.2 %collective-permute-done.2.args_5_.args_7_ = bf16[2,128,896]{2,1,0:T(8,128)(2,1)} collective-permute-done((bf16[2,128,896]{2,1,0:T(8,128)(2,1)}, bf16[2,128,896]{2,1,0:T(8,128)(2,1)}, u32[]{:S(2)}, u32[]{:S(2)}) %collective-permute-start.2) | collective-permute-done | bytes 458784 | tf_op jit(solution)/shard_map/ppermute | solution.py:21
  42.0 8.7 %step_gg.7 = (bf16[2,256,1024]{2,1,0:T(8,128)(2,1)}, bf16[2,256,896]{2,1,0:T(8,128)(2,1)}) custom-call(s32[5]{0:T(128)} %pad_add_fusion.table_ref, bf16[2048,6656]{1,0:T(8,128)(2,1)} %args_0_.36, bf16[2048,6656]{1,0:T(8,128)(2,1)} %args_1_.36, bf16[6656,2048]{1,0:T(8,128)(2,1)} %args_2_.36, bf16[128,2048]{1,0:T(8,128)(2,1)} %collective-permute-done.4.args_3_, ...), custom_call_target="tpu_custom_call" | custom-call | flops 1000 | bytes 1000 | tf_op jit(solution)/shard_map/step_gg/pallas_call | solution.py:351
  50.7 7.7 %step_gg.8 = (bf16[2,256,768]{2,1,0:T(8,128)(2,1)}, bf16[2,256,768]{2,1,0:T(8,128)(2,1)}) custom-call(s32[5]{0:T(128)} %pad_add_fusion.table_ref, bf16[2048,6656]{1,0:T(8,128)(2,1)} %args_0_.36, bf16[2048,6656]{1,0:T(8,128)(2,1)} %args_1_.36, bf16[6656,2048]{1,0:T(8,128)(2,1)} %args_2_.36, bf16[128,2048]{1,0:T(8,128)(2,1)} %collective-permute-done.4.args_3_, ...), custom_call_target="tpu_custom_call" | custom-call | flops 99999997952 | bytes 1000 | tf_op jit(solution)/shard_map/step_gg/pallas_call | solution.py:351
  61.0 6.3 %step_g.12 = (bf16[2,256,1024]{2,1,0:T(8,128)(2,1)}, f32[256,128]{1,0:T(8,128)}) custom-call(s32[5]{0:T(128)} %pad_add_fusion.table_ref, bf16[2048,6656]{1,0:T(8,128)(2,1)} %args_0_.36, bf16[2048,6656]{1,0:T(8,128)(2,1)} %args_1_.36, bf16[6656,2048]{1,0:T(8,128)(2,1)} %args_2_.36, bf16[128,2048]{1,0:T(8,128)(2,1)} %collective-permute-done.4.args_3_, ...), custom_call_target="tpu_custom_call" | custom-call | flops 1000 | bytes 1000 | tf_op jit(solution)/shard_map/step_g/pallas_call | solution.py:351
  69.4 5.3 %step_g.13.args_8_.args_3_ = bf16[128,768]{1,0:T(8,128)(2,1)} custom-call(s32[5]{0:T(128)} %pad_add_fusion.table_ref, bf16[2048,6656]{1,0:T(8,128)(2,1)} %args_0_.36, bf16[2048,6656]{1,0:T(8,128)(2,1)} %args_1_.36, bf16[6656,2048]{1,0:T(8,128)(2,1)} %args_2_.36, bf16[128,2048]{1,0:T(8,128)(2,1)} %args_3_.14, ...), custom_call_target="tpu_custom_call" | custom-call | flops 1000 | bytes 1000 | tf_op jit(solution)/shard_map/step_g/pallas_call | solution.py:351
  74.6 5.6 %step_g.14.args_6_.args_7_ = bf16[128,896]{1,0:T(8,128)(2,1)} custom-call(s32[5]{0:T(128)} %pad_add_fusion.table_ref, bf16[2048,6656]{1,0:T(8,128)(2,1)} %args_0_.36, bf16[2048,6656]{1,0:T(8,128)(2,1)} %args_1_.36, bf16[6656,2048]{1,0:T(8,128)(2,1)} %args_2_.36, bf16[128,2048]{1,0:T(8,128)(2,1)} %args_3_.14, ...), custom_call_target="tpu_custom_call" | custom-call | flops 1000 | bytes 1000 | tf_op jit(solution)/shard_map/step_g/pallas_call | solution.py:351
  80.3 5.8 %step_g.15.args_4_ = bf16[2,256,768]{2,1,0:T(8,128)(2,1)} custom-call(s32[5]{0:T(128)} %pad_add_fusion.table_ref, bf16[2048,6656]{1,0:T(8,128)(2,1)} %args_0_.36, bf16[2048,6656]{1,0:T(8,128)(2,1)} %args_1_.36, bf16[6656,2048]{1,0:T(8,128)(2,1)} %args_2_.36, bf16[128,2048]{1,0:T(8,128)(2,1)} %collective-permute-done.4.args_3_, ...), custom_call_target="tpu_custom_call" | custom-call | flops 1000 | bytes 1000 | tf_op jit(solution)/shard_map/step_g/pallas_call | solution.py:351
  86.7 12.0 %step_gg.9 = (bf16[2,128,1792]{2,1,0:T(8,128)(2,1)}, bf16[2,128,1664]{2,1,0:T(8,128)(2,1)}) custom-call(s32[5]{0:T(128)} %pad_add_fusion.table_ref, bf16[2048,6656]{1,0:T(8,128)(2,1)} %args_0_.36, bf16[2048,6656]{1,0:T(8,128)(2,1)} %args_1_.36, bf16[6656,2048]{1,0:T(8,128)(2,1)} %args_2_.36, bf16[128,2048]{1,0:T(8,128)(2,1)} %collective-permute-done.16.args_3_, ...), custom_call_target="tpu_custom_call" | custom-call | flops 1000 | bytes 1000 | tf_op jit(solution)/shard_map/step_gg/pallas_call | solution.py:351
  101.1 6.8 %step_g.16.args_9_.args_3_ = bf16[256,896]{1,0:T(8,128)(2,1)} custom-call(s32[5]{0:T(128)} %pad_add_fusion.table_ref, bf16[2048,6656]{1,0:T(8,128)(2,1)} %args_0_.36, bf16[2048,6656]{1,0:T(8,128)(2,1)} %args_1_.36, bf16[6656,2048]{1,0:T(8,128)(2,1)} %args_2_.36, bf16[128,2048]{1,0:T(8,128)(2,1)} %collective-permute-done.4.args_3_, ...), custom_call_target="tpu_custom_call" | custom-call | flops 1000 | bytes 1000 | tf_op jit(solution)/shard_map/step_g/pallas_call | solution.py:351
  107.9 2.7 %collective-permute-done.13.args_6_ = bf16[2,256,768]{2,1,0:T(8,128)(2,1)} collective-permute-done((bf16[2,256,768]{2,1,0:T(8,128)(2,1)}, bf16[2,256,768]{2,1,0:T(8,128)(2,1)}, u32[]{:S(2)}, u32[]{:S(2)}) %collective-permute-start.13) | collective-permute-done | bytes 786464 | tf_op jit(solution)/shard_map/ppermute | solution.py:21
  112.1 6.3 %step_g.17.args_5_.args_7_ = bf16[256,768]{1,0:T(8,128)(2,1)} custom-call(s32[5]{0:T(128)} %pad_add_fusion.table_ref, bf16[2048,6656]{1,0:T(8,128)(2,1)} %args_0_.36, bf16[2048,6656]{1,0:T(8,128)(2,1)} %args_1_.36, bf16[6656,2048]{1,0:T(8,128)(2,1)} %args_2_.36, bf16[128,2048]{1,0:T(8,128)(2,1)} %collective-permute-done.4.args_3_, ...), custom_call_target="tpu_custom_call" | custom-call | flops 1000 | bytes 1000 | tf_op jit(solution)/shard_map/step_g/pallas_call | solution.py:351
  120.4 7.7 %step_g.18 = (bf16[2,128,1792]{2,1,0:T(8,128)(2,1)}, f32[128,128]{1,0:T(8,128)}) custom-call(s32[5]{0:T(128)} %pad_add_fusion.table_ref, bf16[2048,6656]{1,0:T(8,128)(2,1)} %args_0_.36, bf16[2048,6656]{1,0:T(8,128)(2,1)} %args_1_.36, bf16[6656,2048]{1,0:T(8,128)(2,1)} %args_2_.36, bf16[128,2048]{1,0:T(8,128)(2,1)} %collective-permute-done.16.args_3_, ...), custom_call_target="tpu_custom_call" | custom-call | flops 1000 | bytes 1000 | tf_op jit(solution)/shard_map/step_g/pallas_call | solution.py:351
  131.0 7.0 %collective-permute-done.28.args_9_ = bf16[256,768]{1,0:T(8,128)(2,1)} collective-permute-done((bf16[256,768]{1,0:T(8,128)(2,1)}, bf16[256,768]{1,0:T(8,128)(2,1)}, u32[]{:S(2)}, u32[]{:S(2)}) %collective-permute-start.28) | collective-permute-done | bytes 393248 | tf_op jit(solution)/shard_map/ppermute | solution.py:21
  140.1 13.8 %step_d.2 = (bf16[128,2048]{1,0:T(8,128)(2,1)}, bf16[128,2048]{1,0:T(8,128)(2,1)}) custom-call(s32[5]{0:T(128)} %pad_add_fusion.table_ref, bf16[2048,6656]{1,0:T(8,128)(2,1)} %args_0_.36, bf16[2048,6656]{1,0:T(8,128)(2,1)} %args_1_.36, bf16[6656,2048]{1,0:T(8,128)(2,1)} %args_2_.36, bf16[256,896]{1,0:T(8,128)(2,1)} %step_g.16.args_9_.args_3_, ...), custom_call_target="tpu_custom_call" | custom-call | flops 1000 | bytes 1000 | tf_op jit(solution)/shard_map/step_d/pallas_call | solution.py:351
  156.5 7.9 %step_g.19.args_11_.args_15_ = bf16[128,1664]{1,0:T(8,128)(2,1)} custom-call(s32[5]{0:T(128)} %pad_add_fusion.table_ref, bf16[2048,6656]{1,0:T(8,128)(2,1)} %args_0_.36, bf16[2048,6656]{1,0:T(8,128)(2,1)} %args_1_.36, bf16[6656,2048]{1,0:T(8,128)(2,1)} %args_2_.36, bf16[128,2048]{1,0:T(8,128)(2,1)} %collective-permute-done.16.args_3_, ...), custom_call_target="tpu_custom_call" | custom-call | flops 1000 | bytes 1000 | tf_op jit(solution)/shard_map/step_g/pallas_call | solution.py:351
  170.4 2.5 %collective-permute-start.34 = (bf16[128,2048]{1,0:T(8,128)(2,1)}, bf16[128,2048]{1,0:T(8,128)(2,1)}, u32[]{:S(2)}, u32[]{:S(2)}) collective-permute-start(bf16[128,2048]{1,0:T(8,128)(2,1)} %add_convert_fusion.1), channel_id=1, source_target_pairs={{0,2},{1,3},{2,0},{3,1},{4,6},{5,7},{6,4},{7,5},{8,10},{9,11},{10,... | collective-permute-start | bytes 1572872 | tf_op jit(solution)/shard_map/ppermute | solution.py:21
  177.9 13.9 %step_d.3 = (bf16[128,2048]{1,0:T(8,128)(2,1)}, bf16[128,2048]{1,0:T(8,128)(2,1)}) custom-call(s32[5]{0:T(128)} %pad_add_fusion.table_ref, bf16[2048,6656]{1,0:T(8,128)(2,1)} %args_0_.36, bf16[2048,6656]{1,0:T(8,128)(2,1)} %args_1_.36, bf16[6656,2048]{1,0:T(8,128)(2,1)} %args_2_.36, bf16[128,768]{1,0:T(8,128)(2,1)} %step_g.13.args_8_.args_3_, ...), custom_call_target="tpu_custom_call" | custom-call | flops 1000 | bytes 1000 | tf_op jit(solution)/shard_map/step_d/pallas_call | solution.py:351
  191.9 4.1 %collective-permute-done.34 = bf16[128,2048]{1,0:T(8,128)(2,1)} collective-permute-done((bf16[128,2048]{1,0:T(8,128)(2,1)}, bf16[128,2048]{1,0:T(8,128)(2,1)}, u32[]{:S(2)}, u32[]{:S(2)}) %collective-permute-start.34) | collective-permute-done | bytes 524320 | tf_op jit(solution)/shard_map/ppermute | solution.py:21
  196.5 12.6 %collective-permute-done.35 = bf16[128,2048]{1,0:T(8,128)(2,1)S(1)} collective-permute-done((bf16[128,2048]{1,0:T(8,128)(2,1)}, bf16[128,2048]{1,0:T(8,128)(2,1)S(1)}, u32[]{:S(2)}, u32[]{:S(2)}) %collective-permute-start.35) | collective-permute-done | bytes 524320 | tf_op jit(solution)/shard_map/ppermute | solution.py:21
  (71 shorter events, 38.7 us)
Async XLA Ops:
  0.0 27.5 %collective-permute-start.4 = (bf16[128,2048]{1,0:T(8,128)(2,1)}, bf16[128,2048]{1,0:T(8,128)(2,1)}, u32[]{:S(2)}, u32[]{:S(2)}) collective-permute-start(bf16[128,2048]{1,0:T(8,128)(2,1)} %args_3_.14), channel_id=1, source_target_pairs={{0,2},{1,3},{2,0},{3,1},{4,6},{5,7},{6,4},{7,5},{8,10},{9,11},{10,... | collective-permute-start | bytes 1572872 | tf_op jit(solution)/shard_map/ppermute | solution.py:21
  27.5 14.5 %collective-permute-start.5 = (bf16[128,2048]{1,0:T(8,128)(2,1)}, bf16[128,2048]{1,0:T(8,128)(2,1)}, u32[]{:S(2)}, u32[]{:S(2)}) collective-permute-start(bf16[128,2048]{1,0:T(8,128)(2,1)} %collective-permute-done.4.args_3_), channel_id=1, source_target_pairs={{0,1},{1,0},{2,3},{3,2},{4,5},{5,4},{6,7},{7,6},{8,9},{9,8},{10,11... | collective-permute-start | bytes 1572872 | tf_op jit(solution)/shard_map/ppermute | solution.py:21
  28.2 13.7 %collective-permute-start.2 = (bf16[2,128,896]{2,1,0:T(8,128)(2,1)}, bf16[2,128,896]{2,1,0:T(8,128)(2,1)}, u32[]{:S(2)}, u32[]{:S(2)}) collective-permute-start(bf16[2,128,896]{2,1,0:T(8,128)(2,1)} %get-tuple-element.61.args_5_), channel_id=1, source_target_pairs={{0,8},{4,12},{8,0},{12,4},{1,9},{5,13},{9,1},{13,5},{2,10},{6,14},... | collective-permute-start | bytes 1376264 | tf_op jit(solution)/shard_map/ppermute | solution.py:21
  35.1 15.6 %collective-permute-start.7 = (bf16[2,128,896]{2,1,0:T(8,128)(2,1)}, bf16[2,128,896]{2,1,0:T(8,128)(2,1)}, u32[]{:S(2)}, u32[]{:S(2)}) collective-permute-start(bf16[2,128,896]{2,1,0:T(8,128)(2,1)} %step_g.11.args_5_), channel_id=1, source_target_pairs={{0,8},{4,12},{8,0},{12,4},{1,9},{5,13},{9,1},{13,5},{2,10},{6,14},... | collective-permute-start | bytes 1376264 | tf_op jit(solution)/shard_map/ppermute | solution.py:21
  58.5 21.8 %collective-permute-start.11 = (bf16[2,256,768]{2,1,0:T(8,128)(2,1)}, bf16[2,256,768]{2,1,0:T(8,128)(2,1)}, u32[]{:S(2)}, u32[]{:S(2)}) collective-permute-start(bf16[2,256,768]{2,1,0:T(8,128)(2,1)} %get-tuple-element.68.args_6_), channel_id=1, source_target_pairs={{0,4},{4,0},{8,12},{12,8},{1,5},{5,1},{9,13},{13,9},{2,6},{6,2},{1... | collective-permute-start | bytes 2359304 | tf_op jit(solution)/shard_map/ppermute | solution.py:21
  59.6 27.1 %collective-permute-start.16 = (bf16[128,2048]{1,0:T(8,128)(2,1)}, bf16[128,2048]{1,0:T(8,128)(2,1)}, u32[]{:S(2)}, u32[]{:S(2)}) collective-permute-start(bf16[128,2048]{1,0:T(8,128)(2,1)} %args_3_.14), channel_id=1, source_target_pairs={{0,1},{1,0},{2,3},{3,2},{4,5},{5,4},{6,7},{7,6},{8,9},{9,8},{10,11... | collective-permute-start | bytes 1572872 | tf_op jit(solution)/shard_map/ppermute | solution.py:21
  67.3 33.2 %collective-permute-start.14 = (bf16[2,256,1024]{2,1,0:T(8,128)(2,1)}, bf16[2,256,1024]{2,1,0:T(8,128)(2,1)}, u32[]{:S(2)}, u32[]{:S(2)}) collective-permute-start(bf16[2,256,1024]{2,1,0:T(8,128)(2,1)} %get-tuple-element.69.args_7_), channel_id=1, source_target_pairs={{0,8},{4,12},{8,0},{12,4},{1,9},{5,13},{9,1},{13,5},{2,10},{6,14},... | collective-permute-start | bytes 3145736 | tf_op jit(solution)/shard_map/ppermute | solution.py:21
  68.8 31.5 %collective-permute-start.15 = (bf16[2,256,896]{2,1,0:T(8,128)(2,1)}, bf16[2,256,896]{2,1,0:T(8,128)(2,1)}, u32[]{:S(2)}, u32[]{:S(2)}) collective-permute-start(bf16[2,256,896]{2,1,0:T(8,128)(2,1)} %get-tuple-element.74), channel_id=1, source_target_pairs={{0,4},{4,0},{8,12},{12,8},{1,5},{5,1},{9,13},{13,9},{2,6},{6,2},{1... | collective-permute-start | bytes 2752520 | tf_op jit(solution)/shard_map/ppermute | solution.py:21
  68.8 30.0 %collective-permute-start.10 = (bf16[2,256,768]{2,1,0:T(8,128)(2,1)}, bf16[2,256,768]{2,1,0:T(8,128)(2,1)}, u32[]{:S(2)}, u32[]{:S(2)}) collective-permute-start(bf16[2,256,768]{2,1,0:T(8,128)(2,1)} %get-tuple-element.70), channel_id=1, source_target_pairs={{0,4},{4,0},{8,12},{12,8},{1,5},{5,1},{9,13},{13,9},{2,6},{6,2},{1... | collective-permute-start | bytes 2359304 | tf_op jit(solution)/shard_map/ppermute | solution.py:21
  86.0 24.6 %collective-permute-start.13 = (bf16[2,256,768]{2,1,0:T(8,128)(2,1)}, bf16[2,256,768]{2,1,0:T(8,128)(2,1)}, u32[]{:S(2)}, u32[]{:S(2)}) collective-permute-start(bf16[2,256,768]{2,1,0:T(8,128)(2,1)} %step_g.15.args_4_), channel_id=1, source_target_pairs={{0,8},{4,12},{8,0},{12,4},{1,9},{5,13},{9,1},{13,5},{2,10},{6,14},... | collective-permute-start | bytes 2359304 | tf_op jit(solution)/shard_map/ppermute | solution.py:21
  98.7 21.0 %collective-permute-start.18 = (bf16[2,128,1792]{2,1,0:T(8,128)(2,1)}, bf16[2,128,1792]{2,1,0:T(8,128)(2,1)}, u32[]{:S(2)}, u32[]{:S(2)}) collective-permute-start(bf16[2,128,1792]{2,1,0:T(8,128)(2,1)} %get-tuple-element.77.args_8_), channel_id=1, source_target_pairs={{0,4},{4,0},{8,12},{12,8},{1,5},{5,1},{9,13},{13,9},{2,6},{6,2},{1... | collective-permute-start | bytes 2752520 | tf_op jit(solution)/shard_map/ppermute | solution.py:21
  98.8 19.6 %collective-permute-start.9 = (bf16[128,768]{1,0:T(8,128)(2,1)}, bf16[128,768]{1,0:T(8,128)(2,1)}, u32[]{:S(2)}, u32[]{:S(2)}) collective-permute-start(bf16[128,768]{1,0:T(8,128)(2,1)} %step_g.13.args_8_.args_3_), channel_id=1, source_target_pairs={{0,8},{4,12},{8,0},{12,4},{1,9},{5,13},{9,1},{13,5},{2,10},{6,14},... | collective-permute-start | bytes 589832 | tf_op jit(solution)/shard_map/ppermute | solution.py:21
  100.3 18.1 %collective-permute-start.8 = (bf16[128,768]{1,0:T(8,128)(2,1)}, bf16[128,768]{1,0:T(8,128)(2,1)}, u32[]{:S(2)}, u32[]{:S(2)}) collective-permute-start(bf16[128,768]{1,0:T(8,128)(2,1)} %step_g.13.args_8_.args_3_), channel_id=1, source_target_pairs={{0,4},{4,0},{8,12},{12,8},{1,5},{5,1},{9,13},{13,9},{2,6},{6,2},{1... | collective-permute-start | bytes 589832 | tf_op jit(solution)/shard_map/ppermute | solution.py:21
  100.5 19.2 %collective-permute-start.19 = (bf16[128,896]{1,0:T(8,128)(2,1)}, bf16[128,896]{1,0:T(8,128)(2,1)}, u32[]{:S(2)}, u32[]{:S(2)}) collective-permute-start(bf16[128,896]{1,0:T(8,128)(2,1)} %step_g.14.args_6_.args_7_), channel_id=1, source_target_pairs={{0,8},{4,12},{8,0},{12,4},{1,9},{5,13},{9,1},{13,5},{2,10},{6,14},... | collective-permute-start | bytes 688136 | tf_op jit(solution)/shard_map/ppermute | solution.py:21
  110.6 19.0 %collective-permute-start.25 = (bf16[256,896]{1,0:T(8,128)(2,1)}, bf16[256,896]{1,0:T(8,128)(2,1)}, u32[]{:S(2)}, u32[]{:S(2)}) collective-permute-start(bf16[256,896]{1,0:T(8,128)(2,1)} %step_g.16.args_9_.args_3_), channel_id=1, source_target_pairs={{0,8},{4,12},{8,0},{12,4},{1,9},{5,13},{9,1},{13,5},{2,10},{6,14},... | collective-permute-start | bytes 1376264 | tf_op jit(solution)/shard_map/ppermute | solution.py:21
  118.5 19.5 %collective-permute-start.28 = (bf16[256,768]{1,0:T(8,128)(2,1)}, bf16[256,768]{1,0:T(8,128)(2,1)}, u32[]{:S(2)}, u32[]{:S(2)}) collective-permute-start(bf16[256,768]{1,0:T(8,128)(2,1)} %step_g.17.args_5_.args_7_), channel_id=1, source_target_pairs={{0,8},{4,12},{8,0},{12,4},{1,9},{5,13},{9,1},{13,5},{2,10},{6,14},... | collective-permute-start | bytes 1179656 | tf_op jit(solution)/shard_map/ppermute | solution.py:21
  119.7 18.3 %collective-permute-start.27 = (bf16[256,768]{1,0:T(8,128)(2,1)}, bf16[256,768]{1,0:T(8,128)(2,1)}, u32[]{:S(2)}, u32[]{:S(2)}) collective-permute-start(bf16[256,768]{1,0:T(8,128)(2,1)} %step_g.17.args_5_.args_7_), channel_id=1, source_target_pairs={{0,4},{4,0},{8,12},{12,8},{1,5},{5,1},{9,13},{13,9},{2,6},{6,2},{1... | collective-permute-start | bytes 1179656 | tf_op jit(solution)/shard_map/ppermute | solution.py:21
  129.6 10.5 %collective-permute-start.26 = (bf16[256,896]{1,0:T(8,128)(2,1)}, bf16[256,896]{1,0:T(8,128)(2,1)}, u32[]{:S(2)}, u32[]{:S(2)}) collective-permute-start(bf16[256,896]{1,0:T(8,128)(2,1)} %collective-permute-done.25.args_5_), channel_id=1, source_target_pairs={{0,4},{4,0},{8,12},{12,8},{1,5},{5,1},{9,13},{13,9},{2,6},{6,2},{1... | collective-permute-start | bytes 1376264 | tf_op jit(solution)/shard_map/ppermute | solution.py:21
  129.6 26.9 %collective-permute-start.23 = (bf16[2,128,1792]{2,1,0:T(8,128)(2,1)}, bf16[2,128,1792]{2,1,0:T(8,128)(2,1)}, u32[]{:S(2)}, u32[]{:S(2)}) collective-permute-start(bf16[2,128,1792]{2,1,0:T(8,128)(2,1)} %get-tuple-element.98.args_11_), channel_id=1, source_target_pairs={{0,8},{4,12},{8,0},{12,4},{1,9},{5,13},{9,1},{13,5},{2,10},{6,14},... | collective-permute-start | bytes 2752520 | tf_op jit(solution)/shard_map/ppermute | solution.py:21
  138.0 16.6 %collective-permute-start.22 = (bf16[2,128,1664]{2,1,0:T(8,128)(2,1)}, bf16[2,128,1664]{2,1,0:T(8,128)(2,1)}, u32[]{:S(2)}, u32[]{:S(2)}) collective-permute-start(bf16[2,128,1664]{2,1,0:T(8,128)(2,1)} %get-tuple-element.92), channel_id=1, source_target_pairs={{0,4},{4,0},{8,12},{12,8},{1,5},{5,1},{9,13},{13,9},{2,6},{6,2},{1... | collective-permute-start | bytes 2555912 | tf_op jit(solution)/shard_map/ppermute | solution.py:21
  153.9 14.3 %collective-permute-start.32 = (bf16[128,2048]{1,0:T(8,128)(2,1)}, bf16[128,2048]{1,0:T(8,128)(2,1)}, u32[]{:S(2)}, u32[]{:S(2)}) collective-permute-start(bf16[128,2048]{1,0:T(8,128)(2,1)} %get-tuple-element.100), channel_id=1, source_target_pairs={{0,1},{1,0},{2,3},{3,2},{4,5},{5,4},{6,7},{7,6},{8,9},{9,8},{10,11... | collective-permute-start | bytes 1572872 | tf_op jit(solution)/shard_map/ppermute | solution.py:21
  164.4 10.9 %collective-permute-start.31 = (bf16[128,1664]{1,0:T(8,128)(2,1)}, bf16[128,1664]{1,0:T(8,128)(2,1)S(1)}, u32[]{:S(2)}, u32[]{:S(2)}) collective-permute-start(bf16[128,1664]{1,0:T(8,128)(2,1)} %step_g.19.args_11_.args_15_), channel_id=1, source_target_pairs={{0,8},{4,12},{8,0},{12,4},{1,9},{5,13},{9,1},{13,5},{2,10},{6,14},... | collective-permute-start | bytes 1277960 | tf_op jit(solution)/shard_map/ppermute | solution.py:21
  170.4 25.6 %collective-permute-start.34 = (bf16[128,2048]{1,0:T(8,128)(2,1)}, bf16[128,2048]{1,0:T(8,128)(2,1)}, u32[]{:S(2)}, u32[]{:S(2)}) collective-permute-start(bf16[128,2048]{1,0:T(8,128)(2,1)} %add_convert_fusion.1), channel_id=1, source_target_pairs={{0,2},{1,3},{2,0},{3,1},{4,6},{5,7},{6,4},{7,5},{8,10},{9,11},{10,... | collective-permute-start | bytes 1572872 | tf_op jit(solution)/shard_map/ppermute | solution.py:21
  196.0 13.1 %collective-permute-start.35 = (bf16[128,2048]{1,0:T(8,128)(2,1)}, bf16[128,2048]{1,0:T(8,128)(2,1)S(1)}, u32[]{:S(2)}, u32[]{:S(2)}) collective-permute-start(bf16[128,2048]{1,0:T(8,128)(2,1)} %get-tuple-element.108), channel_id=1, source_target_pairs={{0,1},{1,0},{2,3},{3,2},{4,5},{5,4},{6,7},{7,6},{8,9},{9,8},{10,11... | collective-permute-start | bytes 1572872 | tf_op jit(solution)/shard_map/ppermute | solution.py:21
  (13 other events, 85.1 us)

commit v11 on v10

--- a/solution.py
+++ b/solution.py
@@ -26,6 +26,23 @@
     return gate / (1.0 + jnp.exp(-gate)) * (up * scale)
 
 
+def row_squares(tok):
+    values = tok.astype(jnp.float32)
+    return jnp.sum(values * values, axis=1, keepdims=True)
+
+
+def to_carry(total):
+    high = total.astype(jnp.bfloat16).astype(jnp.float32)
+    shape = (total.shape[0], LANES)
+    first = lax.broadcasted_iota(jnp.int32, shape, 1) < LANES // 2
+    return jnp.where(first, jnp.broadcast_to(high, shape), jnp.broadcast_to(total - high, shape)).astype(jnp.bfloat16)
+
+
+def carried(columns):
+    values = columns.astype(jnp.float32)
+    return values[:, :1] + values[:, LANES // 2 : LANES // 2 + 1]
+
+
 class Group:
     def __init__(self, blocks, names, block):
         self.blocks, self.names, self.block, self.rows = blocks, names, block, block * len(names)
@@ -38,8 +55,8 @@
     def __init__(self, group, place, low, width, recvs=(), carry=False, emit=False, squares=None, at=0, features=1):
         self.group, self.place, self.low, self.width, self.recvs = group, place, low, width, list(recvs)
         self.carry, self.emit, self.squares, self.at, self.features = carry, emit, squares, at, features
-        rows, wide = group.rows, width + (LANES if carry else 0)
-        self.outs = [jax.ShapeDtypeStruct((2, rows, wide) if squares is None else (rows, width), jnp.bfloat16)]
+        rows, wide = group.rows, width if squares else 2 * width + (LANES if carry else 0)
+        self.outs = [jax.ShapeDtypeStruct((rows, wide), jnp.bfloat16)]
         if emit:
             self.outs.append(jax.ShapeDtypeStruct((rows, LANES), jnp.float32))
 
@@ -51,30 +68,22 @@
 
     def plain(self, table, gate_matrix, up_matrix, down_matrix):
         tok, n = jnp.concatenate(self.group.arrays(), axis=0), self.width
-        gate, up = (
+        both = [
             jnp.dot(
                 tok, lax.dynamic_slice_in_dim(m, table[self.place] + self.low, n, 1), preferred_element_type=jnp.float32
             )
             for m in (gate_matrix, up_matrix)
-        )
-        for r in self.recvs:
-            gate, up = gate + r[0, :, :n].astype(jnp.float32), up + r[1, :, :n].astype(jnp.float32)
+        ]
+        both = jnp.concatenate(both, axis=1) + sum(r[:, : 2 * n].astype(jnp.float32) for r in self.recvs)
         if self.squares:
-            total = self.squares[0]
-            for part in self.squares[1]:
-                part = part[:, :, self.at : self.at + LANES].astype(jnp.float32)
-                total = total + part[0] + part[1]
-            return [silu_product(gate, up, lax.rsqrt(total[:, :1] / self.features + EPS)).astype(jnp.bfloat16)]
+            total = self.squares[0][:, :1] + sum(carried(r[:, self.at : self.at + LANES]) for r in self.squares[1])
+            scale = lax.rsqrt(total / self.features + EPS)
+            return [silu_product(both[:, :n], both[:, n:], scale).astype(jnp.bfloat16)]
         if not self.carry:
-            return [jnp.stack([gate, up]).astype(jnp.bfloat16)]
-        values = tok.astype(jnp.float32)
-        total = jnp.broadcast_to(jnp.sum(values * values, axis=1, keepdims=True), (tok.shape[0], LANES))
-        for r in self.recvs:
-            part = r[:, :, n : n + LANES].astype(jnp.float32)
-            total = total + part[0] + part[1]
-        high = total.astype(jnp.bfloat16).astype(jnp.float32)
-        both = jnp.stack([jnp.concatenate([gate, high], axis=1), jnp.concatenate([up, total - high], axis=1)])
-        return [both.astype(jnp.bfloat16)] + ([total] if self.emit else [])
+            return [both.astype(jnp.bfloat16)]
+        total = row_squares(tok) + sum(carried(r[:, 2 * n : 2 * n + LANES]) for r in self.recvs)
+        result = jnp.concatenate([both.astype(jnp.bfloat16), to_carry(total)], axis=1)
+        return [result] + ([jnp.broadcast_to(total, (tok.shape[0], LANES))] if self.emit else [])
 
     def scratch(self, depth):
         rows, n, tiles, n_recv = self.group.rows, self.width, pl.cdiv(self.width, GU_TILE), len(self.recvs)
@@ -82,13 +91,13 @@
         return [
             pltpu.VMEM((tiles, depth, 2 * GU_TILE), jnp.bfloat16),
             pltpu.VMEM((n_recv, 2, rows, n) if n_recv else (1, 2, 16, LANES), jnp.bfloat16),
-            pltpu.VMEM((extra, 2, rows, LANES) if extra else (1, 2, 16, LANES), jnp.bfloat16),
+            pltpu.VMEM((extra, rows, LANES) if extra else (1, 16, LANES), jnp.bfloat16),
             pltpu.VMEM((rows, LANES) if self.squares or self.emit else (8, LANES), jnp.float32),
             pltpu.VMEM((tiles, 1 if self.squares else 2, rows, GU_TILE), jnp.bfloat16),
-            pltpu.VMEM((2, rows, LANES) if self.carry else (2, 16, LANES), jnp.bfloat16),
+            pltpu.VMEM((rows if self.carry else 16, LANES), jnp.bfloat16),
             pltpu.SemaphoreType.DMA((2, tiles)),
-            pltpu.SemaphoreType.DMA((n_recv + extra + 1,)),
-            pltpu.SemaphoreType.DMA((tiles + 2,)),
+            pltpu.SemaphoreType.DMA((2 * n_recv + extra + 1,)),
+            pltpu.SemaphoreType.DMA((2, tiles + 1)),
         ]
 
     def bind(self, refs, table, arrays, outs, scratch):
@@ -107,10 +116,14 @@
             ]
 
         def write(j, m):
-            columns = pl.ds(pl.multiple_of(j * GU_TILE, LANES), m)
-            if hidden:
-                return pltpu.make_async_copy(obuf.at[j, 0, :, pl.ds(0, m)], outs[0].at[:, columns], osem.at[j])
-            return pltpu.make_async_copy(obuf.at[j, :, :, pl.ds(0, m)], outs[0].at[:, :, columns], osem.at[j])
+            return [
+                pltpu.make_async_copy(
+                    obuf.at[j, i, :, pl.ds(0, m)],
+                    outs[0].at[:, pl.ds(pl.multiple_of(i * n + j * GU_TILE, LANES), m)],
+                    osem.at[i, j],
+                )
+                for i in range(1 if hidden else 2)
+            ]
 
         def over_tiles(step):
             if full:
@@ -121,20 +134,24 @@
                 step(full, rest)
 
         copies = [
-            pltpu.make_async_copy(a.at[:, :, pl.ds(0, n)], rbuf.at[i], rsem.at[i]) for i, a in enumerate(arrays[:n_recv])
+            pltpu.make_async_copy(a.at[:, pl.ds(h * n, n)], rbuf.at[i, h], rsem.at[2 * i + h])
+            for i, a in enumerate(arrays[:n_recv])
+            for h in range(2)
         ]
         extras = arrays[n_recv + 1 :] if hidden else arrays[:n_recv] if self.carry else []
         copies += [
-            pltpu.make_async_copy(a.at[:, :, pl.ds(self.at if hidden else n, LANES)], ebuf.at[i], rsem.at[n_recv + i])
+            pltpu.make_async_copy(
+                a.at[:, pl.ds(self.at if hidden else 2 * n, LANES)], ebuf.at[i], rsem.at[2 * n_recv + i]
+            )
             for i, a in enumerate(extras)
         ]
         if hidden:
-            copies.append(pltpu.make_async_copy(arrays[n_recv], qbuf, rsem.at[n_recv + len(extras)]))
+            copies.append(pltpu.make_async_copy(arrays[n_recv], qbuf, rsem.at[2 * n_recv + len(extras)]))
         writes = []
         if self.carry:
-            writes.append(pltpu.make_async_copy(cbuf, outs[0].at[:, :, pl.ds(n, LANES)], osem.at[tiles]))
+            writes.append(pltpu.make_async_copy(cbuf, outs[0].at[:, pl.ds(2 * n, LANES)], osem.at[0, tiles]))
         if self.emit:
-            writes.append(pltpu.make_async_copy(qbuf, outs[1], osem.at[tiles + 1]))
+            writes.append(pltpu.make_async_copy(qbuf, outs[1], osem.at[1, tiles]))
 
         def begin():
             def step(j, m):
@@ -146,24 +163,18 @@
         def compute():
             for copy in copies:
                 copy.wait()
-            extra = None
-            for i in range(len(extras)):
-                term = ebuf[i, 0].astype(jnp.float32) + ebuf[i, 1].astype(jnp.float32)
-                extra = term if extra is None else extra + term
+            if hidden or self.carry:
+                total = qbuf[:, :1] if hidden else row_squares(xbuf[...])
+                for i in range(len(extras)):
+                    total = total + carried(ebuf[i])
             if self.carry:
-                values = xbuf[...].astype(jnp.float32)
-                total = jnp.broadcast_to(jnp.sum(values * values, axis=1, keepdims=True), (rows, LANES))
-                total = total if extra is None else total + extra
-                high = total.astype(jnp.bfloat16)
-                cbuf[0] = high
-                cbuf[1] = (total - high.astype(jnp.float32)).astype(jnp.bfloat16)
+                cbuf[...] = to_carry(total)
                 if self.emit:
-                    qbuf[...] = total
+                    qbuf[...] = jnp.broadcast_to(total, (rows, LANES))
                 for copy in writes:
                     copy.start()
             if hidden:
-                total = qbuf[...] if extra is None else qbuf[...] + extra
-                qbuf[...] = lax.rsqrt(total / self.features + EPS)
+                qbuf[...] = jnp.broadcast_to(lax.rsqrt(total / self.features + EPS), (rows, LANES))
 
             def step(j, m):
                 for copy in weights(j, m):
@@ -179,12 +190,17 @@
                 else:
                     obuf[j, 0, :, pl.ds(0, m)] = gate.astype(jnp.bfloat16)
                     obuf[j, 1, :, pl.ds(0, m)] = up.astype(jnp.bfloat16)
-                write(j, m).start()
+                for copy in write(j, m):
+                    copy.start()
 
             over_tiles(step)
 
         def drain():
-            over_tiles(lambda j, m: write(j, m).wait())
+            def step(j, m):
+                for copy in write(j, m):
+                    copy.wait()
+
+            over_tiles(step)
             for copy in writes:
                 copy.wait()
 
@@ -411,8 +427,8 @@
     sets = [[0], list(range(2, n_gy)), [1]]
     groups = [Group(blocks, js, block) for js in sets]
     squares = {}
-    half = cut(width, 7, 13)
-    early = cut(width, 6, 13)
+    half = cut(width, 8, 13)
+    early = cut(width, 7, 13)
     jobs = [(0, 0, early), (0, early, width - early), (1, 0, half), (1, half, width - half), (2, 0, width)]
     firsts = [min(i for i, job in enumerate(jobs) if job[0] == g) for g in range(len(groups))]
     state = [dict() for _ in jobs]
@@ -431,7 +447,7 @@
             ]
         if kind == "h":
             recvs = [st["lent"][-1], *st["far"]]
-            return [GateUp(group, 0, low, n, recvs, squares=squares[g], at=jobs[firsts[g]][2], features=features)]
+            return [GateUp(group, 0, low, n, recvs, squares=squares[g], at=2 * jobs[firsts[g]][2], features=features)]
 
     def down(gs, half):
         parts = [

time: 212 us -> 217 us (1.024)
  waiting for transfers between devices: 46.5 us -> 49.4 us
    ppermute x36, waiting for transfers between devices: 46.5 us -> 49.4 us  [swap(): return lax.ppermute(value, axis, [(i, i ^ mask) for i in range(size)])]
  transfers between devices with their start and end apart: 36 -> 36, of which waited for: 13 -> 12; matrix products, arithmetic and copies ran while one was open for 1% -> 1% of each run, Pallas kernels for 63% -> 62%
where the time goes in v11:
time: 217 us; the launch traced here: 216 us
  Pallas kernels  135 us (62%)
  waiting for transfers between devices  49.4 us (23%)
  starting transfers between devices  25.7 us (12%)
  other arithmetic  4.92 us (2%)
    pallas_call x17, Pallas kernels, run(): pl.pallas_call(kernel, out_shape=outs, in_specs=[SMEM] + [ANY] * len(oper...  135 us
    ppermute x36, waiting for transfers between devices, swap(): return lax.ppermute(value, axis, [(i, i ^ mask) for i in range(size)])  49.4 us
    ppermute x36, starting transfers between devices, swap(): return lax.ppermute(value, axis, [(i, i ^ mask) for i in range(size)])  25.7 us
  transfers between devices with their start and end apart: 36, of which 12 were waited for; matrix products, arithmetic and copies ran while one was open for 1% of the time, Pallas kernels for 62%

profile of v11, /device:TPU:0, one launch (start us, length us, event | category | flops | bytes accessed | tf_op | source)
XLA Modules:
  0.0 216.4 jit_solution(9277493751381962917)
XLA Ops:
  0.0 4.0 %collective-permute-start.4 = (bf16[128,2048]{1,0:T(8,128)(2,1)}, bf16[128,2048]{1,0:T(8,128)(2,1)}, u32[]{:S(2)}, u32[]{:S(2)}) collective-permute-start(bf16[128,2048]{1,0:T(8,128)(2,1)} %args_3_.14), channel_id=1, source_target_pairs={{0,2},{1,3},{2,0},{3,1},{4,6},{5,7},{6,4},{7,5},{8,10},{9,11},{10,... | collective-permute-start | bytes 1572872 | tf_op jit(solution)/shard_map/ppermute | solution.py:21
  4.6 7.9 %step_gg.5 = (bf16[128,1920]{1,0:T(8,128)(2,1)}, bf16[128,1792]{1,0:T(8,128)(2,1)}) custom-call(s32[5]{0:T(128)} %pad_add_fusion.table_ref, bf16[2048,6656]{1,0:T(8,128)(2,1)} %args_0_.36, bf16[2048,6656]{1,0:T(8,128)(2,1)} %args_1_.36, bf16[6656,2048]{1,0:T(8,128)(2,1)} %args_2_.36, bf16[128,2048]{1,0:T(8,128)(2,1)} %args_3_.14, bf16[128,2048]{1,0:T(8,128)(2,1)} %args_3_.14), custom_call_target="tpu_custom_call" | custom-call | flops 1000 | bytes 1000 | tf_op jit(solution)/shard_map/step_gg/pallas_call | solution.py:367
  12.6 7.2 %step_gg.6 = (bf16[128,1536]{1,0:T(8,128)(2,1)}, bf16[128,1536]{1,0:T(8,128)(2,1)}) custom-call(s32[5]{0:T(128)} %pad_add_fusion.table_ref, bf16[2048,6656]{1,0:T(8,128)(2,1)} %args_0_.36, bf16[2048,6656]{1,0:T(8,128)(2,1)} %args_1_.36, bf16[6656,2048]{1,0:T(8,128)(2,1)} %args_2_.36, bf16[128,2048]{1,0:T(8,128)(2,1)} %args_3_.14, ...), custom_call_target="tpu_custom_call" | custom-call | flops 1000 | bytes 1000 | tf_op jit(solution)/shard_map/step_gg/pallas_call | solution.py:367
  20.5 5.6 %step_g.10 = (bf16[128,1920]{1,0:T(8,128)(2,1)}, f32[128,128]{1,0:T(8,128)}) custom-call(s32[5]{0:T(128)} %pad_add_fusion.table_ref, bf16[2048,6656]{1,0:T(8,128)(2,1)} %args_0_.36, bf16[2048,6656]{1,0:T(8,128)(2,1)} %args_1_.36, bf16[6656,2048]{1,0:T(8,128)(2,1)} %args_2_.36, bf16[128,2048]{1,0:T(8,128)(2,1)} %args_3_.14, ...), custom_call_target="tpu_custom_call" | custom-call | flops 1000 | bytes 1000 | tf_op jit(solution)/shard_map/step_g/pallas_call | solution.py:367
  29.7 5.2 %step_g.11.args_5_ = bf16[128,1536]{1,0:T(8,128)(2,1)} custom-call(s32[5]{0:T(128)} %pad_add_fusion.table_ref, bf16[2048,6656]{1,0:T(8,128)(2,1)} %args_0_.36, bf16[2048,6656]{1,0:T(8,128)(2,1)} %args_1_.36, bf16[6656,2048]{1,0:T(8,128)(2,1)} %args_2_.36, bf16[128,2048]{1,0:T(8,128)(2,1)} %args_3_.14, bf16[128,1536]{1,0:T(8,128)(2,1)} %collective-permute-done.3.args_4_, ...), custom_call_target="tpu_custom_call" | custom-call | flops 1000 | bytes 1000 | tf_op jit(solution)/shard_map/step_g/pallas_call | solution.py:367
  35.5 7.2 %collective-permute-done.2.args_5_.args_7_ = bf16[128,1920]{1,0:T(8,128)(2,1)} collective-permute-done((bf16[128,1920]{1,0:T(8,128)(2,1)}, bf16[128,1920]{1,0:T(8,128)(2,1)}, u32[]{:S(2)}, u32[]{:S(2)}) %collective-permute-start.2) | collective-permute-done | bytes 491552 | tf_op jit(solution)/shard_map/ppermute | solution.py:21
  42.7 9.3 %step_gg.7 = (bf16[256,2176]{1,0:T(8,128)(2,1)}, bf16[256,2048]{1,0:T(8,128)(2,1)}) custom-call(s32[5]{0:T(128)} %pad_add_fusion.table_ref, bf16[2048,6656]{1,0:T(8,128)(2,1)} %args_0_.36, bf16[2048,6656]{1,0:T(8,128)(2,1)} %args_1_.36, bf16[6656,2048]{1,0:T(8,128)(2,1)} %args_2_.36, bf16[128,2048]{1,0:T(8,128)(2,1)} %collective-permute-done.4.args_3_, ...), custom_call_target="tpu_custom_call" | custom-call | flops 1000 | bytes 1000 | tf_op jit(solution)/shard_map/step_gg/pallas_call | solution.py:367
  52.1 7.2 %step_gg.8 = (bf16[256,1280]{1,0:T(8,128)(2,1)}, bf16[256,1280]{1,0:T(8,128)(2,1)}) custom-call(s32[5]{0:T(128)} %pad_add_fusion.table_ref, bf16[2048,6656]{1,0:T(8,128)(2,1)} %args_0_.36, bf16[2048,6656]{1,0:T(8,128)(2,1)} %args_1_.36, bf16[6656,2048]{1,0:T(8,128)(2,1)} %args_2_.36, bf16[128,2048]{1,0:T(8,128)(2,1)} %collective-permute-done.4.args_3_, ...), custom_call_target="tpu_custom_call" | custom-call | flops 99999997952 | bytes 1000 | tf_op jit(solution)/shard_map/step_gg/pallas_call | solution.py:367
  59.9 6.7 %step_g.12 = (bf16[256,2176]{1,0:T(8,128)(2,1)}, f32[256,128]{1,0:T(8,128)}) custom-call(s32[5]{0:T(128)} %pad_add_fusion.table_ref, bf16[2048,6656]{1,0:T(8,128)(2,1)} %args_0_.36, bf16[2048,6656]{1,0:T(8,128)(2,1)} %args_1_.36, bf16[6656,2048]{1,0:T(8,128)(2,1)} %args_2_.36, bf16[128,2048]{1,0:T(8,128)(2,1)} %collective-permute-done.4.args_3_, ...), custom_call_target="tpu_custom_call" | custom-call | flops 1000 | bytes 1000 | tf_op jit(solution)/shard_map/step_g/pallas_call | solution.py:367
  71.9 5.8 %step_g.13.args_8_.args_3_ = bf16[128,896]{1,0:T(8,128)(2,1)} custom-call(s32[5]{0:T(128)} %pad_add_fusion.table_ref, bf16[2048,6656]{1,0:T(8,128)(2,1)} %args_0_.36, bf16[2048,6656]{1,0:T(8,128)(2,1)} %args_1_.36, bf16[6656,2048]{1,0:T(8,128)(2,1)} %args_2_.36, bf16[128,2048]{1,0:T(8,128)(2,1)} %args_3_.14, bf16[128,1792]{1,0:T(8,128)(2,1)} %collective-permute-done.args_4_, ...), custom_call_target="tpu_custom_call" | custom-call | flops 1000 | bytes 1000 | tf_op jit(solution)/shard_map/step_g/pallas_call | solution.py:367
  77.7 5.4 %step_g.14.args_6_.args_7_ = bf16[128,768]{1,0:T(8,128)(2,1)} custom-call(s32[5]{0:T(128)} %pad_add_fusion.table_ref, bf16[2048,6656]{1,0:T(8,128)(2,1)} %args_0_.36, bf16[2048,6656]{1,0:T(8,128)(2,1)} %args_1_.36, bf16[6656,2048]{1,0:T(8,128)(2,1)} %args_2_.36, bf16[128,2048]{1,0:T(8,128)(2,1)} %args_3_.14, ...), custom_call_target="tpu_custom_call" | custom-call | flops 1000 | bytes 1000 | tf_op jit(solution)/shard_map/step_g/pallas_call | solution.py:367
  83.2 5.5 %step_g.15.args_4_ = bf16[256,1280]{1,0:T(8,128)(2,1)} custom-call(s32[5]{0:T(128)} %pad_add_fusion.table_ref, bf16[2048,6656]{1,0:T(8,128)(2,1)} %args_0_.36, bf16[2048,6656]{1,0:T(8,128)(2,1)} %args_1_.36, bf16[6656,2048]{1,0:T(8,128)(2,1)} %args_2_.36, bf16[128,2048]{1,0:T(8,128)(2,1)} %collective-permute-done.4.args_3_, ...), custom_call_target="tpu_custom_call" | custom-call | flops 1000 | bytes 1000 | tf_op jit(solution)/shard_map/step_g/pallas_call | solution.py:367
  89.2 12.2 %step_gg.9 = (bf16[128,3456]{1,0:T(8,128)(2,1)}, bf16[128,3328]{1,0:T(8,128)(2,1)}) custom-call(s32[5]{0:T(128)} %pad_add_fusion.table_ref, bf16[2048,6656]{1,0:T(8,128)(2,1)} %args_0_.36, bf16[2048,6656]{1,0:T(8,128)(2,1)} %args_1_.36, bf16[6656,2048]{1,0:T(8,128)(2,1)} %args_2_.36, bf16[128,2048]{1,0:T(8,128)(2,1)} %collective-permute-done.16.args_3_, ...), custom_call_target="tpu_custom_call" | custom-call | flops 1000 | bytes 1000 | tf_op jit(solution)/shard_map/step_gg/pallas_call | solution.py:367
  103.1 7.3 %step_g.16.args_9_.args_3_ = bf16[256,1024]{1,0:T(8,128)(2,1)} custom-call(s32[5]{0:T(128)} %pad_add_fusion.table_ref, bf16[2048,6656]{1,0:T(8,128)(2,1)} %args_0_.36, bf16[2048,6656]{1,0:T(8,128)(2,1)} %args_1_.36, bf16[6656,2048]{1,0:T(8,128)(2,1)} %args_2_.36, bf16[128,2048]{1,0:T(8,128)(2,1)} %collective-permute-done.4.args_3_, ...), custom_call_target="tpu_custom_call" | custom-call | flops 1000 | bytes 1000 | tf_op jit(solution)/shard_map/step_g/pallas_call | solution.py:367
  112.5 5.9 %step_g.17.args_5_.args_7_ = bf16[256,640]{1,0:T(8,128)(2,1)} custom-call(s32[5]{0:T(128)} %pad_add_fusion.table_ref, bf16[2048,6656]{1,0:T(8,128)(2,1)} %args_0_.36, bf16[2048,6656]{1,0:T(8,128)(2,1)} %args_1_.36, bf16[6656,2048]{1,0:T(8,128)(2,1)} %args_2_.36, bf16[128,2048]{1,0:T(8,128)(2,1)} %collective-permute-done.4.args_3_, ...), custom_call_target="tpu_custom_call" | custom-call | flops 1000 | bytes 1000 | tf_op jit(solution)/shard_map/step_g/pallas_call | solution.py:367
  118.7 10.3 %collective-permute-done.19.args_9_ = bf16[128,768]{1,0:T(8,128)(2,1)} collective-permute-done((bf16[128,768]{1,0:T(8,128)(2,1)}, bf16[128,768]{1,0:T(8,128)(2,1)}, u32[]{:S(2)}, u32[]{:S(2)}) %collective-permute-start.19) | collective-permute-done | bytes 196640 | tf_op jit(solution)/shard_map/ppermute | solution.py:21
  130.4 7.8 %step_g.18 = (bf16[128,3456]{1,0:T(8,128)(2,1)}, f32[128,128]{1,0:T(8,128)}) custom-call(s32[5]{0:T(128)} %pad_add_fusion.table_ref, bf16[2048,6656]{1,0:T(8,128)(2,1)} %args_0_.36, bf16[2048,6656]{1,0:T(8,128)(2,1)} %args_1_.36, bf16[6656,2048]{1,0:T(8,128)(2,1)} %args_2_.36, bf16[128,2048]{1,0:T(8,128)(2,1)} %collective-permute-done.16.args_3_, ...), custom_call_target="tpu_custom_call" | custom-call | flops 1000 | bytes 1000 | tf_op jit(solution)/shard_map/step_g/pallas_call | solution.py:367
  143.1 13.8 %step_d.2 = (bf16[128,2048]{1,0:T(8,128)(2,1)}, bf16[128,2048]{1,0:T(8,128)(2,1)}) custom-call(s32[5]{0:T(128)} %pad_add_fusion.table_ref, bf16[2048,6656]{1,0:T(8,128)(2,1)} %args_0_.36, bf16[2048,6656]{1,0:T(8,128)(2,1)} %args_1_.36, bf16[6656,2048]{1,0:T(8,128)(2,1)} %args_2_.36, bf16[256,1024]{1,0:T(8,128)(2,1)} %step_g.16.args_9_.args_3_, ...), custom_call_target="tpu_custom_call" | custom-call | flops 1000 | bytes 1000 | tf_op jit(solution)/shard_map/step_d/pallas_call | solution.py:367
  161.1 8.0 %step_g.19.args_11_.args_15_ = bf16[128,1664]{1,0:T(8,128)(2,1)} custom-call(s32[5]{0:T(128)} %pad_add_fusion.table_ref, bf16[2048,6656]{1,0:T(8,128)(2,1)} %args_0_.36, bf16[2048,6656]{1,0:T(8,128)(2,1)} %args_1_.36, bf16[6656,2048]{1,0:T(8,128)(2,1)} %args_2_.36, bf16[128,2048]{1,0:T(8,128)(2,1)} %collective-permute-done.16.args_3_, ...), custom_call_target="tpu_custom_call" | custom-call | flops 1000 | bytes 1000 | tf_op jit(solution)/shard_map/step_g/pallas_call | solution.py:367
  173.6 3.4 %collective-permute-start.34 = (bf16[128,2048]{1,0:T(8,128)(2,1)}, bf16[128,2048]{1,0:T(8,128)(2,1)}, u32[]{:S(2)}, u32[]{:S(2)}) collective-permute-start(bf16[128,2048]{1,0:T(8,128)(2,1)} %add_convert_fusion.1), channel_id=1, source_target_pairs={{0,2},{1,3},{2,0},{3,1},{4,6},{5,7},{6,4},{7,5},{8,10},{9,11},{10,... | collective-permute-start | bytes 1572872 | tf_op jit(solution)/shard_map/ppermute | solution.py:21
  177.0 3.8 %collective-permute-done.31.args_13_ = bf16[128,1664]{1,0:T(8,128)(2,1)S(1)} collective-permute-done((bf16[128,1664]{1,0:T(8,128)(2,1)}, bf16[128,1664]{1,0:T(8,128)(2,1)S(1)}, u32[]{:S(2)}, u32[]{:S(2)}) %collective-permute-start.31) | collective-permute-done | bytes 426016 | tf_op jit(solution)/shard_map/ppermute | solution.py:21
  182.7 13.9 %step_d.3 = (bf16[128,2048]{1,0:T(8,128)(2,1)}, bf16[128,2048]{1,0:T(8,128)(2,1)}) custom-call(s32[5]{0:T(128)} %pad_add_fusion.table_ref, bf16[2048,6656]{1,0:T(8,128)(2,1)} %args_0_.36, bf16[2048,6656]{1,0:T(8,128)(2,1)} %args_1_.36, bf16[6656,2048]{1,0:T(8,128)(2,1)} %args_2_.36, bf16[128,896]{1,0:T(8,128)(2,1)} %step_g.13.args_8_.args_3_, ...), custom_call_target="tpu_custom_call" | custom-call | flops 1000 | bytes 1000 | tf_op jit(solution)/shard_map/step_d/pallas_call | solution.py:367
  196.6 3.5 %collective-permute-done.34 = bf16[128,2048]{1,0:T(8,128)(2,1)} collective-permute-done((bf16[128,2048]{1,0:T(8,128)(2,1)}, bf16[128,2048]{1,0:T(8,128)(2,1)}, u32[]{:S(2)}, u32[]{:S(2)}) %collective-permute-start.34) | collective-permute-done | bytes 524320 | tf_op jit(solution)/shard_map/ppermute | solution.py:21
  200.2 14.0 %collective-permute-done.35 = bf16[128,2048]{1,0:T(8,128)(2,1)S(1)} collective-permute-done((bf16[128,2048]{1,0:T(8,128)(2,1)}, bf16[128,2048]{1,0:T(8,128)(2,1)S(1)}, u32[]{:S(2)}, u32[]{:S(2)}) %collective-permute-start.35) | collective-permute-done | bytes 524320 | tf_op jit(solution)/shard_map/ppermute | solution.py:21
  (75 shorter events, 35.4 us)
Async XLA Ops:
  0.0 27.5 %collective-permute-start.4 = (bf16[128,2048]{1,0:T(8,128)(2,1)}, bf16[128,2048]{1,0:T(8,128)(2,1)}, u32[]{:S(2)}, u32[]{:S(2)}) collective-permute-start(bf16[128,2048]{1,0:T(8,128)(2,1)} %args_3_.14), channel_id=1, source_target_pairs={{0,2},{1,3},{2,0},{3,1},{4,6},{5,7},{6,4},{7,5},{8,10},{9,11},{10,... | collective-permute-start | bytes 1572872 | tf_op jit(solution)/shard_map/ppermute | solution.py:21
  27.5 15.2 %collective-permute-start.5 = (bf16[128,2048]{1,0:T(8,128)(2,1)}, bf16[128,2048]{1,0:T(8,128)(2,1)}, u32[]{:S(2)}, u32[]{:S(2)}) collective-permute-start(bf16[128,2048]{1,0:T(8,128)(2,1)} %collective-permute-done.4.args_3_), channel_id=1, source_target_pairs={{0,1},{1,0},{2,3},{3,2},{4,5},{5,4},{6,7},{7,6},{8,9},{9,8},{10,11... | collective-permute-start | bytes 1572872 | tf_op jit(solution)/shard_map/ppermute | solution.py:21
  28.2 14.4 %collective-permute-start.2 = (bf16[128,1920]{1,0:T(8,128)(2,1)}, bf16[128,1920]{1,0:T(8,128)(2,1)}, u32[]{:S(2)}, u32[]{:S(2)}) collective-permute-start(bf16[128,1920]{1,0:T(8,128)(2,1)} %get-tuple-element.61.args_5_), channel_id=1, source_target_pairs={{0,8},{4,12},{8,0},{12,4},{1,9},{5,13},{9,1},{13,5},{2,10},{6,14},... | collective-permute-start | bytes 1474568 | tf_op jit(solution)/shard_map/ppermute | solution.py:21
  34.9 17.2 %collective-permute-start.7 = (bf16[128,1536]{1,0:T(8,128)(2,1)}, bf16[128,1536]{1,0:T(8,128)(2,1)}, u32[]{:S(2)}, u32[]{:S(2)}) collective-permute-start(bf16[128,1536]{1,0:T(8,128)(2,1)} %step_g.11.args_5_), channel_id=1, source_target_pairs={{0,8},{4,12},{8,0},{12,4},{1,9},{5,13},{9,1},{13,5},{2,10},{6,14},... | collective-permute-start | bytes 1179656 | tf_op jit(solution)/shard_map/ppermute | solution.py:21
  35.5 34.1 %collective-permute-start.12 = (bf16[128,1536]{1,0:T(8,128)(2,1)}, bf16[128,1536]{1,0:T(8,128)(2,1)}, u32[]{:S(2)}, u32[]{:S(2)}) collective-permute-start(bf16[128,1536]{1,0:T(8,128)(2,1)} %get-tuple-element.71), channel_id=1, source_target_pairs={{0,4},{4,0},{8,12},{12,8},{1,5},{5,1},{9,13},{13,9},{2,6},{6,2},{1... | collective-permute-start | bytes 1179656 | tf_op jit(solution)/shard_map/ppermute | solution.py:21
  59.3 23.8 %collective-permute-start.11 = (bf16[256,1280]{1,0:T(8,128)(2,1)}, bf16[256,1280]{1,0:T(8,128)(2,1)}, u32[]{:S(2)}, u32[]{:S(2)}) collective-permute-start(bf16[256,1280]{1,0:T(8,128)(2,1)} %get-tuple-element.68.args_6_), channel_id=1, source_target_pairs={{0,4},{4,0},{8,12},{12,8},{1,5},{5,1},{9,13},{13,9},{2,6},{6,2},{1... | collective-permute-start | bytes 1966088 | tf_op jit(solution)/shard_map/ppermute | solution.py:21
  59.9 41.7 %collective-permute-start.15 = (bf16[256,2048]{1,0:T(8,128)(2,1)}, bf16[256,2048]{1,0:T(8,128)(2,1)}, u32[]{:S(2)}, u32[]{:S(2)}) collective-permute-start(bf16[256,2048]{1,0:T(8,128)(2,1)} %get-tuple-element.74), channel_id=1, source_target_pairs={{0,4},{4,0},{8,12},{12,8},{1,5},{5,1},{9,13},{13,9},{2,6},{6,2},{1... | collective-permute-start | bytes 3145736 | tf_op jit(solution)/shard_map/ppermute | solution.py:21
  66.7 36.4 %collective-permute-start.14 = (bf16[256,2176]{1,0:T(8,128)(2,1)}, bf16[256,2176]{1,0:T(8,128)(2,1)}, u32[]{:S(2)}, u32[]{:S(2)}) collective-permute-start(bf16[256,2176]{1,0:T(8,128)(2,1)} %get-tuple-element.69.args_7_), channel_id=1, source_target_pairs={{0,8},{4,12},{8,0},{12,4},{1,9},{5,13},{9,1},{13,5},{2,10},{6,14},... | collective-permute-start | bytes 3342344 | tf_op jit(solution)/shard_map/ppermute | solution.py:21
  68.2 21.0 %collective-permute-start.16 = (bf16[128,2048]{1,0:T(8,128)(2,1)}, bf16[128,2048]{1,0:T(8,128)(2,1)}, u32[]{:S(2)}, u32[]{:S(2)}) collective-permute-start(bf16[128,2048]{1,0:T(8,128)(2,1)} %args_3_.14), channel_id=1, source_target_pairs={{0,1},{1,0},{2,3},{3,2},{4,5},{5,4},{6,7},{7,6},{8,9},{9,8},{10,11... | collective-permute-start | bytes 1572872 | tf_op jit(solution)/shard_map/ppermute | solution.py:21
  71.8 39.2 %collective-permute-start.10 = (bf16[256,1280]{1,0:T(8,128)(2,1)}, bf16[256,1280]{1,0:T(8,128)(2,1)}, u32[]{:S(2)}, u32[]{:S(2)}) collective-permute-start(bf16[256,1280]{1,0:T(8,128)(2,1)} %get-tuple-element.70), channel_id=1, source_target_pairs={{0,4},{4,0},{8,12},{12,8},{1,5},{5,1},{9,13},{13,9},{2,6},{6,2},{1... | collective-permute-start | bytes 1966088 | tf_op jit(solution)/shard_map/ppermute | solution.py:21
  88.6 22.3 %collective-permute-start.13 = (bf16[256,1280]{1,0:T(8,128)(2,1)}, bf16[256,1280]{1,0:T(8,128)(2,1)}, u32[]{:S(2)}, u32[]{:S(2)}) collective-permute-start(bf16[256,1280]{1,0:T(8,128)(2,1)} %step_g.15.args_4_), channel_id=1, source_target_pairs={{0,8},{4,12},{8,0},{12,4},{1,9},{5,13},{9,1},{13,5},{2,10},{6,14},... | collective-permute-start | bytes 1966088 | tf_op jit(solution)/shard_map/ppermute | solution.py:21
  101.3 28.1 %collective-permute-start.18 = (bf16[128,3456]{1,0:T(8,128)(2,1)}, bf16[128,3456]{1,0:T(8,128)(2,1)}, u32[]{:S(2)}, u32[]{:S(2)}) collective-permute-start(bf16[128,3456]{1,0:T(8,128)(2,1)} %get-tuple-element.77.args_8_), channel_id=1, source_target_pairs={{0,4},{4,0},{8,12},{12,8},{1,5},{5,1},{9,13},{13,9},{2,6},{6,2},{1... | collective-permute-start | bytes 2654216 | tf_op jit(solution)/shard_map/ppermute | solution.py:21
  101.6 16.9 %collective-permute-start.9 = (bf16[128,896]{1,0:T(8,128)(2,1)}, bf16[128,896]{1,0:T(8,128)(2,1)}, u32[]{:S(2)}, u32[]{:S(2)}) collective-permute-start(bf16[128,896]{1,0:T(8,128)(2,1)} %step_g.13.args_8_.args_3_), channel_id=1, source_target_pairs={{0,8},{4,12},{8,0},{12,4},{1,9},{5,13},{9,1},{13,5},{2,10},{6,14},... | collective-permute-start | bytes 688136 | tf_op jit(solution)/shard_map/ppermute | solution.py:21
  110.4 28.3 %collective-permute-start.25 = (bf16[256,1024]{1,0:T(8,128)(2,1)}, bf16[256,1024]{1,0:T(8,128)(2,1)}, u32[]{:S(2)}, u32[]{:S(2)}) collective-permute-start(bf16[256,1024]{1,0:T(8,128)(2,1)} %step_g.16.args_9_.args_3_), channel_id=1, source_target_pairs={{0,8},{4,12},{8,0},{12,4},{1,9},{5,13},{9,1},{13,5},{2,10},{6,14},... | collective-permute-start | bytes 1572872 | tf_op jit(solution)/shard_map/ppermute | solution.py:21
  111.0 18.0 %collective-permute-start.8 = (bf16[128,896]{1,0:T(8,128)(2,1)}, bf16[128,896]{1,0:T(8,128)(2,1)}, u32[]{:S(2)}, u32[]{:S(2)}) collective-permute-start(bf16[128,896]{1,0:T(8,128)(2,1)} %step_g.13.args_8_.args_3_), channel_id=1, source_target_pairs={{0,4},{4,0},{8,12},{12,8},{1,5},{5,1},{9,13},{13,9},{2,6},{6,2},{1... | collective-permute-start | bytes 688136 | tf_op jit(solution)/shard_map/ppermute | solution.py:21
  111.0 18.0 %collective-permute-start.19 = (bf16[128,768]{1,0:T(8,128)(2,1)}, bf16[128,768]{1,0:T(8,128)(2,1)}, u32[]{:S(2)}, u32[]{:S(2)}) collective-permute-start(bf16[128,768]{1,0:T(8,128)(2,1)} %step_g.14.args_6_.args_7_), channel_id=1, source_target_pairs={{0,8},{4,12},{8,0},{12,4},{1,9},{5,13},{9,1},{13,5},{2,10},{6,14},... | collective-permute-start | bytes 589832 | tf_op jit(solution)/shard_map/ppermute | solution.py:21
  118.4 11.9 %collective-permute-start.17 = (bf16[128,896]{1,0:T(8,128)(2,1)}, bf16[128,896]{1,0:T(8,128)(2,1)}, u32[]{:S(2)}, u32[]{:S(2)}) collective-permute-start(bf16[128,896]{1,0:T(8,128)(2,1)} %collective-permute-done.9.args_5_), channel_id=1, source_target_pairs={{0,4},{4,0},{8,12},{12,8},{1,5},{5,1},{9,13},{13,9},{2,6},{6,2},{1... | collective-permute-start | bytes 688136 | tf_op jit(solution)/shard_map/ppermute | solution.py:21
  129.4 10.5 %collective-permute-start.28 = (bf16[256,640]{1,0:T(8,128)(2,1)}, bf16[256,640]{1,0:T(8,128)(2,1)}, u32[]{:S(2)}, u32[]{:S(2)}) collective-permute-start(bf16[256,640]{1,0:T(8,128)(2,1)} %step_g.17.args_5_.args_7_), channel_id=1, source_target_pairs={{0,8},{4,12},{8,0},{12,4},{1,9},{5,13},{9,1},{13,5},{2,10},{6,14},... | collective-permute-start | bytes 983048 | tf_op jit(solution)/shard_map/ppermute | solution.py:21
  138.8 22.3 %collective-permute-start.23 = (bf16[128,3456]{1,0:T(8,128)(2,1)}, bf16[128,3456]{1,0:T(8,128)(2,1)}, u32[]{:S(2)}, u32[]{:S(2)}) collective-permute-start(bf16[128,3456]{1,0:T(8,128)(2,1)} %get-tuple-element.98.args_11_), channel_id=1, source_target_pairs={{0,8},{4,12},{8,0},{12,4},{1,9},{5,13},{9,1},{13,5},{2,10},{6,14},... | collective-permute-start | bytes 2654216 | tf_op jit(solution)/shard_map/ppermute | solution.py:21
  139.9 18.4 %collective-permute-start.22 = (bf16[128,3328]{1,0:T(8,128)(2,1)}, bf16[128,3328]{1,0:T(8,128)(2,1)}, u32[]{:S(2)}, u32[]{:S(2)}) collective-permute-start(bf16[128,3328]{1,0:T(8,128)(2,1)} %get-tuple-element.92), channel_id=1, source_target_pairs={{0,4},{4,0},{8,12},{12,8},{1,5},{5,1},{9,13},{13,9},{2,6},{6,2},{1... | collective-permute-start | bytes 2555912 | tf_op jit(solution)/shard_map/ppermute | solution.py:21
  157.0 14.5 %collective-permute-start.32 = (bf16[128,2048]{1,0:T(8,128)(2,1)}, bf16[128,2048]{1,0:T(8,128)(2,1)}, u32[]{:S(2)}, u32[]{:S(2)}) collective-permute-start(bf16[128,2048]{1,0:T(8,128)(2,1)} %get-tuple-element.100), channel_id=1, source_target_pairs={{0,1},{1,0},{2,3},{3,2},{4,5},{5,4},{6,7},{7,6},{8,9},{9,8},{10,11... | collective-permute-start | bytes 1572872 | tf_op jit(solution)/shard_map/ppermute | solution.py:21
  169.1 11.6 %collective-permute-start.31 = (bf16[128,1664]{1,0:T(8,128)(2,1)}, bf16[128,1664]{1,0:T(8,128)(2,1)S(1)}, u32[]{:S(2)}, u32[]{:S(2)}) collective-permute-start(bf16[128,1664]{1,0:T(8,128)(2,1)} %step_g.19.args_11_.args_15_), channel_id=1, source_target_pairs={{0,8},{4,12},{8,0},{12,4},{1,9},{5,13},{9,1},{13,5},{2,10},{6,14},... | collective-permute-start | bytes 1277960 | tf_op jit(solution)/shard_map/ppermute | solution.py:21
  173.6 26.6 %collective-permute-start.34 = (bf16[128,2048]{1,0:T(8,128)(2,1)}, bf16[128,2048]{1,0:T(8,128)(2,1)}, u32[]{:S(2)}, u32[]{:S(2)}) collective-permute-start(bf16[128,2048]{1,0:T(8,128)(2,1)} %add_convert_fusion.1), channel_id=1, source_target_pairs={{0,2},{1,3},{2,0},{3,1},{4,6},{5,7},{6,4},{7,5},{8,10},{9,11},{10,... | collective-permute-start | bytes 1572872 | tf_op jit(solution)/shard_map/ppermute | solution.py:21
  200.2 14.0 %collective-permute-start.35 = (bf16[128,2048]{1,0:T(8,128)(2,1)}, bf16[128,2048]{1,0:T(8,128)(2,1)S(1)}, u32[]{:S(2)}, u32[]{:S(2)}) collective-permute-start(bf16[128,2048]{1,0:T(8,128)(2,1)} %get-tuple-element.108), channel_id=1, source_target_pairs={{0,1},{1,0},{2,3},{3,2},{4,5},{5,4},{6,7},{7,6},{8,9},{9,8},{10,11... | collective-permute-start | bytes 1572872 | tf_op jit(solution)/shard_map/ppermute | solution.py:21
  (15 other events, 81.7 us)

commit v12 on v11

--- a/solution.py
+++ b/solution.py
@@ -397,7 +397,7 @@
     ("h1",),
     ("x3",),
     ("b", "s4"),
-    ("h2",),
+    ("h2", "long"),
     ("h3",),
     ("r0", "r1", "x4"),
     ("f0", "f1", "r2", "r3", "d1"),
@@ -427,7 +427,7 @@
     sets = [[0], list(range(2, n_gy)), [1]]
     groups = [Group(blocks, js, block) for js in sets]
     squares = {}
-    half = cut(width, 8, 13)
+    half = cut(width, 7, 13)
     early = cut(width, 7, 13)
     jobs = [(0, 0, early), (0, early, width - early), (1, 0, half), (1, half, width - half), (2, 0, width)]
     firsts = [min(i for i, job in enumerate(jobs) if job[0] == g) for g in range(len(groups))]

time: 217 us -> 211 us (0.972)
  waiting for transfers between devices: 49.4 us -> 44.1 us
    ppermute x36, waiting for transfers between devices: 49.4 us -> 44.1 us  [swap(): return lax.ppermute(value, axis, [(i, i ^ mask) for i in range(size)])]
  transfers between devices with their start and end apart: 36 -> 36, of which waited for: 12 -> 11; matrix products, arithmetic and copies ran while one was open for 1% -> 1% of each run, Pallas kernels for 62% -> 64%
where the time goes in v12:
time: 211 us
  Pallas kernels  135 us (64%)
  waiting for transfers between devices  44.1 us (21%)
  starting transfers between devices  26.5 us (13%)
  other arithmetic  4.99 us (2%)
    pallas_call x17, Pallas kernels, run(): pl.pallas_call(kernel, out_shape=outs, in_specs=[SMEM] + [ANY] * len(oper...  135 us
    ppermute x36, waiting for transfers between devices, swap(): return lax.ppermute(value, axis, [(i, i ^ mask) for i in range(size)])  44.1 us
    ppermute x36, starting transfers between devices, swap(): return lax.ppermute(value, axis, [(i, i ^ mask) for i in range(size)])  26.5 us
  transfers between devices with their start and end apart: 36, of which 11 were waited for; matrix products, arithmetic and copies ran while one was open for 1% of the time, Pallas kernels for 64%

profile of v12, /device:TPU:0, one launch (start us, length us, event | category | flops | bytes accessed | tf_op | source)
XLA Modules:
  0.0 211.1 jit_solution(12351446877920440088)
XLA Ops:
  0.0 4.0 %collective-permute-start.4 = (bf16[128,2048]{1,0:T(8,128)(2,1)}, bf16[128,2048]{1,0:T(8,128)(2,1)}, u32[]{:S(2)}, u32[]{:S(2)}) collective-permute-start(bf16[128,2048]{1,0:T(8,128)(2,1)} %args_3_.14), channel_id=1, source_target_pairs={{0,2},{1,3},{2,0},{3,1},{4,6},{5,7},{6,4},{7,5},{8,10},{9,11},{10,... | collective-permute-start | bytes 1572872 | tf_op jit(solution)/shard_map/ppermute | solution.py:21
  4.7 7.9 %step_gg.5 = (bf16[128,1920]{1,0:T(8,128)(2,1)}, bf16[128,1792]{1,0:T(8,128)(2,1)}) custom-call(s32[5]{0:T(128)} %pad_add_fusion.table_ref, bf16[2048,6656]{1,0:T(8,128)(2,1)} %args_0_.36, bf16[2048,6656]{1,0:T(8,128)(2,1)} %args_1_.36, bf16[6656,2048]{1,0:T(8,128)(2,1)} %args_2_.36, bf16[128,2048]{1,0:T(8,128)(2,1)} %args_3_.14, bf16[128,2048]{1,0:T(8,128)(2,1)} %args_3_.14), custom_call_target="tpu_custom_call" | custom-call | flops 1000 | bytes 1000 | tf_op jit(solution)/shard_map/step_gg/pallas_call | solution.py:367
  12.6 7.1 %step_gg.6 = (bf16[128,1536]{1,0:T(8,128)(2,1)}, bf16[128,1536]{1,0:T(8,128)(2,1)}) custom-call(s32[5]{0:T(128)} %pad_add_fusion.table_ref, bf16[2048,6656]{1,0:T(8,128)(2,1)} %args_0_.36, bf16[2048,6656]{1,0:T(8,128)(2,1)} %args_1_.36, bf16[6656,2048]{1,0:T(8,128)(2,1)} %args_2_.36, bf16[128,2048]{1,0:T(8,128)(2,1)} %args_3_.14, ...), custom_call_target="tpu_custom_call" | custom-call | flops 1000 | bytes 1000 | tf_op jit(solution)/shard_map/step_gg/pallas_call | solution.py:367
  20.5 5.6 %step_g.10 = (bf16[128,1920]{1,0:T(8,128)(2,1)}, f32[128,128]{1,0:T(8,128)}) custom-call(s32[5]{0:T(128)} %pad_add_fusion.table_ref, bf16[2048,6656]{1,0:T(8,128)(2,1)} %args_0_.36, bf16[2048,6656]{1,0:T(8,128)(2,1)} %args_1_.36, bf16[6656,2048]{1,0:T(8,128)(2,1)} %args_2_.36, bf16[128,2048]{1,0:T(8,128)(2,1)} %args_3_.14, ...), custom_call_target="tpu_custom_call" | custom-call | flops 1000 | bytes 1000 | tf_op jit(solution)/shard_map/step_g/pallas_call | solution.py:367
  29.7 5.2 %step_g.11.args_5_ = bf16[128,1536]{1,0:T(8,128)(2,1)} custom-call(s32[5]{0:T(128)} %pad_add_fusion.table_ref, bf16[2048,6656]{1,0:T(8,128)(2,1)} %args_0_.36, bf16[2048,6656]{1,0:T(8,128)(2,1)} %args_1_.36, bf16[6656,2048]{1,0:T(8,128)(2,1)} %args_2_.36, bf16[128,2048]{1,0:T(8,128)(2,1)} %args_3_.14, bf16[128,1536]{1,0:T(8,128)(2,1)} %collective-permute-done.3.args_4_, ...), custom_call_target="tpu_custom_call" | custom-call | flops 1000 | bytes 1000 | tf_op jit(solution)/shard_map/step_g/pallas_call | solution.py:367
  36.0 6.7 %collective-permute-done.2.args_5_.args_7_ = bf16[128,1920]{1,0:T(8,128)(2,1)} collective-permute-done((bf16[128,1920]{1,0:T(8,128)(2,1)}, bf16[128,1920]{1,0:T(8,128)(2,1)}, u32[]{:S(2)}, u32[]{:S(2)}) %collective-permute-start.2) | collective-permute-done | bytes 491552 | tf_op jit(solution)/shard_map/ppermute | solution.py:21
  42.7 8.7 %step_gg.7 = (bf16[256,1920]{1,0:T(8,128)(2,1)}, bf16[256,1792]{1,0:T(8,128)(2,1)}) custom-call(s32[5]{0:T(128)} %pad_add_fusion.table_ref, bf16[2048,6656]{1,0:T(8,128)(2,1)} %args_0_.36, bf16[2048,6656]{1,0:T(8,128)(2,1)} %args_1_.36, bf16[6656,2048]{1,0:T(8,128)(2,1)} %args_2_.36, bf16[128,2048]{1,0:T(8,128)(2,1)} %collective-permute-done.4.args_3_, ...), custom_call_target="tpu_custom_call" | custom-call | flops 1000 | bytes 1000 | tf_op jit(solution)/shard_map/step_gg/pallas_call | solution.py:367
  51.5 7.8 %step_gg.8 = (bf16[256,1536]{1,0:T(8,128)(2,1)}, bf16[256,1536]{1,0:T(8,128)(2,1)}) custom-call(s32[5]{0:T(128)} %pad_add_fusion.table_ref, bf16[2048,6656]{1,0:T(8,128)(2,1)} %args_0_.36, bf16[2048,6656]{1,0:T(8,128)(2,1)} %args_1_.36, bf16[6656,2048]{1,0:T(8,128)(2,1)} %args_2_.36, bf16[128,2048]{1,0:T(8,128)(2,1)} %collective-permute-done.4.args_3_, ...), custom_call_target="tpu_custom_call" | custom-call | flops 99999997952 | bytes 1000 | tf_op jit(solution)/shard_map/step_gg/pallas_call | solution.py:367
  59.3 6.3 %step_g.12 = (bf16[256,1920]{1,0:T(8,128)(2,1)}, f32[256,128]{1,0:T(8,128)}) custom-call(s32[5]{0:T(128)} %pad_add_fusion.table_ref, bf16[2048,6656]{1,0:T(8,128)(2,1)} %args_0_.36, bf16[2048,6656]{1,0:T(8,128)(2,1)} %args_1_.36, bf16[6656,2048]{1,0:T(8,128)(2,1)} %args_2_.36, bf16[128,2048]{1,0:T(8,128)(2,1)} %collective-permute-done.4.args_3_, ...), custom_call_target="tpu_custom_call" | custom-call | flops 1000 | bytes 1000 | tf_op jit(solution)/shard_map/step_g/pallas_call | solution.py:367
  69.3 5.8 %step_g.13.args_8_.args_3_ = bf16[128,896]{1,0:T(8,128)(2,1)} custom-call(s32[5]{0:T(128)} %pad_add_fusion.table_ref, bf16[2048,6656]{1,0:T(8,128)(2,1)} %args_0_.36, bf16[2048,6656]{1,0:T(8,128)(2,1)} %args_1_.36, bf16[6656,2048]{1,0:T(8,128)(2,1)} %args_2_.36, bf16[128,2048]{1,0:T(8,128)(2,1)} %args_3_.14, bf16[128,1792]{1,0:T(8,128)(2,1)} %collective-permute-done.args_4_, ...), custom_call_target="tpu_custom_call" | custom-call | flops 1000 | bytes 1000 | tf_op jit(solution)/shard_map/step_g/pallas_call | solution.py:367
  75.2 5.4 %step_g.14.args_6_.args_7_ = bf16[128,768]{1,0:T(8,128)(2,1)} custom-call(s32[5]{0:T(128)} %pad_add_fusion.table_ref, bf16[2048,6656]{1,0:T(8,128)(2,1)} %args_0_.36, bf16[2048,6656]{1,0:T(8,128)(2,1)} %args_1_.36, bf16[6656,2048]{1,0:T(8,128)(2,1)} %args_2_.36, bf16[128,2048]{1,0:T(8,128)(2,1)} %args_3_.14, ...), custom_call_target="tpu_custom_call" | custom-call | flops 1000 | bytes 1000 | tf_op jit(solution)/shard_map/step_g/pallas_call | solution.py:367
  81.2 5.8 %step_g.15.args_4_ = bf16[256,1536]{1,0:T(8,128)(2,1)} custom-call(s32[5]{0:T(128)} %pad_add_fusion.table_ref, bf16[2048,6656]{1,0:T(8,128)(2,1)} %args_0_.36, bf16[2048,6656]{1,0:T(8,128)(2,1)} %args_1_.36, bf16[6656,2048]{1,0:T(8,128)(2,1)} %args_2_.36, bf16[128,2048]{1,0:T(8,128)(2,1)} %collective-permute-done.4.args_3_, ...), custom_call_target="tpu_custom_call" | custom-call | flops 1000 | bytes 1000 | tf_op jit(solution)/shard_map/step_g/pallas_call | solution.py:367
  88.6 12.1 %step_gg.9 = (bf16[128,3456]{1,0:T(8,128)(2,1)}, bf16[128,3328]{1,0:T(8,128)(2,1)}) custom-call(s32[5]{0:T(128)} %pad_add_fusion.table_ref, bf16[2048,6656]{1,0:T(8,128)(2,1)} %args_0_.36, bf16[2048,6656]{1,0:T(8,128)(2,1)} %args_1_.36, bf16[6656,2048]{1,0:T(8,128)(2,1)} %args_2_.36, bf16[128,2048]{1,0:T(8,128)(2,1)} %collective-permute-done.16.args_3_, ...), custom_call_target="tpu_custom_call" | custom-call | flops 1000 | bytes 1000 | tf_op jit(solution)/shard_map/step_gg/pallas_call | solution.py:367
  101.9 7.0 %step_g.16.args_9_.args_3_ = bf16[256,896]{1,0:T(8,128)(2,1)} custom-call(s32[5]{0:T(128)} %pad_add_fusion.table_ref, bf16[2048,6656]{1,0:T(8,128)(2,1)} %args_0_.36, bf16[2048,6656]{1,0:T(8,128)(2,1)} %args_1_.36, bf16[6656,2048]{1,0:T(8,128)(2,1)} %args_2_.36, bf16[128,2048]{1,0:T(8,128)(2,1)} %collective-permute-done.4.args_3_, ...), custom_call_target="tpu_custom_call" | custom-call | flops 99999997952 | bytes 1000 | tf_op jit(solution)/shard_map/step_g/pallas_call | solution.py:367
  108.9 3.5 %collective-permute-done.13.args_6_ = bf16[256,1536]{1,0:T(8,128)(2,1)} collective-permute-done((bf16[256,1536]{1,0:T(8,128)(2,1)}, bf16[256,1536]{1,0:T(8,128)(2,1)}, u32[]{:S(2)}, u32[]{:S(2)}) %collective-permute-start.13) | collective-permute-done | bytes 786464 | tf_op jit(solution)/shard_map/ppermute | solution.py:21
  113.9 6.3 %step_g.17.args_5_.args_7_ = bf16[256,768]{1,0:T(8,128)(2,1)} custom-call(s32[5]{0:T(128)} %pad_add_fusion.table_ref, bf16[2048,6656]{1,0:T(8,128)(2,1)} %args_0_.36, bf16[2048,6656]{1,0:T(8,128)(2,1)} %args_1_.36, bf16[6656,2048]{1,0:T(8,128)(2,1)} %args_2_.36, bf16[128,2048]{1,0:T(8,128)(2,1)} %collective-permute-done.4.args_3_, ...), custom_call_target="tpu_custom_call" | custom-call | flops 1000 | bytes 1000 | tf_op jit(solution)/shard_map/step_g/pallas_call | solution.py:367
  122.2 7.8 %step_g.18 = (bf16[128,3456]{1,0:T(8,128)(2,1)}, f32[128,128]{1,0:T(8,128)}) custom-call(s32[5]{0:T(128)} %pad_add_fusion.table_ref, bf16[2048,6656]{1,0:T(8,128)(2,1)} %args_0_.36, bf16[2048,6656]{1,0:T(8,128)(2,1)} %args_1_.36, bf16[6656,2048]{1,0:T(8,128)(2,1)} %args_2_.36, bf16[128,2048]{1,0:T(8,128)(2,1)} %collective-permute-done.16.args_3_, ...), custom_call_target="tpu_custom_call" | custom-call | flops 1000 | bytes 1000 | tf_op jit(solution)/shard_map/step_g/pallas_call | solution.py:367
  130.6 3.9 %collective-permute-done.28.args_9_ = bf16[256,768]{1,0:T(8,128)(2,1)} collective-permute-done((bf16[256,768]{1,0:T(8,128)(2,1)}, bf16[256,768]{1,0:T(8,128)(2,1)}, u32[]{:S(2)}, u32[]{:S(2)}) %collective-permute-start.28) | collective-permute-done | bytes 393248 | tf_op jit(solution)/shard_map/ppermute | solution.py:21
  136.6 13.8 %step_d.2 = (bf16[128,2048]{1,0:T(8,128)(2,1)}, bf16[128,2048]{1,0:T(8,128)(2,1)}) custom-call(s32[5]{0:T(128)} %pad_add_fusion.table_ref, bf16[2048,6656]{1,0:T(8,128)(2,1)} %args_0_.36, bf16[2048,6656]{1,0:T(8,128)(2,1)} %args_1_.36, bf16[6656,2048]{1,0:T(8,128)(2,1)} %args_2_.36, bf16[256,896]{1,0:T(8,128)(2,1)} %step_g.16.args_9_.args_3_, ...), custom_call_target="tpu_custom_call" | custom-call | flops 1000 | bytes 1000 | tf_op jit(solution)/shard_map/step_d/pallas_call | solution.py:367
  151.8 5.1 %collective-permute-done.23.args_5_ = bf16[128,3456]{1,0:T(8,128)(2,1)} collective-permute-done((bf16[128,3456]{1,0:T(8,128)(2,1)}, bf16[128,3456]{1,0:T(8,128)(2,1)}, u32[]{:S(2)}, u32[]{:S(2)}) %collective-permute-start.23) | collective-permute-done | bytes 884768 | tf_op jit(solution)/shard_map/ppermute | solution.py:21
  156.9 8.0 %step_g.19.args_11_.args_15_ = bf16[128,1664]{1,0:T(8,128)(2,1)} custom-call(s32[5]{0:T(128)} %pad_add_fusion.table_ref, bf16[2048,6656]{1,0:T(8,128)(2,1)} %args_0_.36, bf16[2048,6656]{1,0:T(8,128)(2,1)} %args_1_.36, bf16[6656,2048]{1,0:T(8,128)(2,1)} %args_2_.36, bf16[128,2048]{1,0:T(8,128)(2,1)} %collective-permute-done.16.args_3_, ...), custom_call_target="tpu_custom_call" | custom-call | flops 1000 | bytes 1000 | tf_op jit(solution)/shard_map/step_g/pallas_call | solution.py:367
  171.9 4.7 %collective-permute-done.31.args_13_ = bf16[128,1664]{1,0:T(8,128)(2,1)S(1)} collective-permute-done((bf16[128,1664]{1,0:T(8,128)(2,1)}, bf16[128,1664]{1,0:T(8,128)(2,1)S(1)}, u32[]{:S(2)}, u32[]{:S(2)}) %collective-permute-start.31) | collective-permute-done | bytes 426016 | tf_op jit(solution)/shard_map/ppermute | solution.py:21
  179.2 13.9 %step_d.3 = (bf16[128,2048]{1,0:T(8,128)(2,1)}, bf16[128,2048]{1,0:T(8,128)(2,1)}) custom-call(s32[5]{0:T(128)} %pad_add_fusion.table_ref, bf16[2048,6656]{1,0:T(8,128)(2,1)} %args_0_.36, bf16[2048,6656]{1,0:T(8,128)(2,1)} %args_1_.36, bf16[6656,2048]{1,0:T(8,128)(2,1)} %args_2_.36, bf16[128,896]{1,0:T(8,128)(2,1)} %step_g.13.args_8_.args_3_, ...), custom_call_target="tpu_custom_call" | custom-call | flops 1000 | bytes 1000 | tf_op jit(solution)/shard_map/step_d/pallas_call | solution.py:367
  194.9 14.0 %collective-permute-done.35 = bf16[128,2048]{1,0:T(8,128)(2,1)S(1)} collective-permute-done((bf16[128,2048]{1,0:T(8,128)(2,1)}, bf16[128,2048]{1,0:T(8,128)(2,1)S(1)}, u32[]{:S(2)}, u32[]{:S(2)}) %collective-permute-start.35) | collective-permute-done | bytes 524320 | tf_op jit(solution)/shard_map/ppermute | solution.py:21
  (71 shorter events, 34.4 us)
Async XLA Ops:
  0.0 27.5 %collective-permute-start.4 = (bf16[128,2048]{1,0:T(8,128)(2,1)}, bf16[128,2048]{1,0:T(8,128)(2,1)}, u32[]{:S(2)}, u32[]{:S(2)}) collective-permute-start(bf16[128,2048]{1,0:T(8,128)(2,1)} %args_3_.14), channel_id=1, source_target_pairs={{0,2},{1,3},{2,0},{3,1},{4,6},{5,7},{6,4},{7,5},{8,10},{9,11},{10,... | collective-permute-start | bytes 1572872 | tf_op jit(solution)/shard_map/ppermute | solution.py:21
  27.5 15.2 %collective-permute-start.5 = (bf16[128,2048]{1,0:T(8,128)(2,1)}, bf16[128,2048]{1,0:T(8,128)(2,1)}, u32[]{:S(2)}, u32[]{:S(2)}) collective-permute-start(bf16[128,2048]{1,0:T(8,128)(2,1)} %collective-permute-done.4.args_3_), channel_id=1, source_target_pairs={{0,1},{1,0},{2,3},{3,2},{4,5},{5,4},{6,7},{7,6},{8,9},{9,8},{10,11... | collective-permute-start | bytes 1572872 | tf_op jit(solution)/shard_map/ppermute | solution.py:21
  28.2 14.4 %collective-permute-start.2 = (bf16[128,1920]{1,0:T(8,128)(2,1)}, bf16[128,1920]{1,0:T(8,128)(2,1)}, u32[]{:S(2)}, u32[]{:S(2)}) collective-permute-start(bf16[128,1920]{1,0:T(8,128)(2,1)} %get-tuple-element.61.args_5_), channel_id=1, source_target_pairs={{0,8},{4,12},{8,0},{12,4},{1,9},{5,13},{9,1},{13,5},{2,10},{6,14},... | collective-permute-start | bytes 1474568 | tf_op jit(solution)/shard_map/ppermute | solution.py:21
  34.9 16.6 %collective-permute-start.7 = (bf16[128,1536]{1,0:T(8,128)(2,1)}, bf16[128,1536]{1,0:T(8,128)(2,1)}, u32[]{:S(2)}, u32[]{:S(2)}) collective-permute-start(bf16[128,1536]{1,0:T(8,128)(2,1)} %step_g.11.args_5_), channel_id=1, source_target_pairs={{0,8},{4,12},{8,0},{12,4},{1,9},{5,13},{9,1},{13,5},{2,10},{6,14},... | collective-permute-start | bytes 1179656 | tf_op jit(solution)/shard_map/ppermute | solution.py:21
  35.5 32.5 %collective-permute-start = (bf16[128,1792]{1,0:T(8,128)(2,1)}, bf16[128,1792]{1,0:T(8,128)(2,1)}, u32[]{:S(2)}, u32[]{:S(2)}) collective-permute-start(bf16[128,1792]{1,0:T(8,128)(2,1)} %get-tuple-element.57), channel_id=1, source_target_pairs={{0,4},{4,0},{8,12},{12,8},{1,5},{5,1},{9,13},{13,9},{2,6},{6,2},{1... | collective-permute-start | bytes 1376264 | tf_op jit(solution)/shard_map/ppermute | solution.py:21
  35.5 32.2 %collective-permute-start.12 = (bf16[128,1536]{1,0:T(8,128)(2,1)}, bf16[128,1536]{1,0:T(8,128)(2,1)}, u32[]{:S(2)}, u32[]{:S(2)}) collective-permute-start(bf16[128,1536]{1,0:T(8,128)(2,1)} %get-tuple-element.71), channel_id=1, source_target_pairs={{0,4},{4,0},{8,12},{12,8},{1,5},{5,1},{9,13},{13,9},{2,6},{6,2},{1... | collective-permute-start | bytes 1179656 | tf_op jit(solution)/shard_map/ppermute | solution.py:21
  65.7 35.7 %collective-permute-start.14 = (bf16[256,1920]{1,0:T(8,128)(2,1)}, bf16[256,1920]{1,0:T(8,128)(2,1)}, u32[]{:S(2)}, u32[]{:S(2)}) collective-permute-start(bf16[256,1920]{1,0:T(8,128)(2,1)} %get-tuple-element.69.args_7_), channel_id=1, source_target_pairs={{0,8},{4,12},{8,0},{12,4},{1,9},{5,13},{9,1},{13,5},{2,10},{6,14},... | collective-permute-start | bytes 2949128 | tf_op jit(solution)/shard_map/ppermute | solution.py:21
  67.2 34.1 %collective-permute-start.15 = (bf16[256,1792]{1,0:T(8,128)(2,1)}, bf16[256,1792]{1,0:T(8,128)(2,1)}, u32[]{:S(2)}, u32[]{:S(2)}) collective-permute-start(bf16[256,1792]{1,0:T(8,128)(2,1)} %get-tuple-element.74), channel_id=1, source_target_pairs={{0,4},{4,0},{8,12},{12,8},{1,5},{5,1},{9,13},{13,9},{2,6},{6,2},{1... | collective-permute-start | bytes 2752520 | tf_op jit(solution)/shard_map/ppermute | solution.py:21
  67.4 13.1 %collective-permute-start.11 = (bf16[256,1536]{1,0:T(8,128)(2,1)}, bf16[256,1536]{1,0:T(8,128)(2,1)}, u32[]{:S(2)}, u32[]{:S(2)}) collective-permute-start(bf16[256,1536]{1,0:T(8,128)(2,1)} %get-tuple-element.68.args_6_), channel_id=1, source_target_pairs={{0,4},{4,0},{8,12},{12,8},{1,5},{5,1},{9,13},{13,9},{2,6},{6,2},{1... | collective-permute-start | bytes 2359304 | tf_op jit(solution)/shard_map/ppermute | solution.py:21
  67.7 33.0 %collective-permute-start.10 = (bf16[256,1536]{1,0:T(8,128)(2,1)}, bf16[256,1536]{1,0:T(8,128)(2,1)}, u32[]{:S(2)}, u32[]{:S(2)}) collective-permute-start(bf16[256,1536]{1,0:T(8,128)(2,1)} %get-tuple-element.70), channel_id=1, source_target_pairs={{0,4},{4,0},{8,12},{12,8},{1,5},{5,1},{9,13},{13,9},{2,6},{6,2},{1... | collective-permute-start | bytes 2359304 | tf_op jit(solution)/shard_map/ppermute | solution.py:21
  67.9 19.1 %collective-permute-start.16 = (bf16[128,2048]{1,0:T(8,128)(2,1)}, bf16[128,2048]{1,0:T(8,128)(2,1)}, u32[]{:S(2)}, u32[]{:S(2)}) collective-permute-start(bf16[128,2048]{1,0:T(8,128)(2,1)} %args_3_.14), channel_id=1, source_target_pairs={{0,1},{1,0},{2,3},{3,2},{4,5},{5,4},{6,7},{7,6},{8,9},{9,8},{10,11... | collective-permute-start | bytes 1572872 | tf_op jit(solution)/shard_map/ppermute | solution.py:21
  80.6 39.6 %collective-permute-start.9 = (bf16[128,896]{1,0:T(8,128)(2,1)}, bf16[128,896]{1,0:T(8,128)(2,1)}, u32[]{:S(2)}, u32[]{:S(2)}) collective-permute-start(bf16[128,896]{1,0:T(8,128)(2,1)} %step_g.13.args_8_.args_3_), channel_id=1, source_target_pairs={{0,8},{4,12},{8,0},{12,4},{1,9},{5,13},{9,1},{13,5},{2,10},{6,14},... | collective-permute-start | bytes 688136 | tf_op jit(solution)/shard_map/ppermute | solution.py:21
  87.0 25.3 %collective-permute-start.13 = (bf16[256,1536]{1,0:T(8,128)(2,1)}, bf16[256,1536]{1,0:T(8,128)(2,1)}, u32[]{:S(2)}, u32[]{:S(2)}) collective-permute-start(bf16[256,1536]{1,0:T(8,128)(2,1)} %step_g.15.args_4_), channel_id=1, source_target_pairs={{0,8},{4,12},{8,0},{12,4},{1,9},{5,13},{9,1},{13,5},{2,10},{6,14},... | collective-permute-start | bytes 2359304 | tf_op jit(solution)/shard_map/ppermute | solution.py:21
  100.7 19.5 %collective-permute-start.19 = (bf16[128,768]{1,0:T(8,128)(2,1)}, bf16[128,768]{1,0:T(8,128)(2,1)}, u32[]{:S(2)}, u32[]{:S(2)}) collective-permute-start(bf16[128,768]{1,0:T(8,128)(2,1)} %step_g.14.args_6_.args_7_), channel_id=1, source_target_pairs={{0,8},{4,12},{8,0},{12,4},{1,9},{5,13},{9,1},{13,5},{2,10},{6,14},... | collective-permute-start | bytes 589832 | tf_op jit(solution)/shard_map/ppermute | solution.py:21
  101.3 19.5 %collective-permute-start.8 = (bf16[128,896]{1,0:T(8,128)(2,1)}, bf16[128,896]{1,0:T(8,128)(2,1)}, u32[]{:S(2)}, u32[]{:S(2)}) collective-permute-start(bf16[128,896]{1,0:T(8,128)(2,1)} %step_g.13.args_8_.args_3_), channel_id=1, source_target_pairs={{0,4},{4,0},{8,12},{12,8},{1,5},{5,1},{9,13},{13,9},{2,6},{6,2},{1... | collective-permute-start | bytes 688136 | tf_op jit(solution)/shard_map/ppermute | solution.py:21
  101.4 19.7 %collective-permute-start.18 = (bf16[128,3456]{1,0:T(8,128)(2,1)}, bf16[128,3456]{1,0:T(8,128)(2,1)}, u32[]{:S(2)}, u32[]{:S(2)}) collective-permute-start(bf16[128,3456]{1,0:T(8,128)(2,1)} %get-tuple-element.77.args_8_), channel_id=1, source_target_pairs={{0,4},{4,0},{8,12},{12,8},{1,5},{5,1},{9,13},{13,9},{2,6},{6,2},{1... | collective-permute-start | bytes 2654216 | tf_op jit(solution)/shard_map/ppermute | solution.py:21
  112.4 18.1 %collective-permute-start.25 = (bf16[256,896]{1,0:T(8,128)(2,1)}, bf16[256,896]{1,0:T(8,128)(2,1)}, u32[]{:S(2)}, u32[]{:S(2)}) collective-permute-start(bf16[256,896]{1,0:T(8,128)(2,1)} %step_g.16.args_9_.args_3_), channel_id=1, source_target_pairs={{0,8},{4,12},{8,0},{12,4},{1,9},{5,13},{9,1},{13,5},{2,10},{6,14},... | collective-permute-start | bytes 1376264 | tf_op jit(solution)/shard_map/ppermute | solution.py:21
  120.3 14.2 %collective-permute-start.28 = (bf16[256,768]{1,0:T(8,128)(2,1)}, bf16[256,768]{1,0:T(8,128)(2,1)}, u32[]{:S(2)}, u32[]{:S(2)}) collective-permute-start(bf16[256,768]{1,0:T(8,128)(2,1)} %step_g.17.args_5_.args_7_), channel_id=1, source_target_pairs={{0,8},{4,12},{8,0},{12,4},{1,9},{5,13},{9,1},{13,5},{2,10},{6,14},... | collective-permute-start | bytes 1179656 | tf_op jit(solution)/shard_map/ppermute | solution.py:21
  120.9 15.1 %collective-permute-start.27 = (bf16[256,768]{1,0:T(8,128)(2,1)}, bf16[256,768]{1,0:T(8,128)(2,1)}, u32[]{:S(2)}, u32[]{:S(2)}) collective-permute-start(bf16[256,768]{1,0:T(8,128)(2,1)} %step_g.17.args_5_.args_7_), channel_id=1, source_target_pairs={{0,4},{4,0},{8,12},{12,8},{1,5},{5,1},{9,13},{13,9},{2,6},{6,2},{1... | collective-permute-start | bytes 1179656 | tf_op jit(solution)/shard_map/ppermute | solution.py:21
  134.5 22.4 %collective-permute-start.23 = (bf16[128,3456]{1,0:T(8,128)(2,1)}, bf16[128,3456]{1,0:T(8,128)(2,1)}, u32[]{:S(2)}, u32[]{:S(2)}) collective-permute-start(bf16[128,3456]{1,0:T(8,128)(2,1)} %get-tuple-element.98.args_11_), channel_id=1, source_target_pairs={{0,8},{4,12},{8,0},{12,4},{1,9},{5,13},{9,1},{13,5},{2,10},{6,14},... | collective-permute-start | bytes 2654216 | tf_op jit(solution)/shard_map/ppermute | solution.py:21
  135.9 15.8 %collective-permute-start.22 = (bf16[128,3328]{1,0:T(8,128)(2,1)}, bf16[128,3328]{1,0:T(8,128)(2,1)}, u32[]{:S(2)}, u32[]{:S(2)}) collective-permute-start(bf16[128,3328]{1,0:T(8,128)(2,1)} %get-tuple-element.92), channel_id=1, source_target_pairs={{0,4},{4,0},{8,12},{12,8},{1,5},{5,1},{9,13},{13,9},{2,6},{6,2},{1... | collective-permute-start | bytes 2555912 | tf_op jit(solution)/shard_map/ppermute | solution.py:21
  150.4 16.0 %collective-permute-start.32 = (bf16[128,2048]{1,0:T(8,128)(2,1)}, bf16[128,2048]{1,0:T(8,128)(2,1)}, u32[]{:S(2)}, u32[]{:S(2)}) collective-permute-start(bf16[128,2048]{1,0:T(8,128)(2,1)} %get-tuple-element.100), channel_id=1, source_target_pairs={{0,1},{1,0},{2,3},{3,2},{4,5},{5,4},{6,7},{7,6},{8,9},{9,8},{10,11... | collective-permute-start | bytes 1572872 | tf_op jit(solution)/shard_map/ppermute | solution.py:21
  168.5 26.5 %collective-permute-start.34 = (bf16[128,2048]{1,0:T(8,128)(2,1)}, bf16[128,2048]{1,0:T(8,128)(2,1)}, u32[]{:S(2)}, u32[]{:S(2)}) collective-permute-start(bf16[128,2048]{1,0:T(8,128)(2,1)} %add_convert_fusion.1), channel_id=1, source_target_pairs={{0,2},{1,3},{2,0},{3,1},{4,6},{5,7},{6,4},{7,5},{8,10},{9,11},{10,... | collective-permute-start | bytes 1572872 | tf_op jit(solution)/shard_map/ppermute | solution.py:21
  194.9 14.0 %collective-permute-start.35 = (bf16[128,2048]{1,0:T(8,128)(2,1)}, bf16[128,2048]{1,0:T(8,128)(2,1)S(1)}, u32[]{:S(2)}, u32[]{:S(2)}) collective-permute-start(bf16[128,2048]{1,0:T(8,128)(2,1)} %get-tuple-element.108), channel_id=1, source_target_pairs={{0,1},{1,0},{2,3},{3,2},{4,5},{5,4},{6,7},{7,6},{8,9},{9,8},{10,11... | collective-permute-start | bytes 1572872 | tf_op jit(solution)/shard_map/ppermute | solution.py:21
  (13 other events, 79.3 us)

commit v13 on v12

--- a/solution.py
+++ b/solution.py
@@ -11,6 +11,7 @@
 LANES = 128
 GU_TILE = 256
 OUT_TILE = 512
+CUTS = 4
 SHORT, LONG = 1000, 10**11
 VMEM_LIMIT = 64 * 1024 * 1024 - 64 * 1024
 ANY = pl.BlockSpec(memory_space=pl.ANY)
@@ -61,7 +62,7 @@
             self.outs.append(jax.ShapeDtypeStruct((rows, LANES), jnp.float32))
 
     def fits(self, depth, columns):
-        return self.width % LANES == 0 and depth % LANES == 0 and self.group.block % 16 == 0
+        return self.width % LANES == 0 and depth % (16 * CUTS) == 0 and self.group.block % 16 == 0
 
     def arrays(self):
         return [*self.recvs, *([self.squares[0], *self.squares[1]] if self.squares else [])]
@@ -108,10 +109,16 @@
         tiles = full + (rest > 0)
         start = table[self.place] + self.low
 
-        def weights(j, m):
+        def weights(j, m, cuts=1):
             columns = pl.ds(pl.multiple_of(start + j * GU_TILE, LANES), m)
+            rows_each = wbuf.shape[1] // cuts
             return [
-                pltpu.make_async_copy(refs[name].at[:, columns], wbuf.at[j, :, pl.ds(i * m, m)], wsem.at[i, j])
+                pltpu.make_async_copy(
+                    refs[name].at[pl.ds(k * rows_each, rows_each), columns],
+                    wbuf.at[j, pl.ds(k * rows_each, rows_each), pl.ds(i * m, m)],
+                    wsem.at[i, j],
+                )
+                for k in range(cuts)
                 for i, name in enumerate(("gate", "up"))
             ]
 
@@ -155,7 +162,7 @@
 
         def begin():
             def step(j, m):
-                for copy in weights(j, m):
+                for copy in weights(j, m, CUTS):
                     copy.start()
 
             over_tiles(step)
@@ -216,7 +223,8 @@
 
     def fits(self, depth, columns):
         sizes = [a.shape[1] for part in self.parts for a, _, _ in part]
-        return all(n % LANES == 0 for n in sizes) and self.columns % OUT_TILE == 0 and self.block % 16 == 0
+        whole = all(n % LANES == 0 for n in sizes) and self.width % (16 * CUTS) == 0
+        return whole and self.columns % OUT_TILE == 0 and self.block % 16 == 0
 
     def arrays(self):
         return [a for part in self.parts for a, _, _ in part]
@@ -258,13 +266,17 @@
         def columns(j):
             return pl.ds(pl.multiple_of(j * OUT_TILE, LANES), OUT_TILE)
 
-        def weights(p, j):
+        def weights(p, j, cuts=1):
             taken = pl.ds(pl.multiple_of(self.first + j * OUT_TILE, LANES), OUT_TILE)
-            return pltpu.make_async_copy(
-                refs["down"].at[pl.ds(pl.multiple_of(table[self.places[p]], LANES), width), taken],
-                dbuf.at[j, pl.ds(p * width, width)],
-                dsem.at[p, j],
-            )
+            each = width // cuts
+            return [
+                pltpu.make_async_copy(
+                    refs["down"].at[pl.ds(pl.multiple_of(table[self.places[p]] + k * each, 16), each), taken],
+                    dbuf.at[j, pl.ds(p * width + k * each, each)],
+                    dsem.at[p, j],
+                )
+                for k in range(cuts)
+            ]
 
         def write(i, j):
             return pltpu.make_async_copy(
@@ -284,7 +296,8 @@
             @pl.loop(0, tiles)
             def _(j):
                 for p in range(len(self.places)):
-                    weights(p, j).start()
+                    for copy in weights(p, j, CUTS):
+                        copy.start()
 
         def compute():
             for copy in copies:
@@ -293,7 +306,7 @@
             @pl.loop(0, tiles)
             def _(j):
                 for p in range(len(self.places)):
-                    weights(p, j).wait()
+                    weights(p, j)[0].wait()
                 result = jnp.dot(hbuf[...], dbuf[j], preferred_element_type=jnp.float32)
                 obuf[j] = result.astype(jnp.bfloat16)
                 for i in range(len(outs)):

time: 211 us -> 211 us (level)
  transfers between devices with their start and end apart: 36 -> 36, of which waited for: 11 -> 11; matrix products, arithmetic and copies ran while one was open for 1% -> 1% of each run, Pallas kernels for 64% -> 63%
where the time goes in v13:
time: 211 us
  Pallas kernels  134 us (64%)
  waiting for transfers between devices  44.7 us (21%)
  starting transfers between devices  26.5 us (13%)
  other arithmetic  4.99 us (2%)
    pallas_call x17, Pallas kernels, run(): pl.pallas_call(kernel, out_shape=outs, in_specs=[SMEM] + [ANY] * len(oper...  134 us
    ppermute x36, waiting for transfers between devices, swap(): return lax.ppermute(value, axis, [(i, i ^ mask) for i in range(size)])  44.7 us
    ppermute x36, starting transfers between devices, swap(): return lax.ppermute(value, axis, [(i, i ^ mask) for i in range(size)])  26.5 us
  transfers between devices with their start and end apart: 36, of which 11 were waited for; matrix products, arithmetic and copies ran while one was open for 1% of the time, Pallas kernels for 63%

profile of v13, /device:TPU:0, one launch (start us, length us, event | category | flops | bytes accessed | tf_op | source)
XLA Modules:
  0.0 211.1 jit_solution(5352432998496466409)
XLA Ops:
  0.0 4.0 %collective-permute-start.4 = (bf16[128,2048]{1,0:T(8,128)(2,1)}, bf16[128,2048]{1,0:T(8,128)(2,1)}, u32[]{:S(2)}, u32[]{:S(2)}) collective-permute-start(bf16[128,2048]{1,0:T(8,128)(2,1)} %args_3_.14), channel_id=1, source_target_pairs={{0,2},{1,3},{2,0},{3,1},{4,6},{5,7},{6,4},{7,5},{8,10},{9,11},{10,... | collective-permute-start | bytes 1572872 | tf_op jit(solution)/shard_map/ppermute | solution.py:22
  4.7 7.8 %step_gg.5 = (bf16[128,1920]{1,0:T(8,128)(2,1)}, bf16[128,1792]{1,0:T(8,128)(2,1)}) custom-call(s32[5]{0:T(128)} %pad_add_fusion.table_ref, bf16[2048,6656]{1,0:T(8,128)(2,1)} %args_0_.36, bf16[2048,6656]{1,0:T(8,128)(2,1)} %args_1_.36, bf16[6656,2048]{1,0:T(8,128)(2,1)} %args_2_.36, bf16[128,2048]{1,0:T(8,128)(2,1)} %args_3_.14, bf16[128,2048]{1,0:T(8,128)(2,1)} %args_3_.14), custom_call_target="tpu_custom_call" | custom-call | flops 1000 | bytes 1000 | tf_op jit(solution)/shard_map/step_gg/pallas_call | solution.py:380
  12.6 7.1 %step_gg.6 = (bf16[128,1536]{1,0:T(8,128)(2,1)}, bf16[128,1536]{1,0:T(8,128)(2,1)}) custom-call(s32[5]{0:T(128)} %pad_add_fusion.table_ref, bf16[2048,6656]{1,0:T(8,128)(2,1)} %args_0_.36, bf16[2048,6656]{1,0:T(8,128)(2,1)} %args_1_.36, bf16[6656,2048]{1,0:T(8,128)(2,1)} %args_2_.36, bf16[128,2048]{1,0:T(8,128)(2,1)} %args_3_.14, ...), custom_call_target="tpu_custom_call" | custom-call | flops 1000 | bytes 1000 | tf_op jit(solution)/shard_map/step_gg/pallas_call | solution.py:380
  20.4 5.5 %step_g.10 = (bf16[128,1920]{1,0:T(8,128)(2,1)}, f32[128,128]{1,0:T(8,128)}) custom-call(s32[5]{0:T(128)} %pad_add_fusion.table_ref, bf16[2048,6656]{1,0:T(8,128)(2,1)} %args_0_.36, bf16[2048,6656]{1,0:T(8,128)(2,1)} %args_1_.36, bf16[6656,2048]{1,0:T(8,128)(2,1)} %args_2_.36, bf16[128,2048]{1,0:T(8,128)(2,1)} %args_3_.14, ...), custom_call_target="tpu_custom_call" | custom-call | flops 1000 | bytes 1000 | tf_op jit(solution)/shard_map/step_g/pallas_call | solution.py:380
  29.7 5.2 %step_g.11.args_5_ = bf16[128,1536]{1,0:T(8,128)(2,1)} custom-call(s32[5]{0:T(128)} %pad_add_fusion.table_ref, bf16[2048,6656]{1,0:T(8,128)(2,1)} %args_0_.36, bf16[2048,6656]{1,0:T(8,128)(2,1)} %args_1_.36, bf16[6656,2048]{1,0:T(8,128)(2,1)} %args_2_.36, bf16[128,2048]{1,0:T(8,128)(2,1)} %args_3_.14, bf16[128,1536]{1,0:T(8,128)(2,1)} %collective-permute-done.3.args_4_, ...), custom_call_target="tpu_custom_call" | custom-call | flops 1000 | bytes 1000 | tf_op jit(solution)/shard_map/step_g/pallas_call | solution.py:380
  36.0 6.7 %collective-permute-done.2.args_5_.args_7_ = bf16[128,1920]{1,0:T(8,128)(2,1)} collective-permute-done((bf16[128,1920]{1,0:T(8,128)(2,1)}, bf16[128,1920]{1,0:T(8,128)(2,1)}, u32[]{:S(2)}, u32[]{:S(2)}) %collective-permute-start.2) | collective-permute-done | bytes 491552 | tf_op jit(solution)/shard_map/ppermute | solution.py:22
  42.7 8.7 %step_gg.7 = (bf16[256,1920]{1,0:T(8,128)(2,1)}, bf16[256,1792]{1,0:T(8,128)(2,1)}) custom-call(s32[5]{0:T(128)} %pad_add_fusion.table_ref, bf16[2048,6656]{1,0:T(8,128)(2,1)} %args_0_.36, bf16[2048,6656]{1,0:T(8,128)(2,1)} %args_1_.36, bf16[6656,2048]{1,0:T(8,128)(2,1)} %args_2_.36, bf16[128,2048]{1,0:T(8,128)(2,1)} %collective-permute-done.4.args_3_, ...), custom_call_target="tpu_custom_call" | custom-call | flops 1000 | bytes 1000 | tf_op jit(solution)/shard_map/step_gg/pallas_call | solution.py:380
  51.5 7.8 %step_gg.8 = (bf16[256,1536]{1,0:T(8,128)(2,1)}, bf16[256,1536]{1,0:T(8,128)(2,1)}) custom-call(s32[5]{0:T(128)} %pad_add_fusion.table_ref, bf16[2048,6656]{1,0:T(8,128)(2,1)} %args_0_.36, bf16[2048,6656]{1,0:T(8,128)(2,1)} %args_1_.36, bf16[6656,2048]{1,0:T(8,128)(2,1)} %args_2_.36, bf16[128,2048]{1,0:T(8,128)(2,1)} %collective-permute-done.4.args_3_, ...), custom_call_target="tpu_custom_call" | custom-call | flops 99999997952 | bytes 1000 | tf_op jit(solution)/shard_map/step_gg/pallas_call | solution.py:380
  59.3 6.3 %step_g.12 = (bf16[256,1920]{1,0:T(8,128)(2,1)}, f32[256,128]{1,0:T(8,128)}) custom-call(s32[5]{0:T(128)} %pad_add_fusion.table_ref, bf16[2048,6656]{1,0:T(8,128)(2,1)} %args_0_.36, bf16[2048,6656]{1,0:T(8,128)(2,1)} %args_1_.36, bf16[6656,2048]{1,0:T(8,128)(2,1)} %args_2_.36, bf16[128,2048]{1,0:T(8,128)(2,1)} %collective-permute-done.4.args_3_, ...), custom_call_target="tpu_custom_call" | custom-call | flops 1000 | bytes 1000 | tf_op jit(solution)/shard_map/step_g/pallas_call | solution.py:380
  69.3 5.8 %step_g.13.args_8_.args_3_ = bf16[128,896]{1,0:T(8,128)(2,1)} custom-call(s32[5]{0:T(128)} %pad_add_fusion.table_ref, bf16[2048,6656]{1,0:T(8,128)(2,1)} %args_0_.36, bf16[2048,6656]{1,0:T(8,128)(2,1)} %args_1_.36, bf16[6656,2048]{1,0:T(8,128)(2,1)} %args_2_.36, bf16[128,2048]{1,0:T(8,128)(2,1)} %args_3_.14, bf16[128,1792]{1,0:T(8,128)(2,1)} %collective-permute-done.args_4_, ...), custom_call_target="tpu_custom_call" | custom-call | flops 1000 | bytes 1000 | tf_op jit(solution)/shard_map/step_g/pallas_call | solution.py:380
  75.1 5.3 %step_g.14.args_6_.args_7_ = bf16[128,768]{1,0:T(8,128)(2,1)} custom-call(s32[5]{0:T(128)} %pad_add_fusion.table_ref, bf16[2048,6656]{1,0:T(8,128)(2,1)} %args_0_.36, bf16[2048,6656]{1,0:T(8,128)(2,1)} %args_1_.36, bf16[6656,2048]{1,0:T(8,128)(2,1)} %args_2_.36, bf16[128,2048]{1,0:T(8,128)(2,1)} %args_3_.14, ...), custom_call_target="tpu_custom_call" | custom-call | flops 1000 | bytes 1000 | tf_op jit(solution)/shard_map/step_g/pallas_call | solution.py:380
  81.0 5.8 %step_g.15.args_4_ = bf16[256,1536]{1,0:T(8,128)(2,1)} custom-call(s32[5]{0:T(128)} %pad_add_fusion.table_ref, bf16[2048,6656]{1,0:T(8,128)(2,1)} %args_0_.36, bf16[2048,6656]{1,0:T(8,128)(2,1)} %args_1_.36, bf16[6656,2048]{1,0:T(8,128)(2,1)} %args_2_.36, bf16[128,2048]{1,0:T(8,128)(2,1)} %collective-permute-done.4.args_3_, ...), custom_call_target="tpu_custom_call" | custom-call | flops 1000 | bytes 1000 | tf_op jit(solution)/shard_map/step_g/pallas_call | solution.py:380
  88.4 12.1 %step_gg.9 = (bf16[128,3456]{1,0:T(8,128)(2,1)}, bf16[128,3328]{1,0:T(8,128)(2,1)}) custom-call(s32[5]{0:T(128)} %pad_add_fusion.table_ref, bf16[2048,6656]{1,0:T(8,128)(2,1)} %args_0_.36, bf16[2048,6656]{1,0:T(8,128)(2,1)} %args_1_.36, bf16[6656,2048]{1,0:T(8,128)(2,1)} %args_2_.36, bf16[128,2048]{1,0:T(8,128)(2,1)} %collective-permute-done.16.args_3_, ...), custom_call_target="tpu_custom_call" | custom-call | flops 1000 | bytes 1000 | tf_op jit(solution)/shard_map/step_gg/pallas_call | solution.py:380
  101.7 6.8 %step_g.16.args_9_.args_3_ = bf16[256,896]{1,0:T(8,128)(2,1)} custom-call(s32[5]{0:T(128)} %pad_add_fusion.table_ref, bf16[2048,6656]{1,0:T(8,128)(2,1)} %args_0_.36, bf16[2048,6656]{1,0:T(8,128)(2,1)} %args_1_.36, bf16[6656,2048]{1,0:T(8,128)(2,1)} %args_2_.36, bf16[128,2048]{1,0:T(8,128)(2,1)} %collective-permute-done.4.args_3_, ...), custom_call_target="tpu_custom_call" | custom-call | flops 99999997952 | bytes 1000 | tf_op jit(solution)/shard_map/step_g/pallas_call | solution.py:380
  108.5 3.8 %collective-permute-done.13.args_6_ = bf16[256,1536]{1,0:T(8,128)(2,1)} collective-permute-done((bf16[256,1536]{1,0:T(8,128)(2,1)}, bf16[256,1536]{1,0:T(8,128)(2,1)}, u32[]{:S(2)}, u32[]{:S(2)}) %collective-permute-start.13) | collective-permute-done | bytes 786464 | tf_op jit(solution)/shard_map/ppermute | solution.py:22
  113.8 6.3 %step_g.17.args_5_.args_7_ = bf16[256,768]{1,0:T(8,128)(2,1)} custom-call(s32[5]{0:T(128)} %pad_add_fusion.table_ref, bf16[2048,6656]{1,0:T(8,128)(2,1)} %args_0_.36, bf16[2048,6656]{1,0:T(8,128)(2,1)} %args_1_.36, bf16[6656,2048]{1,0:T(8,128)(2,1)} %args_2_.36, bf16[128,2048]{1,0:T(8,128)(2,1)} %collective-permute-done.4.args_3_, ...), custom_call_target="tpu_custom_call" | custom-call | flops 1000 | bytes 1000 | tf_op jit(solution)/shard_map/step_g/pallas_call | solution.py:380
  122.1 7.7 %step_g.18 = (bf16[128,3456]{1,0:T(8,128)(2,1)}, f32[128,128]{1,0:T(8,128)}) custom-call(s32[5]{0:T(128)} %pad_add_fusion.table_ref, bf16[2048,6656]{1,0:T(8,128)(2,1)} %args_0_.36, bf16[2048,6656]{1,0:T(8,128)(2,1)} %args_1_.36, bf16[6656,2048]{1,0:T(8,128)(2,1)} %args_2_.36, bf16[128,2048]{1,0:T(8,128)(2,1)} %collective-permute-done.16.args_3_, ...), custom_call_target="tpu_custom_call" | custom-call | flops 1000 | bytes 1000 | tf_op jit(solution)/shard_map/step_g/pallas_call | solution.py:380
  130.4 4.0 %collective-permute-done.28.args_9_ = bf16[256,768]{1,0:T(8,128)(2,1)} collective-permute-done((bf16[256,768]{1,0:T(8,128)(2,1)}, bf16[256,768]{1,0:T(8,128)(2,1)}, u32[]{:S(2)}, u32[]{:S(2)}) %collective-permute-start.28) | collective-permute-done | bytes 393248 | tf_op jit(solution)/shard_map/ppermute | solution.py:22
  136.5 13.8 %step_d.2 = (bf16[128,2048]{1,0:T(8,128)(2,1)}, bf16[128,2048]{1,0:T(8,128)(2,1)}) custom-call(s32[5]{0:T(128)} %pad_add_fusion.table_ref, bf16[2048,6656]{1,0:T(8,128)(2,1)} %args_0_.36, bf16[2048,6656]{1,0:T(8,128)(2,1)} %args_1_.36, bf16[6656,2048]{1,0:T(8,128)(2,1)} %args_2_.36, bf16[256,896]{1,0:T(8,128)(2,1)} %step_g.16.args_9_.args_3_, ...), custom_call_target="tpu_custom_call" | custom-call | flops 1000 | bytes 1000 | tf_op jit(solution)/shard_map/step_d/pallas_call | solution.py:380
  151.7 5.1 %collective-permute-done.23.args_5_ = bf16[128,3456]{1,0:T(8,128)(2,1)} collective-permute-done((bf16[128,3456]{1,0:T(8,128)(2,1)}, bf16[128,3456]{1,0:T(8,128)(2,1)}, u32[]{:S(2)}, u32[]{:S(2)}) %collective-permute-start.23) | collective-permute-done | bytes 884768 | tf_op jit(solution)/shard_map/ppermute | solution.py:22
  156.8 7.9 %step_g.19.args_11_.args_15_ = bf16[128,1664]{1,0:T(8,128)(2,1)} custom-call(s32[5]{0:T(128)} %pad_add_fusion.table_ref, bf16[2048,6656]{1,0:T(8,128)(2,1)} %args_0_.36, bf16[2048,6656]{1,0:T(8,128)(2,1)} %args_1_.36, bf16[6656,2048]{1,0:T(8,128)(2,1)} %args_2_.36, bf16[128,2048]{1,0:T(8,128)(2,1)} %collective-permute-done.16.args_3_, ...), custom_call_target="tpu_custom_call" | custom-call | flops 1000 | bytes 1000 | tf_op jit(solution)/shard_map/step_g/pallas_call | solution.py:380
  171.8 4.7 %collective-permute-done.31.args_13_ = bf16[128,1664]{1,0:T(8,128)(2,1)S(1)} collective-permute-done((bf16[128,1664]{1,0:T(8,128)(2,1)}, bf16[128,1664]{1,0:T(8,128)(2,1)S(1)}, u32[]{:S(2)}, u32[]{:S(2)}) %collective-permute-start.31) | collective-permute-done | bytes 426016 | tf_op jit(solution)/shard_map/ppermute | solution.py:22
  179.2 13.9 %step_d.3 = (bf16[128,2048]{1,0:T(8,128)(2,1)}, bf16[128,2048]{1,0:T(8,128)(2,1)}) custom-call(s32[5]{0:T(128)} %pad_add_fusion.table_ref, bf16[2048,6656]{1,0:T(8,128)(2,1)} %args_0_.36, bf16[2048,6656]{1,0:T(8,128)(2,1)} %args_1_.36, bf16[6656,2048]{1,0:T(8,128)(2,1)} %args_2_.36, bf16[128,896]{1,0:T(8,128)(2,1)} %step_g.13.args_8_.args_3_, ...), custom_call_target="tpu_custom_call" | custom-call | flops 1000 | bytes 1000 | tf_op jit(solution)/shard_map/step_d/pallas_call | solution.py:380
  194.9 14.0 %collective-permute-done.35 = bf16[128,2048]{1,0:T(8,128)(2,1)S(1)} collective-permute-done((bf16[128,2048]{1,0:T(8,128)(2,1)}, bf16[128,2048]{1,0:T(8,128)(2,1)S(1)}, u32[]{:S(2)}, u32[]{:S(2)}) %collective-permute-start.35) | collective-permute-done | bytes 524320 | tf_op jit(solution)/shard_map/ppermute | solution.py:22
  (71 shorter events, 34.6 us)
Async XLA Ops:
  0.0 27.5 %collective-permute-start.4 = (bf16[128,2048]{1,0:T(8,128)(2,1)}, bf16[128,2048]{1,0:T(8,128)(2,1)}, u32[]{:S(2)}, u32[]{:S(2)}) collective-permute-start(bf16[128,2048]{1,0:T(8,128)(2,1)} %args_3_.14), channel_id=1, source_target_pairs={{0,2},{1,3},{2,0},{3,1},{4,6},{5,7},{6,4},{7,5},{8,10},{9,11},{10,... | collective-permute-start | bytes 1572872 | tf_op jit(solution)/shard_map/ppermute | solution.py:22
  27.5 15.2 %collective-permute-start.5 = (bf16[128,2048]{1,0:T(8,128)(2,1)}, bf16[128,2048]{1,0:T(8,128)(2,1)}, u32[]{:S(2)}, u32[]{:S(2)}) collective-permute-start(bf16[128,2048]{1,0:T(8,128)(2,1)} %collective-permute-done.4.args_3_), channel_id=1, source_target_pairs={{0,1},{1,0},{2,3},{3,2},{4,5},{5,4},{6,7},{7,6},{8,9},{9,8},{10,11... | collective-permute-start | bytes 1572872 | tf_op jit(solution)/shard_map/ppermute | solution.py:22
  28.2 14.4 %collective-permute-start.2 = (bf16[128,1920]{1,0:T(8,128)(2,1)}, bf16[128,1920]{1,0:T(8,128)(2,1)}, u32[]{:S(2)}, u32[]{:S(2)}) collective-permute-start(bf16[128,1920]{1,0:T(8,128)(2,1)} %get-tuple-element.61.args_5_), channel_id=1, source_target_pairs={{0,8},{4,12},{8,0},{12,4},{1,9},{5,13},{9,1},{13,5},{2,10},{6,14},... | collective-permute-start | bytes 1474568 | tf_op jit(solution)/shard_map/ppermute | solution.py:22
  34.9 16.6 %collective-permute-start.7 = (bf16[128,1536]{1,0:T(8,128)(2,1)}, bf16[128,1536]{1,0:T(8,128)(2,1)}, u32[]{:S(2)}, u32[]{:S(2)}) collective-permute-start(bf16[128,1536]{1,0:T(8,128)(2,1)} %step_g.11.args_5_), channel_id=1, source_target_pairs={{0,8},{4,12},{8,0},{12,4},{1,9},{5,13},{9,1},{13,5},{2,10},{6,14},... | collective-permute-start | bytes 1179656 | tf_op jit(solution)/shard_map/ppermute | solution.py:22
  35.4 32.5 %collective-permute-start = (bf16[128,1792]{1,0:T(8,128)(2,1)}, bf16[128,1792]{1,0:T(8,128)(2,1)}, u32[]{:S(2)}, u32[]{:S(2)}) collective-permute-start(bf16[128,1792]{1,0:T(8,128)(2,1)} %get-tuple-element.57), channel_id=1, source_target_pairs={{0,4},{4,0},{8,12},{12,8},{1,5},{5,1},{9,13},{13,9},{2,6},{6,2},{1... | collective-permute-start | bytes 1376264 | tf_op jit(solution)/shard_map/ppermute | solution.py:22
  35.4 32.2 %collective-permute-start.12 = (bf16[128,1536]{1,0:T(8,128)(2,1)}, bf16[128,1536]{1,0:T(8,128)(2,1)}, u32[]{:S(2)}, u32[]{:S(2)}) collective-permute-start(bf16[128,1536]{1,0:T(8,128)(2,1)} %get-tuple-element.71), channel_id=1, source_target_pairs={{0,4},{4,0},{8,12},{12,8},{1,5},{5,1},{9,13},{13,9},{2,6},{6,2},{1... | collective-permute-start | bytes 1179656 | tf_op jit(solution)/shard_map/ppermute | solution.py:22
  65.6 35.6 %collective-permute-start.14 = (bf16[256,1920]{1,0:T(8,128)(2,1)}, bf16[256,1920]{1,0:T(8,128)(2,1)}, u32[]{:S(2)}, u32[]{:S(2)}) collective-permute-start(bf16[256,1920]{1,0:T(8,128)(2,1)} %get-tuple-element.69.args_7_), channel_id=1, source_target_pairs={{0,8},{4,12},{8,0},{12,4},{1,9},{5,13},{9,1},{13,5},{2,10},{6,14},... | collective-permute-start | bytes 2949128 | tf_op jit(solution)/shard_map/ppermute | solution.py:22
  67.2 34.0 %collective-permute-start.15 = (bf16[256,1792]{1,0:T(8,128)(2,1)}, bf16[256,1792]{1,0:T(8,128)(2,1)}, u32[]{:S(2)}, u32[]{:S(2)}) collective-permute-start(bf16[256,1792]{1,0:T(8,128)(2,1)} %get-tuple-element.74), channel_id=1, source_target_pairs={{0,4},{4,0},{8,12},{12,8},{1,5},{5,1},{9,13},{13,9},{2,6},{6,2},{1... | collective-permute-start | bytes 2752520 | tf_op jit(solution)/shard_map/ppermute | solution.py:22
  67.4 13.0 %collective-permute-start.11 = (bf16[256,1536]{1,0:T(8,128)(2,1)}, bf16[256,1536]{1,0:T(8,128)(2,1)}, u32[]{:S(2)}, u32[]{:S(2)}) collective-permute-start(bf16[256,1536]{1,0:T(8,128)(2,1)} %get-tuple-element.68.args_6_), channel_id=1, source_target_pairs={{0,4},{4,0},{8,12},{12,8},{1,5},{5,1},{9,13},{13,9},{2,6},{6,2},{1... | collective-permute-start | bytes 2359304 | tf_op jit(solution)/shard_map/ppermute | solution.py:22
  67.7 32.9 %collective-permute-start.10 = (bf16[256,1536]{1,0:T(8,128)(2,1)}, bf16[256,1536]{1,0:T(8,128)(2,1)}, u32[]{:S(2)}, u32[]{:S(2)}) collective-permute-start(bf16[256,1536]{1,0:T(8,128)(2,1)} %get-tuple-element.70), channel_id=1, source_target_pairs={{0,4},{4,0},{8,12},{12,8},{1,5},{5,1},{9,13},{13,9},{2,6},{6,2},{1... | collective-permute-start | bytes 2359304 | tf_op jit(solution)/shard_map/ppermute | solution.py:22
  67.9 18.9 %collective-permute-start.16 = (bf16[128,2048]{1,0:T(8,128)(2,1)}, bf16[128,2048]{1,0:T(8,128)(2,1)}, u32[]{:S(2)}, u32[]{:S(2)}) collective-permute-start(bf16[128,2048]{1,0:T(8,128)(2,1)} %args_3_.14), channel_id=1, source_target_pairs={{0,1},{1,0},{2,3},{3,2},{4,5},{5,4},{6,7},{7,6},{8,9},{9,8},{10,11... | collective-permute-start | bytes 1572872 | tf_op jit(solution)/shard_map/ppermute | solution.py:22
  80.4 39.6 %collective-permute-start.9 = (bf16[128,896]{1,0:T(8,128)(2,1)}, bf16[128,896]{1,0:T(8,128)(2,1)}, u32[]{:S(2)}, u32[]{:S(2)}) collective-permute-start(bf16[128,896]{1,0:T(8,128)(2,1)} %step_g.13.args_8_.args_3_), channel_id=1, source_target_pairs={{0,8},{4,12},{8,0},{12,4},{1,9},{5,13},{9,1},{13,5},{2,10},{6,14},... | collective-permute-start | bytes 688136 | tf_op jit(solution)/shard_map/ppermute | solution.py:22
  86.9 25.4 %collective-permute-start.13 = (bf16[256,1536]{1,0:T(8,128)(2,1)}, bf16[256,1536]{1,0:T(8,128)(2,1)}, u32[]{:S(2)}, u32[]{:S(2)}) collective-permute-start(bf16[256,1536]{1,0:T(8,128)(2,1)} %step_g.15.args_4_), channel_id=1, source_target_pairs={{0,8},{4,12},{8,0},{12,4},{1,9},{5,13},{9,1},{13,5},{2,10},{6,14},... | collective-permute-start | bytes 2359304 | tf_op jit(solution)/shard_map/ppermute | solution.py:22
  100.5 19.6 %collective-permute-start.19 = (bf16[128,768]{1,0:T(8,128)(2,1)}, bf16[128,768]{1,0:T(8,128)(2,1)}, u32[]{:S(2)}, u32[]{:S(2)}) collective-permute-start(bf16[128,768]{1,0:T(8,128)(2,1)} %step_g.14.args_6_.args_7_), channel_id=1, source_target_pairs={{0,8},{4,12},{8,0},{12,4},{1,9},{5,13},{9,1},{13,5},{2,10},{6,14},... | collective-permute-start | bytes 589832 | tf_op jit(solution)/shard_map/ppermute | solution.py:22
  101.2 19.6 %collective-permute-start.8 = (bf16[128,896]{1,0:T(8,128)(2,1)}, bf16[128,896]{1,0:T(8,128)(2,1)}, u32[]{:S(2)}, u32[]{:S(2)}) collective-permute-start(bf16[128,896]{1,0:T(8,128)(2,1)} %step_g.13.args_8_.args_3_), channel_id=1, source_target_pairs={{0,4},{4,0},{8,12},{12,8},{1,5},{5,1},{9,13},{13,9},{2,6},{6,2},{1... | collective-permute-start | bytes 688136 | tf_op jit(solution)/shard_map/ppermute | solution.py:22
  101.2 19.8 %collective-permute-start.18 = (bf16[128,3456]{1,0:T(8,128)(2,1)}, bf16[128,3456]{1,0:T(8,128)(2,1)}, u32[]{:S(2)}, u32[]{:S(2)}) collective-permute-start(bf16[128,3456]{1,0:T(8,128)(2,1)} %get-tuple-element.77.args_8_), channel_id=1, source_target_pairs={{0,4},{4,0},{8,12},{12,8},{1,5},{5,1},{9,13},{13,9},{2,6},{6,2},{1... | collective-permute-start | bytes 2654216 | tf_op jit(solution)/shard_map/ppermute | solution.py:22
  112.3 18.0 %collective-permute-start.25 = (bf16[256,896]{1,0:T(8,128)(2,1)}, bf16[256,896]{1,0:T(8,128)(2,1)}, u32[]{:S(2)}, u32[]{:S(2)}) collective-permute-start(bf16[256,896]{1,0:T(8,128)(2,1)} %step_g.16.args_9_.args_3_), channel_id=1, source_target_pairs={{0,8},{4,12},{8,0},{12,4},{1,9},{5,13},{9,1},{13,5},{2,10},{6,14},... | collective-permute-start | bytes 1376264 | tf_op jit(solution)/shard_map/ppermute | solution.py:22
  120.2 14.3 %collective-permute-start.28 = (bf16[256,768]{1,0:T(8,128)(2,1)}, bf16[256,768]{1,0:T(8,128)(2,1)}, u32[]{:S(2)}, u32[]{:S(2)}) collective-permute-start(bf16[256,768]{1,0:T(8,128)(2,1)} %step_g.17.args_5_.args_7_), channel_id=1, source_target_pairs={{0,8},{4,12},{8,0},{12,4},{1,9},{5,13},{9,1},{13,5},{2,10},{6,14},... | collective-permute-start | bytes 1179656 | tf_op jit(solution)/shard_map/ppermute | solution.py:22
  120.8 15.1 %collective-permute-start.27 = (bf16[256,768]{1,0:T(8,128)(2,1)}, bf16[256,768]{1,0:T(8,128)(2,1)}, u32[]{:S(2)}, u32[]{:S(2)}) collective-permute-start(bf16[256,768]{1,0:T(8,128)(2,1)} %step_g.17.args_5_.args_7_), channel_id=1, source_target_pairs={{0,4},{4,0},{8,12},{12,8},{1,5},{5,1},{9,13},{13,9},{2,6},{6,2},{1... | collective-permute-start | bytes 1179656 | tf_op jit(solution)/shard_map/ppermute | solution.py:22
  134.5 22.4 %collective-permute-start.23 = (bf16[128,3456]{1,0:T(8,128)(2,1)}, bf16[128,3456]{1,0:T(8,128)(2,1)}, u32[]{:S(2)}, u32[]{:S(2)}) collective-permute-start(bf16[128,3456]{1,0:T(8,128)(2,1)} %get-tuple-element.98.args_11_), channel_id=1, source_target_pairs={{0,8},{4,12},{8,0},{12,4},{1,9},{5,13},{9,1},{13,5},{2,10},{6,14},... | collective-permute-start | bytes 2654216 | tf_op jit(solution)/shard_map/ppermute | solution.py:22
  135.9 15.8 %collective-permute-start.22 = (bf16[128,3328]{1,0:T(8,128)(2,1)}, bf16[128,3328]{1,0:T(8,128)(2,1)}, u32[]{:S(2)}, u32[]{:S(2)}) collective-permute-start(bf16[128,3328]{1,0:T(8,128)(2,1)} %get-tuple-element.92), channel_id=1, source_target_pairs={{0,4},{4,0},{8,12},{12,8},{1,5},{5,1},{9,13},{13,9},{2,6},{6,2},{1... | collective-permute-start | bytes 2555912 | tf_op jit(solution)/shard_map/ppermute | solution.py:22
  150.3 16.0 %collective-permute-start.32 = (bf16[128,2048]{1,0:T(8,128)(2,1)}, bf16[128,2048]{1,0:T(8,128)(2,1)}, u32[]{:S(2)}, u32[]{:S(2)}) collective-permute-start(bf16[128,2048]{1,0:T(8,128)(2,1)} %get-tuple-element.100), channel_id=1, source_target_pairs={{0,1},{1,0},{2,3},{3,2},{4,5},{5,4},{6,7},{7,6},{8,9},{9,8},{10,11... | collective-permute-start | bytes 1572872 | tf_op jit(solution)/shard_map/ppermute | solution.py:22
  168.4 26.5 %collective-permute-start.34 = (bf16[128,2048]{1,0:T(8,128)(2,1)}, bf16[128,2048]{1,0:T(8,128)(2,1)}, u32[]{:S(2)}, u32[]{:S(2)}) collective-permute-start(bf16[128,2048]{1,0:T(8,128)(2,1)} %add_convert_fusion.1), channel_id=1, source_target_pairs={{0,2},{1,3},{2,0},{3,1},{4,6},{5,7},{6,4},{7,5},{8,10},{9,11},{10,... | collective-permute-start | bytes 1572872 | tf_op jit(solution)/shard_map/ppermute | solution.py:22
  194.9 14.0 %collective-permute-start.35 = (bf16[128,2048]{1,0:T(8,128)(2,1)}, bf16[128,2048]{1,0:T(8,128)(2,1)S(1)}, u32[]{:S(2)}, u32[]{:S(2)}) collective-permute-start(bf16[128,2048]{1,0:T(8,128)(2,1)} %get-tuple-element.108), channel_id=1, source_target_pairs={{0,1},{1,0},{2,3},{3,2},{4,5},{5,4},{6,7},{7,6},{8,9},{9,8},{10,11... | collective-permute-start | bytes 1572872 | tf_op jit(solution)/shard_map/ppermute | solution.py:22
  (13 other events, 79.5 us)

commit v14 on v13

--- a/solution.py
+++ b/solution.py
@@ -91,7 +91,7 @@
         extra = len(self.squares[1]) if self.squares else n_recv if self.carry else 0
         return [
             pltpu.VMEM((tiles, depth, 2 * GU_TILE), jnp.bfloat16),
-            pltpu.VMEM((n_recv, 2, rows, n) if n_recv else (1, 2, 16, LANES), jnp.bfloat16),
+            pltpu.VMEM((n_recv, 2, rows, tiles * GU_TILE) if n_recv else (1, 2, 16, LANES), jnp.bfloat16),
             pltpu.VMEM((extra, rows, LANES) if extra else (1, 16, LANES), jnp.bfloat16),
             pltpu.VMEM((rows, LANES) if self.squares or self.emit else (8, LANES), jnp.float32),
             pltpu.VMEM((tiles, 1 if self.squares else 2, rows, GU_TILE), jnp.bfloat16),
@@ -115,7 +115,7 @@
             return [
                 pltpu.make_async_copy(
                     refs[name].at[pl.ds(k * rows_each, rows_each), columns],
-                    wbuf.at[j, pl.ds(k * rows_each, rows_each), pl.ds(i * m, m)],
+                    wbuf.at[j, pl.ds(k * rows_each, rows_each), pl.ds(i * GU_TILE, m)],
                     wsem.at[i, j],
                 )
                 for k in range(cuts)
@@ -141,7 +141,7 @@
                 step(full, rest)
 
         copies = [
-            pltpu.make_async_copy(a.at[:, pl.ds(h * n, n)], rbuf.at[i, h], rsem.at[2 * i + h])
+            pltpu.make_async_copy(a.at[:, pl.ds(h * n, n)], rbuf.at[i, h, :, pl.ds(0, n)], rsem.at[2 * i + h])
             for i, a in enumerate(arrays[:n_recv])
             for h in range(2)
         ]
@@ -183,24 +183,36 @@
             if hidden:
                 qbuf[...] = jnp.broadcast_to(lax.rsqrt(total / self.features + EPS), (rows, LANES))
 
-            def step(j, m):
+            def with_width(j, step):
+                if not rest:
+                    return step(j, GU_TILE)
+                if full:
+                    pl.when(j < full)(lambda: step(j, GU_TILE))
+                pl.when(j == full)(lambda: step(full, rest))
+
+            def wait(j, m):
                 for copy in weights(j, m):
                     copy.wait()
-                both = jnp.dot(xbuf[...], wbuf[j, :, pl.ds(0, 2 * m)], preferred_element_type=jnp.float32)
-                gate, up = both[:, :m], both[:, m:]
-                columns = pl.ds(pl.multiple_of(j * GU_TILE, LANES), m)
+
+            def send(j, m):
+                for copy in write(j, m):
+                    copy.start()
+
+            @pl.loop(0, tiles)
+            def _(j):
+                with_width(j, wait)
+                both = jnp.dot(xbuf[...], wbuf[j], preferred_element_type=jnp.float32)
+                gate, up = both[:, :GU_TILE], both[:, GU_TILE:]
+                columns = pl.ds(pl.multiple_of(j * GU_TILE, LANES), GU_TILE)
                 for r in range(n_recv):
                     gate = gate + rbuf[r, 0, :, columns].astype(jnp.float32)
                     up = up + rbuf[r, 1, :, columns].astype(jnp.float32)
                 if hidden:
-                    obuf[j, 0, :, pl.ds(0, m)] = silu_product(gate, up, qbuf[:, :1]).astype(jnp.bfloat16)
+                    obuf[j, 0] = silu_product(gate, up, qbuf[:, :1]).astype(jnp.bfloat16)
                 else:
-                    obuf[j, 0, :, pl.ds(0, m)] = gate.astype(jnp.bfloat16)
-                    obuf[j, 1, :, pl.ds(0, m)] = up.astype(jnp.bfloat16)
-                for copy in write(j, m):
-                    copy.start()
-
-            over_tiles(step)
+                    obuf[j, 0] = gate.astype(jnp.bfloat16)
+                    obuf[j, 1] = up.astype(jnp.bfloat16)
+                with_width(j, send)
 
         def drain():
             def step(j, m):

time: 211 us -> 212 us (level)
  transfers between devices with their start and end apart: 36 -> 36, of which waited for: 11 -> 11; matrix products, arithmetic and copies ran while one was open for 1% -> 1% of each run, Pallas kernels for 63% -> 64%
where the time goes in v14:
time: 212 us
  Pallas kernels  136 us (64%)
  waiting for transfers between devices  43.7 us (21%)
  starting transfers between devices  26.5 us (12%)
  other arithmetic  4.99 us (2%)
    pallas_call x17, Pallas kernels, run(): pl.pallas_call(kernel, out_shape=outs, in_specs=[SMEM] + [ANY] * len(oper...  136 us
    ppermute x36, waiting for transfers between devices, swap(): return lax.ppermute(value, axis, [(i, i ^ mask) for i in range(size)])  43.7 us
    ppermute x36, starting transfers between devices, swap(): return lax.ppermute(value, axis, [(i, i ^ mask) for i in range(size)])  26.5 us
  transfers between devices with their start and end apart: 36, of which 11 were waited for; matrix products, arithmetic and copies ran while one was open for 1% of the time, Pallas kernels for 64%

profile of v14, /device:TPU:0, one launch (start us, length us, event | category | flops | bytes accessed | tf_op | source)
XLA Modules:
  0.0 212.0 jit_solution(16609874415186758735)
XLA Ops:
  0.0 4.0 %collective-permute-start.4 = (bf16[128,2048]{1,0:T(8,128)(2,1)}, bf16[128,2048]{1,0:T(8,128)(2,1)}, u32[]{:S(2)}, u32[]{:S(2)}) collective-permute-start(bf16[128,2048]{1,0:T(8,128)(2,1)} %args_3_.14), channel_id=1, source_target_pairs={{0,2},{1,3},{2,0},{3,1},{4,6},{5,7},{6,4},{7,5},{8,10},{9,11},{10,... | collective-permute-start | bytes 1572872 | tf_op jit(solution)/shard_map/ppermute | solution.py:22
  4.7 8.0 %step_gg.5 = (bf16[128,1920]{1,0:T(8,128)(2,1)}, bf16[128,1792]{1,0:T(8,128)(2,1)}) custom-call(s32[5]{0:T(128)} %pad_add_fusion.table_ref, bf16[2048,6656]{1,0:T(8,128)(2,1)} %args_0_.36, bf16[2048,6656]{1,0:T(8,128)(2,1)} %args_1_.36, bf16[6656,2048]{1,0:T(8,128)(2,1)} %args_2_.36, bf16[128,2048]{1,0:T(8,128)(2,1)} %args_3_.14, bf16[128,2048]{1,0:T(8,128)(2,1)} %args_3_.14), custom_call_target="tpu_custom_call" | custom-call | flops 1000 | bytes 1000 | tf_op jit(solution)/shard_map/step_gg/pallas_call | solution.py:392
  12.7 7.1 %step_gg.6 = (bf16[128,1536]{1,0:T(8,128)(2,1)}, bf16[128,1536]{1,0:T(8,128)(2,1)}) custom-call(s32[5]{0:T(128)} %pad_add_fusion.table_ref, bf16[2048,6656]{1,0:T(8,128)(2,1)} %args_0_.36, bf16[2048,6656]{1,0:T(8,128)(2,1)} %args_1_.36, bf16[6656,2048]{1,0:T(8,128)(2,1)} %args_2_.36, bf16[128,2048]{1,0:T(8,128)(2,1)} %args_3_.14, ...), custom_call_target="tpu_custom_call" | custom-call | flops 1000 | bytes 1000 | tf_op jit(solution)/shard_map/step_gg/pallas_call | solution.py:392
  20.6 5.7 %step_g.10 = (bf16[128,1920]{1,0:T(8,128)(2,1)}, f32[128,128]{1,0:T(8,128)}) custom-call(s32[5]{0:T(128)} %pad_add_fusion.table_ref, bf16[2048,6656]{1,0:T(8,128)(2,1)} %args_0_.36, bf16[2048,6656]{1,0:T(8,128)(2,1)} %args_1_.36, bf16[6656,2048]{1,0:T(8,128)(2,1)} %args_2_.36, bf16[128,2048]{1,0:T(8,128)(2,1)} %args_3_.14, ...), custom_call_target="tpu_custom_call" | custom-call | flops 1000 | bytes 1000 | tf_op jit(solution)/shard_map/step_g/pallas_call | solution.py:392
  29.7 5.2 %step_g.11.args_5_ = bf16[128,1536]{1,0:T(8,128)(2,1)} custom-call(s32[5]{0:T(128)} %pad_add_fusion.table_ref, bf16[2048,6656]{1,0:T(8,128)(2,1)} %args_0_.36, bf16[2048,6656]{1,0:T(8,128)(2,1)} %args_1_.36, bf16[6656,2048]{1,0:T(8,128)(2,1)} %args_2_.36, bf16[128,2048]{1,0:T(8,128)(2,1)} %args_3_.14, bf16[128,1536]{1,0:T(8,128)(2,1)} %collective-permute-done.3.args_4_, ...), custom_call_target="tpu_custom_call" | custom-call | flops 1000 | bytes 1000 | tf_op jit(solution)/shard_map/step_g/pallas_call | solution.py:392
  36.0 6.7 %collective-permute-done.2.args_5_.args_7_ = bf16[128,1920]{1,0:T(8,128)(2,1)} collective-permute-done((bf16[128,1920]{1,0:T(8,128)(2,1)}, bf16[128,1920]{1,0:T(8,128)(2,1)}, u32[]{:S(2)}, u32[]{:S(2)}) %collective-permute-start.2) | collective-permute-done | bytes 491552 | tf_op jit(solution)/shard_map/ppermute | solution.py:22
  42.7 9.3 %step_gg.7 = (bf16[256,1920]{1,0:T(8,128)(2,1)}, bf16[256,1792]{1,0:T(8,128)(2,1)}) custom-call(s32[5]{0:T(128)} %pad_add_fusion.table_ref, bf16[2048,6656]{1,0:T(8,128)(2,1)} %args_0_.36, bf16[2048,6656]{1,0:T(8,128)(2,1)} %args_1_.36, bf16[6656,2048]{1,0:T(8,128)(2,1)} %args_2_.36, bf16[128,2048]{1,0:T(8,128)(2,1)} %collective-permute-done.4.args_3_, ...), custom_call_target="tpu_custom_call" | custom-call | flops 1000 | bytes 1000 | tf_op jit(solution)/shard_map/step_gg/pallas_call | solution.py:392
  52.0 7.8 %step_gg.8 = (bf16[256,1536]{1,0:T(8,128)(2,1)}, bf16[256,1536]{1,0:T(8,128)(2,1)}) custom-call(s32[5]{0:T(128)} %pad_add_fusion.table_ref, bf16[2048,6656]{1,0:T(8,128)(2,1)} %args_0_.36, bf16[2048,6656]{1,0:T(8,128)(2,1)} %args_1_.36, bf16[6656,2048]{1,0:T(8,128)(2,1)} %args_2_.36, bf16[128,2048]{1,0:T(8,128)(2,1)} %collective-permute-done.4.args_3_, ...), custom_call_target="tpu_custom_call" | custom-call | flops 99999997952 | bytes 1000 | tf_op jit(solution)/shard_map/step_gg/pallas_call | solution.py:392
  59.8 6.6 %step_g.12 = (bf16[256,1920]{1,0:T(8,128)(2,1)}, f32[256,128]{1,0:T(8,128)}) custom-call(s32[5]{0:T(128)} %pad_add_fusion.table_ref, bf16[2048,6656]{1,0:T(8,128)(2,1)} %args_0_.36, bf16[2048,6656]{1,0:T(8,128)(2,1)} %args_1_.36, bf16[6656,2048]{1,0:T(8,128)(2,1)} %args_2_.36, bf16[128,2048]{1,0:T(8,128)(2,1)} %collective-permute-done.4.args_3_, ...), custom_call_target="tpu_custom_call" | custom-call | flops 1000 | bytes 1000 | tf_op jit(solution)/shard_map/step_g/pallas_call | solution.py:392
  70.1 5.9 %step_g.13.args_8_.args_3_ = bf16[128,896]{1,0:T(8,128)(2,1)} custom-call(s32[5]{0:T(128)} %pad_add_fusion.table_ref, bf16[2048,6656]{1,0:T(8,128)(2,1)} %args_0_.36, bf16[2048,6656]{1,0:T(8,128)(2,1)} %args_1_.36, bf16[6656,2048]{1,0:T(8,128)(2,1)} %args_2_.36, bf16[128,2048]{1,0:T(8,128)(2,1)} %args_3_.14, bf16[128,1792]{1,0:T(8,128)(2,1)} %collective-permute-done.args_4_, ...), custom_call_target="tpu_custom_call" | custom-call | flops 1000 | bytes 1000 | tf_op jit(solution)/shard_map/step_g/pallas_call | solution.py:392
  76.0 5.3 %step_g.14.args_6_.args_7_ = bf16[128,768]{1,0:T(8,128)(2,1)} custom-call(s32[5]{0:T(128)} %pad_add_fusion.table_ref, bf16[2048,6656]{1,0:T(8,128)(2,1)} %args_0_.36, bf16[2048,6656]{1,0:T(8,128)(2,1)} %args_1_.36, bf16[6656,2048]{1,0:T(8,128)(2,1)} %args_2_.36, bf16[128,2048]{1,0:T(8,128)(2,1)} %args_3_.14, ...), custom_call_target="tpu_custom_call" | custom-call | flops 1000 | bytes 1000 | tf_op jit(solution)/shard_map/step_g/pallas_call | solution.py:392
  82.0 5.8 %step_g.15.args_4_ = bf16[256,1536]{1,0:T(8,128)(2,1)} custom-call(s32[5]{0:T(128)} %pad_add_fusion.table_ref, bf16[2048,6656]{1,0:T(8,128)(2,1)} %args_0_.36, bf16[2048,6656]{1,0:T(8,128)(2,1)} %args_1_.36, bf16[6656,2048]{1,0:T(8,128)(2,1)} %args_2_.36, bf16[128,2048]{1,0:T(8,128)(2,1)} %collective-permute-done.4.args_3_, ...), custom_call_target="tpu_custom_call" | custom-call | flops 1000 | bytes 1000 | tf_op jit(solution)/shard_map/step_g/pallas_call | solution.py:392
  89.4 12.2 %step_gg.9 = (bf16[128,3456]{1,0:T(8,128)(2,1)}, bf16[128,3328]{1,0:T(8,128)(2,1)}) custom-call(s32[5]{0:T(128)} %pad_add_fusion.table_ref, bf16[2048,6656]{1,0:T(8,128)(2,1)} %args_0_.36, bf16[2048,6656]{1,0:T(8,128)(2,1)} %args_1_.36, bf16[6656,2048]{1,0:T(8,128)(2,1)} %args_2_.36, bf16[128,2048]{1,0:T(8,128)(2,1)} %collective-permute-done.16.args_3_, ...), custom_call_target="tpu_custom_call" | custom-call | flops 1000 | bytes 1000 | tf_op jit(solution)/shard_map/step_gg/pallas_call | solution.py:392
  102.8 7.1 %step_g.16.args_9_.args_3_ = bf16[256,896]{1,0:T(8,128)(2,1)} custom-call(s32[5]{0:T(128)} %pad_add_fusion.table_ref, bf16[2048,6656]{1,0:T(8,128)(2,1)} %args_0_.36, bf16[2048,6656]{1,0:T(8,128)(2,1)} %args_1_.36, bf16[6656,2048]{1,0:T(8,128)(2,1)} %args_2_.36, bf16[128,2048]{1,0:T(8,128)(2,1)} %collective-permute-done.4.args_3_, ...), custom_call_target="tpu_custom_call" | custom-call | flops 99999997952 | bytes 1000 | tf_op jit(solution)/shard_map/step_g/pallas_call | solution.py:392
  114.6 6.3 %step_g.17.args_5_.args_7_ = bf16[256,768]{1,0:T(8,128)(2,1)} custom-call(s32[5]{0:T(128)} %pad_add_fusion.table_ref, bf16[2048,6656]{1,0:T(8,128)(2,1)} %args_0_.36, bf16[2048,6656]{1,0:T(8,128)(2,1)} %args_1_.36, bf16[6656,2048]{1,0:T(8,128)(2,1)} %args_2_.36, bf16[128,2048]{1,0:T(8,128)(2,1)} %collective-permute-done.4.args_3_, ...), custom_call_target="tpu_custom_call" | custom-call | flops 1000 | bytes 1000 | tf_op jit(solution)/shard_map/step_g/pallas_call | solution.py:392
  122.9 7.8 %step_g.18 = (bf16[128,3456]{1,0:T(8,128)(2,1)}, f32[128,128]{1,0:T(8,128)}) custom-call(s32[5]{0:T(128)} %pad_add_fusion.table_ref, bf16[2048,6656]{1,0:T(8,128)(2,1)} %args_0_.36, bf16[2048,6656]{1,0:T(8,128)(2,1)} %args_1_.36, bf16[6656,2048]{1,0:T(8,128)(2,1)} %args_2_.36, bf16[128,2048]{1,0:T(8,128)(2,1)} %collective-permute-done.16.args_3_, ...), custom_call_target="tpu_custom_call" | custom-call | flops 1000 | bytes 1000 | tf_op jit(solution)/shard_map/step_g/pallas_call | solution.py:392
  131.4 3.9 %collective-permute-done.28.args_9_ = bf16[256,768]{1,0:T(8,128)(2,1)} collective-permute-done((bf16[256,768]{1,0:T(8,128)(2,1)}, bf16[256,768]{1,0:T(8,128)(2,1)}, u32[]{:S(2)}, u32[]{:S(2)}) %collective-permute-start.28) | collective-permute-done | bytes 393248 | tf_op jit(solution)/shard_map/ppermute | solution.py:22
  137.3 13.8 %step_d.2 = (bf16[128,2048]{1,0:T(8,128)(2,1)}, bf16[128,2048]{1,0:T(8,128)(2,1)}) custom-call(s32[5]{0:T(128)} %pad_add_fusion.table_ref, bf16[2048,6656]{1,0:T(8,128)(2,1)} %args_0_.36, bf16[2048,6656]{1,0:T(8,128)(2,1)} %args_1_.36, bf16[6656,2048]{1,0:T(8,128)(2,1)} %args_2_.36, bf16[256,896]{1,0:T(8,128)(2,1)} %step_g.16.args_9_.args_3_, ...), custom_call_target="tpu_custom_call" | custom-call | flops 1000 | bytes 1000 | tf_op jit(solution)/shard_map/step_d/pallas_call | solution.py:392
  152.5 5.1 %collective-permute-done.23.args_5_ = bf16[128,3456]{1,0:T(8,128)(2,1)} collective-permute-done((bf16[128,3456]{1,0:T(8,128)(2,1)}, bf16[128,3456]{1,0:T(8,128)(2,1)}, u32[]{:S(2)}, u32[]{:S(2)}) %collective-permute-start.23) | collective-permute-done | bytes 884768 | tf_op jit(solution)/shard_map/ppermute | solution.py:22
  157.6 8.1 %step_g.19.args_11_.args_15_ = bf16[128,1664]{1,0:T(8,128)(2,1)} custom-call(s32[5]{0:T(128)} %pad_add_fusion.table_ref, bf16[2048,6656]{1,0:T(8,128)(2,1)} %args_0_.36, bf16[2048,6656]{1,0:T(8,128)(2,1)} %args_1_.36, bf16[6656,2048]{1,0:T(8,128)(2,1)} %args_2_.36, bf16[128,2048]{1,0:T(8,128)(2,1)} %collective-permute-done.16.args_3_, ...), custom_call_target="tpu_custom_call" | custom-call | flops 1000 | bytes 1000 | tf_op jit(solution)/shard_map/step_g/pallas_call | solution.py:392
  169.4 3.4 %collective-permute-start.34 = (bf16[128,2048]{1,0:T(8,128)(2,1)}, bf16[128,2048]{1,0:T(8,128)(2,1)}, u32[]{:S(2)}, u32[]{:S(2)}) collective-permute-start(bf16[128,2048]{1,0:T(8,128)(2,1)} %add_convert_fusion.1), channel_id=1, source_target_pairs={{0,2},{1,3},{2,0},{3,1},{4,6},{5,7},{6,4},{7,5},{8,10},{9,11},{10,... | collective-permute-start | bytes 1572872 | tf_op jit(solution)/shard_map/ppermute | solution.py:22
  172.8 4.7 %collective-permute-done.31.args_13_ = bf16[128,1664]{1,0:T(8,128)(2,1)S(1)} collective-permute-done((bf16[128,1664]{1,0:T(8,128)(2,1)}, bf16[128,1664]{1,0:T(8,128)(2,1)S(1)}, u32[]{:S(2)}, u32[]{:S(2)}) %collective-permute-start.31) | collective-permute-done | bytes 426016 | tf_op jit(solution)/shard_map/ppermute | solution.py:22
  180.1 13.9 %step_d.3 = (bf16[128,2048]{1,0:T(8,128)(2,1)}, bf16[128,2048]{1,0:T(8,128)(2,1)}) custom-call(s32[5]{0:T(128)} %pad_add_fusion.table_ref, bf16[2048,6656]{1,0:T(8,128)(2,1)} %args_0_.36, bf16[2048,6656]{1,0:T(8,128)(2,1)} %args_1_.36, bf16[6656,2048]{1,0:T(8,128)(2,1)} %args_2_.36, bf16[128,896]{1,0:T(8,128)(2,1)} %step_g.13.args_8_.args_3_, ...), custom_call_target="tpu_custom_call" | custom-call | flops 1000 | bytes 1000 | tf_op jit(solution)/shard_map/step_d/pallas_call | solution.py:392
  195.8 14.0 %collective-permute-done.35 = bf16[128,2048]{1,0:T(8,128)(2,1)S(1)} collective-permute-done((bf16[128,2048]{1,0:T(8,128)(2,1)}, bf16[128,2048]{1,0:T(8,128)(2,1)S(1)}, u32[]{:S(2)}, u32[]{:S(2)}) %collective-permute-start.35) | collective-permute-done | bytes 524320 | tf_op jit(solution)/shard_map/ppermute | solution.py:22
  (71 shorter events, 34.2 us)
Async XLA Ops:
  0.0 27.5 %collective-permute-start.4 = (bf16[128,2048]{1,0:T(8,128)(2,1)}, bf16[128,2048]{1,0:T(8,128)(2,1)}, u32[]{:S(2)}, u32[]{:S(2)}) collective-permute-start(bf16[128,2048]{1,0:T(8,128)(2,1)} %args_3_.14), channel_id=1, source_target_pairs={{0,2},{1,3},{2,0},{3,1},{4,6},{5,7},{6,4},{7,5},{8,10},{9,11},{10,... | collective-permute-start | bytes 1572872 | tf_op jit(solution)/shard_map/ppermute | solution.py:22
  27.5 15.2 %collective-permute-start.5 = (bf16[128,2048]{1,0:T(8,128)(2,1)}, bf16[128,2048]{1,0:T(8,128)(2,1)}, u32[]{:S(2)}, u32[]{:S(2)}) collective-permute-start(bf16[128,2048]{1,0:T(8,128)(2,1)} %collective-permute-done.4.args_3_), channel_id=1, source_target_pairs={{0,1},{1,0},{2,3},{3,2},{4,5},{5,4},{6,7},{7,6},{8,9},{9,8},{10,11... | collective-permute-start | bytes 1572872 | tf_op jit(solution)/shard_map/ppermute | solution.py:22
  28.2 14.4 %collective-permute-start.2 = (bf16[128,1920]{1,0:T(8,128)(2,1)}, bf16[128,1920]{1,0:T(8,128)(2,1)}, u32[]{:S(2)}, u32[]{:S(2)}) collective-permute-start(bf16[128,1920]{1,0:T(8,128)(2,1)} %get-tuple-element.61.args_5_), channel_id=1, source_target_pairs={{0,8},{4,12},{8,0},{12,4},{1,9},{5,13},{9,1},{13,5},{2,10},{6,14},... | collective-permute-start | bytes 1474568 | tf_op jit(solution)/shard_map/ppermute | solution.py:22
  34.9 17.1 %collective-permute-start.7 = (bf16[128,1536]{1,0:T(8,128)(2,1)}, bf16[128,1536]{1,0:T(8,128)(2,1)}, u32[]{:S(2)}, u32[]{:S(2)}) collective-permute-start(bf16[128,1536]{1,0:T(8,128)(2,1)} %step_g.11.args_5_), channel_id=1, source_target_pairs={{0,8},{4,12},{8,0},{12,4},{1,9},{5,13},{9,1},{13,5},{2,10},{6,14},... | collective-permute-start | bytes 1179656 | tf_op jit(solution)/shard_map/ppermute | solution.py:22
  35.4 33.3 %collective-permute-start = (bf16[128,1792]{1,0:T(8,128)(2,1)}, bf16[128,1792]{1,0:T(8,128)(2,1)}, u32[]{:S(2)}, u32[]{:S(2)}) collective-permute-start(bf16[128,1792]{1,0:T(8,128)(2,1)} %get-tuple-element.57), channel_id=1, source_target_pairs={{0,4},{4,0},{8,12},{12,8},{1,5},{5,1},{9,13},{13,9},{2,6},{6,2},{1... | collective-permute-start | bytes 1376264 | tf_op jit(solution)/shard_map/ppermute | solution.py:22
  35.4 33.0 %collective-permute-start.12 = (bf16[128,1536]{1,0:T(8,128)(2,1)}, bf16[128,1536]{1,0:T(8,128)(2,1)}, u32[]{:S(2)}, u32[]{:S(2)}) collective-permute-start(bf16[128,1536]{1,0:T(8,128)(2,1)} %get-tuple-element.71), channel_id=1, source_target_pairs={{0,4},{4,0},{8,12},{12,8},{1,5},{5,1},{9,13},{13,9},{2,6},{6,2},{1... | collective-permute-start | bytes 1179656 | tf_op jit(solution)/shard_map/ppermute | solution.py:22
  66.4 35.9 %collective-permute-start.14 = (bf16[256,1920]{1,0:T(8,128)(2,1)}, bf16[256,1920]{1,0:T(8,128)(2,1)}, u32[]{:S(2)}, u32[]{:S(2)}) collective-permute-start(bf16[256,1920]{1,0:T(8,128)(2,1)} %get-tuple-element.69.args_7_), channel_id=1, source_target_pairs={{0,8},{4,12},{8,0},{12,4},{1,9},{5,13},{9,1},{13,5},{2,10},{6,14},... | collective-permute-start | bytes 2949128 | tf_op jit(solution)/shard_map/ppermute | solution.py:22
  68.0 34.3 %collective-permute-start.15 = (bf16[256,1792]{1,0:T(8,128)(2,1)}, bf16[256,1792]{1,0:T(8,128)(2,1)}, u32[]{:S(2)}, u32[]{:S(2)}) collective-permute-start(bf16[256,1792]{1,0:T(8,128)(2,1)} %get-tuple-element.74), channel_id=1, source_target_pairs={{0,4},{4,0},{8,12},{12,8},{1,5},{5,1},{9,13},{13,9},{2,6},{6,2},{1... | collective-permute-start | bytes 2752520 | tf_op jit(solution)/shard_map/ppermute | solution.py:22
  68.2 13.2 %collective-permute-start.11 = (bf16[256,1536]{1,0:T(8,128)(2,1)}, bf16[256,1536]{1,0:T(8,128)(2,1)}, u32[]{:S(2)}, u32[]{:S(2)}) collective-permute-start(bf16[256,1536]{1,0:T(8,128)(2,1)} %get-tuple-element.68.args_6_), channel_id=1, source_target_pairs={{0,4},{4,0},{8,12},{12,8},{1,5},{5,1},{9,13},{13,9},{2,6},{6,2},{1... | collective-permute-start | bytes 2359304 | tf_op jit(solution)/shard_map/ppermute | solution.py:22
  68.5 33.2 %collective-permute-start.10 = (bf16[256,1536]{1,0:T(8,128)(2,1)}, bf16[256,1536]{1,0:T(8,128)(2,1)}, u32[]{:S(2)}, u32[]{:S(2)}) collective-permute-start(bf16[256,1536]{1,0:T(8,128)(2,1)} %get-tuple-element.70), channel_id=1, source_target_pairs={{0,4},{4,0},{8,12},{12,8},{1,5},{5,1},{9,13},{13,9},{2,6},{6,2},{1... | collective-permute-start | bytes 2359304 | tf_op jit(solution)/shard_map/ppermute | solution.py:22
  68.7 19.1 %collective-permute-start.16 = (bf16[128,2048]{1,0:T(8,128)(2,1)}, bf16[128,2048]{1,0:T(8,128)(2,1)}, u32[]{:S(2)}, u32[]{:S(2)}) collective-permute-start(bf16[128,2048]{1,0:T(8,128)(2,1)} %args_3_.14), channel_id=1, source_target_pairs={{0,1},{1,0},{2,3},{3,2},{4,5},{5,4},{6,7},{7,6},{8,9},{9,8},{10,11... | collective-permute-start | bytes 1572872 | tf_op jit(solution)/shard_map/ppermute | solution.py:22
  81.4 39.5 %collective-permute-start.9 = (bf16[128,896]{1,0:T(8,128)(2,1)}, bf16[128,896]{1,0:T(8,128)(2,1)}, u32[]{:S(2)}, u32[]{:S(2)}) collective-permute-start(bf16[128,896]{1,0:T(8,128)(2,1)} %step_g.13.args_8_.args_3_), channel_id=1, source_target_pairs={{0,8},{4,12},{8,0},{12,4},{1,9},{5,13},{9,1},{13,5},{2,10},{6,14},... | collective-permute-start | bytes 688136 | tf_op jit(solution)/shard_map/ppermute | solution.py:22
  87.8 25.3 %collective-permute-start.13 = (bf16[256,1536]{1,0:T(8,128)(2,1)}, bf16[256,1536]{1,0:T(8,128)(2,1)}, u32[]{:S(2)}, u32[]{:S(2)}) collective-permute-start(bf16[256,1536]{1,0:T(8,128)(2,1)} %step_g.15.args_4_), channel_id=1, source_target_pairs={{0,8},{4,12},{8,0},{12,4},{1,9},{5,13},{9,1},{13,5},{2,10},{6,14},... | collective-permute-start | bytes 2359304 | tf_op jit(solution)/shard_map/ppermute | solution.py:22
  101.6 19.3 %collective-permute-start.19 = (bf16[128,768]{1,0:T(8,128)(2,1)}, bf16[128,768]{1,0:T(8,128)(2,1)}, u32[]{:S(2)}, u32[]{:S(2)}) collective-permute-start(bf16[128,768]{1,0:T(8,128)(2,1)} %step_g.14.args_6_.args_7_), channel_id=1, source_target_pairs={{0,8},{4,12},{8,0},{12,4},{1,9},{5,13},{9,1},{13,5},{2,10},{6,14},... | collective-permute-start | bytes 589832 | tf_op jit(solution)/shard_map/ppermute | solution.py:22
  102.3 19.3 %collective-permute-start.8 = (bf16[128,896]{1,0:T(8,128)(2,1)}, bf16[128,896]{1,0:T(8,128)(2,1)}, u32[]{:S(2)}, u32[]{:S(2)}) collective-permute-start(bf16[128,896]{1,0:T(8,128)(2,1)} %step_g.13.args_8_.args_3_), channel_id=1, source_target_pairs={{0,4},{4,0},{8,12},{12,8},{1,5},{5,1},{9,13},{13,9},{2,6},{6,2},{1... | collective-permute-start | bytes 688136 | tf_op jit(solution)/shard_map/ppermute | solution.py:22
  102.3 19.5 %collective-permute-start.18 = (bf16[128,3456]{1,0:T(8,128)(2,1)}, bf16[128,3456]{1,0:T(8,128)(2,1)}, u32[]{:S(2)}, u32[]{:S(2)}) collective-permute-start(bf16[128,3456]{1,0:T(8,128)(2,1)} %get-tuple-element.77.args_8_), channel_id=1, source_target_pairs={{0,4},{4,0},{8,12},{12,8},{1,5},{5,1},{9,13},{13,9},{2,6},{6,2},{1... | collective-permute-start | bytes 2654216 | tf_op jit(solution)/shard_map/ppermute | solution.py:22
  113.1 18.1 %collective-permute-start.25 = (bf16[256,896]{1,0:T(8,128)(2,1)}, bf16[256,896]{1,0:T(8,128)(2,1)}, u32[]{:S(2)}, u32[]{:S(2)}) collective-permute-start(bf16[256,896]{1,0:T(8,128)(2,1)} %step_g.16.args_9_.args_3_), channel_id=1, source_target_pairs={{0,8},{4,12},{8,0},{12,4},{1,9},{5,13},{9,1},{13,5},{2,10},{6,14},... | collective-permute-start | bytes 1376264 | tf_op jit(solution)/shard_map/ppermute | solution.py:22
  121.0 14.3 %collective-permute-start.28 = (bf16[256,768]{1,0:T(8,128)(2,1)}, bf16[256,768]{1,0:T(8,128)(2,1)}, u32[]{:S(2)}, u32[]{:S(2)}) collective-permute-start(bf16[256,768]{1,0:T(8,128)(2,1)} %step_g.17.args_5_.args_7_), channel_id=1, source_target_pairs={{0,8},{4,12},{8,0},{12,4},{1,9},{5,13},{9,1},{13,5},{2,10},{6,14},... | collective-permute-start | bytes 1179656 | tf_op jit(solution)/shard_map/ppermute | solution.py:22
  121.6 15.1 %collective-permute-start.27 = (bf16[256,768]{1,0:T(8,128)(2,1)}, bf16[256,768]{1,0:T(8,128)(2,1)}, u32[]{:S(2)}, u32[]{:S(2)}) collective-permute-start(bf16[256,768]{1,0:T(8,128)(2,1)} %step_g.17.args_5_.args_7_), channel_id=1, source_target_pairs={{0,4},{4,0},{8,12},{12,8},{1,5},{5,1},{9,13},{13,9},{2,6},{6,2},{1... | collective-permute-start | bytes 1179656 | tf_op jit(solution)/shard_map/ppermute | solution.py:22
  135.3 22.4 %collective-permute-start.23 = (bf16[128,3456]{1,0:T(8,128)(2,1)}, bf16[128,3456]{1,0:T(8,128)(2,1)}, u32[]{:S(2)}, u32[]{:S(2)}) collective-permute-start(bf16[128,3456]{1,0:T(8,128)(2,1)} %get-tuple-element.98.args_11_), channel_id=1, source_target_pairs={{0,8},{4,12},{8,0},{12,4},{1,9},{5,13},{9,1},{13,5},{2,10},{6,14},... | collective-permute-start | bytes 2654216 | tf_op jit(solution)/shard_map/ppermute | solution.py:22
  136.7 15.8 %collective-permute-start.22 = (bf16[128,3328]{1,0:T(8,128)(2,1)}, bf16[128,3328]{1,0:T(8,128)(2,1)}, u32[]{:S(2)}, u32[]{:S(2)}) collective-permute-start(bf16[128,3328]{1,0:T(8,128)(2,1)} %get-tuple-element.92), channel_id=1, source_target_pairs={{0,4},{4,0},{8,12},{12,8},{1,5},{5,1},{9,13},{13,9},{2,6},{6,2},{1... | collective-permute-start | bytes 2555912 | tf_op jit(solution)/shard_map/ppermute | solution.py:22
  151.1 16.1 %collective-permute-start.32 = (bf16[128,2048]{1,0:T(8,128)(2,1)}, bf16[128,2048]{1,0:T(8,128)(2,1)}, u32[]{:S(2)}, u32[]{:S(2)}) collective-permute-start(bf16[128,2048]{1,0:T(8,128)(2,1)} %get-tuple-element.100), channel_id=1, source_target_pairs={{0,1},{1,0},{2,3},{3,2},{4,5},{5,4},{6,7},{7,6},{8,9},{9,8},{10,11... | collective-permute-start | bytes 1572872 | tf_op jit(solution)/shard_map/ppermute | solution.py:22
  169.4 26.5 %collective-permute-start.34 = (bf16[128,2048]{1,0:T(8,128)(2,1)}, bf16[128,2048]{1,0:T(8,128)(2,1)}, u32[]{:S(2)}, u32[]{:S(2)}) collective-permute-start(bf16[128,2048]{1,0:T(8,128)(2,1)} %add_convert_fusion.1), channel_id=1, source_target_pairs={{0,2},{1,3},{2,0},{3,1},{4,6},{5,7},{6,4},{7,5},{8,10},{9,11},{10,... | collective-permute-start | bytes 1572872 | tf_op jit(solution)/shard_map/ppermute | solution.py:22
  195.8 14.0 %collective-permute-start.35 = (bf16[128,2048]{1,0:T(8,128)(2,1)}, bf16[128,2048]{1,0:T(8,128)(2,1)S(1)}, u32[]{:S(2)}, u32[]{:S(2)}) collective-permute-start(bf16[128,2048]{1,0:T(8,128)(2,1)} %get-tuple-element.108), channel_id=1, source_target_pairs={{0,1},{1,0},{2,3},{3,2},{4,5},{5,4},{6,7},{7,6},{8,9},{9,8},{10,11... | collective-permute-start | bytes 1572872 | tf_op jit(solution)/shard_map/ppermute | solution.py:22
  (13 other events, 79.3 us)
